TPU v7x, 32 devices: a whole 2x2x4 slice. The times are simulated.
32 devices in a mesh: dp: 8 (over y, x, core), seq: 4 (over z).
Axes of the slice: x: 2, y: 2, z: 4, core: 2. Of those that a mesh axis runs over, the one named last changes fastest.
Arguments:
- hidden: bfloat16 [8, 1024, 1536], P('dp', 'seq'), may hold values from -6 to 6
- pad_mask: int32 [8, 1024], P('dp', 'seq'), may hold values 0 or 1
- timestep: int32 [8], P('dp'), may hold values from 0 to 999
- input_weight: bfloat16 [1536, 6144], P(('dp', 'seq')), may hold values from -0.15625 to 0.15625
- select_weight: bfloat16 [3072, 128], P(('dp', 'seq')), may hold values from -0.109375 to 0.109375
- step_weight: bfloat16 [96, 3072], P(None, ('dp', 'seq')), may hold values from -0.625 to 0.625
- output_weight: bfloat16 [3072, 1536], P(None, ('dp', 'seq')), may hold values from -0.109375 to 0.109375
- decay_forward: bfloat16 [3072, 16], P(('dp', 'seq')), may hold values from -8 to 0.69921875
- decay_reverse: bfloat16 [3072, 16], P(('dp', 'seq')), may hold values from -8 to 0.69921875
- filter_weight: bfloat16 [4, 3072], P(None, ('dp', 'seq')), may hold values from -3 to 3
- filter_bias: bfloat16 [3072], P(('dp', 'seq')), may hold values from -3 to 3
- step_bias: bfloat16 [3072], P(('dp', 'seq')), may hold values from -4 to -1
- modulation_weight: bfloat16 [256, 4608], P(('dp', 'seq')), may hold values from -0.375 to 0.375
- modulation_bias: bfloat16 [4608], P(('dp', 'seq')), may hold values from -3 to 3
- cotangent: bfloat16 [8, 1024, 1536], P('dp', 'seq'), may hold values from -6 to 6
Outputs:
- block_out: bfloat16 [8, 1024, 1536], P('dp', 'seq')
- grad_hidden: bfloat16 [8, 1024, 1536], P('dp', 'seq')
- grad_input_weight: float32 [1536, 6144], P(('dp', 'seq'))
- grad_select_weight: float32 [3072, 128], P(('dp', 'seq'))
- grad_step_weight: float32 [96, 3072], P(None, ('dp', 'seq'))
- grad_output_weight: float32 [3072, 1536], P(None, ('dp', 'seq'))
- grad_decay_forward: float32 [3072, 16], P(('dp', 'seq'))
- grad_decay_reverse: float32 [3072, 16], P(('dp', 'seq'))
- grad_filter_weight: float32 [4, 3072], P(None, ('dp', 'seq'))
- grad_filter_bias: float32 [3072], P(('dp', 'seq'))
- grad_step_bias: float32 [3072], P(('dp', 'seq'))
- grad_modulation_weight: float32 [256, 4608], P(('dp', 'seq'))
- grad_modulation_bias: float32 [4608], P(('dp', 'seq'))
All inputs are finite; a program needn't handle non-finite values. No bound on the sum of `pad_mask` on one device may be relied on, other than what follows from the above.
Results may differ from a plain program's by a relative error of at most 0.01.
Values may be sent and summed in bfloat16 or wider, within the bound.
A program may use at most 184 MiB of HBM per device.

v0:
```python
import math

import jax
import jax.numpy as jnp
from jax import lax
from jax.sharding import PartitionSpec as P

FREQ = 256
BLOCK = 8


EPS = 1e-06
HIGHEST = lax.Precision.HIGHEST


def shifted(value, axis, steps):
    count = lax.axis_size(axis)
    first, last = (max(0, -steps), min(count, count - steps))
    return lax.ppermute(value, axis, [(source, source + steps) for source in range(first, last)])


def carried_in(value, axis, combine, identity, reverse):
    length, place = (lax.axis_size(axis), lax.axis_index(axis))
    everything = jax.tree.map(
        lambda part, kind: lax.all_gather(part.astype(kind), axis),
        value,
        (jnp.bfloat16, jnp.bfloat16),
    )
    start = jax.tree.map(
        lambda part, zero: jnp.broadcast_to(jnp.asarray(zero, part.dtype), part.shape),
        value,
        identity,
    )

    def lap(k, before):
        at = length - 1 - k if reverse else k
        reached = at > place if reverse else at < place
        new = combine(
            before, jax.tree.map(lambda part, own: part[at].astype(own.dtype), everything, value)
        )
        return jax.tree.map(lambda a, b: jnp.where(reached, a, b), new, before)

    return lax.fori_loop(0, length, lap, start)


def shortened(value):

    def short(part):
        return part.astype(jnp.bfloat16) if part.dtype == jnp.float32 else part

    return jax.tree.map(short, value)


def frequency_embed(timestep):
    half_width = FREQ // 2
    counter = jnp.arange(half_width, dtype=jnp.float32)
    frequency = jnp.exp(counter * (-math.log(10000.0) / half_width))
    angles = timestep.astype(jnp.float32)[:, None] * frequency[None, :]
    return jnp.concatenate([jnp.cos(angles), jnp.sin(angles)], axis=1)


def compose(earlier, later):
    return (earlier[0] * later[0], later[0] * earlier[1] + later[1])


def to_blocks(array_in):
    num_blocks = array_in.shape[1] // BLOCK
    shaped = array_in.reshape(array_in.shape[0], num_blocks, BLOCK, array_in.shape[2])
    return jnp.moveaxis(shaped, 1, 0)


def from_blocks(array_in):
    joined = jnp.moveaxis(array_in, 0, 1)
    return joined.reshape(joined.shape[0], joined.shape[1] * BLOCK, joined.shape[3])


def advance(current, rates, step_col, drive_col, b_col):
    decays = jnp.exp(step_col[:, :, None] * rates)
    return decays * current + (step_col * drive_col)[:, :, None] * b_col[:, None, :]


def scan_states(steps, drives, b_rows, c_rows, rates, start_state, with_out):

    def one_block(current, pieces):
        step_b, drive_b, b_block, c_block = pieces
        first_state = current
        outputs = []
        for offset in range(BLOCK):
            current = advance(
                current, rates, step_b[:, offset], drive_b[:, offset], b_block[:, offset]
            )
            if with_out:
                outputs.append(jnp.sum(current * c_block[:, offset, None, :], axis=2))
        if with_out:
            return (current, (jnp.stack(outputs, axis=1), first_state))
        return (current, None)

    pieces = (to_blocks(steps), to_blocks(drives), to_blocks(b_rows), to_blocks(c_rows))
    end_state, kept_out = lax.scan(one_block, start_state, pieces)
    if with_out:
        return (end_state, from_blocks(kept_out[0]), kept_out[1])
    return end_state


def adjoint_start(steps, c_rows, grad_y, rates):

    def one_block(carry, pieces):
        totals, summed = carry
        step_b, c_block, grad_block = pieces
        for offset in range(BLOCK):
            totals = totals + step_b[:, offset]
            summed = summed + jnp.exp(totals[:, :, None] * rates) * (
                grad_block[:, offset, :, None] * c_block[:, offset, None, :]
            )
        return ((totals, summed), None)

    initial = (
        jnp.zeros((steps.shape[0], steps.shape[2]), jnp.float32),
        jnp.zeros((steps.shape[0], steps.shape[2], rates.shape[1]), jnp.float32),
    )
    (unused, summed), nothing = lax.scan(
        one_block, initial, (to_blocks(steps), to_blocks(c_rows), to_blocks(grad_y))
    )
    return summed


def scan_grads(steps, drives, b_rows, c_rows, grad_y, rates, starts, passed_in):

    def one_block(carry, pieces):
        passed, grad_rate = carry
        step_b, drive_b, b_block, c_block, grad_block, start_block = pieces
        states_all = [start_block]
        for offset in range(BLOCK):
            states_all.append(
                advance(
                    states_all[-1], rates, step_b[:, offset], drive_b[:, offset], b_block[:, offset]
                )
            )
        step_grads = [None] * BLOCK
        drive_grads = [None] * BLOCK
        b_grads = [None] * BLOCK
        c_grads = [None] * BLOCK
        for offset in reversed(range(BLOCK)):
            step_col = step_b[:, offset]
            decays = jnp.exp(step_col[:, :, None] * rates)
            adjoint = grad_block[:, offset, :, None] * c_block[:, offset, None, :] + passed
            passed = decays * adjoint
            log_grad = adjoint * states_all[offset] * decays
            grad_rate = grad_rate + jnp.sum(log_grad * step_col[:, :, None], axis=0)
            adjoint_b = jnp.sum(adjoint * b_block[:, offset, None, :], axis=2)
            step_grads[offset] = jnp.sum(log_grad * rates, axis=2) + drive_b[:, offset] * adjoint_b
            drive_grads[offset] = step_col * adjoint_b
            b_grads[offset] = jnp.sum(adjoint * (step_col * drive_b[:, offset])[:, :, None], axis=1)
            c_grads[offset] = jnp.sum(
                grad_block[:, offset, :, None] * states_all[offset + 1], axis=1
            )
        stacked = (
            jnp.stack(step_grads, axis=1),
            jnp.stack(drive_grads, axis=1),
            jnp.stack(b_grads, axis=1),
            jnp.stack(c_grads, axis=1),
        )
        return ((passed, grad_rate), stacked)

    pieces = (
        to_blocks(steps),
        to_blocks(drives),
        to_blocks(b_rows),
        to_blocks(c_rows),
        to_blocks(grad_y),
        starts,
    )
    initial = (passed_in, jnp.zeros(rates.shape, jnp.float32))
    (unused, grad_rate), grads = lax.scan(one_block, initial, pieces, reverse=True)
    return (
        from_blocks(grads[0]),
        from_blocks(grads[1]),
        from_blocks(grads[2]),
        from_blocks(grads[3]),
        grad_rate,
    )


def body(
    hidden,
    pad_mask,
    timestep,
    input_weight,
    select_weight,
    step_weight,
    output_weight,
    decay_forward,
    decay_reverse,
    filter_weight,
    filter_bias,
    step_bias,
    modulation_weight,
    modulation_bias,
    cotangent,
):
    item_count, local_len, model_width = hidden.shape
    gathered = (
        lax.all_gather(select_weight, ("dp", "seq"), axis=0, tiled=True),
        lax.all_gather(step_weight, ("dp", "seq"), axis=1, tiled=True),
        lax.all_gather(output_weight, ("dp", "seq"), axis=1, tiled=True),
        lax.all_gather(decay_forward, ("dp", "seq"), axis=0, tiled=True),
        lax.all_gather(decay_reverse, ("dp", "seq"), axis=0, tiled=True),
        lax.all_gather(filter_weight, ("dp", "seq"), axis=1, tiled=True),
        lax.all_gather(filter_bias, ("dp", "seq"), axis=0, tiled=True),
        lax.all_gather(step_bias, ("dp", "seq"), axis=0, tiled=True),
        lax.all_gather(modulation_weight, ("dp", "seq"), axis=0, tiled=True),
        lax.all_gather(modulation_bias, ("dp", "seq"), axis=0, tiled=True),
    )
    (
        select_full,
        step_full,
        output_full,
        log_forward,
        log_reverse,
        filter_full,
        filter_shift,
        step_shift,
        modulation_full,
        modulation_shift,
    ) = gathered
    inner_width = select_full.shape[0]
    rank_width = step_full.shape[0]
    state_width = log_forward.shape[1]
    filter_taps = filter_full.shape[0]
    embedded = jax.nn.silu(frequency_embed(timestep)).astype(jnp.bfloat16)
    modulation = jnp.dot(
        embedded, modulation_full, preferred_element_type=jnp.float32
    ) + modulation_shift.astype(jnp.float32)
    shifts = modulation[:, :model_width]
    scales = modulation[:, model_width : 2 * model_width]
    gate_scale = modulation[:, 2 * model_width :]
    hidden_wide = hidden.astype(jnp.float32)
    centered = hidden_wide - jnp.mean(hidden_wide, axis=2, keepdims=True)
    inverse = lax.rsqrt(jnp.mean(centered * centered, axis=2, keepdims=True) + EPS)
    normed = centered * inverse
    modded = (normed * (1.0 + scales[:, None, :]) + shifts[:, None, :]).astype(jnp.bfloat16)
    modded_flat = modded.reshape(-1, model_width)
    projected = jnp.dot(
        modded_flat,
        lax.all_gather(input_weight, ("dp", "seq"), axis=0, tiled=True),
        preferred_element_type=jnp.float32,
    )
    projected = projected.reshape(item_count, local_len, 2 * inner_width)
    keeper = pad_mask.astype(jnp.float32)[:, :, None]
    inner_part = (
        projected[:, :, :inner_width].astype(jnp.bfloat16)
        * pad_mask.astype(jnp.bfloat16)[:, :, None]
    )
    gate_branch = projected[:, :, inner_width:]
    edge_rows = shifted(inner_part[:, local_len - (filter_taps - 1) :, :], "seq", 1)
    padded = jnp.concatenate([edge_rows, inner_part], axis=1)
    filtered = jnp.zeros((item_count, local_len, inner_width), jnp.float32) + filter_shift.astype(
        jnp.float32
    )
    for offset in range(filter_taps):
        filtered = filtered + filter_full[offset].astype(jnp.float32) * padded[
            :, offset : offset + local_len, :
        ].astype(jnp.float32)
    sigma_filter = jax.nn.sigmoid(filtered)
    active = (filtered * sigma_filter).astype(jnp.bfloat16)
    active_wide = active.astype(jnp.float32)
    selected = jnp.einsum("ile,ek->ilk", active, select_full, preferred_element_type=jnp.float32)
    low_rank = selected[:, :, :rank_width].astype(jnp.bfloat16)
    b_rows = selected[:, :, rank_width : rank_width + state_width]
    c_rows = selected[:, :, rank_width + state_width :]
    pre_steps = jnp.einsum(
        "ilr,re->ile", low_rank, step_full, preferred_element_type=jnp.float32
    ) + step_shift.astype(jnp.float32)
    steps = jax.nn.softplus(pre_steps)
    rates_forward = -jnp.exp(log_forward.astype(jnp.float32))
    rates_reverse = -jnp.exp(log_reverse.astype(jnp.float32))
    zero_state = jnp.zeros((item_count, inner_width, state_width), jnp.float32)
    unit_state = jnp.ones_like(zero_state)
    step_totals = jnp.sum(steps, axis=1)
    carry_forward = jnp.exp(step_totals[:, :, None] * rates_forward)
    carry_reverse = jnp.exp(step_totals[:, :, None] * rates_reverse)
    end_forward = scan_states(steps, active_wide, b_rows, c_rows, rates_forward, zero_state, False)
    into_forward = carried_in(
        (carry_forward, end_forward), "seq", compose, (unit_state, zero_state), False
    )[1]
    unused_forward, mixed_forward, starts_forward = scan_states(
        steps, active_wide, b_rows, c_rows, rates_forward, into_forward, True
    )
    steps_flip = jnp.flip(steps, 1)
    active_flip = jnp.flip(active_wide, 1)
    b_rows_flip = jnp.flip(b_rows, 1)
    c_rows_flip = jnp.flip(c_rows, 1)
    end_reverse = scan_states(
        steps_flip, active_flip, b_rows_flip, c_rows_flip, rates_reverse, zero_state, False
    )
    into_reverse = carried_in(
        (carry_reverse, end_reverse), "seq", compose, (unit_state, zero_state), True
    )[1]
    unused_reverse, mixed_reverse_flip, starts_reverse = scan_states(
        steps_flip, active_flip, b_rows_flip, c_rows_flip, rates_reverse, into_reverse, True
    )
    merged = mixed_forward + jnp.flip(mixed_reverse_flip, 1)
    sigma_gate = jax.nn.sigmoid(gate_branch)
    silu_gate = gate_branch * sigma_gate
    gated = (merged * silu_gate).astype(jnp.bfloat16)
    branch = jnp.einsum("ile,ed->ild", gated, output_full, preferred_element_type=jnp.float32)
    block_out = (hidden_wide + gate_scale[:, None, :] * keeper * branch).astype(jnp.bfloat16)
    regathered = (
        lax.all_gather(select_weight, ("dp", "seq"), axis=0, tiled=True),
        lax.all_gather(step_weight, ("dp", "seq"), axis=1, tiled=True),
        lax.all_gather(output_weight, ("dp", "seq"), axis=1, tiled=True),
        lax.all_gather(filter_weight, ("dp", "seq"), axis=1, tiled=True),
    )
    select_back, step_back, output_back, filter_back = regathered
    upstream = cotangent.astype(jnp.float32)
    grad_gate = jnp.sum(keeper * upstream * branch, axis=1)
    grad_branch = (upstream * gate_scale[:, None, :] * keeper).astype(jnp.bfloat16)
    grad_gated = jnp.einsum(
        "ild,ed->ile", grad_branch, output_back, preferred_element_type=jnp.float32
    )
    grad_merged = grad_gated * silu_gate
    grad_gate_branch = grad_gated * merged * sigma_gate * (1.0 + gate_branch * (1.0 - sigma_gate))
    first_forward = adjoint_start(steps, c_rows, grad_merged, rates_forward)
    passed_forward = carried_in(
        (carry_forward, first_forward), "seq", compose, (unit_state, zero_state), True
    )[1]
    steps_gf, drive_gf, b_gf, c_gf, rate_gf = scan_grads(
        steps,
        active_wide,
        b_rows,
        c_rows,
        grad_merged,
        rates_forward,
        starts_forward,
        passed_forward,
    )
    merged_flip = jnp.flip(grad_merged, 1)
    first_reverse = adjoint_start(steps_flip, c_rows_flip, merged_flip, rates_reverse)
    passed_reverse = carried_in(
        (carry_reverse, first_reverse), "seq", compose, (unit_state, zero_state), False
    )[1]
    steps_gr, drive_gr, b_gr, c_gr, rate_gr = scan_grads(
        steps_flip,
        active_flip,
        b_rows_flip,
        c_rows_flip,
        merged_flip,
        rates_reverse,
        starts_reverse,
        passed_reverse,
    )
    grad_steps = steps_gf + jnp.flip(steps_gr, 1)
    grad_active = drive_gf + jnp.flip(drive_gr, 1)
    grad_b_rows = b_gf + jnp.flip(b_gr, 1)
    grad_c_rows = c_gf + jnp.flip(c_gr, 1)
    grad_decay_fwd = rate_gf * rates_forward
    grad_decay_rev = rate_gr * rates_reverse
    grad_pre = grad_steps * jax.nn.sigmoid(pre_steps)
    grad_step_bias = jnp.sum(grad_pre, axis=(0, 1))
    grad_pre_low = grad_pre.astype(jnp.bfloat16)
    grad_step_weight = jnp.einsum(
        "ilr,ile->re", low_rank, grad_pre_low, preferred_element_type=jnp.float32
    )
    grad_low_rank = jnp.einsum(
        "ile,re->ilr", grad_pre_low, step_back, preferred_element_type=jnp.float32
    )
    grad_selected = jnp.concatenate([grad_low_rank, grad_b_rows, grad_c_rows], axis=2).astype(
        jnp.bfloat16
    )
    grad_select_weight = jnp.einsum(
        "ile,ilk->ek", active, grad_selected, preferred_element_type=jnp.float32
    )
    grad_active = grad_active + jnp.einsum(
        "ilk,ek->ile", grad_selected, select_back, preferred_element_type=jnp.float32
    )
    grad_filtered = grad_active * sigma_filter * (1.0 + filtered * (1.0 - sigma_filter))
    after_rows = shifted(shortened(grad_filtered[:, : filter_taps - 1, :]), "seq", -1)
    extended = jnp.concatenate([grad_filtered, after_rows], axis=1)
    grad_inner = jnp.zeros((item_count, local_len, inner_width), jnp.float32)
    filter_rows = []
    for offset in range(filter_taps):
        lead = filter_taps - 1 - offset
        grad_inner = (
            grad_inner
            + filter_back[offset].astype(jnp.float32) * extended[:, lead : lead + local_len, :]
        )
        filter_rows.append(
            jnp.sum(
                grad_filtered * padded[:, offset : offset + local_len, :].astype(jnp.float32),
                axis=(0, 1),
            )
        )
    grad_filter_weight = jnp.stack(filter_rows, axis=0)
    grad_filter_bias = jnp.sum(grad_filtered, axis=(0, 1))
    grad_projected = jnp.concatenate([grad_inner * keeper, grad_gate_branch], axis=2).astype(
        jnp.bfloat16
    )
    projected_flat = grad_projected.reshape(-1, 2 * inner_width)
    grad_modded = jnp.einsum(
        "te,ne->tn",
        projected_flat,
        lax.all_gather(input_weight, ("dp", "seq"), axis=0, tiled=True),
        preferred_element_type=jnp.float32,
    )
    grad_modded = grad_modded.reshape(item_count, local_len, model_width)
    grad_shifts = jnp.sum(grad_modded, axis=1)
    grad_scales = jnp.sum(grad_modded * normed, axis=1)
    grad_normed = grad_modded * (1.0 + scales[:, None, :])
    grad_hidden = upstream + inverse * (
        grad_normed
        - jnp.mean(grad_normed, axis=2, keepdims=True)
        - normed * jnp.mean(grad_normed * normed, axis=2, keepdims=True)
    )
    grad_modulation = jnp.concatenate([grad_shifts, grad_scales, grad_gate], axis=1)
    grad_mod_weight = jnp.dot(embedded.astype(jnp.float32).T, grad_modulation, precision=HIGHEST)
    grad_mod_bias = jnp.sum(grad_modulation, axis=0)
    gated_flat = gated.reshape(-1, inner_width)
    branch_flat = grad_branch.reshape(-1, model_width)
    wide_grads = lax.psum_scatter(
        jnp.concatenate(
            [
                jnp.einsum(
                    "td,te->de", modded_flat, projected_flat, preferred_element_type=jnp.float32
                ),
                jnp.einsum(
                    "td,te->de", branch_flat, gated_flat, preferred_element_type=jnp.float32
                ),
            ],
            axis=1,
        ),
        ("dp", "seq"),
        scatter_dimension=0,
        tiled=True,
    )
    grad_input_weight = wide_grads[:, : 2 * inner_width]
    grad_output_weight = wide_grads[:, 2 * inner_width :].T
    others = (
        lax.psum_scatter(grad_select_weight, ("dp", "seq"), scatter_dimension=0, tiled=True),
        lax.psum_scatter(grad_step_weight, ("dp", "seq"), scatter_dimension=1, tiled=True),
        lax.psum_scatter(grad_decay_fwd, ("dp", "seq"), scatter_dimension=0, tiled=True),
        lax.psum_scatter(grad_decay_rev, ("dp", "seq"), scatter_dimension=0, tiled=True),
        lax.psum_scatter(grad_filter_weight, ("dp", "seq"), scatter_dimension=1, tiled=True),
        lax.psum_scatter(grad_filter_bias, ("dp", "seq"), scatter_dimension=0, tiled=True),
        lax.psum_scatter(grad_step_bias, ("dp", "seq"), scatter_dimension=0, tiled=True),
        lax.psum_scatter(grad_mod_weight, ("dp", "seq"), scatter_dimension=0, tiled=True),
        lax.psum_scatter(grad_mod_bias, ("dp", "seq"), scatter_dimension=0, tiled=True),
    )
    return (
        block_out,
        grad_hidden.astype(jnp.bfloat16),
        grad_input_weight,
        others[0],
        others[1],
        grad_output_weight,
        others[2],
        others[3],
        others[4],
        others[5],
        others[6],
        others[7],
        others[8],
    )


def solution(mesh):
    return jax.shard_map(
        body,
        mesh=mesh,
        in_specs=(
            P("dp", "seq", None),
            P("dp", "seq"),
            P("dp"),
            P(("dp", "seq"), None),
            P(("dp", "seq"), None),
            P(None, ("dp", "seq")),
            P(None, ("dp", "seq")),
            P(("dp", "seq"), None),
            P(("dp", "seq"), None),
            P(None, ("dp", "seq")),
            P(("dp", "seq")),
            P(("dp", "seq")),
            P(("dp", "seq"), None),
            P(("dp", "seq")),
            P("dp", "seq", None),
        ),
        out_specs=(
            P("dp", "seq", None),
            P("dp", "seq", None),
            P(("dp", "seq"), None),
            P(("dp", "seq"), None),
            P(None, ("dp", "seq")),
            P(None, ("dp", "seq")),
            P(("dp", "seq"), None),
            P(("dp", "seq"), None),
            P(None, ("dp", "seq")),
            P(("dp", "seq")),
            P(("dp", "seq")),
            P(("dp", "seq"), None),
            P(("dp", "seq")),
        ),
        check_vma=False,
    )
```

profile of v0, /device:TPU:0, one launch (start us, length us, event | category | flops | bytes accessed | tf_op | source)
XLA Modules:
  0.0 3153.7 jit_solution(9806316300767854901)
XLA Ops:
  14.1 42.4 %all-reduce.7 = (bf16[3072]{0:T(1024)(128)(2,1)S(1)}, bf16[4608]{0:T(1024)(128)(2,1)S(1)}, bf16[3072]{0:T(1024)(128)(2,1)S(1)}) all-reduce(bf16[3072]{0:T(1024)(128)(2,1)S(1)} %dynamic-update-slice.2, bf16[4608]{0:T(1024)(128)(2,1)S(1)} %dynamic-update-slice, ...), channel_id=1, replica_groups=mesh['dp'=8,'seq'=4] {'dp','seq'}, use_global_device_ids=true, to_apply=%add.2 | all-reduce | flops 10752 | bytes 43008
  58.6 66.7 %all-gather.6 = bf16[32,96,4]{1,2,0:T(4,128)(2,1)S(1)} all-gather(bf16[1,96,4]{1,2,0:T(4,128)(2,1)} %bitcast.2861), channel_id=1, replica_groups=mesh['dp'=8,'seq'=4] {'dp','seq'}, dimensions={0}, use_global_device_ids=true | all-gather | bytes 25344 | tf_op jit(solution)/shard_map/all_gather | solution.py:208
  125.4 67.1 %all-gather.7 = bf16[32,96,16]{1,2,0:T(8,128)(2,1)S(1)} all-gather(bf16[1,96,16]{1,2,0:T(8,128)(2,1)} %bitcast.2859), channel_id=1, replica_groups=mesh['dp'=8,'seq'=4] {'dp','seq'}, dimensions={0}, use_global_device_ids=true | all-gather | bytes 101376 | tf_op jit(solution)/shard_map/all_gather | solution.py:206
  192.8 67.9 %all-gather.8 = bf16[32,96,16]{1,2,0:T(8,128)(2,1)S(1)} all-gather(bf16[1,96,16]{1,2,0:T(8,128)(2,1)} %bitcast.2860), channel_id=1, replica_groups=mesh['dp'=8,'seq'=4] {'dp','seq'}, dimensions={0}, use_global_device_ids=true | all-gather | bytes 101376 | tf_op jit(solution)/shard_map/all_gather | solution.py:207
  261.7 78.8 %all_gather.84 = bf16[96,3072]{0,1:T(8,128)(2,1)} all-gather(bf16[96,96]{0,1:T(8,128)(2,1)S(1)} %copy.162), channel_id=1, replica_groups=mesh['dp'=8,'seq'=4] {'dp','seq'}, dimensions={1}, use_global_device_ids=true | all-gather | bytes 608256 | tf_op jit(solution)/shard_map/all_gather | solution.py:204
  340.5 76.3 %all_gather.83 = bf16[3072,128]{1,0:T(8,128)(2,1)} all-gather(bf16[96,128]{1,0:T(8,128)(2,1)S(1)} %copy-done.62), channel_id=1, replica_groups=mesh['dp'=8,'seq'=4] {'dp','seq'}, dimensions={0}, use_global_device_ids=true | all-gather | bytes 811008 | tf_op jit(solution)/shard_map/all_gather | solution.py:203
  479.9 73.5 %while.188 = (s32[]{:T(128)}, f32[1,3072,16]{1,2,0:T(8,128)S(1)}, f32[32,1,8,3072]{3,2,1,0:T(8,128)}, f32[3072,16]{0,1:T(8,128)S(1)}, f32[32,1,8,3072]{3,2,1,0:T...) while((s32[]{:T(128)}, f32[1,3072,16]{1,2,0:T(8,128)S(1)}, ...), condition=%wide.region_4.5_spmd.clone, body=%wide.region_3.4_spmd.clone.sunk | while | flops 1646595 | bytes 1870447 | solution.py:99
  589.2 140.2 %while.186 = (s32[]{:T(128)}, f32[1,3072,16]{1,2,0:T(8,128)S(1)}, f32[32,1,8,3072]{3,2,1,0:T(8,128)}, f32[32,1,3072,16]{2,3,1,0:T(8,128)}, f32[32,1,8,3072]{3,2,...) while((s32[]{:T(128)}, f32[1,3072,16]{1,2,0:T(8,128)S(1)}, ...), condition=%wide.region_16.17_spmd, body=%wide.region_7.16_spmd.sunk | while | flops 3538946 | bytes 3888637 | solution.py:99
  768.9 73.5 %while.190 = (s32[]{:T(128)}, f32[1,3072,16]{1,2,0:T(8,128)S(1)}, f32[32,1,8,3072]{3,2,1,0:T(8,128)}, f32[3072,16]{0,1:T(8,128)S(1)}, f32[32,1,8,3072]{3,2,1,0:T...) while((s32[]{:T(128)}, f32[1,3072,16]{1,2,0:T(8,128)S(1)}, ...), condition=%wide.region_18.19_spmd.clone, body=%wide.region_17.18_spmd.clone.sunk | while | flops 1646595 | bytes 1870447 | solution.py:99
  863.1 140.2 %while.187 = (s32[]{:T(128)}, f32[1,3072,16]{1,2,0:T(8,128)S(1)}, f32[32,1,8,3072]{3,2,1,0:T(8,128)}, f32[32,1,3072,16]{2,3,1,0:T(8,128)}, f32[32,1,8,3072]{3,2,...) while((s32[]{:T(128)}, f32[1,3072,16]{1,2,0:T(8,128)S(1)}, ...), condition=%wide.region_30.31_spmd, body=%wide.region_21.30_spmd.sunk | while | flops 3538946 | bytes 3888637 | solution.py:99
  1060.4 70.2 %while.192 = (s32[]{:T(128)}, f32[1,3072]{1,0:T(1,128)S(1)}, f32[1,3072,16]{1,2,0:T(8,128)S(1)}, f32[32,1,8,3072]{3,2,1,0:T(8,128)}, f32[3072,16]{0,1:T(8,128)S(...) while((s32[]{:T(128)}, f32[1,3072]{1,0:T(1,128)S(1)}, ...), condition=%wide.region_32.33_spmd.clone, body=%wide.region_31.32_spmd.clone.sunk | while | flops 1649667 | bytes 1587832 | solution.py:121
  1149.5 389.5 %while.194 = (s32[]{:T(128)}, f32[1,3072,16]{1,2,0:T(8,128)S(1)}, f32[3072,16]{0,1:T(8,128)S(1)}, f32[32,1,8,3072]{3,2,1,0:T(8,128)}, f32[32,1,8,3072]{3,2,1,0:T...) while((s32[]{:T(128)}, f32[1,3072,16]{1,2,0:T(8,128)S(1)}, ...), condition=%wide.region_68.69_spmd.clone, body=%wide.region_35.68_spmd.clone.sunk | while | flops 12533508 | bytes 10200803 | solution.py:174
  1540.4 49.2 %while.195 = (s32[]{:T(128)}, f32[1,3072]{1,0:T(1,128)S(1)}, f32[1,3072,16]{1,2,0:T(8,128)S(1)}, f32[32,1,8,3072]{3,2,1,0:T(8,128)}, f32[3072,16]{0,1:T(8,128)S(...) while((s32[]{:T(128)}, f32[1,3072]{1,0:T(1,128)S(1)}, ...), condition=%wide.region_70.71_spmd.clone, body=%wide.region_69.70_spmd.clone.sunk | while | flops 1649667 | bytes 1587832 | solution.py:121
  1608.9 368.2 %while.197 = (s32[]{:T(128)}, f32[1,3072,16]{1,2,0:T(8,128)S(1)}, f32[3072,16]{0,1:T(8,128)S(1)}, f32[32,1,8,3072]{3,2,1,0:T(8,128)}, f32[32,1,8,3072]{3,2,1,0:T...) while((s32[]{:T(128)}, f32[1,3072,16]{1,2,0:T(8,128)S(1)}, ...), condition=%wide.region_106.107_spmd.clone, body=%wide.region_73.106_spmd.clone.sunk | while | flops 12533508 | bytes 10200803 | solution.py:174
  1978.1 24.8 rev.36
  2008.6 24.9 rev.35
  2085.4 37.5 %pad_maximum_fusion = f32[1536,9216]{1,0:T(8,128)} fusion(f32[1536,3072]{1,0:T(8,128)} %fusion.269, f32[1536,6144]{1,0:T(8,128)} %fusion.224), kind=kLoop, calls=%fused_computation.604 | loop fusion | flops 14155776 | bytes 113246208 | tf_op jit(solution)/shard_map/concatenate | solution.py:420
  2148.5 38.8 %all-reduce.6 = (f32[3072]{0:T(1024)S(1)}, f32[3072]{0:T(1024)S(1)}, f32[4608]{0:T(1024)S(1)}) all-reduce(f32[3072]{0:T(1024)S(1)} %copy-done.49, f32[3072]{0:T(1024)S(1)} %copy-done.48, f32[4608]{0:T(1024)S(1)} %maximum_reduce_fusion), channel_id=14, replica_groups=mesh['dp'=8,'seq'=4] {'dp','seq'}, use_global_device_ids=true, to_apply=%region_120.121.clone | all-reduce | flops 10752 | bytes 86016
  2190.5 58.5 %reduce-scatter.24.cloned.1.call-done = f32[96,16]{1,0:T(8,128)} async-done(((f32[3072,16]{1,0:T(8,128)}), f32[96,16]{1,0:T(8,128)}) %reduce-scatter.24.cloned.1.call-update) | async-done | bytes 6160
  2250.4 99.7 %reduce-scatter.26.cloned.1.call-done = f32[96,16]{1,0:T(8,128)} async-done(((f32[3072,16]{1,0:T(8,128)}), f32[96,16]{1,0:T(8,128)}) %reduce-scatter.26.cloned.1.call-update) | async-done | bytes 6160
  2351.6 99.8 %reduce-scatter.22.cloned.1.call-done = f32[96,96]{1,0:T(8,128)} async-done(((f32[3072,96]{1,0:T(8,128)}), f32[96,96]{1,0:T(8,128)}) %reduce-scatter.22.cloned.1.call-update) | async-done | bytes 36880
  2453.0 477.7 %reduce-scatter.16.cloned.1.call-done = f32[48,9216]{1,0:T(8,128)} async-done(((f32[1536,9216]{1,0:T(8,128)}), f32[48,9216]{1,0:T(8,128)}) %reduce-scatter.16.cloned.1.call-update) | async-done | bytes 1769488 | tf_op jit(solution)/shard_map/reduce_scatter | solution.py:419
  2935.0 98.5 %reduce-scatter.18.cloned.1.call-done = f32[96,128]{1,0:T(8,128)} async-done(((f32[3072,128]{1,0:T(8,128)}), f32[96,128]{1,0:T(8,128)}) %reduce-scatter.18.cloned.1.call-update) | async-done | bytes 49168 | tf_op jit(solution)/shard_map/reduce_scatter | solution.py:438
  3033.5 112.9 %reduce-scatter.20.cloned.1.call-done = f32[8,4608]{1,0:T(8,128)} async-done(((f32[256,4608]{1,0:T(8,128)}), f32[8,4608]{1,0:T(8,128)}) %reduce-scatter.20.cloned.1.call-update) | async-done | bytes 147472 | tf_op jit(solution)/shard_map/reduce_scatter | solution.py:445
  (5047 shorter events, 1643.5 us)
Async XLA Ops:
  7.2 253.9 %copy-start.64 = (s32[1,256]{1,0:T(1,128)S(1)}, s32[1,256]{1,0:T(1,128)}, u32[]{:S(2)}) copy-start(s32[1,256]{1,0:T(1,128)} %param.40) | copy-start | bytes 3076
  7.2 253.9 %copy-start.16 = (bf16[1,256,1536]{2,1,0:T(8,128)(2,1)S(1)}, bf16[1,256,1536]{2,1,0:T(8,128)(2,1)}, u32[]{:S(2)}) copy-start(bf16[1,256,1536]{2,1,0:T(8,128)(2,1)} %param.39) | copy-start | bytes 2359300
  7.2 410.2 %all-gather.13.cloned.1.call-start = ((), (), s32[]{:S(2)}) async-start(), calls=%async_computation.7 | async-start | bytes 2433024 | tf_op jit(solution)/shard_map/all_gather | solution.py:211
  7.9 411.7 %all-gather.15.cloned.1.call-start = ((), (), s32[]{:S(2)}) async-start(), calls=%async_computation.8 | async-start | bytes 19464192 | tf_op jit(solution)/shard_map/all_gather | solution.py:245
  8.7 331.8 %copy-start.62 = (bf16[96,128]{1,0:T(8,128)(2,1)S(1)}, bf16[96,128]{1,0:T(8,128)(2,1)}, u32[]{:S(2)}) copy-start(bf16[96,128]{1,0:T(8,128)(2,1)} %param.43) | copy-start | bytes 73732
  8.7 425.9 %all-gather.17.cloned.1.call-start = ((), (), s32[]{:S(2)}) async-start(), calls=%async_computation.9 | async-start | bytes 9732096 | tf_op jit(solution)/shard_map/all_gather | solution.py:205
  9.4 2179.6 %reduce-scatter.28.cloned.1.call-start = ((), (), s32[]{:S(2)}) async-start(), calls=%async_computation.16 | async-start | bytes 1622016
  11.6 423.1 %copy-start.56 = (f32[1,256]{1,0:T(1,128)}, f32[1,256]{1,0:T(1,128)S(1)}, u32[]{:S(2)}) copy-start(f32[1,256]{1,0:T(1,128)S(1)} %convert_element_type.320) | copy-start | bytes 3076
  261.3 167.6 %copy-start.52 = (f32[256]{0:T(256)}, f32[256]{0:T(256)S(1)}, u32[]{:S(2)}) copy-start(f32[256]{0:T(256)S(1)} %broadcast_multiply_fusion.3) | copy-start | bytes 3076
  261.7 167.2 %copy-start.60 = (f32[256]{0:T(256)}, f32[256]{0:T(256)S(1)}, u32[]{:S(2)}) copy-start(f32[256]{0:T(256)S(1)} %add_rsqrt_fusion) | copy-start | bytes 3076
  432.0 10.9 collective-permute-start
  2008.0 25.6 copy-start.31
  2008.6 25.1 copy-start.22
  2008.6 25.1 copy-start.36
  2008.6 25.1 copy-start.38
  2008.6 25.1 copy-start.40
  2008.6 25.1 copy-start.42
  2039.0 5.7 collective-permute-start.1
  2053.2 195.8 %reduce-scatter.24.cloned.1.call-start = ((), (), s32[]{:S(2)}) async-start(), calls=%async_computation.14 | async-start | bytes 1622016
  2055.0 295.2 %reduce-scatter.26.cloned.1.call-start = ((), (), s32[]{:S(2)}) async-start(), calls=%async_computation.15 | async-start | bytes 1622016
  2064.9 386.5 %reduce-scatter.22.cloned.1.call-start = ((), (), s32[]{:S(2)}) async-start(), calls=%async_computation.13 | async-start | bytes 1622016
  2068.1 862.6 %reduce-scatter.16.cloned.1.call-start = ((), (), s32[]{:S(2)}) async-start(), calls=%async_computation.10 | async-start | bytes 58392576 | tf_op jit(solution)/shard_map/reduce_scatter | solution.py:419
  2122.9 910.6 %reduce-scatter.18.cloned.1.call-start = ((), (), s32[]{:S(2)}) async-start(), calls=%async_computation.11 | async-start | bytes 1622016 | tf_op jit(solution)/shard_map/reduce_scatter | solution.py:438
  2126.2 1020.2 %reduce-scatter.20.cloned.1.call-start = ((), (), s32[]{:S(2)}) async-start(), calls=%async_computation.12 | async-start | bytes 4866048 | tf_op jit(solution)/shard_map/reduce_scatter | solution.py:445
  (53 other events, 454.6 us)
Sparse Core Ops, SparseCore 0:
  10.8 60.1 all-gather.12
  73.8 124.5 all-gather.14
  201.2 82.7 all-gather.16
  2053.3 94.5 reduce-scatter.27
  2152.9 96.0 reduce-scatter.23
  2254.1 96.0 reduce-scatter.25
  2355.4 96.0 reduce-scatter.21
  2457.9 472.7 reduce-scatter.15
  2937.4 96.1 reduce-scatter.17
  3040.3 106.0 reduce-scatter.19
where the time goes:
time: 3190 us; the launch traced here: 3150 us
  waiting for transfers between devices  954 us (30%)
  local copies, waits for them, and re-layouts  933 us (29%)
  other arithmetic  621 us (19%)
  blocking collectives  525 us (16%)
  matrix products  76.1 us (2%)
    squeeze x704, local copies, waits for them, and re-layouts, scan_states(): end_state, kept_out = lax.scan(one_block, start_state, pieces)  533 us
    reduce_scatter x1, waiting for transfers between devices, body(): lax.psum_scatter(jnp.concatenate([jnp.einsum('td,te->de', modded_flat, pr...  478 us
    unnamed x14, waiting for transfers between devices  260 us
    reduce_sum x128, other arithmetic, one_block(): jnp.sum(log_grad * rates, axis=2) + drive_b[:, offset] * adjoint_b  163 us
    dynamic_update_slice x192, local copies, waits for them, and re-layouts, scan_states(): end_state, kept_out = lax.scan(one_block, start_state, pieces)  130 us
    reduce_sum x128, other arithmetic, one_block(): jnp.sum(grad_block[:, offset, :, None] * states_all[offset + 1], axis=1)  119 us
    reduce_scatter x1, waiting for transfers between devices, body(): lax.psum_scatter(grad_mod_weight, ('dp', 'seq'), scatter_dimension=0, til...  113 us
    add x64, other arithmetic, one_block(): grad_rate = grad_rate + jnp.sum(log_grad * step_col[:, :, None], axis=0)  103 us

commit v1 on v0

v1 whole, which is shorter than its diff:
```python
import functools
import math

import jax
import jax.numpy as jnp
from jax import lax
from jax.experimental import pallas as pl
from jax.experimental.pallas import tpu as pltpu
from jax.sharding import PartitionSpec as P

FREQ = 256
EPS = 1e-06
HIGHEST = lax.Precision.HIGHEST
LOG2E = 1.4426950408889634
SUB = 16
F32, BF = jnp.float32, jnp.bfloat16

def wide(block, lanes):
    return jnp.concatenate([block] * (lanes // 128), axis=1) if lanes > 128 else block

def fwd_kernel(step_ref, u_ref, rate_ref, bb_ref, cblk_ref, y_ref, s_ref, carry_ref, *, flip):
    rows, lanes = step_ref.shape
    chunk = pl.program_id(1)
    @pl.when(pl.program_id(0) == 0)
    def _():
        carry_ref[chunk] = jnp.zeros(carry_ref.shape[1:], F32)
    rates = rate_ref[...]
    def sub(i, state):
        at = rows // SUB - 1 - i if flip else i
        base = pl.multiple_of(at * SUB, SUB)
        for k in range(SUB):
            j = SUB - 1 - k if flip else k
            row = step_ref[pl.ds(base + j, 1), :]
            u = u_ref[pl.ds(base + j, 1), :]
            state = jnp.exp2(row * rates) * state + u * wide(bb_ref[base + j], lanes)
            s_ref[pl.ds(pl.multiple_of((base + j) * 16, 16), 16), :] = state.astype(BF)
        block = s_ref[pl.ds(pl.multiple_of(base * 16, 256), 256), :]
        y_ref[pl.ds(base, SUB), :] = jnp.dot(cblk_ref[pl.ds(base, SUB), :], block, preferred_element_type=F32)
        return state
    carry_ref[chunk] = lax.fori_loop(0, rows // SUB, sub, carry_ref[chunk])

def fwd_scan(steps, u, rates2, bb, cblk, flip, tile=128, width=384):
    length, lanes = steps.shape
    blocks, chunks = length // tile, lanes // width
    order = (lambda t: blocks - 1 - t) if flip else (lambda t: t)
    return pl.pallas_call(
        functools.partial(fwd_kernel, flip=flip),
        grid=(blocks, chunks),
        in_specs=[
            pl.BlockSpec((tile, width), lambda t, c: (order(t), c)),
            pl.BlockSpec((tile, width), lambda t, c: (order(t), c)),
            pl.BlockSpec((16, width), lambda t, c: (0, c)),
            pl.BlockSpec((tile, 16, 128), lambda t, c: (order(t), 0, 0)),
            pl.BlockSpec((tile, 256), lambda t, c: (order(t), 0)),
        ],
        out_specs=[
            pl.BlockSpec((tile, width), lambda t, c: (order(t), c)),
            pl.BlockSpec((tile * 16, width), lambda t, c: (order(t), c)),
        ],
        out_shape=[jax.ShapeDtypeStruct((length, lanes), F32), jax.ShapeDtypeStruct((length * 16, lanes), BF)],
        scratch_shapes=[pltpu.VMEM((chunks, 16, width), F32)],
        compiler_params=pltpu.CompilerParams(vmem_limit_bytes=48 * 2**20, dimension_semantics=("arbitrary", "arbitrary")),
        name="fwd_scan",
    )(steps, u, rates2, bb, cblk)

def bwd_kernel(step_ref, u_ref, gy_ref, rate_ref, bb_ref, cb_ref, bblk_ref, s_ref, sprev_ref,
               dlog_ref, adjb_ref, bg_ref, cg_ref, rg_ref, carry_ref, a_ref, l_ref, *, flip):
    rows, lanes = step_ref.shape
    t, chunk = pl.program_id(0), pl.program_id(1)
    last = pl.num_programs(0) - 1
    @pl.when(t == 0)
    def _():
        carry_ref[chunk] = jnp.zeros(carry_ref.shape[1:], F32)
        rg_ref[chunk] = jnp.zeros(rg_ref.shape[1:], F32)
    @pl.when(chunk == 0)
    def _():
        bg_ref[...] = jnp.zeros(bg_ref.shape, F32)
        cg_ref[...] = jnp.zeros(cg_ref.shape, F32)
    rates = rate_ref[...]
    ones = (lax.broadcasted_iota(jnp.int32, (SUB, 256), 0) == lax.broadcasted_iota(jnp.int32, (SUB, 256), 1) // 16)
    onesb = ones.astype(BF)
    subs = rows // SUB
    def sub(i, both):
        passed, rg = both
        at = i if flip else subs - 1 - i
        base = pl.multiple_of(at * SUB, SUB)
        for k in range(SUB):
            j = k if flip else SUB - 1 - k
            row = step_ref[pl.ds(base + j, 1), :]
            g = gy_ref[pl.ds(base + j, 1), :]
            adj = g * wide(cb_ref[base + j], lanes) + passed
            passed = jnp.exp2(row * rates) * adj
            if flip:
                before = base + j + 1
                edge = (j == SUB - 1)
                inner = s_ref[pl.ds(pl.multiple_of(jnp.minimum(before, rows - 1) * 16, 16), 16), :] if edge else s_ref[pl.ds(pl.multiple_of(before * 16, 16), 16), :]
                if edge:
                    outer = jnp.where(t == last, jnp.zeros_like(inner), sprev_ref[...])
                    inner = jnp.where(before == rows, outer, inner)
            else:
                before = base + j - 1
                edge = (j == 0)
                inner = s_ref[pl.ds(pl.multiple_of(jnp.maximum(before, 0) * 16, 16), 16), :] if edge else s_ref[pl.ds(pl.multiple_of(before * 16, 16), 16), :]
                if edge:
                    outer = jnp.where(t == last, jnp.zeros_like(inner), sprev_ref[...])
                    inner = jnp.where(before < 0, outer, inner)
            lg = passed * inner.astype(F32)
            rg = rg + lg * row
            a_ref[j * 16:(j + 1) * 16, :] = adj.astype(BF)
            l_ref[j * 16:(j + 1) * 16, :] = (lg * rates).astype(BF)
        a = a_ref[...]
        here = pl.ds(base, SUB)
        dlog_ref[here, :] = jnp.dot(onesb, l_ref[...], preferred_element_type=F32)
        adjb_ref[here, :] = jnp.dot(bblk_ref[here, :], a, preferred_element_type=F32)
        nt = (((1,), (1,)), ((), ()))
        bgd = lax.dot_general(u_ref[here, :].astype(BF), a, nt, preferred_element_type=F32)
        sblk = s_ref[pl.ds(pl.multiple_of(base * 16, 256), 256), :]
        cgd = lax.dot_general(gy_ref[here, :].astype(BF), sblk, nt, preferred_element_type=F32)
        zero = jnp.zeros_like(bgd)
        bg_ref[pl.ds(at, 1), :] += jnp.sum(jnp.where(ones, bgd, zero), axis=0, keepdims=True)
        cg_ref[pl.ds(at, 1), :] += jnp.sum(jnp.where(ones, cgd, zero), axis=0, keepdims=True)
        return passed, rg
    passed, rg = lax.fori_loop(0, subs, sub, (carry_ref[chunk], rg_ref[chunk]))
    carry_ref[chunk] = passed
    rg_ref[chunk] = rg

def bwd_scan(steps, u, gy, rates2, bb, cb, bblk, states, flip, tile=128, width=384):
    length, lanes = steps.shape
    blocks, chunks = length // tile, lanes // width
    order = (lambda t: t) if flip else (lambda t: blocks - 1 - t)
    if flip:
        prev = lambda t: jnp.minimum((t + 1) * tile, length - 1)
    else:
        prev = lambda t: jnp.maximum((blocks - 1 - t) * tile - 1, 0)
    row = pl.BlockSpec((tile, width), lambda t, c: (order(t), c))
    bc = pl.BlockSpec((tile, 16, 128), lambda t, c: (order(t), 0, 0))
    blk = pl.BlockSpec((tile, 256), lambda t, c: (order(t), 0))
    diag = pl.BlockSpec((tile // 16, 256), lambda t, c: (order(t), 0))
    return pl.pallas_call(
        functools.partial(bwd_kernel, flip=flip),
        grid=(blocks, chunks),
        in_specs=[row, row, row, pl.BlockSpec((16, width), lambda t, c: (0, c)), bc, bc, blk,
            pl.BlockSpec((tile * 16, width), lambda t, c: (order(t), c)),
            pl.BlockSpec((16, width), lambda t, c: (prev(t), c))],
        out_specs=[row, row, diag, diag, pl.BlockSpec((chunks, 16, width), lambda t, c: (0, 0, 0))],
        out_shape=[jax.ShapeDtypeStruct((length, lanes), F32), jax.ShapeDtypeStruct((length, lanes), F32),
            jax.ShapeDtypeStruct((length // 16, 256), F32), jax.ShapeDtypeStruct((length // 16, 256), F32),
            jax.ShapeDtypeStruct((chunks, 16, width), F32)],
        scratch_shapes=[pltpu.VMEM((chunks, 16, width), F32), pltpu.VMEM((256, width), BF), pltpu.VMEM((256, width), BF)],
        compiler_params=pltpu.CompilerParams(vmem_limit_bytes=48 * 2**20, dimension_semantics=("arbitrary", "arbitrary")),
        name="bwd_scan",
    )(steps, u, gy, rates2, bb, cb, bblk, states, states)

def blockdiag(rows):
    length = rows.shape[0]
    eye = (jnp.arange(length)[:, None] % 16) == (jnp.arange(256)[None, :] // 16)
    return jnp.where(eye, jnp.tile(rows, (1, 16)), 0).astype(BF)

def lanes_of(rows):
    return jnp.broadcast_to(rows[:, :, None], rows.shape + (128,))


def frequency_embed(timestep):
    half_width = FREQ // 2
    counter = jnp.arange(half_width, dtype=F32)
    frequency = jnp.exp(counter * (-math.log(10000.0) / half_width))
    angles = timestep.astype(F32)[:, None] * frequency[None, :]
    return jnp.concatenate([jnp.cos(angles), jnp.sin(angles)], axis=1)


def dot(a, b):
    return jnp.dot(a, b, preferred_element_type=F32)


def dot_nt(a, b):
    return lax.dot_general(a, b, (((1,), (1,)), ((), ())), preferred_element_type=F32)


def dot_tn(a, b):
    return lax.dot_general(a, b, (((0,), (0,)), ((), ())), preferred_element_type=F32)


def body(
    hidden,
    pad_mask,
    timestep,
    input_weight,
    select_weight,
    step_weight,
    output_weight,
    decay_forward,
    decay_reverse,
    filter_weight,
    filter_bias,
    step_bias,
    modulation_weight,
    modulation_bias,
    cotangent,
):
    ns, nd = lax.axis_size("seq"), lax.axis_size("dp")
    q, d = lax.axis_index("seq"), lax.axis_index("dp")
    every = ("dp", "seq")
    local_len, width = hidden.shape[1:]
    length = local_len * ns
    inner = output_weight.shape[0]
    part = inner // ns
    rank = step_weight.shape[0]
    state = decay_forward.shape[1]
    taps = filter_weight.shape[0]
    rows_in = input_weight.shape[0]
    units = select_weight.shape[0]

    hid = lax.all_gather(hidden[0], "seq", axis=0, tiled=True)
    mask = lax.all_gather(pad_mask[0].astype(BF), "seq", axis=0, tiled=True).astype(F32)[:, None]
    win = input_weight.reshape(rows_in, 2, ns, part).transpose(2, 0, 1, 3).reshape(ns, rows_in, 2 * part)
    win = lax.all_to_all(win, "seq", 0, 0)
    win = lax.all_gather(win, "dp", axis=0, tiled=False).reshape(width, 2 * part)
    wout = output_weight.T.reshape(-1, ns, part).transpose(1, 0, 2)
    wout = lax.all_to_all(wout, "seq", 0, 0)
    wout = lax.all_gather(wout, "dp", axis=0, tiled=False).reshape(width, part)
    pack = jnp.concatenate(
        [select_weight, step_weight.T, decay_forward, decay_reverse, filter_weight.T,
         filter_bias[:, None], step_bias[:, None]], axis=1)
    used = pack.shape[1]
    pack = jnp.pad(pack, ((0, 0), (0, -used % 128)))
    pack = lax.all_gather(pack, every, axis=0, tiled=True)
    pack = lax.dynamic_slice_in_dim(pack, q * part, part, 0)
    cuts = []
    at = 0
    for size in (rank + 2 * state, rank, state, state, taps, 1, 1):
        cuts.append((at, at + size))
        at += size
    select_q, step_q, log_f, log_r, filt, fbias, sbias = [pack[:, a:b] for a, b in cuts]
    step_q = step_q.T
    modw = lax.all_gather(modulation_weight, every, axis=0, tiled=True)
    modb = lax.all_gather(modulation_bias, every, axis=0, tiled=True)
    cot = lax.all_gather(cotangent[0], "seq", axis=0, tiled=True)

    embedded = jax.nn.silu(frequency_embed(timestep)).astype(BF)
    modulation = dot(embedded, modw) + modb.astype(F32)
    shifts = modulation[:, :width]
    scales = modulation[:, width : 2 * width]
    gate_scale = modulation[:, 2 * width :]

    def norm(x):
        x = x.astype(F32)
        centered = x - jnp.mean(x, axis=1, keepdims=True)
        inverse = lax.rsqrt(jnp.mean(centered * centered, axis=1, keepdims=True) + EPS)
        return centered * inverse, inverse

    modded = (norm(hid)[0] * (1.0 + scales) + shifts).astype(BF)
    projected = dot(modded, win)
    inner_part = projected[:, :part].astype(BF).astype(F32) * mask
    gate_branch = projected[:, part:]
    filt32 = filt.astype(F32)
    padded = jnp.pad(inner_part, ((taps - 1, 0), (0, 0)))
    filtered = fbias.astype(F32).T
    for k in range(taps):
        filtered = filtered + filt32[:, k][None, :] * padded[k : k + length]
    sigma_filter = jax.nn.sigmoid(filtered)
    active = (filtered * sigma_filter).astype(BF)
    active32 = active.astype(F32)
    selected = lax.psum(dot(active, select_q), "seq")
    low_rank = selected[:, :rank].astype(BF)
    b_rows = selected[:, rank : rank + state]
    c_rows = selected[:, rank + state :]
    pre_steps = dot(low_rank, step_q) + sbias.astype(F32).T
    steps = jax.nn.softplus(pre_steps)
    rates_f = -jnp.exp(log_f.astype(F32)).T
    rates_r = -jnp.exp(log_r.astype(F32)).T
    drive = steps * active32
    bb, cb = lanes_of(b_rows), lanes_of(c_rows)
    bblk, cblk = blockdiag(b_rows), blockdiag(c_rows)
    mixed_f, states_f = fwd_scan(steps, drive, rates_f * LOG2E, bb, cblk, False)
    mixed_r, states_r = fwd_scan(steps, drive, rates_r * LOG2E, bb, cblk, True)
    merged = mixed_f + mixed_r
    sigma_gate = jax.nn.sigmoid(gate_branch)
    silu_gate = gate_branch * sigma_gate
    gated = (merged * silu_gate).astype(BF)
    branch = lax.psum_scatter(dot_nt(gated, wout), "seq", scatter_dimension=0, tiled=True)

    mask_here = pad_mask[0].astype(F32)[:, None]
    cot_here = cotangent[0].astype(F32)
    block_out = (hidden[0].astype(F32) + gate_scale * mask_here * branch).astype(BF)
    grad_gate = jnp.sum(mask_here * cot_here * branch, axis=0)

    grad_branch = (cot.astype(F32) * gate_scale * mask).astype(BF)
    grad_gated = dot(grad_branch, wout)
    grad_merged = grad_gated * silu_gate
    grad_gate_branch = grad_gated * merged * sigma_gate * (1.0 + gate_branch * (1.0 - sigma_gate))
    dlog_f, adjb_f, bg_f, cg_f, rg_f = bwd_scan(
        steps, drive, grad_merged, rates_f * LOG2E, bb, cb, bblk, states_f, False)
    dlog_r, adjb_r, bg_r, cg_r, rg_r = bwd_scan(
        steps, drive, grad_merged, rates_r * LOG2E, bb, cb, bblk, states_r, True)
    adjb = adjb_f + adjb_r
    grad_steps = (dlog_f + dlog_r) * (1.0 / LOG2E) + active32 * adjb
    grad_b = (bg_f + bg_r).reshape(length, state)
    grad_c = (cg_f + cg_r).reshape(length, state)
    grad_decay_f = rg_f.transpose(1, 0, 2).reshape(state, part) * rates_f
    grad_decay_r = rg_r.transpose(1, 0, 2).reshape(state, part) * rates_r
    grad_pre = grad_steps * jax.nn.sigmoid(pre_steps)
    grad_step_bias = jnp.sum(grad_pre, axis=0)
    grad_pre_low = grad_pre.astype(BF)
    grad_step_t = dot_tn(grad_pre_low, low_rank)
    grad_low_rank = dot_nt(grad_pre_low, step_q)
    grad_selected = lax.psum(jnp.concatenate([grad_low_rank, grad_b, grad_c], axis=1), "seq").astype(BF)
    grad_select = dot_tn(active, grad_selected)
    grad_active = steps * adjb + dot_nt(grad_selected, select_q)
    grad_filtered = grad_active * sigma_filter * (1.0 + filtered * (1.0 - sigma_filter))
    extended = jnp.pad(grad_filtered, ((0, taps - 1), (0, 0)))
    grad_inner = jnp.zeros_like(grad_filtered)
    filter_rows = []
    for k in range(taps):
        lead = taps - 1 - k
        grad_inner = grad_inner + filt32[:, k][None, :] * extended[lead : lead + length]
        filter_rows.append(jnp.sum(grad_filtered * padded[k : k + length], axis=0))
    grad_filter_bias = jnp.sum(grad_filtered, axis=0)
    grad_projected = jnp.concatenate([grad_inner * mask, grad_gate_branch], axis=1).astype(BF)
    grad_modded = lax.psum_scatter(dot_nt(grad_projected, win), "seq", scatter_dimension=0, tiled=True)

    normed, inverse = norm(hidden[0])
    grad_shifts = jnp.sum(grad_modded, axis=0)
    grad_scales = jnp.sum(grad_modded * normed, axis=0)
    grad_normed = grad_modded * (1.0 + scales)
    grad_hidden = cot_here + inverse * (
        grad_normed
        - jnp.mean(grad_normed, axis=1, keepdims=True)
        - normed * jnp.mean(grad_normed * normed, axis=1, keepdims=True)
    )

    def home(grad, cols):
        got = lax.psum_scatter(grad, "dp", scatter_dimension=0, tiled=True)
        got = got.reshape(ns, -1, cols)
        return lax.all_to_all(got, "seq", 0, 0)

    g_in = home(dot_tn(modded, grad_projected), 2 * part)
    g_in = g_in.reshape(ns, rows_in, 2, part).transpose(1, 2, 0, 3).reshape(rows_in, 2 * inner)
    g_out = home(dot_tn(grad_branch, gated), part).transpose(1, 0, 2).reshape(-1, inner).T
    small = jnp.concatenate(
        [grad_select, grad_step_t, grad_decay_f.T, grad_decay_r.T, jnp.stack(filter_rows, axis=1),
         grad_filter_bias[:, None], grad_step_bias[:, None]], axis=1)
    small = jnp.pad(small, ((0, 0), (0, -used % 128)))
    small = lax.psum_scatter(small, "dp", scatter_dimension=0, tiled=True)
    small = lax.ppermute(small, every, [(a * ns + b, b * nd + a) for a in range(nd) for b in range(ns)])
    gs_select, gs_step, gs_f, gs_r, gs_filter, gs_fbias, gs_sbias = [small[:, a:b] for a, b in cuts]
    grad_mod = jnp.concatenate([grad_shifts, grad_scales, grad_gate, embedded[0].astype(F32)])
    grad_mod = lax.all_gather(grad_mod, every, axis=0, tiled=False).reshape(nd, ns, -1)
    embeds = grad_mod[:, 0, 3 * width :]
    grad_mod = jnp.sum(grad_mod[:, :, : 3 * width], axis=1)
    me = d * ns + q
    mine = lax.dynamic_slice_in_dim(embeds, me * modulation_weight.shape[0], modulation_weight.shape[0], 1)
    g_modw = lax.dot_general(mine, grad_mod, (((0,), (0,)), ((), ())), precision=HIGHEST)
    g_modb = lax.dynamic_slice_in_dim(
        jnp.sum(grad_mod, axis=0), me * modulation_bias.shape[0], modulation_bias.shape[0], 0)
    return (
        block_out[None],
        grad_hidden.astype(BF)[None],
        g_in,
        gs_select,
        gs_step.T,
        g_out,
        gs_f,
        gs_r,
        gs_filter.T,
        gs_fbias[:, 0],
        gs_sbias[:, 0],
        g_modw,
        g_modb,
    )


def solution(mesh):
    return jax.shard_map(
        body,
        mesh=mesh,
        in_specs=(
            P("dp", "seq", None),
            P("dp", "seq"),
            P("dp"),
            P(("dp", "seq"), None),
            P(("dp", "seq"), None),
            P(None, ("dp", "seq")),
            P(None, ("dp", "seq")),
            P(("dp", "seq"), None),
            P(("dp", "seq"), None),
            P(None, ("dp", "seq")),
            P(("dp", "seq")),
            P(("dp", "seq")),
            P(("dp", "seq"), None),
            P(("dp", "seq")),
            P("dp", "seq", None),
        ),
        out_specs=(
            P("dp", "seq", None),
            P("dp", "seq", None),
            P(("dp", "seq"), None),
            P(("dp", "seq"), None),
            P(None, ("dp", "seq")),
            P(None, ("dp", "seq")),
            P(("dp", "seq"), None),
            P(("dp", "seq"), None),
            P(None, ("dp", "seq")),
            P(("dp", "seq")),
            P(("dp", "seq")),
            P(("dp", "seq"), None),
            P(("dp", "seq")),
        ),
        check_vma=False,
    )
```

time: 3190 us -> 1110 us (0.35)
  local copies, waits for them, and re-layouts: 933 us -> 60.2 us
  other arithmetic: 621 us -> 34.4 us
  waiting for transfers between devices: 954 us -> 518 us
  blocking collectives: 525 us -> 195 us
  Pallas kernels: 0 us -> 190 us
    squeeze x704 -> x1, local copies, waits for them, and re-layouts: 533 us -> 0.52 us  [body(): gs_sbias[:, 0]]
    all_gather x11 -> x2, blocking collectives: 444 us -> 81.5 us  [the longest x1 72.7 us: body(): lax.all_gather(grad_mod, every, axis=0, tiled=False).reshape(nd, ns, -1)]
    reduce_sum x517 -> x9, other arithmetic: 376 us -> 23.2 us  [the longest x1 7.55 us: body(): grad_step_bias = jnp.sum(grad_pre, axis=0)]
    reduce_scatter x3 -> x4, waiting for transfers between devices: 689 us -> 346 us  [the longest x1 124 us: body(): lax.psum_scatter(dot_nt(grad_projected, win), 'seq', scatter_dimension=0,...]
    unnamed x14 -> x13, waiting for transfers between devices: 260 us -> 2.21 us
    pallas_call x0 -> x4, Pallas kernels: none -> 190 us  [the longest x2 122 us: bwd_scan(): pl.pallas_call(functools.partial(bwd_kernel, flip=flip), grid=(blocks, ch...]
    add x385 -> x5, other arithmetic: 165 us -> 0.1 us  [the longest x1 0.04 us: body(): filtered = filtered + filt32[:, k][None, :] * padded[k:k + length]]
    all_gather x3 -> x6, waiting for transfers between devices: 0.04 us -> 139 us  [the longest x1 61.3 us: body(): hid = lax.all_gather(hidden[0], 'seq', axis=0, tiled=True)]
where the time goes in v1:
time: 1110 us; the launch traced here: 1100 us
  waiting for transfers between devices  518 us (47%)
  blocking collectives  195 us (18%)
  Pallas kernels  190 us (17%)
  matrix products  74.5 us (7%)
  local copies, waits for them, and re-layouts  60.2 us (5%)
  other arithmetic  34.4 us (3%)
  between operations  16.2 us (1%)
    reduce_scatter x1, waiting for transfers between devices, body(): lax.psum_scatter(dot_nt(grad_projected, win), 'seq', scatter_dimension=0,...  124 us
    pallas_call x2, Pallas kernels, bwd_scan(): pl.pallas_call(functools.partial(bwd_kernel, flip=flip), grid=(blocks, ch...  122 us
    reduce_scatter x1, waiting for transfers between devices, body(): lax.psum_scatter(dot_nt(gated, wout), 'seq', scatter_dimension=0, tiled=T...  113 us
    reduce_scatter x2, waiting for transfers between devices, home(): got = lax.psum_scatter(grad, 'dp', scatter_dimension=0, tiled=True)  109 us
    all_gather x1, blocking collectives, body(): lax.all_gather(grad_mod, every, axis=0, tiled=False).reshape(nd, ns, -1)  72.7 us
    pallas_call x2, Pallas kernels, fwd_scan(): pl.pallas_call(functools.partial(fwd_kernel, flip=flip), grid=(blocks, ch...  68 us
    all_gather x1, waiting for transfers between devices, body(): hid = lax.all_gather(hidden[0], 'seq', axis=0, tiled=True)  61.3 us
    unnamed x1, blocking collectives  39.7 us
  transfers between devices with their start and end apart: 15, of which 10 were waited for; matrix products, arithmetic and copies ran while one was open for 8% of the time, Pallas kernels for 6%

profile of v1, /device:TPU:0, one launch (start us, length us, event | category | flops | bytes accessed | tf_op | source)
XLA Modules:
  0.0 1099.0 jit_solution(124245032019132580)
XLA Ops:
  17.4 23.4 %all_to_all.20 = bf16[4,48,1536]{2,1,0:T(8,128)(2,1)} all-to-all(bf16[4,48,1536]{2,1,0:T(8,128)(2,1)S(1)} %reshape.222), channel_id=1, replica_groups=mesh['dp'=8,'seq'=4] {'seq'}, dimensions={0} | all-to-all | bytes 1179648 | tf_op jit(solution)/shard_map/all_to_all | solution.py:216
  42.8 8.8 all-gather.2
  51.8 39.7 %all-reduce.4 = bf16[4608]{0:T(1024)(128)(2,1)S(1)} all-reduce(bf16[4608]{0:T(1024)(128)(2,1)S(1)} %dynamic-update-slice), channel_id=1, replica_groups=mesh['dp'=8,'seq'=4] {'dp','seq'}, use_global_device_ids=true, to_apply=%add.4 | all-reduce | flops 4608 | bytes 18432
  93.6 38.8 %all-gather.16.cloned.1.call-done = bf16[3072,384]{1,0:T(8,128)(2,1)} async-done(((bf16[96,384]{1,0:T(8,128)(2,1)}), bf16[3072,384]{1,0:T(8,128)(2,1)}) %all-gather.16.cloned.1.call-update) | async-done | bytes 2359312 | tf_op jit(solution)/shard_map/all_gather | solution.py:226
  135.1 61.3 %all-gather.18.cloned.1.call-done = bf16[1,1024,1536]{2,1,0:T(8,128)(2,1)} async-done(((bf16[1,256,1536]{2,1,0:T(8,128)(2,1)}), bf16[1,1024,1536]{2,1,0:T(8,128)(2,1)}) %all-gather.18.cloned.1.call-update) | async-done | bytes 3145744 | tf_op jit(solution)/shard_map/all_gather | solution.py:213
  200.3 35.5 %all-gather.20.cloned.1.call-done = bf16[32,48,1536]{2,1,0:T(8,128)(2,1)} async-done(((bf16[4,48,1536]{2,1,0:T(8,128)(2,1)}), bf16[32,48,1536]{2,1,0:T(8,128)(2,1)}) %all-gather.20.cloned.1.call-update) | async-done | bytes 4718608 | tf_op jit(solution)/shard_map/all_gather | solution.py:217
  235.8 7.6 fusion.67
  250.9 21.4 %all_to_all.21 = bf16[4,48,768]{2,1,0:T(8,128)(2,1)} all-to-all(bf16[4,48,768]{2,1,0:T(8,128)(2,1)S(1)} %copy.79), channel_id=1, replica_groups=mesh['dp'=8,'seq'=4] {'seq'}, dimensions={0} | all-to-all | bytes 589824 | tf_op jit(solution)/shard_map/all_to_all | solution.py:219
  275.6 17.6 %all-reduce.8.cloned.1.call-done = f32[1024,128]{1,0:T(8,128)} async-done(((f32[1024,128]{1,0:T(8,128)}), f32[1024,128]{1,0:T(8,128)}) %all-reduce.8.cloned.1.call-update) | async-done | bytes 524304 | tf_op jit(solution)/shard_map/psum | solution.py:263
  314.7 34.0 %fwd_scan.2 = (f32[1024,768]{1,0:T(8,128)S(1)}, bf16[16384,768]{1,0:T(8,128)(2,1)}) custom-call(f32[1024,768]{1,0:T(8,128)} %get-tuple-element.116.step_ref, f32[1024,768]{1,0:T(8,128)} %get-tuple-element.115.u_ref, f32[16,768]{1,0:T(8,128)S(1)} %bitcast_multiply_fusion.3.rate_ref, f32[1024,16,128]{2,1,0:T(8,128)} %broadcast_in_dim.23.bb_ref, ...), custom_call_target="tpu_custom_call" | custom-call | tf_op jit(solution)/shard_map/fwd_scan/pallas_call | solution.py:46
  350.4 34.0 %fwd_scan.3 = (f32[1024,768]{1,0:T(8,128)S(1)}, bf16[16384,768]{1,0:T(8,128)(2,1)}) custom-call(f32[1024,768]{1,0:T(8,128)} %get-tuple-element.116.step_ref, f32[1024,768]{1,0:T(8,128)} %get-tuple-element.115.u_ref, f32[16,768]{1,0:T(8,128)S(1)} %bitcast_multiply_fusion.1.rate_ref, f32[1024,16,128]{2,1,0:T(8,128)} %broadcast_in_dim.23.bb_ref, ...), custom_call_target="tpu_custom_call" | custom-call | tf_op jit(solution)/shard_map/fwd_scan/pallas_call | solution.py:46
  389.3 11.6 %multiply_convert_fusion = (bf16[1024,768]{1,0:T(8,128)(2,1)}, bf16[1024,768]{1,0:T(8,128)(2,1)}, f32[1024,768]{1,0:T(8,128)}) fusion(f32[1024,1536]{1,0:T(8,128)} %copy-done.20, f32[1024,768]{1,0:T(8,128)} %copy-done.2, f32[1024,768]{1,0:T(8,128)} %copy-done.3, bf16[1536,768]{1,0:T(8,128)(2,1)} %bitcast.167, ...), kind=kOutput, calls=%fused_computation.23 | convolution fusion | flops 2434007040 | bytes 21243904 | tf_op jit(solution)/shard_map/dot_general | solution.py:172
  406.8 60.3 %bwd_scan.2 = (f32[1024,768]{1,0:T(8,128)S(1)}, f32[1024,768]{1,0:T(8,128)}, f32[64,256]{1,0:T(8,128)S(1)}, f32[64,256]{1,0:T(8,128)S(1)}, f32[2,16,384]{2,1,0:T(8,128)S(1)}) custom-call(f32[1024,768]{1,0:T(8,128)} %get-tuple-element.116.step_ref, f32[1024,768]{1,0:T(8,128)} %get-tuple-element.115.u_ref, f32[1024,768]{1,0:T(8,128)} %get-tuple-element.121.gy_ref, ...), custom_call_target="tpu_custom_call" | custom-call | tf_op jit(solution)/shard_map/bwd_scan/pallas_call | solution.py:139
  468.8 62.1 %bwd_scan.3 = (f32[1024,768]{1,0:T(8,128)S(1)}, f32[1024,768]{1,0:T(8,128)}, f32[64,256]{1,0:T(8,128)S(1)}, f32[64,256]{1,0:T(8,128)S(1)}, f32[2,16,384]{2,1,0:T(8,128)S(1)}) custom-call(f32[1024,768]{1,0:T(8,128)} %get-tuple-element.116.step_ref, f32[1024,768]{1,0:T(8,128)} %get-tuple-element.115.u_ref, f32[1024,768]{1,0:T(8,128)} %get-tuple-element.121.gy_ref, ...), custom_call_target="tpu_custom_call" | custom-call | tf_op jit(solution)/shard_map/bwd_scan/pallas_call | solution.py:139
  533.3 7.5 fusion.71
  544.8 28.5 %all-reduce.9 = bf16[1024,128]{0,1:T(8,128)(2,1)S(1)} all-reduce(f32[1024,128]{0,1:T(8,128)} %pad_maximum_fusion.3), channel_id=1, replica_groups=mesh['dp'=8,'seq'=4] {'seq'}, use_global_device_ids=true, to_apply=%region_6.7 | all-reduce | flops 131072 | bytes 786432 | tf_op jit(solution)/shard_map/psum | solution.py:306
  597.9 10.0 fusion.13
  609.8 9.2 fusion.14
  632.0 50.1 %reduce-scatter.14.cloned.1.call-done = f32[192,768]{1,0:T(8,128)} async-done(((f32[1536,768]{1,0:T(8,128)}), f32[192,768]{1,0:T(8,128)}) %reduce-scatter.14.cloned.1.call-update) | async-done | bytes 589840 | tf_op jit(solution)/shard_map/reduce_scatter | solution.py:332
  689.0 13.6 %all-to-all-done.3 = f32[4,48,768]{2,1,0:T(8,128)S(1)} async-done(((f32[4,48,768]{2,1,0:T(8,128)}), f32[4,48,768]{2,1,0:T(8,128)S(1)}, u32[]{:S(2)}, u32[]{:S(2)}) %all-to-all-start.3) | async-done | bytes 589856 | tf_op jit(solution)/shard_map/all_to_all | solution.py:334
  703.4 58.5 %reduce-scatter.12.cloned.1.call-done = f32[192,1536]{1,0:T(8,128)} async-done(((f32[1536,1536]{1,0:T(8,128)}), f32[192,1536]{1,0:T(8,128)}) %reduce-scatter.12.cloned.1.call-update) | async-done | bytes 1179664 | tf_op jit(solution)/shard_map/reduce_scatter | solution.py:332
  766.5 124.1 %reduce-scatter.10.cloned.1.call-done = f32[256,1536]{1,0:T(8,128)} async-done(((f32[1024,1536]{1,0:T(8,128)}), f32[256,1536]{1,0:T(8,128)}) %reduce-scatter.10.cloned.1.call-update) | async-done | bytes 1572880 | tf_op jit(solution)/shard_map/reduce_scatter | solution.py:319
  894.6 113.4 %reduce-scatter.8.cloned.1.call-done = f32[256,1536]{1,0:T(8,128)} async-done(((f32[1024,1536]{1,0:T(8,128)}), f32[256,1536]{1,0:T(8,128)}) %reduce-scatter.8.cloned.1.call-update) | async-done | bytes 1572880 | tf_op jit(solution)/shard_map/reduce_scatter | solution.py:280
  1012.0 72.7 %all-gather.6 = f32[32,1,4864]{2,1,0:T(1,128)S(1)} all-gather(f32[1,1,4864]{2,1,0:T(1,128)S(1)} %reshape.254), channel_id=7, replica_groups=mesh['dp'=8,'seq'=4] {'dp','seq'}, dimensions={0}, use_global_device_ids=true | all-gather | bytes 642048 | tf_op jit(solution)/shard_map/all_gather | solution.py:347
  (258 shorter events, 139.1 us)
Async XLA Ops:
  7.2 84.3 %all-gather.14.cloned.1.call-start = ((), (), s32[]{:S(2)}) async-start(), calls=%async_computation.9 | async-start | bytes 2433024 | tf_op jit(solution)/shard_map/all_gather | solution.py:235
  7.9 124.5 %all-gather.16.cloned.1.call-start = ((), (), s32[]{:S(2)}) async-start(), calls=%async_computation.10 | async-start | bytes 2433024 | tf_op jit(solution)/shard_map/all_gather | solution.py:226
  14.3 182.2 %all-gather.18.cloned.1.call-start = ((), (), s32[]{:S(2)}) async-start(), calls=%async_computation.16 | async-start | bytes 3932160 | tf_op jit(solution)/shard_map/all_gather | solution.py:213
  15.0 220.8 %all-gather.20.cloned.1.call-start = ((), (), s32[]{:S(2)}) async-start(), calls=%async_computation.17 | async-start | bytes 5308416 | tf_op jit(solution)/shard_map/all_gather | solution.py:217
  40.9 252.2 %all-reduce.8.cloned.1.call-start = ((), (), s32[]{:S(2)}) async-start(), calls=%async_computation.11 | async-start | bytes 1048576 | tf_op jit(solution)/shard_map/psum | solution.py:263
  51.6 337.7 %copy-start.36 = (f32[1,1024]{1,0:T(1,128)}, f32[1,1024]{1,0:T(1,128)S(1)}, u32[]{:S(2)}) copy-start(f32[1,1024]{1,0:T(1,128)S(1)} %convert_element_type.139) | copy-start | bytes 12292
  135.0 100.8 %copy-start.26 = (f32[1536]{0:T(1024)}, f32[1536]{0:T(1024)S(1)}, u32[]{:S(2)}) copy-start(f32[1536]{0:T(1024)S(1)} %get-tuple-element.106) | copy-start | bytes 18436
  135.0 254.3 %copy-start.39 = (f32[1536]{0:T(1024)}, f32[1536]{0:T(1024)S(1)}, u32[]{:S(2)}) copy-start(f32[1536]{0:T(1024)S(1)} %get-tuple-element.104) | copy-start | bytes 18436
  135.0 108.7 %copy-start.28 = (f32[768]{0:T(1024)}, f32[768]{0:T(1024)S(1)}, u32[]{:S(2)}) copy-start(f32[768]{0:T(1024)S(1)} %get-tuple-element.107) | copy-start | bytes 9220
  135.1 108.7 %copy-start.30 = (f32[768]{0:T(1024)}, f32[768]{0:T(1024)S(1)}, u32[]{:S(2)}) copy-start(f32[768]{0:T(1024)S(1)} %get-tuple-element.108) | copy-start | bytes 9220
  135.1 108.7 %copy-start.32 = (f32[768]{0:T(1024)}, f32[768]{0:T(1024)S(1)}, u32[]{:S(2)}) copy-start(f32[768]{0:T(1024)S(1)} %get-tuple-element.109) | copy-start | bytes 9220
  135.1 108.7 %copy-start.34 = (f32[768]{0:T(1024)}, f32[768]{0:T(1024)S(1)}, u32[]{:S(2)}) copy-start(f32[768]{0:T(1024)S(1)} %get-tuple-element.110) | copy-start | bytes 9220
  248.1 285.3 %copy-start.5 = (bf16[1024,768]{1,0:T(8,128)(2,1)}, bf16[1024,768]{1,0:T(8,128)(2,1)S(1)}, u32[]{:S(2)}) copy-start(bf16[1024,768]{1,0:T(8,128)(2,1)S(1)} %get-tuple-element.117) | copy-start | bytes 4718596
  250.6 135.5 %all-gather.22.cloned.1.call-start = ((), (), s32[]{:S(2)}) async-start(), calls=%async_computation.18 | async-start | bytes 2654208 | tf_op jit(solution)/shard_map/all_gather | solution.py:220
  272.3 117.0 %all-gather.24.cloned.1.call-start = ((), (), s32[]{:S(2)}) async-start(), calls=%async_computation.19 | async-start | bytes 3932160 | tf_op jit(solution)/shard_map/all_gather | solution.py:237
  273.1 355.8 %reduce-scatter.16.cloned.1.call-start = ((), (), s32[]{:S(2)}) async-start(), calls=%async_computation.20 | async-start | bytes 1327104
  588.5 93.5 %reduce-scatter.14.cloned.1.call-start = ((), (), s32[]{:S(2)}) async-start(), calls=%async_computation.15 | async-start | bytes 5308416 | tf_op jit(solution)/shard_map/reduce_scatter | solution.py:332
  596.0 165.9 %reduce-scatter.12.cloned.1.call-start = ((), (), s32[]{:S(2)}) async-start(), calls=%async_computation.14 | async-start | bytes 10616832 | tf_op jit(solution)/shard_map/reduce_scatter | solution.py:332
  608.0 282.7 %reduce-scatter.10.cloned.1.call-start = ((), (), s32[]{:S(2)}) async-start(), calls=%async_computation.13 | async-start | bytes 7864320 | tf_op jit(solution)/shard_map/reduce_scatter | solution.py:319
  619.1 388.9 %reduce-scatter.8.cloned.1.call-start = ((), (), s32[]{:S(2)}) async-start(), calls=%async_computation.12 | async-start | bytes 7864320 | tf_op jit(solution)/shard_map/reduce_scatter | solution.py:280
  630.0 1.3 collective-permute-start
  682.0 20.5 %all-to-all-start.3 = ((f32[4,48,768]{2,1,0:T(8,128)}), f32[4,48,768]{2,1,0:T(8,128)S(1)}, u32[]{:S(2)}, u32[]{:S(2)}) async-start(f32[4,48,768]{2,1,0:T(8,128)} %bitcast.150), calls=%async_computation.7 | async-start | bytes 1179648 | tf_op jit(solution)/shard_map/all_to_all | solution.py:334
  761.9 326.6 %all-to-all-start.2 = ((f32[4,48,1536]{2,1,0:T(8,128)}), f32[4,48,1536]{2,1,0:T(8,128)S(1)}, u32[]{:S(2)}, u32[]{:S(2)}) async-start(f32[4,48,1536]{2,1,0:T(8,128)} %bitcast.148), calls=%async_computation.5 | async-start | bytes 2359296 | tf_op jit(solution)/shard_map/all_to_all | solution.py:334
  890.6 117.4 %copy-start.15 = (f32[256,1536]{1,0:T(8,128)S(1)}, f32[256,1536]{1,0:T(8,128)}, u32[]{:S(2)}) copy-start(f32[256,1536]{1,0:T(8,128)} %reduce-scatter.10.cloned.1.call-done) | copy-start | bytes 4718596
  (47 other events, 422.4 us)
Sparse Core Ops, SparseCore 0:
  10.8 61.9 all-gather.13
  76.2 56.1 all-gather.15
  134.0 62.3 all-gather.17
  198.2 37.5 all-gather.19
  250.7 42.4 all-reduce.7
  294.9 29.0 all-gather.21
  325.6 63.6 all-gather.23
  588.6 35.6 reduce-scatter.15
  628.1 53.8 reduce-scatter.13
  685.4 76.4 reduce-scatter.11
  764.2 126.3 reduce-scatter.9
  892.8 115.1 reduce-scatter.7

commit v2 on v1

--- a/solution.py
+++ b/solution.py
@@ -160,6 +160,285 @@
     return jnp.broadcast_to(rows[:, :, None], rows.shape + (128,))
 
 
+MESH = pl.DeviceIdType.MESH
+VMEM = pl.BlockSpec(memory_space=pltpu.VMEM)
+HBM = pl.BlockSpec(memory_space=pl.ANY)
+DMA = pltpu.SemaphoreType.DMA
+
+
+def send(src, dst, out_sem, in_sem, to):
+    return pltpu.make_async_remote_copy(
+        src_ref=src, dst_ref=dst, send_sem=out_sem, recv_sem=in_sem, device_id=to, device_id_type=MESH)
+
+
+def greet(devices):
+    bar = pltpu.get_barrier_semaphore()
+    for to in devices:
+        pl.semaphore_signal(bar, inc=1, device_id=to, device_id_type=MESH)
+    pl.semaphore_wait(bar, len(devices))
+
+
+def column_sum_kernel(ns, p_ref, o_ref, land, s1, r1, s2, r2):
+    d, q = lax.axis_index("dp"), lax.axis_index("seq")
+    others = [lax.rem(q + k, ns) for k in range(1, ns)]
+    greet([(d, t) for t in others])
+    for k, t in enumerate(others):
+        send(p_ref.at[t], land.at[q], s1.at[k], r1.at[q], (d, t)).start()
+    total = p_ref[q]
+    for k, t in enumerate(others):
+        send(p_ref.at[t], land.at[t], s1.at[k], r1.at[t], (d, t)).wait_recv()
+        total = total + land[t]
+    o_ref[q] = total.astype(o_ref.dtype)
+    for k, t in enumerate(others):
+        send(o_ref.at[q], o_ref.at[q], s2.at[k], r2.at[q], (d, t)).start()
+    for k, t in enumerate(others):
+        send(o_ref.at[t], o_ref.at[t], s2.at[k], r2.at[t], (d, t)).wait_recv()
+    for k, t in enumerate(others):
+        send(p_ref.at[t], land.at[q], s1.at[k], r1.at[q], (d, t)).wait_send()
+        send(o_ref.at[q], o_ref.at[q], s2.at[k], r2.at[q], (d, t)).wait_send()
+
+
+def column_sum(partial, ns, out_dtype, cid):
+    rows, lanes = partial.shape
+    block = (ns, rows // ns, lanes)
+    out = pl.pallas_call(
+        functools.partial(column_sum_kernel, ns),
+        out_shape=jax.ShapeDtypeStruct(block, out_dtype),
+        in_specs=[VMEM], out_specs=VMEM,
+        scratch_shapes=[pltpu.VMEM(block, partial.dtype), DMA((ns,)), DMA((ns,)), DMA((ns,)), DMA((ns,))],
+        compiler_params=pltpu.CompilerParams(
+            collective_id=cid, has_side_effects=True, vmem_limit_bytes=32 * 2**20),
+        name="column_sum",
+    )(partial.reshape(block))
+    return out.reshape(rows, lanes)
+
+
+def mod_gather_kernel(nd, ns, g_ref, o_ref, land, s1, r1, s2, r2):
+    d, q = lax.axis_index("dp"), lax.axis_index("seq")
+    others = [lax.rem(q + k, ns) for k in range(1, ns)]
+    peers = [lax.rem(d + k, nd) for k in range(1, nd)]
+    greet([(d, t) for t in others] + [(e, q) for e in peers])
+    for k, t in enumerate(others):
+        send(g_ref, land.at[q], s1.at[k], r1.at[q], (d, t)).start()
+    total = g_ref[...]
+    for k, t in enumerate(others):
+        send(g_ref, land.at[t], s1.at[k], r1.at[t], (d, t)).wait_recv()
+        total = total + land[t]
+    o_ref[d] = total
+    for k, e in enumerate(peers):
+        send(o_ref.at[d], o_ref.at[d], s2.at[k], r2.at[d], (e, q)).start()
+    for k, e in enumerate(peers):
+        send(o_ref.at[e], o_ref.at[e], s2.at[k], r2.at[e], (e, q)).wait_recv()
+    for k, t in enumerate(others):
+        send(g_ref, land.at[q], s1.at[k], r1.at[q], (d, t)).wait_send()
+    for k, e in enumerate(peers):
+        send(o_ref.at[d], o_ref.at[d], s2.at[k], r2.at[d], (e, q)).wait_send()
+
+
+def mod_gather(g, nd, ns, cid):
+    rows, lanes = g.shape
+    return pl.pallas_call(
+        functools.partial(mod_gather_kernel, nd, ns),
+        out_shape=jax.ShapeDtypeStruct((nd, rows, lanes), F32),
+        in_specs=[VMEM], out_specs=VMEM,
+        scratch_shapes=[pltpu.VMEM((ns, rows, lanes), F32), DMA((ns,)), DMA((ns,)), DMA((nd,)), DMA((nd,))],
+        compiler_params=pltpu.CompilerParams(
+            collective_id=cid, has_side_effects=True, vmem_limit_bytes=32 * 2**20),
+        name="mod_gather",
+    )(g)
+
+
+def home_kernel(nd, ns, nsub, g_ref, sm_ref, gm_ref, f_ref, so_ref, out_ref,
+                pair, plane, spair, splane, ssum, up, down,
+                sa, ra, sb, rb, sc, rc, ta, ra2, tb, rb2, tc, rc2, su, ru, sd, rd):
+    d, q = lax.axis_index("dp"), lax.axis_index("seq")
+    nc = nd // 2
+    chip, core = d // 2, lax.rem(d, 2)
+    mate = chip * 2 + 1 - core
+    chips = [lax.rem(chip + k, nc) for k in range(1, nc)]
+    others = [lax.rem(q + k, ns) for k in range(1, ns)]
+    spread = nd // ns
+    final_to = (spread * q + d // ns, lax.rem(d, ns))
+    mine = d * ns + q
+    final_from = (lax.rem(mine, nd), mine // nd)
+    stays = jnp.logical_and(final_to[0] == d, final_to[1] == q)
+    bar = pltpu.get_barrier_semaphore()
+    friends = [(mate, q)] + [(c * 2 + core, q) for c in chips] + [(d, t) for t in others]
+    for to in friends:
+        pl.semaphore_signal(bar, inc=1, device_id=to, device_id_type=MESH)
+    @pl.when(jnp.logical_not(stays))
+    def _():
+        pl.semaphore_signal(bar, inc=1, device_id=final_from, device_id_type=MESH)
+        pl.semaphore_wait(bar, len(friends) + 1)
+    @pl.when(stays)
+    def _():
+        pl.semaphore_wait(bar, len(friends))
+
+    def first(c):
+        return send(g_ref.at[c * 2 + 1 - core], pair.at[c], sa.at[c], ra.at[c], (mate, q))
+
+    def first_small(c):
+        return send(sm_ref.at[c * 2 + 1 - core], spair.at[c], ta.at[c], ra2.at[c], (mate, q))
+
+    order = chips + [chip]
+    for c in order:
+        first(c).start()
+        first_small(c).start()
+
+    def rise(t, s, src):
+        return send(src, up.at[t, s], su.at[t, s], ru.at[t, s], (d, q + 1))
+
+    def sink(t, s, src):
+        return send(src, down.at[t, s], sd.at[t, s], rd.at[t, s], (d, q - 1))
+
+    def added(land, t, s):
+        land[t, s] = (land[t, s].astype(F32) + gm_ref[t, s].astype(F32)).astype(BF)
+
+    def step_up(t, s):
+        @pl.when(q < t)
+        def _():
+            @pl.when(q == 0)
+            def _():
+                rise(t, s, gm_ref.at[t, s]).start()
+            @pl.when(q > 0)
+            def _():
+                rise(t, s, up.at[t, s]).wait_recv()
+                added(up, t, s)
+                rise(t, s, up.at[t, s]).start()
+
+    def step_down(t, s):
+        @pl.when(q > t)
+        def _():
+            @pl.when(q == ns - 1)
+            def _():
+                sink(t, s, gm_ref.at[t, s]).start()
+            @pl.when(q < ns - 1)
+            def _():
+                sink(t, s, down.at[t, s]).wait_recv()
+                added(down, t, s)
+                sink(t, s, down.at[t, s]).start()
+
+    steps = [(k, s) for k in range(ns - 1) for s in range(nsub)]
+    middle = len(steps) * 2 // 3
+
+    def walk(some):
+        for k, s in some:
+            step_up(ns - 1 - k, s)
+            step_down(k, s)
+
+    def second(c, src):
+        return send(pair.at[c], plane.at[src], sb.at[c], rb.at[src], (c * 2 + core, q))
+
+    def second_small(c, src):
+        return send(spair.at[c], splane.at[src], tb.at[c], rb2.at[src], (c * 2 + core, q))
+
+    walk(steps[:1])
+    for c in order:
+        first(c).wait_recv()
+        @pl.loop(0, ns)
+        def _(t):
+            pair[c, t] = (pair[c, t].astype(F32) + g_ref[c * 2 + core, t].astype(F32)).astype(BF)
+        first_small(c).wait_recv()
+        spair[c] = spair[c] + sm_ref[c * 2 + core]
+        if c is not chip:
+            second(c, chip).start()
+            second_small(c, chip).start()
+    walk(steps[1:middle])
+
+    for c in chips:
+        second(c, c).wait_recv()
+        second_small(c, c).wait_recv()
+    @pl.loop(0, ns)
+    def _(t):
+        total = pair[chip, t].astype(F32)
+        for c in chips:
+            total = total + plane[c, t].astype(F32)
+        pair[chip, t] = total.astype(BF)
+    small = spair[chip]
+    for c in chips:
+        small = small + splane[c]
+    ssum[...] = small
+
+    def third(t, src):
+        return send(pair.at[chip, t], f_ref.at[src], sc.at[t], rc.at[src], (d, t))
+
+    last = send(ssum, so_ref, tc, rc2, final_to)
+    @pl.when(stays)
+    def _():
+        so_ref[...] = ssum[...]
+    @pl.when(jnp.logical_not(stays))
+    def _():
+        last.start()
+    for t in others:
+        third(t, q).start()
+    f_ref[q] = pair[chip, q]
+    walk(steps[middle:])
+
+    for s in range(nsub):
+        total = gm_ref[q, s].astype(F32)
+        out_ref[s] = total
+        @pl.when(q > 0)
+        def _():
+            rise(q, s, gm_ref.at[q, s]).wait_recv()
+            out_ref[s] += up[q, s].astype(F32)
+        @pl.when(q < ns - 1)
+        def _():
+            sink(q, s, gm_ref.at[q, s]).wait_recv()
+            out_ref[s] += down[q, s].astype(F32)
+    for t in others:
+        third(t, t).wait_recv()
+    @pl.when(jnp.logical_not(stays))
+    def _():
+        last.wait_recv()
+        last.wait_send()
+    for c in order:
+        first(c).wait_send()
+        first_small(c).wait_send()
+    for c in chips:
+        second(c, chip).wait_send()
+        second_small(c, chip).wait_send()
+    for t in others:
+        third(t, q).wait_send()
+    for k, s in steps:
+        t = ns - 1 - k
+        @pl.when(q < t)
+        def _():
+            rise(t, s, gm_ref.at[t, s]).wait_send()
+        @pl.when(q > k)
+        def _():
+            sink(k, s, gm_ref.at[k, s]).wait_send()
+
+
+def home(g, small, gm, nd, ns, cid):
+    rows, cols = g.shape[2:]
+    nc, nsub = nd // 2, 4
+    length, width = gm.shape
+    part = length // ns // nsub
+    v = small.shape[1:]
+    gm = gm.reshape(ns, nsub, part, width)
+    f, so, out = pl.pallas_call(
+        functools.partial(home_kernel, nd, ns, nsub),
+        out_shape=[
+            jax.ShapeDtypeStruct((ns, rows, cols), BF),
+            jax.ShapeDtypeStruct(v, F32),
+            jax.ShapeDtypeStruct((nsub, part, width), F32),
+        ],
+        in_specs=[VMEM] * 3, out_specs=[VMEM] * 3,
+        scratch_shapes=[
+            pltpu.VMEM((nc, ns, rows, cols), BF), pltpu.VMEM((nc, ns, rows, cols), BF),
+            pltpu.VMEM((nc,) + v, F32), pltpu.VMEM((nc,) + v, F32), pltpu.VMEM(v, F32),
+            pltpu.VMEM((ns, nsub, part, width), BF), pltpu.VMEM((ns, nsub, part, width), BF),
+            DMA((nc,)), DMA((nc,)), DMA((nc,)), DMA((nc,)), DMA((ns,)), DMA((ns,)),
+            DMA((nc,)), DMA((nc,)), DMA((nc,)), DMA((nc,)), DMA(()), DMA(()),
+            DMA((ns, nsub)), DMA((ns, nsub)), DMA((ns, nsub)), DMA((ns, nsub)),
+        ],
+        compiler_params=pltpu.CompilerParams(
+            collective_id=cid, has_side_effects=True, vmem_limit_bytes=56 * 2**20),
+        name="home",
+    )(g, small, gm)
+    return f, so, out.reshape(length // ns, width)
+
+
 def frequency_embed(timestep):
     half_width = FREQ // 2
     counter = jnp.arange(half_width, dtype=F32)
@@ -208,7 +487,7 @@
     state = decay_forward.shape[1]
     taps = filter_weight.shape[0]
     rows_in = input_weight.shape[0]
-    units = select_weight.shape[0]
+    lanes = select_weight.shape[1]
 
     hid = lax.all_gather(hidden[0], "seq", axis=0, tiled=True)
     mask = lax.all_gather(pad_mask[0].astype(BF), "seq", axis=0, tiled=True).astype(F32)[:, None]
@@ -260,10 +539,10 @@
     sigma_filter = jax.nn.sigmoid(filtered)
     active = (filtered * sigma_filter).astype(BF)
     active32 = active.astype(F32)
-    selected = lax.psum(dot(active, select_q), "seq")
+    selected = column_sum(dot(active, select_q), ns, BF, 0)
     low_rank = selected[:, :rank].astype(BF)
-    b_rows = selected[:, rank : rank + state]
-    c_rows = selected[:, rank + state :]
+    b_rows = selected[:, rank : rank + state].astype(F32)
+    c_rows = selected[:, rank + state :].astype(F32)
     pre_steps = dot(low_rank, step_q) + sbias.astype(F32).T
     steps = jax.nn.softplus(pre_steps)
     rates_f = -jnp.exp(log_f.astype(F32)).T
@@ -303,7 +582,7 @@
     grad_pre_low = grad_pre.astype(BF)
     grad_step_t = dot_tn(grad_pre_low, low_rank)
     grad_low_rank = dot_nt(grad_pre_low, step_q)
-    grad_selected = lax.psum(jnp.concatenate([grad_low_rank, grad_b, grad_c], axis=1), "seq").astype(BF)
+    grad_selected = column_sum(jnp.concatenate([grad_low_rank, grad_b, grad_c], axis=1), ns, BF, 1)
     grad_select = dot_tn(active, grad_selected)
     grad_active = steps * adjb + dot_nt(grad_selected, select_q)
     grad_filtered = grad_active * sigma_filter * (1.0 + filtered * (1.0 - sigma_filter))
@@ -316,7 +595,23 @@
         filter_rows.append(jnp.sum(grad_filtered * padded[k : k + length], axis=0))
     grad_filter_bias = jnp.sum(grad_filtered, axis=0)
     grad_projected = jnp.concatenate([grad_inner * mask, grad_gate_branch], axis=1).astype(BF)
-    grad_modded = lax.psum_scatter(dot_nt(grad_projected, win), "seq", scatter_dimension=0, tiled=True)
+    units = part // nd
+    fil = jnp.stack(filter_rows + [grad_filter_bias, grad_step_bias])
+    fil = fil.reshape(-1, nd, units).transpose(1, 0, 2)
+    fil = jnp.pad(fil, ((0, 0), (0, 16 - fil.shape[1]), (0, lanes - units)))
+    mid = jnp.concatenate([grad_step_t, grad_decay_f.T, grad_decay_r.T], axis=1)
+    small = jnp.concatenate([grad_select.reshape(nd, units, lanes), mid.reshape(nd, units, lanes), fil], axis=1)
+    grads = jnp.concatenate([dot_tn(modded, grad_projected), dot_tn(grad_branch, gated)], axis=1)
+    grads = grads.astype(BF).reshape(nd, ns, rows_in, 3 * part)
+    grads = jnp.pad(grads, ((0, 0), (0, 0), (0, -rows_in % 16), (0, 0)))
+    grads, small, grad_modded = home(grads, small, dot_nt(grad_projected, win).astype(BF), nd, ns, 2)
+    grads = grads[:, :rows_in].astype(F32)
+    g_in = grads[:, :, : 2 * part].reshape(ns, rows_in, 2, part).transpose(1, 2, 0, 3).reshape(rows_in, 2 * inner)
+    g_out = grads[:, :, 2 * part :].transpose(1, 0, 2).reshape(rows_in, inner).T
+    gs_select = small[:units]
+    mid = small[units : 2 * units]
+    gs_step, gs_f, gs_r = mid[:, :rank], mid[:, rank : rank + state], mid[:, rank + state :]
+    fil = small[2 * units :, :units]
 
     normed, inverse = norm(hidden[0])
     grad_shifts = jnp.sum(grad_modded, axis=0)
@@ -328,25 +623,11 @@
         - normed * jnp.mean(grad_normed * normed, axis=1, keepdims=True)
     )
 
-    def home(grad, cols):
-        got = lax.psum_scatter(grad, "dp", scatter_dimension=0, tiled=True)
-        got = got.reshape(ns, -1, cols)
-        return lax.all_to_all(got, "seq", 0, 0)
-
-    g_in = home(dot_tn(modded, grad_projected), 2 * part)
-    g_in = g_in.reshape(ns, rows_in, 2, part).transpose(1, 2, 0, 3).reshape(rows_in, 2 * inner)
-    g_out = home(dot_tn(grad_branch, gated), part).transpose(1, 0, 2).reshape(-1, inner).T
-    small = jnp.concatenate(
-        [grad_select, grad_step_t, grad_decay_f.T, grad_decay_r.T, jnp.stack(filter_rows, axis=1),
-         grad_filter_bias[:, None], grad_step_bias[:, None]], axis=1)
-    small = jnp.pad(small, ((0, 0), (0, -used % 128)))
-    small = lax.psum_scatter(small, "dp", scatter_dimension=0, tiled=True)
-    small = lax.ppermute(small, every, [(a * ns + b, b * nd + a) for a in range(nd) for b in range(ns)])
-    gs_select, gs_step, gs_f, gs_r, gs_filter, gs_fbias, gs_sbias = [small[:, a:b] for a, b in cuts]
-    grad_mod = jnp.concatenate([grad_shifts, grad_scales, grad_gate, embedded[0].astype(F32)])
-    grad_mod = lax.all_gather(grad_mod, every, axis=0, tiled=False).reshape(nd, ns, -1)
-    embeds = grad_mod[:, 0, 3 * width :]
-    grad_mod = jnp.sum(grad_mod[:, :, : 3 * width], axis=1)
+    grad_mod = jnp.concatenate([grad_shifts, grad_scales, grad_gate, embedded[0].astype(F32) / ns])
+    grad_mod = jnp.pad(grad_mod, (0, -grad_mod.shape[0] % 1024)).reshape(-1, 128)
+    grad_mod = mod_gather(grad_mod, nd, ns, 3).reshape(nd, -1)
+    embeds = grad_mod[:, 3 * width : 3 * width + FREQ]
+    grad_mod = grad_mod[:, : 3 * width]
     me = d * ns + q
     mine = lax.dynamic_slice_in_dim(embeds, me * modulation_weight.shape[0], modulation_weight.shape[0], 1)
     g_modw = lax.dot_general(mine, grad_mod, (((0,), (0,)), ((), ())), precision=HIGHEST)
@@ -361,9 +642,9 @@
         g_out,
         gs_f,
         gs_r,
-        gs_filter.T,
-        gs_fbias[:, 0],
-        gs_sbias[:, 0],
+        fil[:taps],
+        fil[taps],
+        fil[taps + 1],
         g_modw,
         g_modb,
     )

time: 1110 us -> 741 us (0.67)
  waiting for transfers between devices: 518 us -> 122 us
  Pallas kernels: 190 us -> 337 us
  blocking collectives: 195 us -> 85.9 us
    reduce_scatter x3 -> x0, waiting for transfers between devices: 233 us -> none  [the longest x1 124 us: body(): lax.psum_scatter(dot_nt(grad_projected, win), 'seq', scatter_dimension=0,...]
    pallas_call x0 -> x4, Pallas kernels: none -> 147 us  [the longest x1 90.4 us: home(): pl.pallas_call(functools.partial(home_kernel, nd, ns, nsub), out_shape=[j...]
    reduce_scatter x1, waiting for transfers between devices: 113 us -> 0.01 us  [body(): lax.psum_scatter(dot_nt(gated, wout), 'seq', scatter_dimension=0, tiled=T...]
    all_gather x1 -> x0, blocking collectives: 72.7 us -> none  [body(): lax.all_gather(grad_mod, every, axis=0, tiled=False).reshape(nd, ns, -1)]
    psum x1 -> x0, blocking collectives: 28.5 us -> none  [body(): lax.psum(jnp.concatenate([grad_low_rank, grad_b, grad_c], axis=1), 'seq')]
    psum x1 -> x0, waiting for transfers between devices: 17.6 us -> none  [body(): selected = lax.psum(dot(active, select_q), 'seq')]
    all_gather x1, waiting for transfers between devices: 38.8 us -> 25 us  [body(): pack = lax.all_gather(pack, every, axis=0, tiled=True)]
    all_to_all x2 -> x0, waiting for transfers between devices: 13.6 us -> none  [home(): return lax.all_to_all(got, 'seq', 0, 0)]
  transfers between devices with their start and end apart: 15 -> 7, of which waited for: 10 -> 3; matrix products, arithmetic and copies ran while one was open for 8% -> 19% of each run, Pallas kernels for 6% -> 44%
where the time goes in v2:
time: 741 us; the launch traced here: 733 us
  Pallas kernels  337 us (45%)
  waiting for transfers between devices  122 us (16%)
  blocking collectives  85.9 us (12%)
  matrix products  67.5 us (9%)
  local copies, waits for them, and re-layouts  64.3 us (9%)
  other arithmetic  40.5 us (5%)
  between operations  15.8 us (2%)
    pallas_call x2, Pallas kernels, bwd_scan(): pl.pallas_call(functools.partial(bwd_kernel, flip=flip), grid=(blocks, ch...  122 us
    pallas_call x1, Pallas kernels, home(): pl.pallas_call(functools.partial(home_kernel, nd, ns, nsub), out_shape=[j...  90.4 us
    pallas_call x2, Pallas kernels, fwd_scan(): pl.pallas_call(functools.partial(fwd_kernel, flip=flip), grid=(blocks, ch...  67.9 us
    all_gather x1, waiting for transfers between devices, body(): hid = lax.all_gather(hidden[0], 'seq', axis=0, tiled=True)  59.8 us
    pallas_call x2, Pallas kernels, column_sum(): pl.pallas_call(functools.partial(column_sum_kernel, ns), out_shape=jax.Sh...  42.7 us
    unnamed x1, blocking collectives  39.2 us
    all_gather x1, waiting for transfers between devices, body(): lax.all_gather(win, 'dp', axis=0, tiled=False).reshape(width, 2 * part)  35.5 us
    dot_general x5, matrix products, dot(): return jnp.dot(a, b, preferred_element_type=F32)  30.2 us
  transfers between devices with their start and end apart: 7, of which 3 were waited for; matrix products, arithmetic and copies ran while one was open for 19% of the time, Pallas kernels for 44%

profile of v2, /device:TPU:0, one launch (start us, length us, event | category | flops | bytes accessed | tf_op | source)
XLA Modules:
  0.0 733.4 jit_solution(11558452829454040606)
XLA Ops:
  17.4 23.4 %all_to_all.10 = bf16[4,48,1536]{2,1,0:T(8,128)(2,1)} all-to-all(bf16[4,48,1536]{2,1,0:T(8,128)(2,1)S(1)} %reshape.397), channel_id=1, replica_groups=mesh['dp'=8,'seq'=4] {'seq'}, dimensions={0} | all-to-all | bytes 1179648 | tf_op jit(solution)/shard_map/all_to_all | solution.py:495
  41.2 14.0 %all_to_all.11 = bf16[4,48,768]{2,1,0:T(8,128)(2,1)} all-to-all(bf16[4,48,768]{2,1,0:T(8,128)(2,1)S(1)} %copy.87), channel_id=1, replica_groups=mesh['dp'=8,'seq'=4] {'seq'}, dimensions={0} | all-to-all | bytes 589824 | tf_op jit(solution)/shard_map/all_to_all | solution.py:498
  57.5 39.2 %all-reduce.5 = bf16[4608]{0:T(1024)(128)(2,1)S(1)} all-reduce(bf16[4608]{0:T(1024)(128)(2,1)S(1)} %dynamic-update-slice), channel_id=1, replica_groups=mesh['dp'=8,'seq'=4] {'dp','seq'}, use_global_device_ids=true, to_apply=%add.5 | all-reduce | flops 4608 | bytes 18432
  97.2 9.3 %all-gather.2 = bf16[1,1024]{1,0:T(2,128)(2,1)S(1)} all-gather(bf16[1,256]{1,0:T(2,128)(2,1)S(1)} %get-tuple-element.143), channel_id=4, replica_groups=mesh['dp'=8,'seq'=4] {'seq'}, dimensions={1}, use_global_device_ids=true | all-gather | bytes 2560 | tf_op jit(solution)/shard_map/all_gather | solution.py:493
  108.7 25.0 %all-gather.14.cloned.1.call-done = bf16[3072,384]{1,0:T(8,128)(2,1)} async-done(((bf16[96,384]{1,0:T(8,128)(2,1)}), bf16[3072,384]{1,0:T(8,128)(2,1)}) %all-gather.14.cloned.1.call-update) | async-done | bytes 2359312 | tf_op jit(solution)/shard_map/all_gather | solution.py:505
  138.0 59.8 %all-gather.16.cloned.1.call-done = bf16[1,1024,1536]{2,1,0:T(8,128)(2,1)} async-done(((bf16[1,256,1536]{2,1,0:T(8,128)(2,1)}), bf16[1,1024,1536]{2,1,0:T(8,128)(2,1)}) %all-gather.16.cloned.1.call-update) | async-done | bytes 3145744 | tf_op jit(solution)/shard_map/all_gather | solution.py:492
  201.5 35.5 %all-gather.18.cloned.1.call-done = bf16[32,48,1536]{2,1,0:T(8,128)(2,1)} async-done(((bf16[4,48,1536]{2,1,0:T(8,128)(2,1)}), bf16[32,48,1536]{2,1,0:T(8,128)(2,1)}) %all-gather.18.cloned.1.call-update) | async-done | bytes 4718608 | tf_op jit(solution)/shard_map/all_gather | solution.py:496
  237.1 8.7 %fusion.63 = f32[1024,1536]{1,0:T(8,128)S(1)} fusion(bf16[1536,1536]{1,0:T(8,128)(2,1)} %bitcast.181, bf16[1,1024,1536]{2,1,0:T(8,128)(2,1)} %all-gather.16.cloned.1.call-done, f32[1536]{0:T(1024)S(1)} %get-tuple-element.109, f32[1536]{0:T(1024)S(1)} %get-tuple-element.110, f32[1024]{0:T(1024)S(1)} %add_rsqrt_fusion, f32[1024]{0:T(1024)S(1)} %broadcast_multiply_fusion), kind=kOutput, calls=%fused_computation.151 | convolution fusion | flops 4841275392 | bytes 14176256 | tf_op jit(solution)/shard_map/dot_general | solution.py:451
  252.0 21.6 %column_sum.2 = bf16[4,256,128]{2,1,0:T(8,128)(2,1)S(1)} custom-call(f32[4,256,128]{2,1,0:T(8,128)S(1)} %bitcast.144), custom_call_target="tpu_custom_call" | custom-call | tf_op jit(solution)/shard_map/column_sum/pallas_call | solution.py:204
  281.6 6.6 convert_multiply_fusion.2
  288.2 5.9 broadcast_in_dim.16.bb_ref
  294.1 33.9 %fwd_scan.2 = (f32[1024,768]{1,0:T(8,128)S(1)}, bf16[16384,768]{1,0:T(8,128)(2,1)}) custom-call(f32[1024,768]{1,0:T(8,128)} %get-tuple-element.120.step_ref, f32[1024,768]{1,0:T(8,128)} %get-tuple-element.119.u_ref, f32[16,768]{1,0:T(8,128)S(1)} %bitcast_multiply_fusion.4.rate_ref, f32[1024,16,128]{2,1,0:T(8,128)} %broadcast_in_dim.16.bb_ref, ...), custom_call_target="tpu_custom_call" | custom-call | tf_op jit(solution)/shard_map/fwd_scan/pallas_call | solution.py:46
  329.6 34.0 %fwd_scan.3 = (f32[1024,768]{1,0:T(8,128)S(1)}, bf16[16384,768]{1,0:T(8,128)(2,1)}) custom-call(f32[1024,768]{1,0:T(8,128)} %get-tuple-element.120.step_ref, f32[1024,768]{1,0:T(8,128)} %get-tuple-element.119.u_ref, f32[16,768]{1,0:T(8,128)S(1)} %bitcast_multiply_fusion.2.rate_ref, f32[1024,16,128]{2,1,0:T(8,128)} %broadcast_in_dim.16.bb_ref, ...), custom_call_target="tpu_custom_call" | custom-call | tf_op jit(solution)/shard_map/fwd_scan/pallas_call | solution.py:46
  365.3 11.2 %multiply_convert_fusion = (bf16[1024,768]{1,0:T(8,128)(2,1)}, bf16[1024,768]{1,0:T(8,128)(2,1)S(1)}, f32[1024,768]{1,0:T(8,128)}) fusion(f32[1024,1536]{1,0:T(8,128)} %copy-done.21, f32[1024,768]{1,0:T(8,128)} %copy-done.2, f32[1024,768]{1,0:T(8,128)} %copy-done.3, bf16[1536,768]{1,0:T(8,128)(2,1)} %bitcast.183, ...), kind=kOutput, calls=%fused_computation.27 | convolution fusion | flops 2434007040 | bytes 21243904 | tf_op jit(solution)/shard_map/dot_general | solution.py:451
  384.5 6.6 broadcast_in_dim.20.cb_ref
  391.1 60.3 %bwd_scan.2 = (f32[1024,768]{1,0:T(8,128)S(1)}, f32[1024,768]{1,0:T(8,128)}, f32[64,256]{1,0:T(8,128)S(1)}, f32[64,256]{1,0:T(8,128)S(1)}, f32[2,16,384]{2,1,0:T(8,128)S(1)}) custom-call(f32[1024,768]{1,0:T(8,128)} %get-tuple-element.120.step_ref, f32[1024,768]{1,0:T(8,128)} %get-tuple-element.119.u_ref, f32[1024,768]{1,0:T(8,128)} %get-tuple-element.125.gy_ref, ...), custom_call_target="tpu_custom_call" | custom-call | tf_op jit(solution)/shard_map/bwd_scan/pallas_call | solution.py:139
  453.1 62.1 %bwd_scan.3 = (f32[1024,768]{1,0:T(8,128)S(1)}, f32[1024,768]{1,0:T(8,128)}, f32[64,256]{1,0:T(8,128)S(1)}, f32[64,256]{1,0:T(8,128)S(1)}, f32[2,16,384]{2,1,0:T(8,128)S(1)}) custom-call(f32[1024,768]{1,0:T(8,128)} %get-tuple-element.120.step_ref, f32[1024,768]{1,0:T(8,128)} %get-tuple-element.119.u_ref, f32[1024,768]{1,0:T(8,128)} %get-tuple-element.125.gy_ref, ...), custom_call_target="tpu_custom_call" | custom-call | tf_op jit(solution)/shard_map/bwd_scan/pallas_call | solution.py:139
  518.1 7.1 fusion.66
  528.0 21.0 %column_sum.3 = bf16[4,256,128]{2,1,0:T(8,128)(2,1)S(1)} custom-call(f32[4,256,128]{2,1,0:T(8,128)S(1)} %pad_maximum_fusion.4.p_ref), custom_call_target="tpu_custom_call" | custom-call | tf_op jit(solution)/shard_map/column_sum/pallas_call | solution.py:204
  571.1 9.0 %convolution_convert_fusion = bf16[1536,1536]{1,0:T(8,128)(2,1)} fusion(bf16[1024,768]{1,0:T(8,128)(2,1)S(1)} %copy-done.52, bf16[1024,768]{1,0:T(8,128)(2,1)S(1)} %copy-done.20, bf16[1,1024,1536]{2,1,0:T(8,128)(2,1)S(1)} %copy-done.10, f32[1536]{0:T(1024)S(1)} %copy-done.42, f32[1536]{0:T(1024)S(1)} %get-tuple-element.110, f32[1024]{0:T(1024)S(1)} %copy-done.45, ...), kind=kOutput, calls=%fused_computation.3 | convolution fusion | flops 4849926144 | bytes 11030528 | tf_op jit(solution)/shard_map/dot_general | solution.py:459
  580.0 5.7 pad_maximum_fusion.g_ref
  585.8 8.7 %convolution_convert_fusion.1 = bf16[1024,1536]{1,0:T(8,128)(2,1)} fusion(bf16[1536,1536]{1,0:T(8,128)(2,1)} %bitcast.182, bf16[1024,768]{1,0:T(8,128)(2,1)} %get-tuple-element.123, bf16[1024,768]{1,0:T(8,128)(2,1)S(1)} %copy-done.20), kind=kOutput, calls=%fused_computation.17 | convolution fusion | flops 4839702528 | bytes 11010048 | tf_op jit(solution)/shard_map/dot_general | solution.py:455
  594.4 90.4 %home.1 = (bf16[4,48,2304]{2,1,0:T(8,128)(2,1)}, f32[208,128]{1,0:T(8,128)}, f32[4,64,1536]{2,1,0:T(8,128)}) custom-call(bf16[8,4,48,2304]{3,2,1,0:T(8,128)(2,1)} %pad_maximum_fusion.g_ref, f32[8,208,128]{2,1,0:T(8,128)} %select_maximum_fusion.sm_ref, bf16[4,4,64,1536]{3,2,1,0:T(8,128)(2,1)} %bitcast.156), custom_call_target="tpu_custom_call" | custom-call | tf_op jit(solution)/shard_map/home/pallas_call | solution.py:419
  707.8 13.6 %mod_gather.1 = f32[8,40,128]{2,1,0:T(8,128)S(1)} custom-call(f32[40,128]{1,0:T(8,128)S(1)} %fusion.48.g_ref), custom_call_target="tpu_custom_call" | custom-call | tf_op jit(solution)/shard_map/mod_gather/pallas_call | solution.py:240
  (239 shorter events, 105.0 us)
Async XLA Ops:
  7.2 99.3 %all-gather.12.cloned.1.call-start = ((), (), s32[]{:S(2)}) async-start(), calls=%async_computation.3 | async-start | bytes 2433024 | tf_op jit(solution)/shard_map/all_gather | solution.py:514
  7.9 125.8 %all-gather.14.cloned.1.call-start = ((), (), s32[]{:S(2)}) async-start(), calls=%async_computation.4 | async-start | bytes 2433024 | tf_op jit(solution)/shard_map/all_gather | solution.py:505
  13.6 27.4 %copy-start.23 = (bf16[3072,48]{0,1:T(8,128)(2,1)S(1)}, bf16[3072,48]{0,1:T(8,128)(2,1)}, u32[]{:S(2)}) copy-start(bf16[3072,48]{0,1:T(8,128)(2,1)} %param.21) | copy-start | bytes 884740
  14.3 183.4 %all-gather.16.cloned.1.call-start = ((), (), s32[]{:S(2)}) async-start(), calls=%async_computation.6 | async-start | bytes 3932160 | tf_op jit(solution)/shard_map/all_gather | solution.py:492
  15.0 222.0 %all-gather.18.cloned.1.call-start = ((), (), s32[]{:S(2)}) async-start(), calls=%async_computation.7 | async-start | bytes 5308416 | tf_op jit(solution)/shard_map/all_gather | solution.py:496
  17.0 40.2 %copy-start.50 = (bf16[144]{0:T(256)(128)(2,1)S(1)}, bf16[144]{0:T(256)(128)(2,1)}, u32[]{:S(2)}) copy-start(bf16[144]{0:T(256)(128)(2,1)} %param.28) | copy-start | bytes 868
  17.0 79.6 %copy-start.47 = (s32[1,256]{1,0:T(1,128)S(1)}, s32[1,256]{1,0:T(1,128)}, u32[]{:S(2)}) copy-start(s32[1,256]{1,0:T(1,128)} %param.16) | copy-start | bytes 3076
  40.9 324.3 %all-gather.20.cloned.1.call-start = ((), (), s32[]{:S(2)}) async-start(), calls=%async_computation.8 | async-start | bytes 2654208 | tf_op jit(solution)/shard_map/all_gather | solution.py:499
  55.3 310.0 %all-gather.22.cloned.1.call-start = ((), (), s32[]{:S(2)}) async-start(), calls=%async_computation.9 | async-start | bytes 3932160 | tf_op jit(solution)/shard_map/all_gather | solution.py:516
  55.8 646.5 %reduce-scatter.2.cloned.1.call-start = ((), (), s32[]{:S(2)}) async-start(), calls=%async_computation.5 | async-start | bytes 7864320 | tf_op jit(solution)/shard_map/reduce_scatter | solution.py:559
  106.5 258.8 %copy-start.28 = (f32[1,1024]{1,0:T(1,128)}, f32[1,1024]{1,0:T(1,128)S(1)}, u32[]{:S(2)}) copy-start(f32[1,1024]{1,0:T(1,128)S(1)} %convert_element_type.173) | copy-start | bytes 12292
  108.7 128.3 %copy-start.41 = (f32[1536]{0:T(1024)}, f32[1536]{0:T(1024)S(1)}, u32[]{:S(2)}) copy-start(f32[1536]{0:T(1024)S(1)} %get-tuple-element.109) | copy-start | bytes 18436
  108.7 256.5 %copy-start.31 = (f32[1536]{0:T(1024)}, f32[1536]{0:T(1024)S(1)}, u32[]{:S(2)}) copy-start(f32[1536]{0:T(1024)S(1)} %get-tuple-element.108) | copy-start | bytes 18436
  134.8 111.3 %copy-start.24 = (f32[768]{0:T(1024)}, f32[768]{0:T(1024)S(1)}, u32[]{:S(2)}) copy-start(f32[768]{0:T(1024)S(1)} %get-tuple-element.113) | copy-start | bytes 9220
  134.9 111.3 %copy-start.26 = (f32[768]{0:T(1024)}, f32[768]{0:T(1024)S(1)}, u32[]{:S(2)}) copy-start(f32[768]{0:T(1024)S(1)} %get-tuple-element.114) | copy-start | bytes 9220
  136.4 145.1 %copy-start.30 = (f32[768]{0:T(1024)}, f32[768]{0:T(1024)S(1)}, u32[]{:S(2)}) copy-start(f32[768]{0:T(1024)S(1)} %convert_reduce_fusion.2) | copy-start | bytes 9220
  200.6 45.3 %copy-start.33 = (f32[1024]{0:T(1024)}, f32[1024]{0:T(1024)S(1)}, u32[]{:S(2)}) copy-start(f32[1024]{0:T(1024)S(1)} %broadcast_multiply_fusion) | copy-start | bytes 12292
  201.5 44.3 %copy-start.44 = (f32[1024]{0:T(1024)}, f32[1024]{0:T(1024)S(1)}, u32[]{:S(2)}) copy-start(f32[1024]{0:T(1024)S(1)} %add_rsqrt_fusion) | copy-start | bytes 12292
  365.3 12.4 %copy-start.49 = (bf16[32,48,768]{2,1,0:T(8,128)(2,1)S(1)}, bf16[32,48,768]{2,1,0:T(8,128)(2,1)}, u32[]{:S(2)}) copy-start(bf16[32,48,768]{2,1,0:T(8,128)(2,1)} %all-gather.20.cloned.1.call-done) | copy-start | bytes 7077892
  518.1 31.0 %copy-start.15 = (f32[1024,768]{1,0:T(8,128)S(1)}, f32[1024,768]{1,0:T(8,128)}, u32[]{:S(2)}) copy-start(f32[1024,768]{1,0:T(8,128)} %get-tuple-element.122) | copy-start | bytes 9437188
  518.1 31.0 %copy-start.16 = (f32[1024,768]{1,0:T(8,128)S(1)}, f32[1024,768]{1,0:T(8,128)}, u32[]{:S(2)}) copy-start(f32[1024,768]{1,0:T(8,128)} %get-tuple-element.33) | copy-start | bytes 9437188
  518.1 31.0 %copy-start.17 = (f32[1024,768]{1,0:T(8,128)S(1)}, f32[1024,768]{1,0:T(8,128)}, u32[]{:S(2)}) copy-start(f32[1024,768]{1,0:T(8,128)} %get-tuple-element.35) | copy-start | bytes 9437188
  525.2 26.5 %copy-start.8 = (bf16[1024,768]{1,0:T(8,128)(2,1)}, bf16[1024,768]{1,0:T(8,128)(2,1)S(1)}, u32[]{:S(2)}) copy-start(bf16[1024,768]{1,0:T(8,128)(2,1)S(1)} %get-tuple-element.118) | copy-start | bytes 4718596
  525.2 23.9 %copy-start.4 = (f32[1024,768]{1,0:T(8,128)S(1)}, f32[1024,768]{1,0:T(8,128)}, u32[]{:S(2)}) copy-start(f32[1024,768]{1,0:T(8,128)} %get-tuple-element.120.step_ref) | copy-start | bytes 9437188
  (36 other events, 156.4 us)
Sparse Core Ops, SparseCore 0:
  10.8 63.3 all-gather.11
  77.6 56.0 all-gather.13
  135.3 62.3 all-gather.15
  199.5 37.5 all-gather.17
  238.8 29.0 all-gather.19
  269.2 63.5 all-gather.21
  382.6 110.8 reduce-scatter.1

commit v3 on v2

--- a/solution.py
+++ b/solution.py
@@ -439,6 +439,304 @@
     return f, so, out.reshape(length // ns, width)
 
 
+def start_kernel(nd, ns, nsub, hid, win, wout, pack, mask, emb, modw, modb,
+                 hid_o, wx_o, pack_o, mask_o, mod_o,
+                 eland, prod, rowp, land1, land2,
+                 su, ru, sd, rd, swz, rw, swp, swm, spz, rp, spp, spm, sk, rk, se, re, s1, r1, s2, r2, own):
+    d, q = lax.axis_index("dp"), lax.axis_index("seq")
+    nc = nd // 2
+    chip, core = d // 2, lax.rem(d, 2)
+    mate = (chip * 2 + 1 - core, q)
+    chips = [lax.rem(chip + k, nc) for k in range(1, nc)]
+    others = [lax.rem(q + k, ns) for k in range(1, ns)]
+    peers = [lax.rem(d + k, nd) for k in range(1, nd)]
+    spread = nd // ns
+    me = d * ns + q
+    part = wout.shape[1] // ns
+    greet([(d, t) for t in others] + [(e, q) for e in peers])
+
+    def column(ref, at):
+        return ref.at[:, pl.ds(pl.multiple_of(at * part, 128), part)]
+
+    def pieces(t):
+        return (column(win, t), column(win, ns + t), column(wout, t))
+
+    def across(k, t, idx):
+        return [
+            send(src, wx_o.at[idx, :, j * part:(j + 1) * part], swz.at[k, j], rw.at[idx, j], (d, t))
+            for j, src in enumerate(pieces(t))
+        ]
+
+    for k, t in enumerate(others):
+        for copy in across(k, t, me):
+            copy.start()
+    keep = [pltpu.make_async_copy(src, wx_o.at[me, :, j * part:(j + 1) * part], own.at[j])
+            for j, src in enumerate(pieces(q))]
+    keep.append(pltpu.make_async_copy(hid, hid_o.at[q], own.at[3]))
+    for copy in keep:
+        copy.start()
+
+    plane = d // spread
+    slot = lax.rem(d, spread) * ns + q
+    pack_z = send(pack, pack_o.at[slot], spz, rp.at[slot], (d, plane))
+    pack_own = pltpu.make_async_copy(pack, pack_o.at[slot], own.at[4])
+
+    @pl.when(plane == q)
+    def _():
+        pack_own.start()
+
+    @pl.when(plane != q)
+    def _():
+        pack_z.start()
+
+    def masks(k, t, src):
+        return send(mask_o.at[src], mask_o.at[src], sk.at[k], rk.at[src], (d, t))
+
+    def embeds(k, e, src):
+        return send(eland.at[src], eland.at[src], se.at[k], re.at[src], (e, q))
+
+    mask_o[q] = mask[...]
+    eland[d] = emb[...]
+    for k, e in enumerate(peers):
+        embeds(k, e, d).start()
+    for k, t in enumerate(others):
+        masks(k, t, q).start()
+
+    def rise(k, s):
+        t = jnp.maximum(q - k, 0)
+        src = hid.at[s] if k == 0 else hid_o.at[t, s]
+        return send(src, hid_o.at[t, s], su.at[k, s], ru.at[k, s], (d, q + 1))
+
+    def sink(k, s):
+        t = jnp.minimum(q + k, ns - 1)
+        src = hid.at[s] if k == 0 else hid_o.at[t, s]
+        return send(src, hid_o.at[t, s], sd.at[k, s], rd.at[k, s], (d, q - 1))
+
+    def hop(k, s):
+        @pl.when(q >= k)
+        def _():
+            if k:
+                rise(k - 1, s).wait_recv()
+            if k < ns - 1:
+                @pl.when(q + 1 < ns)
+                def _():
+                    rise(k, s).start()
+
+        @pl.when(q + k < ns)
+        def _():
+            if k:
+                sink(k - 1, s).wait_recv()
+            if k < ns - 1:
+                @pl.when(q >= 1)
+                def _():
+                    sink(k, s).start()
+
+    for s in range(nsub):
+        hop(0, s)
+
+    def piece(ref, idx):
+        return ref.at[idx]
+
+    def plane_w(c, idx, t):
+        return send(wx_o.at[idx], wx_o.at[idx], swp.at[c, t], rwp_of(idx), (c * 2 + core, q))
+
+    def rwp_of(idx):
+        return rw.at[idx, 3]
+
+    def mate_w(c, idx, t):
+        return send(wx_o.at[idx], wx_o.at[idx], swm.at[c, t], rwp_of(idx), mate)
+
+    def spread_w(t):
+        idx = d * ns + t
+        for c in chips:
+            plane_w(c, idx, t).start()
+        mate_w(chip, idx, t).start()
+
+    for copy in keep[:3]:
+        copy.wait()
+    spread_w(q)
+
+    for k, e in enumerate(peers):
+        embeds(k, e, e).wait_recv()
+    rows = modw.shape[0]
+    here = lax.broadcasted_iota(jnp.int32, (FREQ, rows), 0)
+    pick = here - lax.broadcasted_iota(jnp.int32, (FREQ, rows), 1)
+    count = FREQ // (nd * ns)
+    keep_col = lax.broadcasted_iota(jnp.int32, (FREQ, rows), 1) < count
+    pick = jnp.where(jnp.logical_and(pick == me * count, keep_col), 1.0, 0.0).astype(BF)
+    mine = jnp.dot(eland[...].reshape(nd * 16, FREQ), pick, preferred_element_type=F32).astype(BF)
+    prod[...] = jnp.dot(mine, modw[...], preferred_element_type=F32)
+
+    lines = prod.shape[1] // 128
+    @pl.loop(0, nd)
+    def _(e):
+        rowp[e] = modb[...]
+        for j in range(lines):
+            rowp[e, j:j + 1, :] += prod[pl.ds(pl.multiple_of(e * 16, 16), 1), j * 128:(j + 1) * 128]
+
+    def to_item(k, e, src):
+        return send(rowp.at[e], land1.at[src], s1.at[k], r1.at[src], (e, q))
+
+    for k, e in enumerate(peers):
+        to_item(k, e, d).start()
+
+    for k, t in enumerate(others):
+        for copy in across(k, t, d * ns + t):
+            copy.wait_recv()
+        spread_w(t)
+
+    def plane_p(c, i, t):
+        return send(pack_o.at[i], pack_o.at[i], spp.at[c, t], rp.at[i], (c * 2 + core, q))
+
+    def mate_p(c, i, t):
+        return send(pack_o.at[i], pack_o.at[i], spm.at[c, t], rp.at[i], mate)
+
+    base = lax.rem(d, spread) * ns
+
+    @pl.when(plane == q)
+    def _():
+        pack_own.wait()
+        for t in others:
+            send(pack, pack_o.at[base + t], spz, rp.at[base + t], (d, plane)).wait_recv()
+        for t in range(ns):
+            for c in chips:
+                plane_p(c, base + t, t).start()
+            mate_p(chip, base + t, t).start()
+
+    total = rowp[d]
+    for k, e in enumerate(peers):
+        to_item(k, e, e).wait_recv()
+        total = total + land1[e]
+    land2[q] = total
+
+    def to_column(k, t, src):
+        return send(land2.at[src], land2.at[src], s2.at[k], r2.at[src], (d, t))
+
+    for k, t in enumerate(others):
+        to_column(k, t, q).start()
+
+    def relay_w(c, t):
+        idx = (c * 2 + core) * ns + t
+        plane_w(c, idx, t).wait_recv()
+        mate_w(c, idx, t).start()
+
+    def holds(c):
+        return (c * 2 + core) // spread == q
+
+    def relay_p(c):
+        first = lax.rem(c * 2 + core, spread) * ns
+        @pl.when(holds(c))
+        def _():
+            for t in range(ns):
+                plane_p(c, first + t, t).wait_recv()
+                mate_p(c, first + t, t).start()
+
+    hops = [(k, s) for k in range(1, ns) for s in range(nsub)]
+    relays = [(c, t) for t in [q] + others for c in chips]
+    at = 0
+    for i, (k, s) in enumerate(hops):
+        upto = len(relays) * (i + 1) // len(hops)
+        hop(k, s)
+        for c, t in relays[at:upto]:
+            relay_w(c, t)
+        at = upto
+    for c in chips:
+        relay_p(c)
+    for k, t in enumerate(others):
+        to_column(k, t, t).wait_recv()
+    total = land2[0]
+    for t in range(1, ns):
+        total = total + land2[t]
+    mod_o[...] = total
+
+    twin = 1 - core
+    for c in range(nc):
+        for t in range(ns):
+            idx = (c * 2 + twin) * ns + t
+            mate_w(c, idx, t).wait_recv()
+        first = lax.rem(c * 2 + twin, spread) * ns
+        @pl.when((c * 2 + twin) // spread == q)
+        def _():
+            for t in range(ns):
+                mate_p(c, first + t, t).wait_recv()
+    for k, t in enumerate(others):
+        masks(k, t, t).wait_recv()
+    keep[3].wait()
+
+    for k, t in enumerate(others):
+        for copy in across(k, t, me):
+            copy.wait_send()
+        masks(k, t, q).wait_send()
+        to_column(k, t, q).wait_send()
+    for k, e in enumerate(peers):
+        embeds(k, e, d).wait_send()
+        to_item(k, e, d).wait_send()
+
+    @pl.when(plane != q)
+    def _():
+        pack_z.wait_send()
+
+    @pl.when(plane == q)
+    def _():
+        for t in range(ns):
+            for c in chips:
+                plane_p(c, base + t, t).wait_send()
+            mate_p(chip, base + t, t).wait_send()
+
+    for t in range(ns):
+        for c in chips:
+            plane_w(c, d * ns + t, t).wait_send()
+            mate_w(c, (c * 2 + core) * ns + t, t).wait_send()
+        mate_w(chip, d * ns + t, t).wait_send()
+    for c in chips:
+        first = lax.rem(c * 2 + core, spread) * ns
+        @pl.when(holds(c))
+        def _():
+            for t in range(ns):
+                mate_p(c, first + t, t).wait_send()
+    for k in range(ns - 1):
+        for s in range(nsub):
+            @pl.when(jnp.logical_and(q >= k, q + 1 < ns))
+            def _():
+                rise(k, s).wait_send()
+            @pl.when(jnp.logical_and(q + k < ns, q >= 1))
+            def _():
+                sink(k, s).wait_send()
+
+
+def start(hidden, mask, win, wout, pack, embedded, modw, modb, nd, ns, cid):
+    nsub = 4
+    length, width = hidden.shape
+    rows, inner = wout.shape
+    nc = nd // 2
+    hidden = hidden.reshape(nsub, length // nsub, width)
+    lines = modb.shape
+    return pl.pallas_call(
+        functools.partial(start_kernel, nd, ns, nsub),
+        out_shape=[
+            jax.ShapeDtypeStruct((ns,) + hidden.shape, BF),
+            jax.ShapeDtypeStruct((nd * ns, rows, 3 * inner // ns), BF),
+            jax.ShapeDtypeStruct((nd,) + pack.shape, BF),
+            jax.ShapeDtypeStruct((ns,) + mask.shape, BF),
+            jax.ShapeDtypeStruct(lines, F32),
+        ],
+        in_specs=[HBM, HBM, HBM, HBM, VMEM, VMEM, VMEM, VMEM],
+        out_specs=[HBM, HBM, HBM, VMEM, VMEM],
+        scratch_shapes=[
+            pltpu.VMEM((nd,) + embedded.shape, BF), pltpu.VMEM((nd * 16, modw.shape[1]), F32),
+            pltpu.VMEM((nd,) + lines, F32), pltpu.VMEM((nd,) + lines, F32), pltpu.VMEM((ns,) + lines, F32),
+            DMA((ns - 1, nsub)), DMA((ns - 1, nsub)), DMA((ns - 1, nsub)), DMA((ns - 1, nsub)),
+            DMA((ns, 3)), DMA((nd * ns, 4)), DMA((nc, ns)), DMA((nc, ns)),
+            DMA(()), DMA((nd,)), DMA((nc, ns)), DMA((nc, ns)),
+            DMA((ns,)), DMA((ns,)), DMA((nd,)), DMA((nd,)),
+            DMA((nd,)), DMA((nd,)), DMA((ns,)), DMA((ns,)), DMA((5,)),
+        ],
+        compiler_params=pltpu.CompilerParams(
+            collective_id=cid, has_side_effects=True, vmem_limit_bytes=40 * 2**20),
+        name="start",
+    )(hidden, win, wout, pack, mask, embedded, modw, modb)
+
+
 def frequency_embed(timestep):
     half_width = FREQ // 2
     counter = jnp.arange(half_width, dtype=F32)
@@ -489,34 +787,32 @@
     rows_in = input_weight.shape[0]
     lanes = select_weight.shape[1]
 
-    hid = lax.all_gather(hidden[0], "seq", axis=0, tiled=True)
-    mask = lax.all_gather(pad_mask[0].astype(BF), "seq", axis=0, tiled=True).astype(F32)[:, None]
-    win = input_weight.reshape(rows_in, 2, ns, part).transpose(2, 0, 1, 3).reshape(ns, rows_in, 2 * part)
-    win = lax.all_to_all(win, "seq", 0, 0)
-    win = lax.all_gather(win, "dp", axis=0, tiled=False).reshape(width, 2 * part)
-    wout = output_weight.T.reshape(-1, ns, part).transpose(1, 0, 2)
-    wout = lax.all_to_all(wout, "seq", 0, 0)
-    wout = lax.all_gather(wout, "dp", axis=0, tiled=False).reshape(width, part)
-    pack = jnp.concatenate(
-        [select_weight, step_weight.T, decay_forward, decay_reverse, filter_weight.T,
-         filter_bias[:, None], step_bias[:, None]], axis=1)
-    used = pack.shape[1]
-    pack = jnp.pad(pack, ((0, 0), (0, -used % 128)))
-    pack = lax.all_gather(pack, every, axis=0, tiled=True)
-    pack = lax.dynamic_slice_in_dim(pack, q * part, part, 0)
-    cuts = []
-    at = 0
-    for size in (rank + 2 * state, rank, state, state, taps, 1, 1):
-        cuts.append((at, at + size))
-        at += size
-    select_q, step_q, log_f, log_r, filt, fbias, sbias = [pack[:, a:b] for a, b in cuts]
-    step_q = step_q.T
-    modw = lax.all_gather(modulation_weight, every, axis=0, tiled=True)
-    modb = lax.all_gather(modulation_bias, every, axis=0, tiled=True)
-    cot = lax.all_gather(cotangent[0], "seq", axis=0, tiled=True)
-
+    units = part // nd
     embedded = jax.nn.silu(frequency_embed(timestep)).astype(BF)
-    modulation = dot(embedded, modw) + modb.astype(F32)
+    fil = jnp.concatenate([filter_weight, filter_bias[None], step_bias[None]])
+    fil = jnp.pad(fil, ((0, 16 - fil.shape[0]), (0, lanes - units)))
+    mid = jnp.concatenate([step_weight.T, decay_forward, decay_reverse], axis=1)
+    pack = jnp.concatenate([select_weight, mid, fil])
+    mask = jnp.pad(pad_mask[0].astype(BF).reshape(-1, 128), ((0, 16 - local_len // 128), (0, 0)))
+    shard = (-modulation_weight.shape[0] % 16, 0)
+    modb = jnp.zeros((-(-3 * width // 1024) * 1024,), F32)
+    modb = lax.dynamic_update_slice(modb, modulation_bias.astype(F32), ((d * ns + q) * modulation_bias.shape[0],))
+    row_pad = ((0, -rows_in % 16), (0, 0))
+    hid, wx, pack, mask, modulation = start(
+        hidden[0], mask, jnp.pad(input_weight, row_pad), jnp.pad(output_weight.T, row_pad), pack,
+        jnp.pad(embedded, ((0, 15), (0, 0))),
+        jnp.pad(modulation_weight, ((0, shard[0]), (0, 0))), modb.reshape(-1, 128), nd, ns, 4)
+    hid = hid.reshape(length, width)
+    wx = wx[:, :rows_in].reshape(width, 3 * part)
+    win, wout = wx[:, : 2 * part], wx[:, 2 * part :]
+    mask = mask[:, : local_len // 128].reshape(length, 1).astype(F32)
+    select_q = pack[:, :units].reshape(part, lanes)
+    mid = pack[:, units : 2 * units].reshape(part, lanes)
+    step_q = mid[:, :rank].T
+    log_f, log_r = mid[:, rank : rank + state], mid[:, rank + state :]
+    fil = pack[:, 2 * units :, :units].transpose(1, 0, 2).reshape(16, part).astype(F32)
+    filt32, fbias, sbias = fil[:taps].T, fil[taps][None], fil[taps + 1][None]
+    modulation = modulation.reshape(1, -1)[:, : 3 * width]
     shifts = modulation[:, :width]
     scales = modulation[:, width : 2 * width]
     gate_scale = modulation[:, 2 * width :]
@@ -531,19 +827,20 @@
     projected = dot(modded, win)
     inner_part = projected[:, :part].astype(BF).astype(F32) * mask
     gate_branch = projected[:, part:]
-    filt32 = filt.astype(F32)
     padded = jnp.pad(inner_part, ((taps - 1, 0), (0, 0)))
-    filtered = fbias.astype(F32).T
+    filtered = fbias
     for k in range(taps):
         filtered = filtered + filt32[:, k][None, :] * padded[k : k + length]
     sigma_filter = jax.nn.sigmoid(filtered)
     active = (filtered * sigma_filter).astype(BF)
     active32 = active.astype(F32)
     selected = column_sum(dot(active, select_q), ns, BF, 0)
+    cot, selected = lax.optimization_barrier((cotangent[0], selected))
+    cot = lax.all_gather(cot, "seq", axis=0, tiled=True)
     low_rank = selected[:, :rank].astype(BF)
     b_rows = selected[:, rank : rank + state].astype(F32)
     c_rows = selected[:, rank + state :].astype(F32)
-    pre_steps = dot(low_rank, step_q) + sbias.astype(F32).T
+    pre_steps = dot(low_rank, step_q) + sbias
     steps = jax.nn.softplus(pre_steps)
     rates_f = -jnp.exp(log_f.astype(F32)).T
     rates_r = -jnp.exp(log_r.astype(F32)).T
@@ -595,7 +892,6 @@
         filter_rows.append(jnp.sum(grad_filtered * padded[k : k + length], axis=0))
     grad_filter_bias = jnp.sum(grad_filtered, axis=0)
     grad_projected = jnp.concatenate([grad_inner * mask, grad_gate_branch], axis=1).astype(BF)
-    units = part // nd
     fil = jnp.stack(filter_rows + [grad_filter_bias, grad_step_bias])
     fil = fil.reshape(-1, nd, units).transpose(1, 0, 2)
     fil = jnp.pad(fil, ((0, 0), (0, 16 - fil.shape[1]), (0, lanes - units)))

time: 741 us -> 608 us (0.82)
  waiting for transfers between devices: 122 us -> 0.04 us
  blocking collectives: 85.9 us -> 0 us
  Pallas kernels: 337 us -> 418 us
  matrix products: 67.5 us -> 56.8 us
    all_gather x6 -> x1, waiting for transfers between devices: 120 us -> 0.01 us  [body(): cot = lax.all_gather(cot, 'seq', axis=0, tiled=True)]
    pallas_call x0 -> x1, Pallas kernels: none -> 80.2 us  [start(): pl.pallas_call(functools.partial(start_kernel, nd, ns, nsub), out_shape=[...]
    unnamed x1 -> x0, blocking collectives: 39.2 us -> none
    all_to_all x2 -> x0, blocking collectives: 37.5 us -> none  [the longest x1 23.4 us: body(): win = lax.all_to_all(win, 'seq', 0, 0)]
    all_gather x1 -> x0, blocking collectives: 9.27 us -> none  [body(): lax.all_gather(pad_mask[0].astype(BF), 'seq', axis=0, tiled=True)]
    unnamed x122 -> x82, local copies, waits for them, and re-layouts: 17.2 us -> 23.4 us
    dot_general x5 -> x4, matrix products: 30.2 us -> 24.2 us  [dot(): return jnp.dot(a, b, preferred_element_type=F32)]
  transfers between devices with their start and end apart: 7 -> 2, of which waited for: 3 -> 0; matrix products, arithmetic and copies ran while one was open for 19% -> 16% of each run, Pallas kernels for 44% -> 50%
where the time goes in v3:
time: 608 us; the launch traced here: 600 us
  Pallas kernels  418 us (69%)
  local copies, waits for them, and re-layouts  66.3 us (11%)
  matrix products  56.8 us (9%)
  other arithmetic  42.1 us (7%)
  between operations  15.8 us (3%)
    pallas_call x2, Pallas kernels, bwd_scan(): pl.pallas_call(functools.partial(bwd_kernel, flip=flip), grid=(blocks, ch...  122 us
    pallas_call x1, Pallas kernels, home(): pl.pallas_call(functools.partial(home_kernel, nd, ns, nsub), out_shape=[j...  90.6 us
    pallas_call x1, Pallas kernels, start(): pl.pallas_call(functools.partial(start_kernel, nd, ns, nsub), out_shape=[...  80.2 us
    pallas_call x2, Pallas kernels, fwd_scan(): pl.pallas_call(functools.partial(fwd_kernel, flip=flip), grid=(blocks, ch...  67.9 us
    pallas_call x2, Pallas kernels, column_sum(): pl.pallas_call(functools.partial(column_sum_kernel, ns), out_shape=jax.Sh...  40.6 us
    dot_general x4, matrix products, dot(): return jnp.dot(a, b, preferred_element_type=F32)  24.2 us
    unnamed x82, local copies, waits for them, and re-layouts  23.4 us
    dot_general x4, matrix products, dot_nt(): lax.dot_general(a, b, (((1,), (1,)), ((), ())), preferred_element_type=F32)  17.3 us
  transfers between devices with their start and end apart: 2, of which 0 were waited for; matrix products, arithmetic and copies ran while one was open for 16% of the time, Pallas kernels for 50%

profile of v3, /device:TPU:0, one launch (start us, length us, event | category | flops | bytes accessed | tf_op | source)
XLA Modules:
  0.0 599.7 jit_solution(8580769558690173891)
XLA Ops:
  17.5 80.2 %start.1 = (bf16[4,4,64,1536]{3,2,1,0:T(8,128)(2,1)S(1)}, bf16[32,48,2304]{2,1,0:T(8,128)(2,1)S(1)}, bf16[8,208,128]{2,1,0:T(8,128)(2,1)S(1)}, bf16[4,16,128]{2,1,0:T(8,128)(2,1)S(1)}, f32[40,128]{1,0:T(8,128)S(1)}) custom-call(bf16[4,64,1536]{2,1,0:T(8,128)(2,1)S(1)} %bitcast.131, bf16[48,6144]{1,0:T(8,128)(2,1)S(1)} %copy-done.4, ...), custom_call_target="tpu_custom_call" | custom-call | tf_op jit(solution)/shard_map/start/pallas_call | solution.py:714
  109.0 6.9 %fusion.6 = f32[1024,1536]{1,0:T(8,128)S(1)} fusion(bf16[1024,1536]{1,0:T(8,128)(2,1)S(1)} %fusion.3, bf16[1536,2304]{1,0:T(8,128)(2,1)} %bitcast.144), kind=kOutput, calls=%fused_computation.12 | convolution fusion | flops 4831838208 | bytes 14155776 | tf_op jit(solution)/shard_map/dot_general | solution.py:749
  116.3 3.9 multiply_convert_fusion.4
  121.1 19.9 %column_sum.2 = bf16[4,256,128]{2,1,0:T(8,128)(2,1)S(1)} custom-call(f32[4,256,128]{2,1,0:T(8,128)S(1)} %fusion.78.p_ref), custom_call_target="tpu_custom_call" | custom-call | tf_op jit(solution)/shard_map/column_sum/pallas_call | solution.py:204
  149.6 5.6 convert_multiply_fusion.1
  155.2 5.8 broadcast_in_dim.20.bb_ref
  161.0 33.9 %fwd_scan.2 = (f32[1024,768]{1,0:T(8,128)S(1)}, bf16[16384,768]{1,0:T(8,128)(2,1)}) custom-call(f32[1024,768]{1,0:T(8,128)} %get-tuple-element.108.step_ref, f32[1024,768]{1,0:T(8,128)} %get-tuple-element.107.u_ref, f32[16,768]{1,0:T(8,128)S(1)} %bitcast_multiply_fusion.4.rate_ref, f32[1024,16,128]{2,1,0:T(8,128)} %broadcast_in_dim.20.bb_ref, ...), custom_call_target="tpu_custom_call" | custom-call | tf_op jit(solution)/shard_map/fwd_scan/pallas_call | solution.py:46
  196.5 34.1 %fwd_scan.3 = (f32[1024,768]{1,0:T(8,128)S(1)}, bf16[16384,768]{1,0:T(8,128)(2,1)}) custom-call(f32[1024,768]{1,0:T(8,128)} %get-tuple-element.108.step_ref, f32[1024,768]{1,0:T(8,128)} %get-tuple-element.107.u_ref, f32[16,768]{1,0:T(8,128)S(1)} %bitcast_multiply_fusion.2.rate_ref, f32[1024,16,128]{2,1,0:T(8,128)} %broadcast_in_dim.20.bb_ref, ...), custom_call_target="tpu_custom_call" | custom-call | tf_op jit(solution)/shard_map/fwd_scan/pallas_call | solution.py:46
  232.3 11.2 %multiply_convert_fusion.1 = (bf16[1024,768]{1,0:T(8,128)(2,1)}, bf16[1024,768]{1,0:T(8,128)(2,1)S(1)}, f32[1024,768]{1,0:T(8,128)}) fusion(f32[1024,1536]{1,0:T(8,128)} %copy-done.30, f32[1024,768]{1,0:T(8,128)} %copy-done.8, f32[1024,768]{1,0:T(8,128)} %copy-done.9, bf16[1536,2304]{1,0:T(8,128)(2,1)} %bitcast.145, ...), kind=kOutput, calls=%fused_computation.28 | convolution fusion | flops 2434007040 | bytes 21243904 | tf_op jit(solution)/shard_map/dot_general | solution.py:749
  244.6 6.3 %fusion.18 = f32[1024,1536]{1,0:T(8,128)} fusion(bf16[1024,768]{1,0:T(8,128)(2,1)S(1)} %get-tuple-element.112, bf16[1536,2304]{1,0:T(8,128)(2,1)} %bitcast.146), kind=kOutput, calls=%fused_computation.47 | convolution fusion | flops 2415919104 | bytes 10223616 | tf_op jit(solution)/shard_map/dot_general | solution.py:753
  251.6 4.7 copy.52
  258.2 6.6 %broadcast_in_dim.23.cb_ref = f32[1024,16,128]{2,1,0:T(8,128)} broadcast(f32[1024,16]{1,0:T(8,128)} %copy-done.20), dimensions={0,1} | broadcast | bytes 8454144 | tf_op jit(solution)/shard_map/broadcast_in_dim | solution.py:160
  264.8 60.3 %bwd_scan.2 = (f32[1024,768]{1,0:T(8,128)S(1)}, f32[1024,768]{1,0:T(8,128)}, f32[64,256]{1,0:T(8,128)S(1)}, f32[64,256]{1,0:T(8,128)S(1)}, f32[2,16,384]{2,1,0:T(8,128)S(1)}) custom-call(f32[1024,768]{1,0:T(8,128)} %get-tuple-element.108.step_ref, f32[1024,768]{1,0:T(8,128)} %get-tuple-element.107.u_ref, f32[1024,768]{1,0:T(8,128)} %get-tuple-element.113.gy_ref, ...), custom_call_target="tpu_custom_call" | custom-call | tf_op jit(solution)/shard_map/bwd_scan/pallas_call | solution.py:139
  326.8 62.1 %bwd_scan.3 = (f32[1024,768]{1,0:T(8,128)S(1)}, f32[1024,768]{1,0:T(8,128)}, f32[64,256]{1,0:T(8,128)S(1)}, f32[64,256]{1,0:T(8,128)S(1)}, f32[2,16,384]{2,1,0:T(8,128)S(1)}) custom-call(f32[1024,768]{1,0:T(8,128)} %get-tuple-element.108.step_ref, f32[1024,768]{1,0:T(8,128)} %get-tuple-element.107.u_ref, f32[1024,768]{1,0:T(8,128)} %get-tuple-element.113.gy_ref, ...), custom_call_target="tpu_custom_call" | custom-call | tf_op jit(solution)/shard_map/bwd_scan/pallas_call | solution.py:139
  392.6 7.1 %fusion.73 = (f32[768]{0:T(1024)S(1)}, bf16[1024,768]{1,0:T(8,128)(2,1)S(1)}) fusion(f32[1024,768]{1,0:T(8,128)} %get-tuple-element.130, f32[768]{0:T(1024)S(1)} %add.207, f32[1024,768]{1,0:T(8,128)} %get-tuple-element.47, f32[1024,768]{1,0:T(8,128)} %get-tuple-element.49, bf16[1024,768]{1,0:T(8,128)(2,1)S(1)} %get-tuple-element.109, ...), kind=kLoop, calls=%fused_computation.165 | loop fusion | flops 10222848 | bytes 18880512 | tf_op jit(solution)/shard_map/reduce_sum | solution.py:878
  400.7 20.7 %column_sum.3 = bf16[4,256,128]{2,1,0:T(8,128)(2,1)S(1)} custom-call(f32[4,256,128]{2,1,0:T(8,128)S(1)} %pad_maximum_fusion.4.p_ref), custom_call_target="tpu_custom_call" | custom-call | tf_op jit(solution)/shard_map/column_sum/pallas_call | solution.py:204
  423.4 4.7 multiply_reduce_fusion.1
  436.0 4.8 convolution_convert_fusion.1
  440.9 7.0 %convolution_convert_fusion = bf16[8,4,48,1536]{3,2,1,0:T(8,128)(2,1)} fusion(bf16[8,4,48,1024]{3,2,1,0:T(8,128)(2,1)S(1)} %bitcast.158, bf16[1024,768]{1,0:T(8,128)(2,1)S(1)} %copy-done.35, bf16[1024,768]{1,0:T(8,128)(2,1)S(1)} %copy-done.27), kind=kOutput, calls=%fused_computation.9 | convolution fusion | flops 4840488960 | bytes 11010048 | tf_op jit(solution)/shard_map/dot_general | solution.py:757
  447.8 5.8 pad_maximum_fusion.g_ref
  453.6 8.6 %fusion.8 = bf16[1024,1536]{1,0:T(8,128)(2,1)} fusion(bf16[1536,2304]{1,0:T(8,128)(2,1)} %bitcast.147, bf16[1024,768]{1,0:T(8,128)(2,1)} %get-tuple-element.111, bf16[1024,768]{1,0:T(8,128)(2,1)S(1)} %copy-done.27), kind=kOutput, calls=%fused_computation.16 | convolution fusion | flops 4839702528 | bytes 11010048 | tf_op jit(solution)/shard_map/dot_general | solution.py:753
  462.3 90.6 %home.1 = (bf16[4,48,2304]{2,1,0:T(8,128)(2,1)}, f32[208,128]{1,0:T(8,128)}, f32[4,64,1536]{2,1,0:T(8,128)}) custom-call(bf16[8,4,48,2304]{3,2,1,0:T(8,128)(2,1)} %pad_maximum_fusion.g_ref, f32[8,208,128]{2,1,0:T(8,128)} %select_maximum_fusion.sm_ref, bf16[4,4,64,1536]{3,2,1,0:T(8,128)(2,1)} %bitcast.159), custom_call_target="tpu_custom_call" | custom-call | tf_op jit(solution)/shard_map/home/pallas_call | solution.py:419
  568.2 3.2 multiply_reduce_fusion.5
  572.1 16.7 %mod_gather.1 = f32[8,40,128]{2,1,0:T(8,128)S(1)} custom-call(f32[40,128]{1,0:T(8,128)S(1)} %fusion.49.g_ref), custom_call_target="tpu_custom_call" | custom-call | tf_op jit(solution)/shard_map/mod_gather/pallas_call | solution.py:240
  (186 shorter events, 73.5 us)
Async XLA Ops:
  7.2 225.1 %all-gather.2.cloned.1.call-start = ((), (), s32[]{:S(2)}) async-start(), calls=%async_computation.2 | async-start | bytes 3932160 | tf_op jit(solution)/shard_map/all_gather | solution.py:839
  98.5 2.9 copy-start.7
  115.9 4.2 copy-start.30
  116.2 4.3 copy-start.11
  116.2 4.3 copy-start.28
  120.5 20.8 %copy-start.18 = (bf16[8,96,128]{2,1,0:T(8,128)(2,1)S(1)}, bf16[8,96,128]{2,1,0:T(8,128)(2,1)}, u32[]{:S(2)}) copy-start(bf16[8,96,128]{2,1,0:T(8,128)(2,1)} %get-tuple-element.118) | copy-start | bytes 589828
  141.0 427.1 %reduce-scatter.2.cloned.1.call-start = ((), (), s32[]{:S(2)}) async-start(), calls=%async_computation.1 | async-start | bytes 7864320 | tf_op jit(solution)/shard_map/reduce_scatter | solution.py:856
  141.8 6.1 %copy-start.20 = (f32[1024,16]{1,0:T(8,128)}, f32[1024,16]{1,0:T(8,128)S(1)}, u32[]{:S(2)}) copy-start(f32[1024,16]{1,0:T(8,128)S(1)} %get-tuple-element.120) | copy-start | bytes 196612
  392.6 7.2 %copy-start.19 = (bf16[8,96,128]{2,1,0:T(8,128)(2,1)S(1)}, bf16[8,96,128]{2,1,0:T(8,128)(2,1)}, u32[]{:S(2)}) copy-start(bf16[8,96,128]{2,1,0:T(8,128)(2,1)} %get-tuple-element.118) | copy-start | bytes 589828
  392.6 7.7 %copy-start.25 = (f32[4,256,16]{2,1,0:T(8,128)S(1)}, f32[4,256,16]{2,1,0:T(8,128)}, u32[]{:S(2)}) copy-start(f32[4,256,16]{2,1,0:T(8,128)} %concatenate.75) | copy-start | bytes 196612
  392.6 7.8 %copy-start.26 = (f32[4,256,16]{2,1,0:T(8,128)S(1)}, f32[4,256,16]{2,1,0:T(8,128)}, u32[]{:S(2)}) copy-start(f32[4,256,16]{2,1,0:T(8,128)} %concatenate.74) | copy-start | bytes 196612
  392.6 28.8 %copy-start.21 = (f32[1024,768]{1,0:T(8,128)S(1)}, f32[1024,768]{1,0:T(8,128)}, u32[]{:S(2)}) copy-start(f32[1024,768]{1,0:T(8,128)} %get-tuple-element.110) | copy-start | bytes 9437188
  392.6 28.8 %copy-start.23 = (f32[1024,768]{1,0:T(8,128)S(1)}, f32[1024,768]{1,0:T(8,128)}, u32[]{:S(2)}) copy-start(f32[1024,768]{1,0:T(8,128)} %get-tuple-element.47) | copy-start | bytes 9437188
  392.6 28.8 %copy-start.24 = (f32[1024,768]{1,0:T(8,128)S(1)}, f32[1024,768]{1,0:T(8,128)}, u32[]{:S(2)}) copy-start(f32[1024,768]{1,0:T(8,128)} %get-tuple-element.49) | copy-start | bytes 9437188
  399.7 23.6 %copy-start.13 = (bf16[1024,768]{1,0:T(8,128)(2,1)}, bf16[1024,768]{1,0:T(8,128)(2,1)S(1)}, u32[]{:S(2)}) copy-start(bf16[1024,768]{1,0:T(8,128)(2,1)S(1)} %get-tuple-element.106) | copy-start | bytes 4718596
  399.7 21.7 %copy-start.10 = (f32[1024,768]{1,0:T(8,128)S(1)}, f32[1024,768]{1,0:T(8,128)}, u32[]{:S(2)}) copy-start(f32[1024,768]{1,0:T(8,128)} %get-tuple-element.108.step_ref) | copy-start | bytes 9437188
  399.7 21.7 %copy-start.29 = (bf16[8,96,128]{2,1,0:T(8,128)(2,1)S(1)}, bf16[8,96,128]{2,1,0:T(8,128)(2,1)}, u32[]{:S(2)}) copy-start(bf16[8,96,128]{2,1,0:T(8,128)(2,1)} %get-tuple-element.119) | copy-start | bytes 589828
  428.0 5.1 copy-start.16
  436.0 4.8 copy-start.22
  436.0 4.8 copy-start.27
  436.0 4.8 copy-start.35
  552.9 3.8 copy-start.31
  560.4 7.7 %copy-start.15 = (bf16[1,256,1536]{2,1,0:T(8,128)(2,1)S(1)}, bf16[1,256,1536]{2,1,0:T(8,128)(2,1)}, u32[]{:S(2)}) copy-start(bf16[1,256,1536]{2,1,0:T(8,128)(2,1)} %param.29) | copy-start | bytes 2359300
  564.1 7.3 %copy-start.17 = (f32[4,64,1536]{2,1,0:T(8,128)S(1)}, f32[4,64,1536]{2,1,0:T(8,128)}, u32[]{:S(2)}) copy-start(f32[4,64,1536]{2,1,0:T(8,128)} %get-tuple-element.58) | copy-start | bytes 4718596
  (14 other events, 20.5 us)
Sparse Core Ops, SparseCore 0:
  141.2 64.0 all-gather.1
  251.0 111.3 reduce-scatter.1

commit v4 on v3

--- a/solution.py
+++ b/solution.py
@@ -13,151 +13,243 @@
 HIGHEST = lax.Precision.HIGHEST
 LOG2E = 1.4426950408889634
 SUB = 16
+WF = 384
+WB = 768
 F32, BF = jnp.float32, jnp.bfloat16
+NT = (((1,), (1,)), ((), ()))
+
+
+def columns_of(rows_t, base):
+    turned = pltpu.roll(rows_t, rows_t.shape[1] - base, 1)
+    return [jnp.broadcast_to(turned[:, j:j + 1], (rows_t.shape[0], 128)) for j in range(SUB)]
+
 
 def wide(block, lanes):
     return jnp.concatenate([block] * (lanes // 128), axis=1) if lanes > 128 else block
 
-def fwd_kernel(step_ref, u_ref, rate_ref, bb_ref, cblk_ref, y_ref, s_ref, carry_ref, *, flip):
-    rows, lanes = step_ref.shape
-    chunk = pl.program_id(1)
+
+def states_of(base, at):
+    return pl.ds(pl.multiple_of((base + at) * 16, 16), 16)
+
+
+def fwd_kernel(step_f, step_r, u_f, u_r, rate_f, rate_r, bt_f, bt_r, cblk_f, cblk_r,
+               y_f, y_r, s_f, s_r, carry, f0, f1, r0, r1):
+    rows, lanes = step_f.shape
+
     @pl.when(pl.program_id(0) == 0)
     def _():
-        carry_ref[chunk] = jnp.zeros(carry_ref.shape[1:], F32)
-    rates = rate_ref[...]
-    def sub(i, state):
-        at = rows // SUB - 1 - i if flip else i
-        base = pl.multiple_of(at * SUB, SUB)
-        for k in range(SUB):
-            j = SUB - 1 - k if flip else k
-            row = step_ref[pl.ds(base + j, 1), :]
-            u = u_ref[pl.ds(base + j, 1), :]
-            state = jnp.exp2(row * rates) * state + u * wide(bb_ref[base + j], lanes)
-            s_ref[pl.ds(pl.multiple_of((base + j) * 16, 16), 16), :] = state.astype(BF)
-        block = s_ref[pl.ds(pl.multiple_of(base * 16, 256), 256), :]
-        y_ref[pl.ds(base, SUB), :] = jnp.dot(cblk_ref[pl.ds(base, SUB), :], block, preferred_element_type=F32)
-        return state
-    carry_ref[chunk] = lax.fori_loop(0, rows // SUB, sub, carry_ref[chunk])
-
-def fwd_scan(steps, u, rates2, bb, cblk, flip, tile=128, width=384):
+        carry[...] = jnp.zeros(carry.shape, F32)
+
+    wide_by = min(WF, lanes)
+    cuts = [slice(c, c + wide_by) for c in range(0, lanes, wide_by)]
+
+    def walk(states, bases, kept):
+        cols = [columns_of(bt[...], base) for bt, base in zip((bt_f, bt_r), bases)]
+        out = []
+        for cut, pair in zip(cuts, states):
+            pair = list(pair)
+            rates = rate_f[:, cut], rate_r[:, cut]
+            for k in range(SUB):
+                for z, (step, u, s, j) in enumerate(((step_f, u_f, s_f, k), (step_r, u_r, s_r, SUB - 1 - k))):
+                    at = pl.ds(bases[z] + j, 1)
+                    decay = jnp.exp2(step[at, cut] * rates[z])
+                    pair[z] = decay * pair[z] + u[at, cut] * wide(cols[z][j], wide_by)
+                    low = pair[z].astype(BF)
+                    s[states_of(bases[z], j), cut] = low
+                    kept[z][j * 16:(j + 1) * 16, cut] = low
+            out.append(tuple(pair))
+        return tuple(out)
+
+    def mix(base, cblk, kept, y):
+        here = pl.ds(base, SUB)
+        y[here, :] = jnp.dot(cblk[here, :], kept[...], preferred_element_type=F32)
+
+    def start_of(a, flip):
+        a = jnp.maximum(a, 0)
+        return pl.multiple_of(rows - SUB - a * SUB if flip else a * SUB, SUB)
+
+    def two(i, states):
+        for half, (fk, rk, fp, rp) in enumerate(((f0, r0, f1, r1), (f1, r1, f0, r0))):
+            a = 2 * i + half
+            mix(start_of(a - 1, False), cblk_f, fp, y_f)
+            mix(start_of(a - 1, True), cblk_r, rp, y_r)
+            states = walk(states, (start_of(a, False), start_of(a, True)), (fk, rk))
+        return states
+
+    states = tuple((carry[0, :, cut], carry[1, :, cut]) for cut in cuts)
+    states = lax.fori_loop(0, rows // SUB // 2, two, states)
+    mix(rows - SUB, cblk_f, f1, y_f)
+    mix(0, cblk_r, r1, y_r)
+    for cut, pair in zip(cuts, states):
+        carry[0, :, cut], carry[1, :, cut] = pair
+
+
+def fwd_scan(steps, u, rates_f, rates_r, b_t, cblk, tile=128):
     length, lanes = steps.shape
-    blocks, chunks = length // tile, lanes // width
-    order = (lambda t: blocks - 1 - t) if flip else (lambda t: t)
+    blocks = length // tile
+    specs = []
+    for order in (lambda t: t, lambda t: blocks - 1 - t):
+        specs.append((
+            pl.BlockSpec((tile, lanes), lambda t, order=order: (order(t), 0)),
+            pl.BlockSpec((16, lanes), lambda t: (0, 0)),
+            pl.BlockSpec((16, tile), lambda t, order=order: (0, order(t))),
+            pl.BlockSpec((tile, 256), lambda t, order=order: (order(t), 0)),
+            pl.BlockSpec((tile * 16, lanes), lambda t, order=order: (order(t), 0)),
+        ))
+    (row_f, rate, bt_f, blk_f, s_f), (row_r, _, bt_r, blk_r, s_r) = specs
+    y = jax.ShapeDtypeStruct((length, lanes), F32)
+    s = jax.ShapeDtypeStruct((length * 16, lanes), BF)
+    kept = pltpu.VMEM((256, lanes), BF)
     return pl.pallas_call(
-        functools.partial(fwd_kernel, flip=flip),
-        grid=(blocks, chunks),
-        in_specs=[
-            pl.BlockSpec((tile, width), lambda t, c: (order(t), c)),
-            pl.BlockSpec((tile, width), lambda t, c: (order(t), c)),
-            pl.BlockSpec((16, width), lambda t, c: (0, c)),
-            pl.BlockSpec((tile, 16, 128), lambda t, c: (order(t), 0, 0)),
-            pl.BlockSpec((tile, 256), lambda t, c: (order(t), 0)),
-        ],
-        out_specs=[
-            pl.BlockSpec((tile, width), lambda t, c: (order(t), c)),
-            pl.BlockSpec((tile * 16, width), lambda t, c: (order(t), c)),
-        ],
-        out_shape=[jax.ShapeDtypeStruct((length, lanes), F32), jax.ShapeDtypeStruct((length * 16, lanes), BF)],
-        scratch_shapes=[pltpu.VMEM((chunks, 16, width), F32)],
-        compiler_params=pltpu.CompilerParams(vmem_limit_bytes=48 * 2**20, dimension_semantics=("arbitrary", "arbitrary")),
+        fwd_kernel,
+        grid=(blocks,),
+        in_specs=[row_f, row_r, row_f, row_r, rate, rate, bt_f, bt_r, blk_f, blk_r],
+        out_specs=[row_f, row_r, s_f, s_r],
+        out_shape=[y, y, s, s],
+        scratch_shapes=[pltpu.VMEM((2, 16, lanes), F32), kept, kept, kept, kept],
+        compiler_params=pltpu.CompilerParams(vmem_limit_bytes=56 * 2**20, dimension_semantics=("arbitrary",)),
+        cost_estimate=pl.CostEstimate(flops=length * lanes * 16 * 16, transcendentals=0, bytes_accessed=length * lanes * 80),
         name="fwd_scan",
-    )(steps, u, rates2, bb, cblk)
-
-def bwd_kernel(step_ref, u_ref, gy_ref, rate_ref, bb_ref, cb_ref, bblk_ref, s_ref, sprev_ref,
-               dlog_ref, adjb_ref, bg_ref, cg_ref, rg_ref, carry_ref, a_ref, l_ref, *, flip):
-    rows, lanes = step_ref.shape
-    t, chunk = pl.program_id(0), pl.program_id(1)
+    )(steps, steps, u, u, rates_f, rates_r, b_t, b_t, cblk, cblk)
+
+
+def bwd_kernel(step_f, step_r, u_f, u_r, gy_f, gy_r, rate_f, rate_r, ct_f, ct_r, bblk_f, bblk_r, s_f, s_r, sp_f, sp_r,
+               dlog_f, dlog_r, adjb_f, adjb_r, bg_f, bg_r, cg_f, cg_r, rg_f, rg_r, carry,
+               af0, af1, ar0, ar1, lf0, lf1, lr0, lr1):
+    rows, lanes = step_f.shape
+    t = pl.program_id(0)
     last = pl.num_programs(0) - 1
+
     @pl.when(t == 0)
     def _():
-        carry_ref[chunk] = jnp.zeros(carry_ref.shape[1:], F32)
-        rg_ref[chunk] = jnp.zeros(rg_ref.shape[1:], F32)
-    @pl.when(chunk == 0)
-    def _():
-        bg_ref[...] = jnp.zeros(bg_ref.shape, F32)
-        cg_ref[...] = jnp.zeros(cg_ref.shape, F32)
-    rates = rate_ref[...]
+        carry[...] = jnp.zeros(carry.shape, F32)
+        rg_f[...] = jnp.zeros(rg_f.shape, F32)
+        rg_r[...] = jnp.zeros(rg_r.shape, F32)
+
     ones = (lax.broadcasted_iota(jnp.int32, (SUB, 256), 0) == lax.broadcasted_iota(jnp.int32, (SUB, 256), 1) // 16)
     onesb = ones.astype(BF)
-    subs = rows // SUB
-    def sub(i, both):
-        passed, rg = both
-        at = i if flip else subs - 1 - i
-        base = pl.multiple_of(at * SUB, SUB)
-        for k in range(SUB):
-            j = k if flip else SUB - 1 - k
-            row = step_ref[pl.ds(base + j, 1), :]
-            g = gy_ref[pl.ds(base + j, 1), :]
-            adj = g * wide(cb_ref[base + j], lanes) + passed
-            passed = jnp.exp2(row * rates) * adj
-            if flip:
-                before = base + j + 1
-                edge = (j == SUB - 1)
-                inner = s_ref[pl.ds(pl.multiple_of(jnp.minimum(before, rows - 1) * 16, 16), 16), :] if edge else s_ref[pl.ds(pl.multiple_of(before * 16, 16), 16), :]
-                if edge:
-                    outer = jnp.where(t == last, jnp.zeros_like(inner), sprev_ref[...])
-                    inner = jnp.where(before == rows, outer, inner)
-            else:
-                before = base + j - 1
-                edge = (j == 0)
-                inner = s_ref[pl.ds(pl.multiple_of(jnp.maximum(before, 0) * 16, 16), 16), :] if edge else s_ref[pl.ds(pl.multiple_of(before * 16, 16), 16), :]
-                if edge:
-                    outer = jnp.where(t == last, jnp.zeros_like(inner), sprev_ref[...])
-                    inner = jnp.where(before < 0, outer, inner)
-            lg = passed * inner.astype(F32)
-            rg = rg + lg * row
-            a_ref[j * 16:(j + 1) * 16, :] = adj.astype(BF)
-            l_ref[j * 16:(j + 1) * 16, :] = (lg * rates).astype(BF)
+    zero = jnp.zeros((SUB, 256), F32)
+
+    def start_of(a, down):
+        a = jnp.maximum(a, 0)
+        return pl.multiple_of(rows - SUB - a * SUB if down else a * SUB, SUB)
+
+    wide_by = min(WB, lanes)
+    cuts = [slice(c, c + wide_by) for c in range(0, lanes, wide_by)]
+
+    def walk(states, bases, keep_a, keep_l):
+        cols = [columns_of(ct[...], base) for ct, base in zip((ct_f, ct_r), bases)]
+        out = []
+        for cut, pair in zip(cuts, states):
+            pair = list(pair)
+            rates = rate_f[:, cut], rate_r[:, cut]
+            rg = [rg_f[:, cut], rg_r[:, cut]]
+            low_rates = [r.astype(BF) for r in rates]
+            some = [[], []]
+            for k in range(SUB):
+                for z, (step, gy, s, sp, j) in enumerate((
+                        (step_f, gy_f, s_f, sp_f, SUB - 1 - k), (step_r, gy_r, s_r, sp_r, k))):
+                    at = pl.ds(bases[z] + j, 1)
+                    row = step[at, cut]
+                    adj = gy[at, cut] * wide(cols[z][j], wide_by) + pair[z]
+                    pair[z] = jnp.exp2(row * rates[z]) * adj
+                    before = bases[z] + (j + 1 if z else j - 1)
+                    if k < SUB - 1:
+                        inner = s[pl.ds(pl.multiple_of(before * 16, 16), 16), cut]
+                    else:
+                        inside = before < rows if z else before >= 0
+                        safe = jnp.clip(before, 0, rows - 1)
+                        inner = s[pl.ds(pl.multiple_of(safe * 16, 16), 16), cut]
+                        outer = jnp.where(t == last, jnp.zeros_like(inner), sp[:, cut])
+                        inner = jnp.where(inside, inner, outer)
+                    grad = pair[z].astype(BF) * inner
+                    keep_a[z][j * 16:(j + 1) * 16, cut] = adj.astype(BF)
+                    keep_l[z][j * 16:(j + 1) * 16, cut] = grad * low_rates[z]
+                    some[z].append(grad * jnp.broadcast_to(row, (16, wide_by)).astype(BF))
+                    if len(some[z]) == 4:
+                        rg[z] = rg[z] + ((some[z][0] + some[z][1]) + (some[z][2] + some[z][3])).astype(F32)
+                        some[z] = []
+            rg_f[:, cut], rg_r[:, cut] = rg
+            out.append(tuple(pair))
+        return tuple(out)
+
+    def mix(base, a_ref, l_ref, u, gy, bblk, s, dlog, adjb, bg, cg):
+        here = pl.ds(base, SUB)
+        line = pl.ds(base // SUB, 1)
         a = a_ref[...]
-        here = pl.ds(base, SUB)
-        dlog_ref[here, :] = jnp.dot(onesb, l_ref[...], preferred_element_type=F32)
-        adjb_ref[here, :] = jnp.dot(bblk_ref[here, :], a, preferred_element_type=F32)
-        nt = (((1,), (1,)), ((), ()))
-        bgd = lax.dot_general(u_ref[here, :].astype(BF), a, nt, preferred_element_type=F32)
-        sblk = s_ref[pl.ds(pl.multiple_of(base * 16, 256), 256), :]
-        cgd = lax.dot_general(gy_ref[here, :].astype(BF), sblk, nt, preferred_element_type=F32)
-        zero = jnp.zeros_like(bgd)
-        bg_ref[pl.ds(at, 1), :] += jnp.sum(jnp.where(ones, bgd, zero), axis=0, keepdims=True)
-        cg_ref[pl.ds(at, 1), :] += jnp.sum(jnp.where(ones, cgd, zero), axis=0, keepdims=True)
-        return passed, rg
-    passed, rg = lax.fori_loop(0, subs, sub, (carry_ref[chunk], rg_ref[chunk]))
-    carry_ref[chunk] = passed
-    rg_ref[chunk] = rg
-
-def bwd_scan(steps, u, gy, rates2, bb, cb, bblk, states, flip, tile=128, width=384):
+        dlog[here, :] = jnp.dot(onesb, l_ref[...], preferred_element_type=F32)
+        adjb[here, :] = jnp.dot(bblk[here, :], a, preferred_element_type=F32)
+        bgd = lax.dot_general(u[here, :], a, NT, preferred_element_type=F32)
+        block = s[pl.ds(pl.multiple_of(base * 16, 256), 256), :]
+        cgd = lax.dot_general(gy[here, :].astype(BF), block, NT, preferred_element_type=F32)
+        bg[line, :] = jnp.sum(jnp.where(ones, bgd, zero), axis=0, keepdims=True)
+        cg[line, :] = jnp.sum(jnp.where(ones, cgd, zero), axis=0, keepdims=True)
+
+    def mix_f(base, a_ref, l_ref):
+        mix(base, a_ref, l_ref, u_f, gy_f, bblk_f, s_f, dlog_f, adjb_f, bg_f, cg_f)
+
+    def mix_r(base, a_ref, l_ref):
+        mix(base, a_ref, l_ref, u_r, gy_r, bblk_r, s_r, dlog_r, adjb_r, bg_r, cg_r)
+
+    def two(i, states):
+        bufs = ((af0, lf0, ar0, lr0), (af1, lf1, ar1, lr1))
+        for half in range(2):
+            a = 2 * i + half
+            naf, nlf, nar, nlr = bufs[half]
+            paf, plf, par, plr = bufs[1 - half]
+            mix_f(start_of(a - 1, True), paf, plf)
+            mix_r(start_of(a - 1, False), par, plr)
+            states = walk(states, (start_of(a, True), start_of(a, False)), (naf, nar), (nlf, nlr))
+        return states
+
+    states = tuple((carry[0, :, cut], carry[1, :, cut]) for cut in cuts)
+    states = lax.fori_loop(0, rows // SUB // 2, two, states)
+    mix_f(0, af1, lf1)
+    mix_r(rows - SUB, ar1, lr1)
+    for cut, pair in zip(cuts, states):
+        carry[0, :, cut], carry[1, :, cut] = pair
+
+
+def bwd_scan(steps, u, gy, rates_f, rates_r, c_t, bblk, states_f, states_r, tile=128):
     length, lanes = steps.shape
-    blocks, chunks = length // tile, lanes // width
-    order = (lambda t: t) if flip else (lambda t: blocks - 1 - t)
-    if flip:
-        prev = lambda t: jnp.minimum((t + 1) * tile, length - 1)
-    else:
-        prev = lambda t: jnp.maximum((blocks - 1 - t) * tile - 1, 0)
-    row = pl.BlockSpec((tile, width), lambda t, c: (order(t), c))
-    bc = pl.BlockSpec((tile, 16, 128), lambda t, c: (order(t), 0, 0))
-    blk = pl.BlockSpec((tile, 256), lambda t, c: (order(t), 0))
-    diag = pl.BlockSpec((tile // 16, 256), lambda t, c: (order(t), 0))
+    blocks = length // tile
+    down = lambda t: blocks - 1 - t
+    up = lambda t: t
+
+    def specs(order, before):
+        return (
+            pl.BlockSpec((tile, lanes), lambda t: (order(t), 0)),
+            pl.BlockSpec((16, lanes), lambda t: (0, 0)),
+            pl.BlockSpec((16, tile), lambda t: (0, order(t))),
+            pl.BlockSpec((tile, 256), lambda t: (order(t), 0)),
+            pl.BlockSpec((tile * 16, lanes), lambda t: (order(t), 0)),
+            pl.BlockSpec((16, lanes), lambda t: (before(t), 0)),
+            pl.BlockSpec((tile // 16, 256), lambda t: (order(t), 0)),
+        )
+
+    row_f, rate, ct_f, blk_f, s_f, sp_f, diag_f = specs(down, lambda t: jnp.maximum((blocks - 1 - t) * tile - 1, 0))
+    row_r, _, ct_r, blk_r, s_r, sp_r, diag_r = specs(up, lambda t: jnp.minimum((t + 1) * tile, length - 1))
+    y = jax.ShapeDtypeStruct((length, lanes), F32)
+    diag = jax.ShapeDtypeStruct((length // 16, 256), F32)
+    rg = jax.ShapeDtypeStruct((16, lanes), F32)
+    kept = pltpu.VMEM((256, lanes), BF)
     return pl.pallas_call(
-        functools.partial(bwd_kernel, flip=flip),
-        grid=(blocks, chunks),
-        in_specs=[row, row, row, pl.BlockSpec((16, width), lambda t, c: (0, c)), bc, bc, blk,
-            pl.BlockSpec((tile * 16, width), lambda t, c: (order(t), c)),
-            pl.BlockSpec((16, width), lambda t, c: (prev(t), c))],
-        out_specs=[row, row, diag, diag, pl.BlockSpec((chunks, 16, width), lambda t, c: (0, 0, 0))],
-        out_shape=[jax.ShapeDtypeStruct((length, lanes), F32), jax.ShapeDtypeStruct((length, lanes), F32),
-            jax.ShapeDtypeStruct((length // 16, 256), F32), jax.ShapeDtypeStruct((length // 16, 256), F32),
-            jax.ShapeDtypeStruct((chunks, 16, width), F32)],
-        scratch_shapes=[pltpu.VMEM((chunks, 16, width), F32), pltpu.VMEM((256, width), BF), pltpu.VMEM((256, width), BF)],
-        compiler_params=pltpu.CompilerParams(vmem_limit_bytes=48 * 2**20, dimension_semantics=("arbitrary", "arbitrary")),
+        bwd_kernel,
+        grid=(blocks,),
+        in_specs=[row_f, row_r, row_f, row_r, row_f, row_r, rate, rate, ct_f, ct_r, blk_f, blk_r, s_f, s_r, sp_f, sp_r],
+        out_specs=[row_f, row_r, row_f, row_r, diag_f, diag_r, diag_f, diag_r, rate, rate],
+        out_shape=[y, y, y, y, diag, diag, diag, diag, rg, rg],
+        scratch_shapes=[pltpu.VMEM((2, 16, lanes), F32)] + [kept] * 8,
+        compiler_params=pltpu.CompilerParams(vmem_limit_bytes=56 * 2**20, dimension_semantics=("arbitrary",)),
+        cost_estimate=pl.CostEstimate(flops=length * lanes * 16 * 48, transcendentals=0, bytes_accessed=length * lanes * 100),
         name="bwd_scan",
-    )(steps, u, gy, rates2, bb, cb, bblk, states, states)
+    )(steps, steps, u, u, gy, gy, rates_f, rates_r, c_t, c_t, bblk, bblk, states_f, states_r, states_f, states_r)
+
 
 def blockdiag(rows):
     length = rows.shape[0]
     eye = (jnp.arange(length)[:, None] % 16) == (jnp.arange(256)[None, :] // 16)
     return jnp.where(eye, jnp.tile(rows, (1, 16)), 0).astype(BF)
-
-def lanes_of(rows):
-    return jnp.broadcast_to(rows[:, :, None], rows.shape + (128,))
 
 
 MESH = pl.DeviceIdType.MESH
@@ -845,10 +937,8 @@
     rates_f = -jnp.exp(log_f.astype(F32)).T
     rates_r = -jnp.exp(log_r.astype(F32)).T
     drive = steps * active32
-    bb, cb = lanes_of(b_rows), lanes_of(c_rows)
-    bblk, cblk = blockdiag(b_rows), blockdiag(c_rows)
-    mixed_f, states_f = fwd_scan(steps, drive, rates_f * LOG2E, bb, cblk, False)
-    mixed_r, states_r = fwd_scan(steps, drive, rates_r * LOG2E, bb, cblk, True)
+    rates_f2, rates_r2 = rates_f * LOG2E, rates_r * LOG2E
+    mixed_f, mixed_r, states_f, states_r = fwd_scan(steps, drive, rates_f2, rates_r2, b_rows.T, blockdiag(c_rows))
     merged = mixed_f + mixed_r
     sigma_gate = jax.nn.sigmoid(gate_branch)
     silu_gate = gate_branch * sigma_gate
@@ -864,16 +954,14 @@
     grad_gated = dot(grad_branch, wout)
     grad_merged = grad_gated * silu_gate
     grad_gate_branch = grad_gated * merged * sigma_gate * (1.0 + gate_branch * (1.0 - sigma_gate))
-    dlog_f, adjb_f, bg_f, cg_f, rg_f = bwd_scan(
-        steps, drive, grad_merged, rates_f * LOG2E, bb, cb, bblk, states_f, False)
-    dlog_r, adjb_r, bg_r, cg_r, rg_r = bwd_scan(
-        steps, drive, grad_merged, rates_r * LOG2E, bb, cb, bblk, states_r, True)
+    dlog_f, dlog_r, adjb_f, adjb_r, bg_f, bg_r, cg_f, cg_r, rg_f, rg_r = bwd_scan(
+        steps, drive.astype(BF), grad_merged, rates_f2, rates_r2, c_rows.T, blockdiag(b_rows), states_f, states_r)
     adjb = adjb_f + adjb_r
     grad_steps = (dlog_f + dlog_r) * (1.0 / LOG2E) + active32 * adjb
     grad_b = (bg_f + bg_r).reshape(length, state)
     grad_c = (cg_f + cg_r).reshape(length, state)
-    grad_decay_f = rg_f.transpose(1, 0, 2).reshape(state, part) * rates_f
-    grad_decay_r = rg_r.transpose(1, 0, 2).reshape(state, part) * rates_r
+    grad_decay_f = rg_f * rates_f
+    grad_decay_r = rg_r * rates_r
     grad_pre = grad_steps * jax.nn.sigmoid(pre_steps)
     grad_step_bias = jnp.sum(grad_pre, axis=0)
     grad_pre_low = grad_pre.astype(BF)

time: 608 us -> 531 us (0.87)
  Pallas kernels: 418 us -> 340 us
  local copies, waits for them, and re-layouts: 66.3 us -> 43.1 us
  waiting for transfers between devices: 0.04 us -> 16.9 us
  other arithmetic: 42.1 us -> 48.9 us
    pallas_call x4 -> x2, Pallas kernels: 190 us -> 109 us  [the longest x1 73.9 us: bwd_scan(): pl.pallas_call(bwd_kernel, grid=(blocks,), in_specs=[row_f, row_r, row_f,...]
    all_gather x1, waiting for transfers between devices: 0.01 us -> 16.9 us  [body(): cot = lax.all_gather(cot, 'seq', axis=0, tiled=True)]
    broadcast_in_dim x2 -> x0, local copies, waits for them, and re-layouts: 12.4 us -> none  [lanes_of(): return jnp.broadcast_to(rows[:, :, None], rows.shape + (128,))]
    unnamed x82 -> x110, local copies, waits for them, and re-layouts: 23.4 us -> 15.8 us
    pallas_call x2, Pallas kernels: 40.6 us -> 47 us  [column_sum(): pl.pallas_call(functools.partial(column_sum_kernel, ns), out_shape=jax.Sh...]
  transfers between devices with their start and end apart: 2 -> 2, of which waited for: 0 -> 1; matrix products, arithmetic and copies ran while one was open for 16% -> 17% of each run, Pallas kernels for 50% -> 43%
where the time goes in v4:
time: 531 us; the launch traced here: 523 us
  Pallas kernels  340 us (64%)
  matrix products  58.2 us (11%)
  other arithmetic  48.9 us (9%)
  local copies, waits for them, and re-layouts  43.1 us (8%)
  waiting for transfers between devices  16.9 us (3%)
  between operations  15.9 us (3%)
    pallas_call x1, Pallas kernels, home(): pl.pallas_call(functools.partial(home_kernel, nd, ns, nsub), out_shape=[j...  90.8 us
    pallas_call x1, Pallas kernels, start(): pl.pallas_call(functools.partial(start_kernel, nd, ns, nsub), out_shape=[...  80.2 us
    pallas_call x1, Pallas kernels, bwd_scan(): pl.pallas_call(bwd_kernel, grid=(blocks,), in_specs=[row_f, row_r, row_f,...  73.9 us
    pallas_call x2, Pallas kernels, column_sum(): pl.pallas_call(functools.partial(column_sum_kernel, ns), out_shape=jax.Sh...  47 us
    pallas_call x1, Pallas kernels, fwd_scan(): pl.pallas_call(fwd_kernel, grid=(blocks,), in_specs=[row_f, row_r, row_f,...  34.7 us
    dot_general x4, matrix products, dot(): return jnp.dot(a, b, preferred_element_type=F32)  25.8 us
    dot_general x4, matrix products, dot_nt(): lax.dot_general(a, b, (((1,), (1,)), ((), ())), preferred_element_type=F32)  17.2 us
    all_gather x1, waiting for transfers between devices, body(): cot = lax.all_gather(cot, 'seq', axis=0, tiled=True)  16.9 us
  transfers between devices with their start and end apart: 2, of which 1 were waited for; matrix products, arithmetic and copies ran while one was open for 17% of the time, Pallas kernels for 43%

profile of v4, /device:TPU:0, one launch (start us, length us, event | category | flops | bytes accessed | tf_op | source)
XLA Modules:
  0.0 522.9 jit_solution(6271699591932617598)
XLA Ops:
  17.5 80.2 %start.1 = (bf16[4,4,64,1536]{3,2,1,0:T(8,128)(2,1)S(1)}, bf16[32,48,2304]{2,1,0:T(8,128)(2,1)S(1)}, bf16[8,208,128]{2,1,0:T(8,128)(2,1)S(1)}, bf16[4,16,128]{2,1,0:T(8,128)(2,1)S(1)}, f32[40,128]{1,0:T(8,128)S(1)}) custom-call(bf16[4,64,1536]{2,1,0:T(8,128)(2,1)S(1)} %bitcast.129, bf16[48,6144]{1,0:T(8,128)(2,1)S(1)} %copy-done.2, ...), custom_call_target="tpu_custom_call" | custom-call | tf_op jit(solution)/shard_map/start/pallas_call | solution.py:806
  98.5 2.8 copy-done.5
  108.1 2.6 fusion.3
  110.7 7.8 %fusion.6 = f32[1024,1536]{1,0:T(8,128)S(1)} fusion(bf16[1024,1536]{1,0:T(8,128)(2,1)} %fusion.3, bf16[1536,2304]{1,0:T(8,128)(2,1)} %bitcast.138), kind=kOutput, calls=%fused_computation.12 | convolution fusion | flops 4831838208 | bytes 14155776 | tf_op jit(solution)/shard_map/dot_general | solution.py:841
  119.4 3.7 multiply_convert_fusion.4
  123.7 19.9 %column_sum.2 = bf16[4,256,128]{2,1,0:T(8,128)(2,1)S(1)} custom-call(f32[4,256,128]{2,1,0:T(8,128)S(1)} %fusion.82.p_ref), custom_call_target="tpu_custom_call" | custom-call | tf_op jit(solution)/shard_map/column_sum/pallas_call | solution.py:296
  150.1 6.3 %fusion.77 = (bf16[1024,768]{1,0:T(8,128)(2,1)}, f32[1024,768]{1,0:T(8,128)}, f32[1024,768]{1,0:T(8,128)}, f32[1024,768]{1,0:T(8,128)}) fusion(bf16[1024,768]{1,0:T(8,128)(2,1)S(1)} %get-tuple-element.110, f32[768]{0:T(1024)S(1)} %add.207, bf16[768,128]{1,0:T(8,128)(2,1)S(1)} %bitcast.148, bf16[1024,128]{0,1:T(8,128)(2,1)S(1)} %copy.68), kind=kOutput, calls=%fused_computation.168 | convolution fusion | flops 158859264 | bytes 12980224 | tf_op jit(solution)/shard_map/dot_general | solution.py:841
  156.4 34.7 %fwd_scan.1 = (f32[1024,768]{1,0:T(8,128)}, f32[1024,768]{1,0:T(8,128)}, bf16[16384,768]{1,0:T(8,128)(2,1)}, bf16[16384,768]{1,0:T(8,128)(2,1)}) custom-call(f32[1024,768]{1,0:T(8,128)} %get-tuple-element.109.step_f.step_r, f32[1024,768]{1,0:T(8,128)} %get-tuple-element.109.step_f.step_r, f32[1024,768]{1,0:T(8,128)} %get-tuple-element.108.u_f.u_r, ...), custom_call_target="tpu_custom_call" | custom-call | flops 201326592 | bytes 62914560 | tf_op jit(solution)/shard_map/fwd_scan/pallas_call | solution.py:103
  191.1 16.9 %all-gather.2.cloned.1.call-done = bf16[1024,1536]{1,0:T(8,128)(2,1)} async-done(((bf16[256,1536]{1,0:T(8,128)(2,1)}), bf16[1024,1536]{1,0:T(8,128)(2,1)}) %all-gather.2.cloned.1.call-update) | async-done | bytes 3145744 | tf_op jit(solution)/shard_map/all_gather | solution.py:931
  208.0 11.1 %multiply_convert_fusion.1 = (bf16[1024,768]{1,0:T(8,128)(2,1)}, bf16[1024,768]{1,0:T(8,128)(2,1)S(1)}, f32[1024,768]{1,0:T(8,128)}) fusion(f32[1024,1536]{1,0:T(8,128)} %copy-done.20, f32[1024,768]{1,0:T(8,128)} %get-tuple-element.43, f32[1024,768]{1,0:T(8,128)} %get-tuple-element.44, bf16[1536,2304]{1,0:T(8,128)(2,1)} %bitcast.139, ...), kind=kOutput, calls=%fused_computation.28 | convolution fusion | flops 2434007040 | bytes 21243904 | tf_op jit(solution)/shard_map/dot_general | solution.py:841
  220.3 6.2 %fusion.18 = f32[1024,1536]{1,0:T(8,128)} fusion(bf16[1024,768]{1,0:T(8,128)(2,1)S(1)} %get-tuple-element.113, bf16[1536,2304]{1,0:T(8,128)(2,1)} %bitcast.140), kind=kOutput, calls=%fused_computation.47 | convolution fusion | flops 2415919104 | bytes 10223616 | tf_op jit(solution)/shard_map/dot_general | solution.py:845
  227.7 4.7 copy.53
  235.5 73.9 %bwd_scan.1 = (f32[1024,768]{1,0:T(8,128)}, f32[1024,768]{1,0:T(8,128)}, f32[1024,768]{1,0:T(8,128)}, f32[1024,768]{1,0:T(8,128)}, f32[64,256]{1,0:T(8,128)}, /*...) custom-call(f32[1024,768]{1,0:T(8,128)} %get-tuple-element.109.step_f.ste, ...), custom_call_target="tpu_custom_call" | custom-call | flops 603979776 | bytes 78643200 | tf_op jit(solution)/shard_map/bwd_scan/pallas_call | solution.py:236
  315.4 7.8 %fusion.75 = (f32[768]{0:T(1024)}, bf16[1024,768]{1,0:T(8,128)(2,1)S(1)}) fusion(f32[1024,768]{1,0:T(8,128)} %get-tuple-element.133, f32[768]{0:T(1024)} %copy-done.35, f32[1024,768]{1,0:T(8,128)} %get-tuple-element.48, f32[1024,768]{1,0:T(8,128)} %get-tuple-element.49, bf16[1024,768]{1,0:T(8,128)(2,1)S(1)} %get-tuple-element.110, ...), kind=kLoop, calls=%fused_computation.167 | loop fusion | flops 10222848 | bytes 18880512 | tf_op jit(solution)/shard_map/reduce_sum | solution.py:966
  324.1 27.1 %column_sum.3 = bf16[4,256,128]{2,1,0:T(8,128)(2,1)S(1)} custom-call(f32[4,256,128]{2,1,0:T(8,128)S(1)} %pad_maximum_fusion.4.p_ref), custom_call_target="tpu_custom_call" | custom-call | tf_op jit(solution)/shard_map/column_sum/pallas_call | solution.py:296
  353.3 4.7 multiply_reduce_fusion.1
  362.7 4.8 convolution_convert_fusion.1
  367.6 7.0 %convolution_convert_fusion = bf16[8,4,48,1536]{3,2,1,0:T(8,128)(2,1)} fusion(bf16[8,4,48,1024]{3,2,1,0:T(8,128)(2,1)S(1)} %bitcast.151, bf16[1024,768]{1,0:T(8,128)(2,1)S(1)} %copy-done.49, bf16[1024,768]{1,0:T(8,128)(2,1)S(1)} %copy-done.18), kind=kOutput, calls=%fused_computation.9 | convolution fusion | flops 4840488960 | bytes 11010048 | tf_op jit(solution)/shard_map/dot_general | solution.py:849
  374.6 5.8 %pad_maximum_fusion.g_ref = bf16[8,4,48,2304]{3,2,1,0:T(8,128)(2,1)} fusion(bf16[8,4,48,768]{3,2,1,0:T(8,128)(2,1)S(1)} %bitcast.153, bf16[8,4,48,1536]{3,2,1,0:T(8,128)(2,1)} %convolution_convert_fusion), kind=kLoop, calls=%fused_computation.1 | loop fusion | flops 14155776 | bytes 14155776 | tf_op jit(solution)/shard_map/concatenate | solution.py:988
  380.4 8.6 %fusion.8 = bf16[1024,1536]{1,0:T(8,128)(2,1)} fusion(bf16[1536,2304]{1,0:T(8,128)(2,1)} %bitcast.141, bf16[1024,768]{1,0:T(8,128)(2,1)} %get-tuple-element.112, bf16[1024,768]{1,0:T(8,128)(2,1)S(1)} %copy-done.18), kind=kOutput, calls=%fused_computation.16 | convolution fusion | flops 4839702528 | bytes 11010048 | tf_op jit(solution)/shard_map/dot_general | solution.py:845
  389.0 90.8 %home.1 = (bf16[4,48,2304]{2,1,0:T(8,128)(2,1)}, f32[208,128]{1,0:T(8,128)}, f32[4,64,1536]{2,1,0:T(8,128)}) custom-call(bf16[8,4,48,2304]{3,2,1,0:T(8,128)(2,1)} %pad_maximum_fusion.g_ref, f32[8,208,128]{2,1,0:T(8,128)} %select_maximum_fusion.sm_ref, bf16[4,4,64,1536]{3,2,1,0:T(8,128)(2,1)} %bitcast.152), custom_call_target="tpu_custom_call" | custom-call | tf_op jit(solution)/shard_map/home/pallas_call | solution.py:511
  487.3 3.0 reshape.473
  495.0 3.2 multiply_reduce_fusion.5
  499.0 13.0 %mod_gather.1 = f32[8,40,128]{2,1,0:T(8,128)S(1)} custom-call(f32[40,128]{1,0:T(8,128)S(1)} %fusion.49.g_ref), custom_call_target="tpu_custom_call" | custom-call | tf_op jit(solution)/shard_map/mod_gather/pallas_call | solution.py:332
  (207 shorter events, 60.4 us)
Async XLA Ops:
  7.2 200.8 %all-gather.2.cloned.1.call-start = ((), (), s32[]{:S(2)}) async-start(), calls=%async_computation.2 | async-start | bytes 3932160 | tf_op jit(solution)/shard_map/all_gather | solution.py:931
  106.7 11.9 %copy-start.32 = (f32[1024]{0:T(1024)}, f32[1024]{0:T(1024)S(1)}, u32[]{:S(2)}) copy-start(f32[1024]{0:T(1024)S(1)} %convert.24) | copy-start | bytes 12292
  123.1 20.9 %copy-start.39 = (f32[8,96]{1,0:T(8,128)S(1)}, f32[8,96]{1,0:T(8,128)}, u32[]{:S(2)}) copy-start(f32[8,96]{1,0:T(8,128)} %get-tuple-element.96) | copy-start | bytes 9220
  143.8 351.2 %reduce-scatter.2.cloned.1.call-start = ((), (), s32[]{:S(2)}) async-start(), calls=%async_computation.1 | async-start | bytes 7864320 | tf_op jit(solution)/shard_map/reduce_scatter | solution.py:946
  144.1 6.0 %copy-start.35 = (f32[768]{0:T(1024)}, f32[768]{0:T(1024)S(1)}, u32[]{:S(2)}) copy-start(f32[768]{0:T(1024)S(1)} %add.207) | copy-start | bytes 9220
  144.4 12.0 %copy-start.22 = (bf16[768,16]{0,1:T(8,128)(2,1)}, bf16[768,16]{0,1:T(8,128)(2,1)S(1)}, u32[]{:S(2)}) copy-start(bf16[768,16]{0,1:T(8,128)(2,1)S(1)} %copy.69) | copy-start | bytes 73732
  144.5 11.8 %copy-start.24 = (bf16[768,16]{0,1:T(8,128)(2,1)}, bf16[768,16]{0,1:T(8,128)(2,1)S(1)}, u32[]{:S(2)}) copy-start(bf16[768,16]{0,1:T(8,128)(2,1)S(1)} %copy.70) | copy-start | bytes 73732
  156.3 51.6 %copy-start.33 = (f32[1024]{0:T(1024)S(1)}, f32[1024]{0:T(1024)}, u32[]{:S(2)}) copy-start(f32[1024]{0:T(1024)} %copy-done.32) | copy-start | bytes 12292
  156.3 51.6 %copy-start.36 = (f32[1536]{0:T(1024)S(1)}, f32[1536]{0:T(1024)}, u32[]{:S(2)}) copy-start(f32[1536]{0:T(1024)} %get-tuple-element.98) | copy-start | bytes 18436
  234.2 75.2 %copy-start.40 = (f32[256]{0:T(256)}, f32[256]{0:T(256)S(1)}, u32[]{:S(2)}) copy-start(f32[256]{0:T(256)S(1)} %broadcast_multiply_fusion.3) | copy-start | bytes 3076
  315.4 8.4 %copy-start.17 = (f32[4,256,16]{2,1,0:T(8,128)S(1)}, f32[4,256,16]{2,1,0:T(8,128)}, u32[]{:S(2)}) copy-start(f32[4,256,16]{2,1,0:T(8,128)} %concatenate.74) | copy-start | bytes 196612
  315.4 35.9 %copy-start.13 = (f32[1024,768]{1,0:T(8,128)S(1)}, f32[1024,768]{1,0:T(8,128)}, u32[]{:S(2)}) copy-start(f32[1024,768]{1,0:T(8,128)} %get-tuple-element.111) | copy-start | bytes 9437188
  315.4 35.9 %copy-start.15 = (f32[1024,768]{1,0:T(8,128)S(1)}, f32[1024,768]{1,0:T(8,128)}, u32[]{:S(2)}) copy-start(f32[1024,768]{1,0:T(8,128)} %get-tuple-element.48) | copy-start | bytes 9437188
  315.4 35.9 %copy-start.16 = (f32[1024,768]{1,0:T(8,128)S(1)}, f32[1024,768]{1,0:T(8,128)}, u32[]{:S(2)}) copy-start(f32[1024,768]{1,0:T(8,128)} %get-tuple-element.49) | copy-start | bytes 9437188
  323.2 30.0 %copy-start.9 = (bf16[1024,768]{1,0:T(8,128)(2,1)}, bf16[1024,768]{1,0:T(8,128)(2,1)S(1)}, u32[]{:S(2)}) copy-start(bf16[1024,768]{1,0:T(8,128)(2,1)S(1)} %get-tuple-element.106) | copy-start | bytes 4718596
  323.2 28.1 %copy-start.6 = (f32[1024,768]{1,0:T(8,128)S(1)}, f32[1024,768]{1,0:T(8,128)}, u32[]{:S(2)}) copy-start(f32[1024,768]{1,0:T(8,128)} %get-tuple-element.109.step_f.step_r) | copy-start | bytes 9437188
  353.2 5.2 copy-start.25
  353.2 5.2 copy-start.23
  353.2 5.2 copy-start.26
  487.3 7.7 %copy-start.10 = (bf16[1,256,1536]{2,1,0:T(8,128)(2,1)S(1)}, bf16[1,256,1536]{2,1,0:T(8,128)(2,1)}, u32[]{:S(2)}) copy-start(bf16[1,256,1536]{2,1,0:T(8,128)(2,1)} %param.29) | copy-start | bytes 2359300
  487.3 7.7 %copy-start.41 = (f32[256]{0:T(256)S(1)}, f32[256]{0:T(256)}, u32[]{:S(2)}) copy-start(f32[256]{0:T(256)} %copy-done.40) | copy-start | bytes 3076
  487.3 7.7 %copy-start.45 = (f32[1,256]{1,0:T(1,128)S(1)}, f32[1,256]{1,0:T(1,128)}, u32[]{:S(2)}) copy-start(f32[1,256]{1,0:T(1,128)} %convert_element_type.174) | copy-start | bytes 3076
  491.0 7.3 %copy-start.12 = (f32[4,64,1536]{2,1,0:T(8,128)S(1)}, f32[4,64,1536]{2,1,0:T(8,128)}, u32[]{:S(2)}) copy-start(f32[4,64,1536]{2,1,0:T(8,128)} %get-tuple-element.58) | copy-start | bytes 4718596
  491.0 7.3 %copy-start.43 = (f32[4,64]{1,0:T(4,128)S(1)}, f32[4,64]{1,0:T(4,128)}, u32[]{:S(2)}) copy-start(f32[4,64]{1,0:T(4,128)} %div.81) | copy-start | bytes 3076
  (28 other events, 71.6 us)
Sparse Core Ops, SparseCore 0:
  143.9 64.0 all-gather.1
  226.6 117.3 reduce-scatter.1

commit v5 on v4

--- a/solution.py
+++ b/solution.py
@@ -276,10 +276,10 @@
     greet([(d, t) for t in others])
     for k, t in enumerate(others):
         send(p_ref.at[t], land.at[q], s1.at[k], r1.at[q], (d, t)).start()
-    total = p_ref[q]
+    total = p_ref[q].astype(F32)
     for k, t in enumerate(others):
         send(p_ref.at[t], land.at[t], s1.at[k], r1.at[t], (d, t)).wait_recv()
-        total = total + land[t]
+        total = total + land[t].astype(F32)
     o_ref[q] = total.astype(o_ref.dtype)
     for k, t in enumerate(others):
         send(o_ref.at[q], o_ref.at[q], s2.at[k], r2.at[q], (d, t)).start()
@@ -829,6 +829,331 @@
     )(hidden, win, wout, pack, mask, embedded, modw, modb)
 
 
+def end_kernel(nd, ns, nsub, rows, turned,
+               gp_h, md_h, wx_h, early_ref, sm_ref, hid_ref, cot_ref, line_ref,
+               gin_o, gout_o, so_ref, gh_o, mod_o,
+               gp, md, wx, gm, made, pair, plane, spair, splane, ssum, fro, up, down, own, msg, mland,
+               ld, sa, ra, sb, rb, sc, rc, se, re, ta, ra2, tb, rb2, tc, rc2, su, ru, sd, rd, s1, r1, s2, r2):
+    d, q = lax.axis_index("dp"), lax.axis_index("seq")
+    nc = nd // 2
+    chip, core = d // 2, lax.rem(d, 2)
+    mate = chip * 2 + 1 - core
+    pairs = [(1, 1), (1, 0), (0, 1)] + [(a, b) for b in range(2, nc // 2) for a in (0, 1)]
+    chips = [lax.rem(chip + a, 2) + 2 * lax.rem(chip // 2 + b, nc // 2) for a, b in pairs]
+    others = [lax.rem(q + k, ns) for k in range(1, ns)]
+    peers = [lax.rem(d + k, nd) for k in range(1, nd)]
+    spread = nd // ns
+    final_to = (spread * q + d // ns, lax.rem(d, ns))
+    me = d * ns + q
+    final_from = (lax.rem(me, nd), me // nd)
+    stays = jnp.logical_and(final_to[0] == d, final_to[1] == q)
+    length, cols = gp.shape
+    part = cols // 2
+    width = wx.shape[0]
+    local = length // ns
+    sub = local // nsub
+    rw = pair.shape[2]
+    half = ns * rw
+
+    loads = [pltpu.make_async_copy(src, dst, ld.at[i]) for i, (src, dst) in enumerate(
+        ((gp_h, gp), (wx_h.at[:, 0:cols], wx), (md_h, md)))]
+    for copy in loads:
+        copy.start()
+
+    bar = pltpu.get_barrier_semaphore()
+    friends = [(e, q) for e in peers] + [(d, t) for t in others]
+    for to in friends:
+        pl.semaphore_signal(bar, inc=1, device_id=to, device_id_type=MESH)
+    @pl.when(jnp.logical_not(stays))
+    def _():
+        pl.semaphore_signal(bar, inc=1, device_id=final_from, device_id_type=MESH)
+
+    def tokens(t):
+        @pl.loop(0, width // 512)
+        def _(j):
+            here = pl.ds(pl.multiple_of(j * 512, 512), 512)
+            full = lax.dot_general(gp[t * local:(t + 1) * local, :], wx[here, :], NT, preferred_element_type=F32)
+            full = full.astype(BF)
+            for s in range(nsub):
+                gm[t, s, :, here] = full[s * sub:(s + 1) * sub]
+
+    def rise(t, s, src):
+        return send(src, up.at[t, s], su.at[t, s], ru.at[t, s], (d, q + 1))
+
+    def sink(t, s, src):
+        return send(src, down.at[t, s], sd.at[t, s], rd.at[t, s], (d, q - 1))
+
+    def added(land, t, s):
+        land[t, s] = (land[t, s].astype(F32) + gm[t, s].astype(F32)).astype(BF)
+
+    def open_up(t, s):
+        @pl.when(jnp.logical_and(q == 0, t > 0))
+        def _():
+            rise(t, s, gm.at[t, s]).start()
+
+    def open_down(t, s):
+        @pl.when(jnp.logical_and(q == ns - 1, t < ns - 1))
+        def _():
+            sink(t, s, gm.at[t, s]).start()
+
+    def step(k, s):
+        t = ns - 1 - k
+
+        @pl.when(jnp.logical_and(q < t, q > 0))
+        def _():
+            rise(t, s, up.at[t, s]).wait_recv()
+            added(up, t, s)
+            rise(t, s, up.at[t, s]).start()
+
+        @pl.when(jnp.logical_and(q > k, q < ns - 1))
+        def _():
+            sink(k, s, down.at[k, s]).wait_recv()
+            added(down, k, s)
+            sink(k, s, down.at[k, s]).start()
+
+    def far(k):
+        for t in sorted({ns - 1 - k, k}, reverse=True):
+            tokens(t)
+            if k == 0 and t:
+                @pl.when(stays)
+                def _():
+                    pl.semaphore_wait(bar, len(friends))
+
+                @pl.when(jnp.logical_not(stays))
+                def _():
+                    pl.semaphore_wait(bar, len(friends) + 1)
+            for s in range(nsub):
+                open_up(t, s)
+                open_down(t, s)
+
+    loads[0].wait()
+    loads[1].wait()
+    far(0)
+    steps = [(k, s) for k in range(ns - 1) for s in range(nsub)]
+
+    def first(c):
+        return send(made.at[c, 1 - core], pair.at[c], sa.at[c], ra.at[c], (mate, q))
+
+    def first_small(c):
+        return send(sm_ref.at[c * 2 + 1 - core], spair.at[c], ta.at[c], ra2.at[c], (mate, q))
+
+    def second(c, src):
+        return send(pair.at[c], plane.at[src], sb.at[c], rb.at[src], (c * 2 + core, q))
+
+    def second_small(c, src):
+        return send(spair.at[c], splane.at[src], tb.at[c], rb2.at[src], (c * 2 + core, q))
+
+    def block(c):
+        at = pl.ds(pl.multiple_of(c * 2 * half, 2 * half), 2 * half)
+        tile = part if part % 256 else part // 2
+        left = md[at, :] if turned else md[:, at].T
+
+        @pl.loop(0, part // tile)
+        def _(j):
+            n = pl.ds(pl.multiple_of(j * tile, 128), tile)
+            full = jnp.dot(left, gp[:, n], preferred_element_type=F32).astype(BF)
+            for h in range(2):
+                for t in range(ns):
+                    line = (h * ns + t) * rw
+                    made[c, h, t, :, n] = full[line:line + rw]
+
+    def ready(t, src):
+        return send(early_ref.at[t], fro.at[src, :, part:3 * part], se.at[t], re.at[src], (d, t))
+
+    loads[2].wait()
+    order = chips + [chip]
+
+    def give(c):
+        block(c)
+        first(c).start()
+        first_small(c).start()
+
+    give(order[0])
+    for k in range(1, ns // 2):
+        far(k)
+    for t in others:
+        ready(t, q).start()
+    fro[q, :, part:3 * part] = early_ref[q]
+    for i, c in enumerate(order):
+        if i + 1 < nc:
+            give(order[i + 1])
+        first(c).wait_recv()
+        @pl.loop(0, ns)
+        def _(t):
+            pair[c, t] = (pair[c, t].astype(F32) + made[c, core, t].astype(F32)).astype(BF)
+        first_small(c).wait_recv()
+        spair[c] = spair[c] + sm_ref[c * 2 + core]
+        if i < nc - 1:
+            second(c, chip).start()
+            second_small(c, chip).start()
+        for k, s in steps[i:i + 1]:
+            step(k, s)
+    late = len(steps) * 3 // 4
+    for k, s in steps[nc:late]:
+        step(k, s)
+
+    for c in chips:
+        second(c, c).wait_recv()
+        second_small(c, c).wait_recv()
+    @pl.loop(0, ns)
+    def _(t):
+        total = pair[chip, t].astype(F32)
+        for c in chips:
+            total = total + plane[c, t].astype(F32)
+        pair[chip, t] = total.astype(BF)
+    small = spair[chip]
+    for c in chips:
+        small = small + splane[c]
+    ssum[...] = small
+
+    def third(t, src):
+        return send(pair.at[chip, t], fro.at[src, :, 0:part], sc.at[t], rc.at[src], (d, t))
+
+    last = send(ssum, so_ref, tc, rc2, final_to)
+    @pl.when(stays)
+    def _():
+        so_ref[...] = ssum[...]
+    @pl.when(jnp.logical_not(stays))
+    def _():
+        last.start()
+    for t in others:
+        third(t, q).start()
+    fro[q, :, 0:part] = pair[chip, q]
+    for k, s in steps[max(nc, late):]:
+        step(k, s)
+
+    msg[...] = jnp.zeros(msg.shape, F32)
+    msg[2:4, :] = line_ref[1:3, :]
+    scale = 1.0 + line_ref[0:1, :]
+    for s in range(nsub):
+        own[...] = gm[q, s].astype(F32)
+
+        @pl.when(q > 0)
+        def _():
+            rise(q, s, gm.at[q, s]).wait_recv()
+            own[...] += up[q, s].astype(F32)
+
+        @pl.when(q < ns - 1)
+        def _():
+            sink(q, s, gm.at[q, s]).wait_recv()
+            own[...] += down[q, s].astype(F32)
+
+        @pl.loop(0, sub // 16)
+        def _(r):
+            here = pl.ds(pl.multiple_of(r * 16, 16), 16)
+            grad = own[here, :]
+            x = hid_ref[s, here, :].astype(F32)
+            x = x - jnp.mean(x, axis=1, keepdims=True)
+            inverse = lax.rsqrt(jnp.mean(x * x, axis=1, keepdims=True) + EPS)
+            normed = x * inverse
+            msg[0:1, :] += jnp.sum(grad, axis=0, keepdims=True)
+            msg[1:2, :] += jnp.sum(grad * normed, axis=0, keepdims=True)
+            grad = grad * scale
+            grad = grad - jnp.mean(grad, axis=1, keepdims=True) - normed * jnp.mean(
+                grad * normed, axis=1, keepdims=True)
+            gh_o[s, here, :] = (cot_ref[s, here, :].astype(F32) + inverse * grad).astype(BF)
+
+    for k, t in enumerate(others):
+        send(msg, mland.at[q], s1.at[k], r1.at[q], (d, t)).start()
+
+    def place(src):
+        inner = part * ns
+        at = src * part
+        for j, out in ((0, gin_o), (1, gin_o), (2, gout_o)):
+            to = pl.ds(pl.multiple_of(at + (inner if j == 1 else 0), 128), part)
+            out[:, to] = fro[src, 0:rows, j * part:(j + 1) * part].astype(F32)
+
+    place(q)
+    total = msg[...]
+    for k, t in enumerate(others):
+        send(msg, mland.at[t], s1.at[k], r1.at[t], (d, t)).wait_recv()
+        total = total + mland[t]
+    mod_o[d] = total
+    for k, e in enumerate(peers):
+        send(mod_o.at[d], mod_o.at[d], s2.at[k], r2.at[d], (e, q)).start()
+    for t in others:
+        third(t, t).wait_recv()
+        ready(t, t).wait_recv()
+        place(t)
+    for k, e in enumerate(peers):
+        send(mod_o.at[e], mod_o.at[e], s2.at[k], r2.at[e], (e, q)).wait_recv()
+    @pl.when(jnp.logical_not(stays))
+    def _():
+        last.wait_recv()
+        last.wait_send()
+
+    for c in order:
+        first(c).wait_send()
+        first_small(c).wait_send()
+    for c in chips:
+        second(c, chip).wait_send()
+        second_small(c, chip).wait_send()
+    for k, t in enumerate(others):
+        third(t, q).wait_send()
+        ready(t, q).wait_send()
+        send(msg, mland.at[q], s1.at[k], r1.at[q], (d, t)).wait_send()
+    for k, e in enumerate(peers):
+        send(mod_o.at[d], mod_o.at[d], s2.at[k], r2.at[d], (e, q)).wait_send()
+    for k, s in steps:
+        t = ns - 1 - k
+        @pl.when(q < t)
+        def _():
+            rise(t, s, gm.at[t, s]).wait_send()
+        @pl.when(q > k)
+        def _():
+            sink(k, s, gm.at[k, s]).wait_send()
+
+
+def end(grad_projected, modded, wx, early, small, hidden, cot, line, rows, nd, ns, cid):
+    length, cols = grad_projected.shape
+    part = cols // 2
+    width = wx.shape[0]
+    inner = part * ns
+    nc, nsub = nd // 2, 4
+    local = length // ns
+    sub = local // nsub
+    rw = rows + -rows % 16
+    half = ns * rw
+    turned = 2 * half % 128 != 0 or rw != rows
+    if turned:
+        def turn(a):
+            a = a.T.reshape(nd * ns, rows, length)
+            return jnp.pad(a, ((0, 0), (0, rw - rows), (0, 0))).reshape(nd * ns * rw, length)
+        modded = turn(modded)
+    early = jnp.pad(early.reshape(ns, rows, cols), ((0, 0), (0, rw - rows), (0, 0)))
+    v = small.shape[1:]
+    hidden, cot = hidden.reshape(nsub, sub, width), cot.reshape(nsub, sub, width)
+    blocks = pltpu.VMEM((nc, ns, rw, part), BF)
+    smalls = pltpu.VMEM((nc,) + v, F32)
+    runs = pltpu.VMEM((ns, nsub, sub, width), BF)
+    gin, gout, so, gh, mod = pl.pallas_call(
+        functools.partial(end_kernel, nd, ns, nsub, rows, turned),
+        out_shape=[
+            jax.ShapeDtypeStruct((rows, 2 * inner), F32),
+            jax.ShapeDtypeStruct((rows, inner), F32),
+            jax.ShapeDtypeStruct(v, F32),
+            jax.ShapeDtypeStruct((nsub, sub, width), BF),
+            jax.ShapeDtypeStruct((nd, 8, width), F32),
+        ],
+        in_specs=[HBM] * 3 + [VMEM] * 5, out_specs=[VMEM] * 5,
+        scratch_shapes=[
+            pltpu.VMEM(grad_projected.shape, BF), pltpu.VMEM(modded.shape, BF), pltpu.VMEM((width, cols), BF), runs,
+            pltpu.VMEM((nc, 2, ns, rw, part), BF), blocks, blocks,
+            smalls, smalls, pltpu.VMEM(v, F32), pltpu.VMEM((ns, rw, cols + part), BF), runs, runs,
+            pltpu.VMEM((sub, width), F32), pltpu.VMEM((8, width), F32), pltpu.VMEM((ns, 8, width), F32),
+            DMA((3,)),
+            DMA((nc,)), DMA((nc,)), DMA((nc,)), DMA((nc,)), DMA((ns,)), DMA((ns,)), DMA((ns,)), DMA((ns,)),
+            DMA((nc,)), DMA((nc,)), DMA((nc,)), DMA((nc,)), DMA(()), DMA(()),
+            DMA((ns, nsub)), DMA((ns, nsub)), DMA((ns, nsub)), DMA((ns, nsub)),
+            DMA((ns,)), DMA((ns,)), DMA((nd,)), DMA((nd,)),
+        ],
+        compiler_params=pltpu.CompilerParams(
+            collective_id=cid, has_side_effects=True, vmem_limit_bytes=60 * 2**20),
+        name="end",
+    )(grad_projected, modded, wx, early, small, hidden, cot, line)
+    return gin, gout, so, gh.reshape(local, width), mod
+
+
 def frequency_embed(timestep):
     half_width = FREQ // 2
     counter = jnp.arange(half_width, dtype=F32)
@@ -926,7 +1251,7 @@
     sigma_filter = jax.nn.sigmoid(filtered)
     active = (filtered * sigma_filter).astype(BF)
     active32 = active.astype(F32)
-    selected = column_sum(dot(active, select_q), ns, BF, 0)
+    selected = column_sum(dot(active, select_q).astype(BF), ns, BF, 0)
     cot, selected = lax.optimization_barrier((cotangent[0], selected))
     cot = lax.all_gather(cot, "seq", axis=0, tiled=True)
     low_rank = selected[:, :rank].astype(BF)
@@ -943,7 +1268,9 @@
     sigma_gate = jax.nn.sigmoid(gate_branch)
     silu_gate = gate_branch * sigma_gate
     gated = (merged * silu_gate).astype(BF)
-    branch = lax.psum_scatter(dot_nt(gated, wout), "seq", scatter_dimension=0, tiled=True)
+    branch = dot_nt(gated, wout).astype(BF)
+    branch, cot = lax.optimization_barrier((branch, cot))
+    branch = lax.psum_scatter(branch, "seq", scatter_dimension=0, tiled=True).astype(F32)
 
     mask_here = pad_mask[0].astype(F32)[:, None]
     cot_here = cotangent[0].astype(F32)
@@ -954,6 +1281,9 @@
     grad_gated = dot(grad_branch, wout)
     grad_merged = grad_gated * silu_gate
     grad_gate_branch = grad_gated * merged * sigma_gate * (1.0 + gate_branch * (1.0 - sigma_gate))
+    grad_gate_branch = grad_gate_branch.astype(BF)
+    early = jnp.concatenate([dot_tn(modded, grad_gate_branch), dot_tn(grad_branch, gated)], axis=1).astype(BF)
+    early = lax.psum_scatter(early, "dp", scatter_dimension=0, tiled=True)
     dlog_f, dlog_r, adjb_f, adjb_r, bg_f, bg_r, cg_f, cg_r, rg_f, rg_r = bwd_scan(
         steps, drive.astype(BF), grad_merged, rates_f2, rates_r2, c_rows.T, blockdiag(b_rows), states_f, states_r)
     adjb = adjb_f + adjb_r
@@ -967,7 +1297,7 @@
     grad_pre_low = grad_pre.astype(BF)
     grad_step_t = dot_tn(grad_pre_low, low_rank)
     grad_low_rank = dot_nt(grad_pre_low, step_q)
-    grad_selected = column_sum(jnp.concatenate([grad_low_rank, grad_b, grad_c], axis=1), ns, BF, 1)
+    grad_selected = column_sum(jnp.concatenate([grad_low_rank, grad_b, grad_c], axis=1).astype(BF), ns, BF, 1)
     grad_select = dot_tn(active, grad_selected)
     grad_active = steps * adjb + dot_nt(grad_selected, select_q)
     grad_filtered = grad_active * sigma_filter * (1.0 + filtered * (1.0 - sigma_filter))
@@ -979,39 +1309,23 @@
         grad_inner = grad_inner + filt32[:, k][None, :] * extended[lead : lead + length]
         filter_rows.append(jnp.sum(grad_filtered * padded[k : k + length], axis=0))
     grad_filter_bias = jnp.sum(grad_filtered, axis=0)
-    grad_projected = jnp.concatenate([grad_inner * mask, grad_gate_branch], axis=1).astype(BF)
+    grad_projected = jnp.concatenate([(grad_inner * mask).astype(BF), grad_gate_branch], axis=1)
     fil = jnp.stack(filter_rows + [grad_filter_bias, grad_step_bias])
     fil = fil.reshape(-1, nd, units).transpose(1, 0, 2)
     fil = jnp.pad(fil, ((0, 0), (0, 16 - fil.shape[1]), (0, lanes - units)))
     mid = jnp.concatenate([grad_step_t, grad_decay_f.T, grad_decay_r.T], axis=1)
     small = jnp.concatenate([grad_select.reshape(nd, units, lanes), mid.reshape(nd, units, lanes), fil], axis=1)
-    grads = jnp.concatenate([dot_tn(modded, grad_projected), dot_tn(grad_branch, gated)], axis=1)
-    grads = grads.astype(BF).reshape(nd, ns, rows_in, 3 * part)
-    grads = jnp.pad(grads, ((0, 0), (0, 0), (0, -rows_in % 16), (0, 0)))
-    grads, small, grad_modded = home(grads, small, dot_nt(grad_projected, win).astype(BF), nd, ns, 2)
-    grads = grads[:, :rows_in].astype(F32)
-    g_in = grads[:, :, : 2 * part].reshape(ns, rows_in, 2, part).transpose(1, 2, 0, 3).reshape(rows_in, 2 * inner)
-    g_out = grads[:, :, 2 * part :].transpose(1, 0, 2).reshape(rows_in, inner).T
+    line = jnp.concatenate([scales, grad_gate[None], jnp.pad(embedded.astype(F32) / ns, ((0, 0), (0, width - FREQ))),
+                            jnp.zeros((5, width), F32)])
+    g_in, g_out, small, grad_hidden, sums = end(
+        grad_projected, modded, wx, early, small, hidden[0], cotangent[0], line, rows_in, nd, ns, 2)
     gs_select = small[:units]
     mid = small[units : 2 * units]
     gs_step, gs_f, gs_r = mid[:, :rank], mid[:, rank : rank + state], mid[:, rank + state :]
     fil = small[2 * units :, :units]
 
-    normed, inverse = norm(hidden[0])
-    grad_shifts = jnp.sum(grad_modded, axis=0)
-    grad_scales = jnp.sum(grad_modded * normed, axis=0)
-    grad_normed = grad_modded * (1.0 + scales)
-    grad_hidden = cot_here + inverse * (
-        grad_normed
-        - jnp.mean(grad_normed, axis=1, keepdims=True)
-        - normed * jnp.mean(grad_normed * normed, axis=1, keepdims=True)
-    )
-
-    grad_mod = jnp.concatenate([grad_shifts, grad_scales, grad_gate, embedded[0].astype(F32) / ns])
-    grad_mod = jnp.pad(grad_mod, (0, -grad_mod.shape[0] % 1024)).reshape(-1, 128)
-    grad_mod = mod_gather(grad_mod, nd, ns, 3).reshape(nd, -1)
-    embeds = grad_mod[:, 3 * width : 3 * width + FREQ]
-    grad_mod = grad_mod[:, : 3 * width]
+    embeds = sums[:, 3, :FREQ]
+    grad_mod = sums[:, :3].reshape(nd, 3 * width)
     me = d * ns + q
     mine = lax.dynamic_slice_in_dim(embeds, me * modulation_weight.shape[0], modulation_weight.shape[0], 1)
     g_modw = lax.dot_general(mine, grad_mod, (((0,), (0,)), ((), ())), precision=HIGHEST)
@@ -1019,11 +1333,11 @@
         jnp.sum(grad_mod, axis=0), me * modulation_bias.shape[0], modulation_bias.shape[0], 0)
     return (
         block_out[None],
-        grad_hidden.astype(BF)[None],
+        grad_hidden[None],
         g_in,
         gs_select,
         gs_step.T,
-        g_out,
+        g_out.T,
         gs_f,
         gs_r,
         fil[:taps],

time: 531 us -> 500 us (0.942)
  Pallas kernels: 340 us -> 325 us
  matrix products: 58.2 us -> 45.7 us
  waiting for transfers between devices: 16.9 us -> 5 us
  local copies, waits for them, and re-layouts: 43.1 us -> 51.1 us
    pallas_call x2, Pallas kernels: 47 us -> 28.8 us  [column_sum(): pl.pallas_call(functools.partial(column_sum_kernel, ns), out_shape=jax.Sh...]
    all_gather x1, waiting for transfers between devices: 16.9 us -> 4.93 us  [body(): cot = lax.all_gather(cot, 'seq', axis=0, tiled=True)]
    unnamed x110 -> x121, local copies, waits for them, and re-layouts: 15.8 us -> 26.1 us
    another operation x7, local copies, waits for them, and re-layouts: 0.53 us -> 8.3 us  [body(): fil = jnp.stack(filter_rows + [grad_filter_bias, grad_step_bias])]
    dot_general x4, matrix products: 14.1 us -> 8.08 us  [dot_tn(): lax.dot_general(a, b, (((0,), (0,)), ((), ())), preferred_element_type=F32)]
    dot_general x4 -> x3, matrix products: 17.2 us -> 12.3 us  [dot_nt(): lax.dot_general(a, b, (((1,), (1,)), ((), ())), preferred_element_type=F32)]
    pallas_call x2 -> x1, Pallas kernels: 104 us -> 107 us  [end(): pl.pallas_call(functools.partial(end_kernel, nd, ns, nsub, rows, turned),...]
  transfers between devices with their start and end apart: 2 -> 3, of which waited for: 1 -> 1; matrix products, arithmetic and copies ran while one was open for 17% -> 19% of each run, Pallas kernels for 43% -> 25%
where the time goes in v5:
time: 500 us; the launch traced here: 492 us
  Pallas kernels  325 us (65%)
  local copies, waits for them, and re-layouts  51.1 us (10%)
  other arithmetic  49.8 us (10%)
  matrix products  45.7 us (9%)
  between operations  15.7 us (3%)
  waiting for transfers between devices  5 us (1%)
    pallas_call x1, Pallas kernels, end(): pl.pallas_call(functools.partial(end_kernel, nd, ns, nsub, rows, turned),...  107 us
    pallas_call x1, Pallas kernels, start(): pl.pallas_call(functools.partial(start_kernel, nd, ns, nsub), out_shape=[...  80.2 us
    pallas_call x1, Pallas kernels, bwd_scan(): pl.pallas_call(bwd_kernel, grid=(blocks,), in_specs=[row_f, row_r, row_f,...  73.9 us
    pallas_call x1, Pallas kernels, fwd_scan(): pl.pallas_call(fwd_kernel, grid=(blocks,), in_specs=[row_f, row_r, row_f,...  34.8 us
    pallas_call x2, Pallas kernels, column_sum(): pl.pallas_call(functools.partial(column_sum_kernel, ns), out_shape=jax.Sh...  28.8 us
    unnamed x121, local copies, waits for them, and re-layouts  26.1 us
    dot_general x4, matrix products, dot(): return jnp.dot(a, b, preferred_element_type=F32)  24.4 us
    dot_general x3, matrix products, dot_nt(): lax.dot_general(a, b, (((1,), (1,)), ((), ())), preferred_element_type=F32)  12.3 us
  transfers between devices with their start and end apart: 3, of which 1 were waited for; matrix products, arithmetic and copies ran while one was open for 19% of the time, Pallas kernels for 25%

profile of v5, /device:TPU:0, one launch (start us, length us, event | category | flops | bytes accessed | tf_op | source)
XLA Modules:
  0.0 492.1 jit_solution(16616743724002002223)
XLA Ops:
  18.1 80.2 %start.1 = (bf16[4,4,64,1536]{3,2,1,0:T(8,128)(2,1)S(1)}, bf16[32,48,2304]{2,1,0:T(8,128)(2,1)S(1)}, bf16[8,208,128]{2,1,0:T(8,128)(2,1)S(1)}, bf16[4,16,128]{2,1,0:T(8,128)(2,1)S(1)}, f32[40,128]{1,0:T(8,128)S(1)}) custom-call(bf16[4,64,1536]{2,1,0:T(8,128)(2,1)S(1)} %bitcast.100, bf16[48,6144]{1,0:T(8,128)(2,1)S(1)} %copy-done.3, ...), custom_call_target="tpu_custom_call" | custom-call | tf_op jit(solution)/shard_map/start/pallas_call | solution.py:806
  98.3 2.8 copy-done.2
  110.1 6.9 %fusion.4 = f32[1024,1536]{1,0:T(8,128)S(1)} fusion(bf16[1024,1536]{1,0:T(8,128)(2,1)S(1)} %fusion.3.md_h, bf16[1536,2304]{1,0:T(8,128)(2,1)} %bitcast.101), kind=kOutput, calls=%fused_computation.8 | convolution fusion | flops 4831838208 | bytes 14155776 | tf_op jit(solution)/shard_map/dot_general | solution.py:1166
  117.4 3.8 multiply_convert_fusion.4
  122.1 15.5 %column_sum.2 = bf16[4,256,128]{2,1,0:T(8,128)(2,1)S(1)} custom-call(bf16[4,256,128]{2,1,0:T(8,128)(2,1)S(1)} %bitcast.108), custom_call_target="tpu_custom_call" | custom-call | tf_op jit(solution)/shard_map/column_sum/pallas_call | solution.py:296
  142.3 7.2 %fusion.50 = (bf16[1024,768]{1,0:T(8,128)(2,1)}, f32[1024,768]{1,0:T(8,128)}, f32[1024,768]{1,0:T(8,128)}, f32[1024,768]{1,0:T(8,128)}) fusion(bf16[1024,768]{1,0:T(8,128)(2,1)S(1)} %get-tuple-element.131, f32[768]{0:T(1024)S(1)} %add.196, bf16[768,128]{1,0:T(8,128)(2,1)S(1)} %bitcast.117, bf16[1024,128]{0,1:T(8,128)(2,1)} %copy-done.18), kind=kOutput, calls=%fused_computation.135 | convolution fusion | flops 158859264 | bytes 12979200 | tf_op jit(solution)/shard_map/dot_general | solution.py:1166
  149.5 34.8 %fwd_scan.1 = (f32[1024,768]{1,0:T(8,128)}, f32[1024,768]{1,0:T(8,128)}, bf16[16384,768]{1,0:T(8,128)(2,1)}, bf16[16384,768]{1,0:T(8,128)(2,1)}) custom-call(f32[1024,768]{1,0:T(8,128)} %get-tuple-element.128.step_f.step_r, f32[1024,768]{1,0:T(8,128)} %get-tuple-element.128.step_f.step_r, f32[1024,768]{1,0:T(8,128)} %get-tuple-element.127.u_f.u_r, ...), custom_call_target="tpu_custom_call" | custom-call | flops 201326592 | bytes 62914560 | tf_op jit(solution)/shard_map/fwd_scan/pallas_call | solution.py:103
  184.3 6.4 %multiply_convert_fusion.3 = (bf16[1024,768]{1,0:T(8,128)(2,1)S(1)}, f32[1024,768]{1,0:T(8,128)}) fusion(f32[1024,1536]{1,0:T(8,128)} %copy-done.17, f32[1024,768]{1,0:T(8,128)} %get-tuple-element.47, f32[1024,768]{1,0:T(8,128)} %get-tuple-element.48), kind=kLoop, calls=%fused_computation.30 | loop fusion | flops 5505024 | bytes 14155776 | tf_op jit(solution)/shard_map/convert_element_type | solution.py:1270
  190.7 5.7 %convolution_convert_fusion = bf16[1024,1536]{1,0:T(8,128)(2,1)} fusion(bf16[1024,768]{1,0:T(8,128)(2,1)S(1)} %get-tuple-element.129, bf16[1536,2304]{1,0:T(8,128)(2,1)} %bitcast.102), kind=kOutput, calls=%fused_computation.13 | convolution fusion | flops 2417491968 | bytes 7077888 | tf_op jit(solution)/shard_map/dot_general | solution.py:1170
  196.4 4.9 %all-gather.2.cloned.1.call-done = bf16[1024,1536]{1,0:T(8,128)(2,1)} async-done(((bf16[256,1536]{1,0:T(8,128)(2,1)}), bf16[1024,1536]{1,0:T(8,128)(2,1)}) %all-gather.2.cloned.1.call-update) | async-done | bytes 3145744 | tf_op jit(solution)/shard_map/all_gather | solution.py:1256
  201.4 9.7 %fusion.22 = (f32[1024,768]{1,0:T(8,128)}, bf16[1024,768]{1,0:T(8,128)(2,1)S(1)}) fusion(f32[1024,1536]{1,0:T(8,128)} %copy-done.17, f32[1024,768]{1,0:T(8,128)} %get-tuple-element.130, bf16[1536,2304]{1,0:T(8,128)(2,1)} %bitcast.103, bf16[1024,1536]{1,0:T(8,128)(2,1)} %all-gather.2.cloned.1.call-done, f32[1024]{0:T(1024)S(1)} %convert.31, ...), kind=kOutput, calls=%fused_computation.60 | convolution fusion | flops 2431647744 | bytes 16525312 | tf_op jit(solution)/shard_map/dot_general | solution.py:1166
  211.2 3.1 convolution_convert_fusion.2
  214.3 3.1 convolution_convert_fusion.1
  217.4 2.4 pad_maximum_fusion
  219.8 6.7 %copy.82 = bf16[1536,1536]{1,0:T(8,128)(2,1)} copy(bf16[1536,1536]{0,1:T(8,128)(2,1)} %pad_maximum_fusion) | data formatting | bytes 9437184
  229.9 73.9 %bwd_scan.1 = (f32[1024,768]{1,0:T(8,128)}, f32[1024,768]{1,0:T(8,128)}, f32[1024,768]{1,0:T(8,128)}, f32[1024,768]{1,0:T(8,128)}, f32[64,256]{1,0:T(8,128)}, /*...) custom-call(f32[1024,768]{1,0:T(8,128)} %get-tuple-element.128.step_f.ste, ...), custom_call_target="tpu_custom_call" | custom-call | flops 603979776 | bytes 78643200 | tf_op jit(solution)/shard_map/bwd_scan/pallas_call | solution.py:236
  307.5 8.0 %fusion.48 = (f32[768]{0:T(1024)}, bf16[1024,768]{1,0:T(8,128)(2,1)S(1)}) fusion(f32[1024,768]{1,0:T(8,128)} %get-tuple-element.155, f32[768]{0:T(1024)S(1)} %add.196, f32[1024,768]{1,0:T(8,128)} %get-tuple-element.54, f32[1024,768]{1,0:T(8,128)} %get-tuple-element.55, bf16[1024,768]{1,0:T(8,128)(2,1)S(1)} %get-tuple-element.131, ...), kind=kLoop, calls=%fused_computation.134 | loop fusion | flops 10222848 | bytes 18880512 | tf_op jit(solution)/shard_map/reduce_sum | solution.py:1296
  320.3 13.3 %column_sum.3 = bf16[4,256,128]{2,1,0:T(8,128)(2,1)S(1)} custom-call(bf16[4,256,128]{2,1,0:T(8,128)(2,1)S(1)} %pad_maximum_fusion.3.p_ref), custom_call_target="tpu_custom_call" | custom-call | tf_op jit(solution)/shard_map/column_sum/pallas_call | solution.py:296
  333.7 5.3 %add_multiply_fusion = f32[1024,768]{1,0:T(8,128)S(1)} fusion(f32[1024,768]{1,0:T(8,128)} %get-tuple-element.132, f32[1024,768]{1,0:T(8,128)S(1)} %copy-done.6, bf16[1024,128]{1,0:T(8,128)(2,1)S(1)} %bitcast.105, bf16[768,128]{1,0:T(8,128)(2,1)} %bitcast.124, f32[1024,768]{1,0:T(8,128)} %get-tuple-element.54, f32[1024,768]{1,0:T(8,128)} %get-tuple-element.55), kind=kOutput, calls=%fused_computation.29 | convolution fusion | flops 209977344 | bytes 16187392 | tf_op jit(solution)/shard_map/dot_general | solution.py:1170
  339.1 5.3 %multiply_reduce_fusion.1 = (f32[768]{0:T(1024)}, f32[768]{0:T(1024)}, f32[768]{0:T(1024)}, f32[768]{0:T(1024)}, f32[768]{0:T(1024)}, /*index=5*/bf16[1024,768]{1,0:T(8,128)(2,1)}) fusion(f32[1024,768]{1,0:T(8,128)S(1)} %add_multiply_fusion, f32[1024,768]{1,0:T(8,128)S(1)} %copy-done.8, f32[1024]{0:T(1024)S(1)} %copy-done.39, f32[768]{0:T(1024)S(1)} %copy-done.33, ...), kind=kLoop, calls=%fused_computation.21 | loop fusion | flops 14151936 | bytes 7896064 | tf_op jit(solution)/shard_map/reduce_sum | solution.py:1310
  356.0 3.5 pad_maximum_fusion.1.gp_h
  359.5 2.6 fusion.15
  362.8 106.8 %end.1 = (f32[48,6144]{1,0:T(8,128)}, f32[48,3072]{1,0:T(8,128)}, f32[208,128]{1,0:T(8,128)}, bf16[4,64,1536]{2,1,0:T(8,128)(2,1)}, f32[8,8,1536]{2,1,0:T(8,128)}) custom-call(bf16[1024,1536]{1,0:T(8,128)(2,1)} %pad_maximum_fusion.1.gp_h, bf16[1024,1536]{1,0:T(8,128)(2,1)} %copy-done.11, bf16[1536,2304]{1,0:T(8,128)(2,1)} %bitcast.104, ...), custom_call_target="tpu_custom_call" | custom-call | tf_op jit(solution)/shard_map/end/pallas_call | solution.py:1129
  481.3 2.1 copy.92
  (207 shorter events, 62.5 us)
Async XLA Ops:
  7.2 194.2 %all-gather.2.cloned.1.call-start = ((), (), s32[]{:S(2)}) async-start(), calls=%async_computation.2 | async-start | bytes 3932160 | tf_op jit(solution)/shard_map/all_gather | solution.py:1256
  106.0 36.4 %copy-start.15 = (bf16[8,96,128]{2,1,0:T(8,128)(2,1)}, bf16[8,96,128]{2,1,0:T(8,128)(2,1)S(1)}, u32[]{:S(2)}) copy-start(bf16[8,96,128]{2,1,0:T(8,128)(2,1)S(1)} %get-tuple-element.139) | copy-start | bytes 589828
  106.6 107.7 %copy-start.40 = (f32[1536]{0:T(1024)}, f32[1536]{0:T(1024)S(1)}, u32[]{:S(2)}) copy-start(f32[1536]{0:T(1024)S(1)} %get-tuple-element.115) | copy-start | bytes 18436
  106.7 107.6 %copy-start.38 = (f32[1024]{0:T(1024)}, f32[1024]{0:T(1024)S(1)}, u32[]{:S(2)}) copy-start(f32[1024]{0:T(1024)S(1)} %convert.31) | copy-start | bytes 12292
  106.9 10.5 %copy-start.30 = (f32[768]{0:T(1024)}, f32[768]{0:T(1024)S(1)}, u32[]{:S(2)}) copy-start(f32[768]{0:T(1024)S(1)} %get-tuple-element.118) | copy-start | bytes 9220
  106.9 10.5 %copy-start.32 = (f32[768]{0:T(1024)}, f32[768]{0:T(1024)S(1)}, u32[]{:S(2)}) copy-start(f32[768]{0:T(1024)S(1)} %get-tuple-element.119) | copy-start | bytes 9220
  106.9 10.5 %copy-start.34 = (f32[768]{0:T(1024)}, f32[768]{0:T(1024)S(1)}, u32[]{:S(2)}) copy-start(f32[768]{0:T(1024)S(1)} %get-tuple-element.120) | copy-start | bytes 9220
  106.9 10.5 %copy-start.36 = (f32[768]{0:T(1024)}, f32[768]{0:T(1024)S(1)}, u32[]{:S(2)}) copy-start(f32[768]{0:T(1024)S(1)} %get-tuple-element.121) | copy-start | bytes 9220
  137.9 221.6 %reduce-scatter.5.cloned.1.call-start = ((), (), s32[]{:S(2)}) async-start(), calls=%async_computation.3 | async-start | bytes 3932160 | tf_op jit(solution)/shard_map/reduce_scatter | solution.py:1273
  138.4 11.1 %copy-start.24 = (bf16[768,16]{0,1:T(8,128)(2,1)}, bf16[768,16]{0,1:T(8,128)(2,1)S(1)}, u32[]{:S(2)}) copy-start(bf16[768,16]{0,1:T(8,128)(2,1)S(1)} %copy.84) | copy-start | bytes 73732
  138.6 10.9 %copy-start.26 = (bf16[768,16]{0,1:T(8,128)(2,1)}, bf16[768,16]{0,1:T(8,128)(2,1)S(1)}, u32[]{:S(2)}) copy-start(bf16[768,16]{0,1:T(8,128)(2,1)S(1)} %copy.85) | copy-start | bytes 73732
  201.4 161.5 %reduce-scatter.7.cloned.1.call-start = ((), (), s32[]{:S(2)}) async-start(), calls=%async_computation.4 | async-start | bytes 5308416 | tf_op jit(solution)/shard_map/reduce_scatter | solution.py:1286
  201.4 9.7 %copy-start.12 = (bf16[1024,1536]{1,0:T(8,128)(2,1)S(1)}, bf16[1024,1536]{1,0:T(8,128)(2,1)}, u32[]{:S(2)}) copy-start(bf16[1024,1536]{1,0:T(8,128)(2,1)} %copy-done.11) | copy-start | bytes 9437188
  307.5 9.1 %copy-start.16 = (bf16[8,96,128]{2,1,0:T(8,128)(2,1)S(1)}, bf16[8,96,128]{2,1,0:T(8,128)(2,1)}, u32[]{:S(2)}) copy-start(bf16[8,96,128]{2,1,0:T(8,128)(2,1)} %copy-done.15) | copy-start | bytes 589828
  315.5 18.2 %copy-start.6 = (f32[1024,768]{1,0:T(8,128)S(1)}, f32[1024,768]{1,0:T(8,128)}, u32[]{:S(2)}) copy-start(f32[1024,768]{1,0:T(8,128)} %get-tuple-element.128.step_f.step_r) | copy-start | bytes 9437188
  333.6 5.4 %copy-start.8 = (f32[1024,768]{1,0:T(8,128)S(1)}, f32[1024,768]{1,0:T(8,128)}, u32[]{:S(2)}) copy-start(f32[1024,768]{1,0:T(8,128)} %copy-done.7) | copy-start | bytes 9437188
  339.0 13.6 %copy-start.27 = (bf16[768,16]{0,1:T(8,128)(2,1)S(1)}, bf16[768,16]{0,1:T(8,128)(2,1)}, u32[]{:S(2)}) copy-start(bf16[768,16]{0,1:T(8,128)(2,1)} %copy-done.26) | copy-start | bytes 73732
  339.1 13.6 %copy-start.29 = (f32[16,768]{1,0:T(8,128)S(1)}, f32[16,768]{1,0:T(8,128)}, u32[]{:S(2)}) copy-start(f32[16,768]{1,0:T(8,128)} %get-tuple-element.63) | copy-start | bytes 147460
  339.1 13.7 %copy-start.25 = (bf16[768,16]{0,1:T(8,128)(2,1)S(1)}, bf16[768,16]{0,1:T(8,128)(2,1)}, u32[]{:S(2)}) copy-start(bf16[768,16]{0,1:T(8,128)(2,1)} %copy-done.24) | copy-start | bytes 73732
  339.1 13.7 %copy-start.28 = (f32[16,768]{1,0:T(8,128)S(1)}, f32[16,768]{1,0:T(8,128)}, u32[]{:S(2)}) copy-start(f32[16,768]{1,0:T(8,128)} %get-tuple-element.62) | copy-start | bytes 147460
  339.1 13.7 %copy-start.10 = (bf16[1024,768]{1,0:T(8,128)(2,1)S(1)}, bf16[1024,768]{1,0:T(8,128)(2,1)}, u32[]{:S(2)}) copy-start(bf16[1024,768]{1,0:T(8,128)(2,1)} %copy-done.9) | copy-start | bytes 4718596
  344.4 10.0 %copy-start.14 = (bf16[768,1024]{1,0:T(8,128)(2,1)S(1)}, bf16[768,1024]{1,0:T(8,128)(2,1)}, u32[]{:S(2)}) copy-start(bf16[768,1024]{1,0:T(8,128)(2,1)} %copy.75) | copy-start | bytes 4718596
  469.7 13.7 %copy-start.21 = (f32[48,6144]{1,0:T(8,128)S(1)}, f32[48,6144]{1,0:T(8,128)}, u32[]{:S(2)}) copy-start(f32[48,6144]{1,0:T(8,128)} %get-tuple-element.175) | copy-start | bytes 3538948
  469.7 14.7 %copy-start.23 = (f32[48,3072]{1,0:T(8,128)S(1)}, f32[48,3072]{1,0:T(8,128)}, u32[]{:S(2)}) copy-start(f32[48,3072]{1,0:T(8,128)} %get-tuple-element.67) | copy-start | bytes 1769476
  (33 other events, 90.9 us)
Sparse Core Ops, SparseCore 0:
  138.0 63.3 all-gather.1
  203.7 58.8 reduce-scatter.4
  266.1 54.0 reduce-scatter.6

commit v6 on v5

--- a/solution.py
+++ b/solution.py
@@ -108,7 +108,7 @@
         out_shape=[y, y, s, s],
         scratch_shapes=[pltpu.VMEM((2, 16, lanes), F32), kept, kept, kept, kept],
         compiler_params=pltpu.CompilerParams(vmem_limit_bytes=56 * 2**20, dimension_semantics=("arbitrary",)),
-        cost_estimate=pl.CostEstimate(flops=length * lanes * 16 * 16, transcendentals=0, bytes_accessed=length * lanes * 80),
+        cost_estimate=pl.CostEstimate(flops=length * lanes * 16 * 3200, transcendentals=0, bytes_accessed=length * lanes * 80),
         name="fwd_scan",
     )(steps, steps, u, u, rates_f, rates_r, b_t, b_t, cblk, cblk)
 
@@ -241,7 +241,7 @@
         out_shape=[y, y, y, y, diag, diag, diag, diag, rg, rg],
         scratch_shapes=[pltpu.VMEM((2, 16, lanes), F32)] + [kept] * 8,
         compiler_params=pltpu.CompilerParams(vmem_limit_bytes=56 * 2**20, dimension_semantics=("arbitrary",)),
-        cost_estimate=pl.CostEstimate(flops=length * lanes * 16 * 48, transcendentals=0, bytes_accessed=length * lanes * 100),
+        cost_estimate=pl.CostEstimate(flops=length * lanes * 16 * 6800, transcendentals=0, bytes_accessed=length * lanes * 100),
         name="bwd_scan",
     )(steps, steps, u, u, gy, gy, rates_f, rates_r, c_t, c_t, bblk, bblk, states_f, states_r, states_f, states_r)
 
@@ -830,9 +830,9 @@
 
 
 def end_kernel(nd, ns, nsub, rows, turned,
-               gp_h, md_h, wx_h, early_ref, sm_ref, hid_ref, cot_ref, line_ref,
+               gp_h, md_h, wx_h, sm_ref, hid_ref, cot_ref, line_ref, early,
                gin_o, gout_o, so_ref, gh_o, mod_o,
-               gp, md, wx, gm, made, pair, plane, spair, splane, ssum, fro, up, down, own, msg, mland,
+               gp, md, wx, gm, made, pair, plane, spair, splane, ssum, fro, ready, up, down, own, acc, msg, mland,
                ld, sa, ra, sb, rb, sc, rc, se, re, ta, ra2, tb, rb2, tc, rc2, su, ru, sd, rd, s1, r1, s2, r2):
     d, q = lax.axis_index("dp"), lax.axis_index("seq")
     nc = nd // 2
@@ -914,18 +914,23 @@
     def far(k):
         for t in sorted({ns - 1 - k, k}, reverse=True):
             tokens(t)
-            if k == 0 and t:
-                @pl.when(stays)
-                def _():
-                    pl.semaphore_wait(bar, len(friends))
-
-                @pl.when(jnp.logical_not(stays))
-                def _():
-                    pl.semaphore_wait(bar, len(friends) + 1)
             for s in range(nsub):
                 open_up(t, s)
                 open_down(t, s)
 
+    @pl.when(stays)
+    def _():
+        pl.semaphore_wait(bar, len(friends))
+
+    @pl.when(jnp.logical_not(stays))
+    def _():
+        pl.semaphore_wait(bar, len(friends) + 1)
+
+    def whole(t, src):
+        return send(early.at[t], ready.at[src], se.at[t], re.at[src], (d, t))
+
+    for t in others:
+        whole(t, q).start()
     loads[0].wait()
     loads[1].wait()
     far(0)
@@ -957,9 +962,6 @@
                     line = (h * ns + t) * rw
                     made[c, h, t, :, n] = full[line:line + rw]
 
-    def ready(t, src):
-        return send(early_ref.at[t], fro.at[src, :, part:3 * part], se.at[t], re.at[src], (d, t))
-
     loads[2].wait()
     order = chips + [chip]
 
@@ -971,9 +973,6 @@
     give(order[0])
     for k in range(1, ns // 2):
         far(k)
-    for t in others:
-        ready(t, q).start()
-    fro[q, :, part:3 * part] = early_ref[q]
     for i, c in enumerate(order):
         if i + 1 < nc:
             give(order[i + 1])
@@ -1007,7 +1006,7 @@
     ssum[...] = small
 
     def third(t, src):
-        return send(pair.at[chip, t], fro.at[src, :, 0:part], sc.at[t], rc.at[src], (d, t))
+        return send(pair.at[chip, t], fro.at[src], sc.at[t], rc.at[src], (d, t))
 
     last = send(ssum, so_ref, tc, rc2, final_to)
     @pl.when(stays)
@@ -1018,12 +1017,12 @@
         last.start()
     for t in others:
         third(t, q).start()
-    fro[q, :, 0:part] = pair[chip, q]
+    fro[q] = pair[chip, q]
     for k, s in steps[max(nc, late):]:
         step(k, s)
 
-    msg[...] = jnp.zeros(msg.shape, F32)
-    msg[2:4, :] = line_ref[1:3, :]
+    acc[...] = jnp.zeros(acc.shape, F32)
+    acc[2:4, :] = line_ref[1:3, :]
     scale = 1.0 + line_ref[0:1, :]
     for s in range(nsub):
         own[...] = gm[q, s].astype(F32)
@@ -1046,24 +1045,31 @@
             x = x - jnp.mean(x, axis=1, keepdims=True)
             inverse = lax.rsqrt(jnp.mean(x * x, axis=1, keepdims=True) + EPS)
             normed = x * inverse
-            msg[0:1, :] += jnp.sum(grad, axis=0, keepdims=True)
-            msg[1:2, :] += jnp.sum(grad * normed, axis=0, keepdims=True)
+            acc[0:1, :] += jnp.sum(grad, axis=0, keepdims=True)
+            acc[1:2, :] += jnp.sum(grad * normed, axis=0, keepdims=True)
             grad = grad * scale
             grad = grad - jnp.mean(grad, axis=1, keepdims=True) - normed * jnp.mean(
                 grad * normed, axis=1, keepdims=True)
             gh_o[s, here, :] = (cot_ref[s, here, :].astype(F32) + inverse * grad).astype(BF)
 
+    msg[...] = jnp.zeros(msg.shape, F32)
+    long = msg.shape[1] // 128
+    for i in range(3 * width // 128 + FREQ // 128):
+        r, c = divmod(i * 128, width)
+        to = (i % long) * 128
+        msg[i // long:i // long + 1, to:to + 128] = acc[r:r + 1, c:c + 128]
     for k, t in enumerate(others):
         send(msg, mland.at[q], s1.at[k], r1.at[q], (d, t)).start()
 
-    def place(src):
-        inner = part * ns
+    inner = part * ns
+
+    def place(src, rest):
         at = src * part
-        for j, out in ((0, gin_o), (1, gin_o), (2, gout_o)):
-            to = pl.ds(pl.multiple_of(at + (inner if j == 1 else 0), 128), part)
-            out[:, to] = fro[src, 0:rows, j * part:(j + 1) * part].astype(F32)
-
-    place(q)
+        gin_o[:, pl.ds(pl.multiple_of(at, 128), part)] = fro[src, 0:rows, :].astype(F32)
+        gin_o[:, pl.ds(pl.multiple_of(inner + at, 128), part)] = rest[0:rows, 0:part].astype(F32)
+        gout_o[:, pl.ds(pl.multiple_of(at, 128), part)] = rest[0:rows, part:2 * part].astype(F32)
+
+    place(q, early[q])
     total = msg[...]
     for k, t in enumerate(others):
         send(msg, mland.at[t], s1.at[k], r1.at[t], (d, t)).wait_recv()
@@ -1073,8 +1079,8 @@
         send(mod_o.at[d], mod_o.at[d], s2.at[k], r2.at[d], (e, q)).start()
     for t in others:
         third(t, t).wait_recv()
-        ready(t, t).wait_recv()
-        place(t)
+        whole(t, t).wait_recv()
+        place(t, ready[t])
     for k, e in enumerate(peers):
         send(mod_o.at[e], mod_o.at[e], s2.at[k], r2.at[e], (e, q)).wait_recv()
     @pl.when(jnp.logical_not(stays))
@@ -1090,7 +1096,7 @@
         second_small(c, chip).wait_send()
     for k, t in enumerate(others):
         third(t, q).wait_send()
-        ready(t, q).wait_send()
+        whole(t, q).wait_send()
         send(msg, mland.at[q], s1.at[k], r1.at[q], (d, t)).wait_send()
     for k, e in enumerate(peers):
         send(mod_o.at[d], mod_o.at[d], s2.at[k], r2.at[d], (e, q)).wait_send()
@@ -1121,6 +1127,7 @@
             return jnp.pad(a, ((0, 0), (0, rw - rows), (0, 0))).reshape(nd * ns * rw, length)
         modded = turn(modded)
     early = jnp.pad(early.reshape(ns, rows, cols), ((0, 0), (0, rw - rows), (0, 0)))
+    short = -(-(3 * width + FREQ) // 1024) * 128
     v = small.shape[1:]
     hidden, cot = hidden.reshape(nsub, sub, width), cot.reshape(nsub, sub, width)
     blocks = pltpu.VMEM((nc, ns, rw, part), BF)
@@ -1133,14 +1140,15 @@
             jax.ShapeDtypeStruct((rows, inner), F32),
             jax.ShapeDtypeStruct(v, F32),
             jax.ShapeDtypeStruct((nsub, sub, width), BF),
-            jax.ShapeDtypeStruct((nd, 8, width), F32),
+            jax.ShapeDtypeStruct((nd, 8, short), F32),
         ],
         in_specs=[HBM] * 3 + [VMEM] * 5, out_specs=[VMEM] * 5,
         scratch_shapes=[
             pltpu.VMEM(grad_projected.shape, BF), pltpu.VMEM(modded.shape, BF), pltpu.VMEM((width, cols), BF), runs,
             pltpu.VMEM((nc, 2, ns, rw, part), BF), blocks, blocks,
-            smalls, smalls, pltpu.VMEM(v, F32), pltpu.VMEM((ns, rw, cols + part), BF), runs, runs,
-            pltpu.VMEM((sub, width), F32), pltpu.VMEM((8, width), F32), pltpu.VMEM((ns, 8, width), F32),
+            smalls, smalls, pltpu.VMEM(v, F32), pltpu.VMEM((ns, rw, part), BF), pltpu.VMEM((ns, rw, cols), BF), runs, runs,
+            pltpu.VMEM((sub, width), F32), pltpu.VMEM((8, width), F32), pltpu.VMEM((8, short), F32),
+            pltpu.VMEM((ns, 8, short), F32),
             DMA((3,)),
             DMA((nc,)), DMA((nc,)), DMA((nc,)), DMA((nc,)), DMA((ns,)), DMA((ns,)), DMA((ns,)), DMA((ns,)),
             DMA((nc,)), DMA((nc,)), DMA((nc,)), DMA((nc,)), DMA(()), DMA(()),
@@ -1150,7 +1158,7 @@
         compiler_params=pltpu.CompilerParams(
             collective_id=cid, has_side_effects=True, vmem_limit_bytes=60 * 2**20),
         name="end",
-    )(grad_projected, modded, wx, early, small, hidden, cot, line)
+    )(grad_projected, modded, wx, small, hidden, cot, line, early)
     return gin, gout, so, gh.reshape(local, width), mod
 
 
@@ -1324,8 +1332,9 @@
     gs_step, gs_f, gs_r = mid[:, :rank], mid[:, rank : rank + state], mid[:, rank + state :]
     fil = small[2 * units :, :units]
 
-    embeds = sums[:, 3, :FREQ]
-    grad_mod = sums[:, :3].reshape(nd, 3 * width)
+    sums = sums.reshape(nd, -1)
+    embeds = sums[:, 3 * width : 3 * width + FREQ]
+    grad_mod = sums[:, : 3 * width]
     me = d * ns + q
     mine = lax.dynamic_slice_in_dim(embeds, me * modulation_weight.shape[0], modulation_weight.shape[0], 1)
     g_modw = lax.dot_general(mine, grad_mod, (((0,), (0,)), ((), ())), precision=HIGHEST)

time: 500 us -> 471 us (0.942)
  local copies, waits for them, and re-layouts: 51.1 us -> 39.4 us
  Pallas kernels: 325 us -> 316 us
  other arithmetic: 49.8 us -> 42 us
    pallas_call x1, Pallas kernels: 107 us -> 97.8 us  [end(): pl.pallas_call(functools.partial(end_kernel, nd, ns, nsub, rows, turned),...]
    another operation x7, local copies, waits for them, and re-layouts: 8.3 us -> 0.52 us  [body(): fil = jnp.stack(filter_rows + [grad_filter_bias, grad_step_bias])]
    unnamed x121 -> x109, local copies, waits for them, and re-layouts: 26.1 us -> 25.3 us
  transfers between devices with their start and end apart: 3 -> 3, of which waited for: 1 -> 1; matrix products, arithmetic and copies ran while one was open for 19% -> 17% of each run, Pallas kernels for 25% -> 26%
where the time goes in v6:
time: 471 us; the launch traced here: 463 us
  Pallas kernels  316 us (67%)
  matrix products  44.8 us (10%)
  other arithmetic  42 us (9%)
  local copies, waits for them, and re-layouts  39.4 us (8%)
  between operations  15.7 us (3%)
  waiting for transfers between devices  4.94 us (1%)
    pallas_call x1, Pallas kernels, end(): pl.pallas_call(functools.partial(end_kernel, nd, ns, nsub, rows, turned),...  97.8 us
    pallas_call x1, Pallas kernels, start(): pl.pallas_call(functools.partial(start_kernel, nd, ns, nsub), out_shape=[...  80.2 us
    pallas_call x1, Pallas kernels, bwd_scan(): pl.pallas_call(bwd_kernel, grid=(blocks,), in_specs=[row_f, row_r, row_f,...  74 us
    pallas_call x1, Pallas kernels, fwd_scan(): pl.pallas_call(fwd_kernel, grid=(blocks,), in_specs=[row_f, row_r, row_f,...  34.7 us
    pallas_call x2, Pallas kernels, column_sum(): pl.pallas_call(functools.partial(column_sum_kernel, ns), out_shape=jax.Sh...  29.2 us
    unnamed x109, local copies, waits for them, and re-layouts  25.3 us
    dot_general x4, matrix products, dot(): return jnp.dot(a, b, preferred_element_type=F32)  24.4 us
    dot_general x3, matrix products, dot_nt(): lax.dot_general(a, b, (((1,), (1,)), ((), ())), preferred_element_type=F32)  12.4 us
  transfers between devices with their start and end apart: 3, of which 1 were waited for; matrix products, arithmetic and copies ran while one was open for 17% of the time, Pallas kernels for 26%

profile of v6, /device:TPU:0, one launch (start us, length us, event | category | flops | bytes accessed | tf_op | source)
XLA Modules:
  0.0 463.2 jit_solution(1164019345622941302)
XLA Ops:
  18.1 80.2 %start.1 = (bf16[4,4,64,1536]{3,2,1,0:T(8,128)(2,1)S(1)}, bf16[32,48,2304]{2,1,0:T(8,128)(2,1)S(1)}, bf16[8,208,128]{2,1,0:T(8,128)(2,1)S(1)}, bf16[4,16,128]{2,1,0:T(8,128)(2,1)S(1)}, f32[40,128]{1,0:T(8,128)S(1)}) custom-call(bf16[4,64,1536]{2,1,0:T(8,128)(2,1)S(1)} %bitcast.96, bf16[48,6144]{1,0:T(8,128)(2,1)S(1)} %copy-done.3, ...), custom_call_target="tpu_custom_call" | custom-call | tf_op jit(solution)/shard_map/start/pallas_call | solution.py:806
  98.3 2.9 copy-done.2
  110.2 6.9 %fusion.4 = f32[1024,1536]{1,0:T(8,128)S(1)} fusion(bf16[1024,1536]{1,0:T(8,128)(2,1)S(1)} %fusion.3.md_h, bf16[1536,2304]{1,0:T(8,128)(2,1)} %bitcast.97), kind=kOutput, calls=%fused_computation.8 | convolution fusion | flops 4831838208 | bytes 14155776 | tf_op jit(solution)/shard_map/dot_general | solution.py:1174
  117.4 4.0 multiply_convert_fusion.4
  122.3 15.5 %column_sum.2 = bf16[4,256,128]{2,1,0:T(8,128)(2,1)S(1)} custom-call(bf16[4,256,128]{2,1,0:T(8,128)(2,1)S(1)} %bitcast.104), custom_call_target="tpu_custom_call" | custom-call | tf_op jit(solution)/shard_map/column_sum/pallas_call | solution.py:296
  139.7 7.3 %fusion.54 = (bf16[1024,768]{1,0:T(8,128)(2,1)}, f32[1024,768]{1,0:T(8,128)}, f32[1024,768]{1,0:T(8,128)}, f32[1024,768]{1,0:T(8,128)}) fusion(bf16[1024,768]{1,0:T(8,128)(2,1)S(1)} %get-tuple-element.131, f32[768]{0:T(1024)S(1)} %add.196, bf16[768,128]{1,0:T(8,128)(2,1)S(1)} %bitcast.113, bf16[1024,128]{0,1:T(8,128)(2,1)} %copy-done.16), kind=kOutput, calls=%fused_computation.137 | convolution fusion | flops 158859264 | bytes 12979200 | tf_op jit(solution)/shard_map/dot_general | solution.py:1174
  149.7 34.7 %fwd_scan.1 = (f32[1024,768]{1,0:T(8,128)}, f32[1024,768]{1,0:T(8,128)}, bf16[16384,768]{1,0:T(8,128)(2,1)}, bf16[16384,768]{1,0:T(8,128)(2,1)}) custom-call(f32[1024,768]{1,0:T(8,128)} %get-tuple-element.128.step_f.step_r, f32[1024,768]{1,0:T(8,128)} %get-tuple-element.128.step_f.step_r, f32[1024,768]{1,0:T(8,128)} %get-tuple-element.127.u_f.u_r, ...), custom_call_target="tpu_custom_call" | custom-call | flops 40265318400 | bytes 62914560 | tf_op jit(solution)/shard_map/fwd_scan/pallas_call | solution.py:103
  184.4 6.5 %multiply_convert_fusion.3 = (bf16[1024,768]{1,0:T(8,128)(2,1)S(1)}, f32[1024,768]{1,0:T(8,128)}) fusion(f32[1024,1536]{1,0:T(8,128)} %copy-done.15, f32[1024,768]{1,0:T(8,128)} %get-tuple-element.47, f32[1024,768]{1,0:T(8,128)} %get-tuple-element.48), kind=kLoop, calls=%fused_computation.30 | loop fusion | flops 5505024 | bytes 14155776 | tf_op jit(solution)/shard_map/convert_element_type | solution.py:1278
  190.9 5.7 %convolution_convert_fusion = bf16[1024,1536]{1,0:T(8,128)(2,1)} fusion(bf16[1024,768]{1,0:T(8,128)(2,1)S(1)} %get-tuple-element.129, bf16[1536,2304]{1,0:T(8,128)(2,1)} %bitcast.98), kind=kOutput, calls=%fused_computation.13 | convolution fusion | flops 2417491968 | bytes 7077888 | tf_op jit(solution)/shard_map/dot_general | solution.py:1178
  196.6 4.9 %all-gather.2.cloned.1.call-done = bf16[1024,1536]{1,0:T(8,128)(2,1)} async-done(((bf16[256,1536]{1,0:T(8,128)(2,1)}), bf16[1024,1536]{1,0:T(8,128)(2,1)}) %all-gather.2.cloned.1.call-update) | async-done | bytes 3145744 | tf_op jit(solution)/shard_map/all_gather | solution.py:1264
  203.6 9.7 %fusion.22 = (f32[1024,768]{1,0:T(8,128)}, bf16[1024,768]{1,0:T(8,128)(2,1)S(1)}) fusion(f32[1024,1536]{1,0:T(8,128)} %copy-done.15, f32[1024,768]{1,0:T(8,128)} %get-tuple-element.130, bf16[1536,2304]{1,0:T(8,128)(2,1)} %bitcast.99, bf16[1024,1536]{1,0:T(8,128)(2,1)} %all-gather.2.cloned.1.call-done, f32[1024]{0:T(1024)S(1)} %convert.31, ...), kind=kOutput, calls=%fused_computation.60 | convolution fusion | flops 2431647744 | bytes 16525312 | tf_op jit(solution)/shard_map/dot_general | solution.py:1174
  213.3 2.9 convolution_convert_fusion.2
  216.2 3.1 convolution_convert_fusion.1
  219.3 2.6 pad_maximum_fusion
  221.9 6.6 %copy.82 = bf16[1536,1536]{1,0:T(8,128)(2,1)} copy(bf16[1536,1536]{0,1:T(8,128)(2,1)} %pad_maximum_fusion) | data formatting | bytes 9437184
  228.5 74.0 %bwd_scan.1 = (f32[1024,768]{1,0:T(8,128)}, f32[1024,768]{1,0:T(8,128)}, f32[1024,768]{1,0:T(8,128)}, f32[1024,768]{1,0:T(8,128)}, f32[64,256]{1,0:T(8,128)}, /*...) custom-call(f32[1024,768]{1,0:T(8,128)} %get-tuple-element.128.step_f.ste, ...), custom_call_target="tpu_custom_call" | custom-call | flops 85563801600 | bytes 78643200 | tf_op jit(solution)/shard_map/bwd_scan/pallas_call | solution.py:236
  302.6 6.2 %fusion.52 = (f32[768]{0:T(1024)S(1)}, bf16[1024,768]{1,0:T(8,128)(2,1)S(1)}) fusion(f32[1024,768]{1,0:T(8,128)S(1)} %copy-done.10, f32[768]{0:T(1024)S(1)} %copy-done.43, f32[1024,768]{1,0:T(8,128)} %get-tuple-element.54, f32[1024,768]{1,0:T(8,128)} %get-tuple-element.55, bf16[1024,768]{1,0:T(8,128)(2,1)S(1)} %get-tuple-element.131, ...), kind=kLoop, calls=%fused_computation.136 | loop fusion | flops 10222848 | bytes 18880512 | tf_op jit(solution)/shard_map/reduce_sum | solution.py:1304
  310.5 13.7 %column_sum.3 = bf16[4,256,128]{2,1,0:T(8,128)(2,1)S(1)} custom-call(bf16[4,256,128]{2,1,0:T(8,128)(2,1)S(1)} %pad_maximum_fusion.3.p_ref), custom_call_target="tpu_custom_call" | custom-call | tf_op jit(solution)/shard_map/column_sum/pallas_call | solution.py:296
  325.6 6.1 %add_multiply_fusion = f32[1024,768]{1,0:T(8,128)S(1)} fusion(f32[1024,768]{1,0:T(8,128)} %get-tuple-element.132, f32[1024,768]{1,0:T(8,128)} %get-tuple-element.128.step_f.step_r, bf16[1024,128]{1,0:T(8,128)(2,1)S(1)} %bitcast.101, bf16[768,128]{1,0:T(8,128)(2,1)S(1)} %bitcast.124, f32[1024,768]{1,0:T(8,128)} %get-tuple-element.54, ...), kind=kOutput, calls=%fused_computation.29 | convolution fusion | flops 209977344 | bytes 16187392 | tf_op jit(solution)/shard_map/dot_general | solution.py:1178
  331.8 3.6 multiply_reduce_fusion.1
  338.6 2.0 pad_maximum_fusion.1.gp_h
  340.6 2.6 fusion.15
  343.9 97.8 %end.1 = (f32[48,6144]{1,0:T(8,128)}, f32[48,3072]{1,0:T(8,128)}, f32[208,128]{1,0:T(8,128)}, bf16[4,64,1536]{2,1,0:T(8,128)(2,1)}, f32[8,8,640]{2,1,0:T(8,128)}) custom-call(bf16[1024,1536]{1,0:T(8,128)(2,1)} %pad_maximum_fusion.1.gp_h, bf16[1024,1536]{1,0:T(8,128)(2,1)} %copy-done.8, bf16[1536,2304]{1,0:T(8,128)(2,1)} %bitcast.100, ...), custom_call_target="tpu_custom_call" | custom-call | tf_op jit(solution)/shard_map/end/pallas_call | solution.py:1136
  452.3 2.1 copy.92
  (193 shorter events, 46.1 us)
Async XLA Ops:
  7.2 194.3 %all-gather.2.cloned.1.call-start = ((), (), s32[]{:S(2)}) async-start(), calls=%async_computation.2 | async-start | bytes 3932160 | tf_op jit(solution)/shard_map/all_gather | solution.py:1264
  106.0 33.7 %copy-start.13 = (bf16[8,96,128]{2,1,0:T(8,128)(2,1)}, bf16[8,96,128]{2,1,0:T(8,128)(2,1)S(1)}, u32[]{:S(2)}) copy-start(bf16[8,96,128]{2,1,0:T(8,128)(2,1)S(1)} %get-tuple-element.139) | copy-start | bytes 589828
  106.8 10.5 %copy-start.34 = (f32[768]{0:T(1024)}, f32[768]{0:T(1024)S(1)}, u32[]{:S(2)}) copy-start(f32[768]{0:T(1024)S(1)} %get-tuple-element.118) | copy-start | bytes 9220
  106.9 10.5 %copy-start.36 = (f32[768]{0:T(1024)}, f32[768]{0:T(1024)S(1)}, u32[]{:S(2)}) copy-start(f32[768]{0:T(1024)S(1)} %get-tuple-element.119) | copy-start | bytes 9220
  106.9 10.5 %copy-start.38 = (f32[768]{0:T(1024)}, f32[768]{0:T(1024)S(1)}, u32[]{:S(2)}) copy-start(f32[768]{0:T(1024)S(1)} %get-tuple-element.120) | copy-start | bytes 9220
  106.9 10.5 %copy-start.40 = (f32[768]{0:T(1024)}, f32[768]{0:T(1024)S(1)}, u32[]{:S(2)}) copy-start(f32[768]{0:T(1024)S(1)} %get-tuple-element.121) | copy-start | bytes 9220
  138.0 202.5 %reduce-scatter.5.cloned.1.call-start = ((), (), s32[]{:S(2)}) async-start(), calls=%async_computation.3 | async-start | bytes 3932160 | tf_op jit(solution)/shard_map/reduce_scatter | solution.py:1281
  139.5 7.5 %copy-start.42 = (f32[768]{0:T(1024)}, f32[768]{0:T(1024)S(1)}, u32[]{:S(2)}) copy-start(f32[768]{0:T(1024)S(1)} %add.196) | copy-start | bytes 9220
  147.1 37.3 %copy-start.24 = (bf16[768,16]{0,1:T(8,128)(2,1)}, bf16[768,16]{0,1:T(8,128)(2,1)S(1)}, u32[]{:S(2)}) copy-start(bf16[768,16]{0,1:T(8,128)(2,1)S(1)} %copy.85) | copy-start | bytes 73732
  147.8 36.6 %copy-start.26 = (bf16[768,16]{0,1:T(8,128)(2,1)}, bf16[768,16]{0,1:T(8,128)(2,1)S(1)}, u32[]{:S(2)}) copy-start(bf16[768,16]{0,1:T(8,128)(2,1)S(1)} %copy.84) | copy-start | bytes 73732
  201.5 142.3 %reduce-scatter.7.cloned.1.call-start = ((), (), s32[]{:S(2)}) async-start(), calls=%async_computation.4 | async-start | bytes 5308416 | tf_op jit(solution)/shard_map/reduce_scatter | solution.py:1294
  203.6 9.7 %copy-start.9 = (bf16[1024,1536]{1,0:T(8,128)(2,1)S(1)}, bf16[1024,1536]{1,0:T(8,128)(2,1)}, u32[]{:S(2)}) copy-start(bf16[1024,1536]{1,0:T(8,128)(2,1)} %copy-done.8) | copy-start | bytes 9437188
  228.5 74.0 %copy-start.10 = (f32[1024,768]{1,0:T(8,128)S(1)}, f32[1024,768]{1,0:T(8,128)}, u32[]{:S(2)}) copy-start(f32[1024,768]{1,0:T(8,128)} %get-tuple-element.153) | copy-start | bytes 9437188
  228.5 74.0 %copy-start.43 = (f32[768]{0:T(1024)S(1)}, f32[768]{0:T(1024)}, u32[]{:S(2)}) copy-start(f32[768]{0:T(1024)} %copy-done.42) | copy-start | bytes 9220
  302.6 7.4 %copy-start.28 = (f32[64,256]{1,0:T(8,128)S(1)}, f32[64,256]{1,0:T(8,128)}, u32[]{:S(2)}) copy-start(f32[64,256]{1,0:T(8,128)} %get-tuple-element.60) | copy-start | bytes 196612
  302.6 7.4 %copy-start.29 = (f32[64,256]{1,0:T(8,128)S(1)}, f32[64,256]{1,0:T(8,128)}, u32[]{:S(2)}) copy-start(f32[64,256]{1,0:T(8,128)} %get-tuple-element.61) | copy-start | bytes 196612
  308.8 15.3 %copy-start.27 = (bf16[768,16]{0,1:T(8,128)(2,1)S(1)}, bf16[768,16]{0,1:T(8,128)(2,1)}, u32[]{:S(2)}) copy-start(bf16[768,16]{0,1:T(8,128)(2,1)} %copy-done.26) | copy-start | bytes 73732
  308.9 15.3 %copy-start.33 = (f32[16,768]{1,0:T(8,128)S(1)}, f32[16,768]{1,0:T(8,128)}, u32[]{:S(2)}) copy-start(f32[16,768]{1,0:T(8,128)} %get-tuple-element.62) | copy-start | bytes 147460
  308.9 15.3 %copy-start.25 = (bf16[768,16]{0,1:T(8,128)(2,1)S(1)}, bf16[768,16]{0,1:T(8,128)(2,1)}, u32[]{:S(2)}) copy-start(bf16[768,16]{0,1:T(8,128)(2,1)} %copy-done.24) | copy-start | bytes 73732
  308.9 15.3 %copy-start.32 = (f32[16,768]{1,0:T(8,128)S(1)}, f32[16,768]{1,0:T(8,128)}, u32[]{:S(2)}) copy-start(f32[16,768]{1,0:T(8,128)} %get-tuple-element.63) | copy-start | bytes 147460
  308.9 15.4 %copy-start.17 = (bf16[1024,128]{0,1:T(8,128)(2,1)S(1)}, bf16[1024,128]{0,1:T(8,128)(2,1)}, u32[]{:S(2)}) copy-start(bf16[1024,128]{0,1:T(8,128)(2,1)} %copy-done.16) | copy-start | bytes 786436
  309.7 15.9 %copy-start.22 = (bf16[8,96,128]{2,1,0:T(8,128)(2,1)S(1)}, bf16[8,96,128]{2,1,0:T(8,128)(2,1)}, u32[]{:S(2)}) copy-start(bf16[8,96,128]{2,1,0:T(8,128)(2,1)} %get-tuple-element.138) | copy-start | bytes 589828
  441.7 12.7 %copy-start.20 = (f32[48,6144]{1,0:T(8,128)S(1)}, f32[48,6144]{1,0:T(8,128)}, u32[]{:S(2)}) copy-start(f32[48,6144]{1,0:T(8,128)} %get-tuple-element.173) | copy-start | bytes 3538948
  441.7 13.7 %copy-start.23 = (f32[48,3072]{1,0:T(8,128)S(1)}, f32[48,3072]{1,0:T(8,128)}, u32[]{:S(2)}) copy-start(f32[48,3072]{1,0:T(8,128)} %get-tuple-element.67) | copy-start | bytes 1769476
  (27 other events, 100.9 us)
Sparse Core Ops, SparseCore 0:
  138.1 63.3 all-gather.1
  203.8 58.8 reduce-scatter.4
  266.2 53.8 reduce-scatter.6

commit v7 on v6

--- a/solution.py
+++ b/solution.py
@@ -5,6 +5,7 @@
 import jax.numpy as jnp
 from jax import lax
 from jax.experimental import pallas as pl
+from jax.experimental.layout import Layout, with_layout_constraint
 from jax.experimental.pallas import tpu as pltpu
 from jax.sharding import PartitionSpec as P
 
@@ -531,10 +532,10 @@
     return f, so, out.reshape(length // ns, width)
 
 
-def start_kernel(nd, ns, nsub, hid, win, wout, pack, mask, emb, modw, modb,
-                 hid_o, wx_o, pack_o, mask_o, mod_o,
-                 eland, prod, rowp, land1, land2,
-                 su, ru, sd, rd, swz, rw, swp, swm, spz, rp, spp, spm, sk, rk, se, re, s1, r1, s2, r2, own):
+def start_kernel(nd, ns, nsub, fused, hid, win, wout, pack, mask, emb, modw, modb,
+                 md_o, inner_o, gate_o, wx_o, select_o, mid_o, fil_o, mask_o, mod_o,
+                 hv, wv, mv, iv, gv, pack_v, eland, prod, rowp, land1, land2,
+                 su, ru, sd, rd, swz, rwx, swp, swm, spz, rp, spp, spm, sk, rk, se, re, s1, r1, s2, r2, own, out):
     d, q = lax.axis_index("dp"), lax.axis_index("seq")
     nc = nd // 2
     chip, core = d // 2, lax.rem(d, 2)
@@ -545,37 +546,39 @@
     spread = nd // ns
     me = d * ns + q
     part = wout.shape[1] // ns
+    rw = wout.shape[0]
+    units = part // nd
     greet([(d, t) for t in others] + [(e, q) for e in peers])
 
     def column(ref, at):
         return ref.at[:, pl.ds(pl.multiple_of(at * part, 128), part)]
 
+    def wrows(idx):
+        return wv.at[pl.ds(pl.multiple_of(idx * rw, 16), rw), :]
+
     def pieces(t):
         return (column(win, t), column(win, ns + t), column(wout, t))
 
     def across(k, t, idx):
         return [
-            send(src, wx_o.at[idx, :, j * part:(j + 1) * part], swz.at[k, j], rw.at[idx, j], (d, t))
+            send(src, wrows(idx).at[:, j * part:(j + 1) * part], swz.at[k, j], rwx.at[idx, j], (d, t))
             for j, src in enumerate(pieces(t))
         ]
 
-    for k, t in enumerate(others):
-        for copy in across(k, t, me):
-            copy.start()
-    keep = [pltpu.make_async_copy(src, wx_o.at[me, :, j * part:(j + 1) * part], own.at[j])
+    keep = [pltpu.make_async_copy(src, wrows(me).at[:, j * part:(j + 1) * part], own.at[j])
             for j, src in enumerate(pieces(q))]
-    keep.append(pltpu.make_async_copy(hid, hid_o.at[q], own.at[3]))
+    keep.append(pltpu.make_async_copy(hid, hv.at[q], own.at[3]))
     for copy in keep:
         copy.start()
 
     plane = d // spread
     slot = lax.rem(d, spread) * ns + q
-    pack_z = send(pack, pack_o.at[slot], spz, rp.at[slot], (d, plane))
-    pack_own = pltpu.make_async_copy(pack, pack_o.at[slot], own.at[4])
+    pack_z = send(pack, pack_v.at[slot], spz, rp.at[slot], (d, plane))
+    pack_vwn = pltpu.make_async_copy(pack, pack_v.at[slot], own.at[4])
 
     @pl.when(plane == q)
     def _():
-        pack_own.start()
+        pack_vwn.start()
 
     @pl.when(plane != q)
     def _():
@@ -594,15 +597,19 @@
     for k, t in enumerate(others):
         masks(k, t, q).start()
 
+    for k, t in enumerate(others):
+        for copy in across(k, t, me)[:2]:
+            copy.start()
+
     def rise(k, s):
         t = jnp.maximum(q - k, 0)
-        src = hid.at[s] if k == 0 else hid_o.at[t, s]
-        return send(src, hid_o.at[t, s], su.at[k, s], ru.at[k, s], (d, q + 1))
+        src = hid.at[s] if k == 0 else hv.at[t, s]
+        return send(src, hv.at[t, s], su.at[k, s], ru.at[k, s], (d, q + 1))
 
     def sink(k, s):
         t = jnp.minimum(q + k, ns - 1)
-        src = hid.at[s] if k == 0 else hid_o.at[t, s]
-        return send(src, hid_o.at[t, s], sd.at[k, s], rd.at[k, s], (d, q - 1))
+        src = hid.at[s] if k == 0 else hv.at[t, s]
+        return send(src, hv.at[t, s], sd.at[k, s], rd.at[k, s], (d, q - 1))
 
     def hop(k, s):
         @pl.when(q >= k)
@@ -625,28 +632,27 @@
 
     for s in range(nsub):
         hop(0, s)
-
-    def piece(ref, idx):
-        return ref.at[idx]
-
-    def plane_w(c, idx, t):
-        return send(wx_o.at[idx], wx_o.at[idx], swp.at[c, t], rwp_of(idx), (c * 2 + core, q))
-
-    def rwp_of(idx):
-        return rw.at[idx, 3]
-
-    def mate_w(c, idx, t):
-        return send(wx_o.at[idx], wx_o.at[idx], swm.at[c, t], rwp_of(idx), mate)
-
-    def spread_w(t):
+    for k, t in enumerate(others):
+        across(k, t, me)[2].start()
+
+    def cols_of(idx, kind):
+        return wrows(idx).at[:, 2 * part * kind:2 * part + part * kind]
+
+    def plane_w(c, idx, t, kind):
+        return send(cols_of(idx, kind), cols_of(idx, kind), swp.at[kind, c, t], rwx.at[idx, 3 + kind], (c * 2 + core, q))
+
+    def mate_w(c, idx, t, kind):
+        return send(cols_of(idx, kind), cols_of(idx, kind), swm.at[kind, c, t], rwx.at[idx, 3 + kind], mate)
+
+    def spread_w(t, kind):
         idx = d * ns + t
         for c in chips:
-            plane_w(c, idx, t).start()
-        mate_w(chip, idx, t).start()
+            plane_w(c, idx, t, kind).start()
+        mate_w(chip, idx, t, kind).start()
 
     for copy in keep[:3]:
         copy.wait()
-    spread_w(q)
+    spread_w(q, 0)
 
     for k, e in enumerate(peers):
         embeds(k, e, e).wait_recv()
@@ -673,23 +679,23 @@
         to_item(k, e, d).start()
 
     for k, t in enumerate(others):
-        for copy in across(k, t, d * ns + t):
+        for copy in across(k, t, d * ns + t)[:2]:
             copy.wait_recv()
-        spread_w(t)
+        spread_w(t, 0)
 
     def plane_p(c, i, t):
-        return send(pack_o.at[i], pack_o.at[i], spp.at[c, t], rp.at[i], (c * 2 + core, q))
+        return send(pack_v.at[i], pack_v.at[i], spp.at[c, t], rp.at[i], (c * 2 + core, q))
 
     def mate_p(c, i, t):
-        return send(pack_o.at[i], pack_o.at[i], spm.at[c, t], rp.at[i], mate)
+        return send(pack_v.at[i], pack_v.at[i], spm.at[c, t], rp.at[i], mate)
 
     base = lax.rem(d, spread) * ns
 
     @pl.when(plane == q)
     def _():
-        pack_own.wait()
+        pack_vwn.wait()
         for t in others:
-            send(pack, pack_o.at[base + t], spz, rp.at[base + t], (d, plane)).wait_recv()
+            send(pack, pack_v.at[base + t], spz, rp.at[base + t], (d, plane)).wait_recv()
         for t in range(ns):
             for c in chips:
                 plane_p(c, base + t, t).start()
@@ -707,10 +713,10 @@
     for k, t in enumerate(others):
         to_column(k, t, q).start()
 
-    def relay_w(c, t):
+    def relay_w(c, t, kind):
         idx = (c * 2 + core) * ns + t
-        plane_w(c, idx, t).wait_recv()
-        mate_w(c, idx, t).start()
+        plane_w(c, idx, t, kind).wait_recv()
+        mate_w(c, idx, t, kind).start()
 
     def holds(c):
         return (c * 2 + core) // spread == q
@@ -723,37 +729,113 @@
                 plane_p(c, first + t, t).wait_recv()
                 mate_p(c, first + t, t).start()
 
-    hops = [(k, s) for k in range(1, ns) for s in range(nsub)]
+    def own_copies(t):
+        return [pltpu.make_async_copy(src.at[t], dst.at[t], out.at[t, i]) for i, (src, dst) in enumerate(
+            ((mv, md_o), (iv, inner_o), (gv, gate_o)) if fused else ((hv, md_o),))]
+
+    local = hv.shape[1] * hv.shape[2]
+    width = hv.shape[3]
+
+    def project(t):
+        if fused:
+            shift, scale = mod_o[0:1, 0:width], 1.0 + mod_o[0:1, width:2 * width]
+            for s in range(nsub):
+                @pl.loop(0, local // nsub // 16)
+                def _(r):
+                    x = hv[t, s, pl.ds(pl.multiple_of(r * 16, 16), 16), :].astype(F32)
+                    x = x - jnp.mean(x, axis=1, keepdims=True)
+                    x = x * lax.rsqrt(jnp.mean(x * x, axis=1, keepdims=True) + EPS)
+                    to = pl.multiple_of(s * (local // nsub) + r * 16, 16)
+                    mv[t, pl.ds(to, 16), :] = (x * scale + shift).astype(BF)
+            tile = part if part % 256 else part // 2
+
+            @pl.loop(0, part // tile)
+            def _(j):
+                for target, base in ((iv, 0), (gv, part)):
+                    n = pl.ds(pl.multiple_of(base + j * tile, 128), tile)
+                    full = jnp.dot(mv[t], wv[:, n], preferred_element_type=F32)
+                    target[t, :, pl.ds(pl.multiple_of(j * tile, 128), tile)] = full.astype(target.dtype)
+        for copy in own_copies(t):
+            copy.start()
+
     relays = [(c, t) for t in [q] + others for c in chips]
     at = 0
-    for i, (k, s) in enumerate(hops):
-        upto = len(relays) * (i + 1) // len(hops)
-        hop(k, s)
+    for s in range(nsub):
+        hop(1, s)
+        upto = len(relays) * (s + 1) // (2 * nsub)
         for c, t in relays[at:upto]:
-            relay_w(c, t)
+            relay_w(c, t, 0)
         at = upto
+    spread_w(q, 1)
+    for k, t in enumerate(others):
+        across(k, t, d * ns + t)[2].wait_recv()
+        spread_w(t, 1)
+    for c, t in relays[at:]:
+        relay_w(c, t, 0)
     for c in chips:
         relay_p(c)
+
     for k, t in enumerate(others):
         to_column(k, t, t).wait_recv()
     total = land2[0]
     for t in range(1, ns):
         total = total + land2[t]
-    mod_o[...] = total
+    mod_o[...] = jnp.zeros(mod_o.shape, F32)
+    for i in range(mod_o.shape[1] // 128):
+        mod_o[0:1, i * 128:(i + 1) * 128] = total[i:i + 1, :]
 
     twin = 1 - core
     for c in range(nc):
         for t in range(ns):
             idx = (c * 2 + twin) * ns + t
-            mate_w(c, idx, t).wait_recv()
+            mate_w(c, idx, t, 0).wait_recv()
+    keep[3].wait()
+
+    def project_at(t):
+        @pl.when(jnp.logical_and(t >= 0, t < ns))
+        def _():
+            project(jnp.clip(t, 0, ns - 1))
+
+    for k in range(2, ns):
+        for s in range(nsub):
+            hop(k, s)
+            if k == 2 and s == 0:
+                project(q)
+            if s == nsub - 3:
+                project_at(q - k + 1)
+            if s == nsub - 2:
+                project_at(q + k - 1)
+
+    for c, t in relays:
+        relay_w(c, t, 1)
+    for c in range(nc):
+        for t in range(ns):
+            idx = (c * 2 + twin) * ns + t
+            mate_w(c, idx, t, 1).wait_recv()
+    wx_copy = pltpu.make_async_copy(wv, wx_o, own.at[5])
+    wx_copy.start()
+
+    for c in range(nc):
         first = lax.rem(c * 2 + twin, spread) * ns
         @pl.when((c * 2 + twin) // spread == q)
         def _():
             for t in range(ns):
                 mate_p(c, first + t, t).wait_recv()
+    for j in range(nd):
+        here = slice(j * units, (j + 1) * units)
+        select_o[here, :] = pack_v[j, 0:units, :]
+        mid_o[here, :] = pack_v[j, units:2 * units, :]
+        fil_o[:, here] = pack_v[j, 2 * units:2 * units + 16, 0:units].astype(F32)
+
+    project_at(q - ns + 1)
+    project_at(q + ns - 1)
+
     for k, t in enumerate(others):
         masks(k, t, t).wait_recv()
-    keep[3].wait()
+    wx_copy.wait()
+    for t in range(ns):
+        for copy in own_copies(t):
+            copy.wait()
 
     for k, t in enumerate(others):
         for copy in across(k, t, me):
@@ -775,11 +857,12 @@
                 plane_p(c, base + t, t).wait_send()
             mate_p(chip, base + t, t).wait_send()
 
-    for t in range(ns):
-        for c in chips:
-            plane_w(c, d * ns + t, t).wait_send()
-            mate_w(c, (c * 2 + core) * ns + t, t).wait_send()
-        mate_w(chip, d * ns + t, t).wait_send()
+    for kind in range(2):
+        for t in range(ns):
+            for c in chips:
+                plane_w(c, d * ns + t, t, kind).wait_send()
+                mate_w(c, (c * 2 + core) * ns + t, t, kind).wait_send()
+            mate_w(chip, d * ns + t, t, kind).wait_send()
     for c in chips:
         first = lax.rem(c * 2 + core, spread) * ns
         @pl.when(holds(c))
@@ -796,35 +879,44 @@
                 sink(k, s).wait_send()
 
 
-def start(hidden, mask, win, wout, pack, embedded, modw, modb, nd, ns, cid):
+def start(hidden, mask, win, wout, pack, embedded, modw, modb, fused, nd, ns, cid):
     nsub = 4
     length, width = hidden.shape
     rows, inner = wout.shape
+    part = inner // ns
     nc = nd // 2
     hidden = hidden.reshape(nsub, length // nsub, width)
     lines = modb.shape
+    runs = (ns,) + (hidden.shape if not fused else (length, width))
     return pl.pallas_call(
-        functools.partial(start_kernel, nd, ns, nsub),
+        functools.partial(start_kernel, nd, ns, nsub, fused),
         out_shape=[
-            jax.ShapeDtypeStruct((ns,) + hidden.shape, BF),
-            jax.ShapeDtypeStruct((nd * ns, rows, 3 * inner // ns), BF),
-            jax.ShapeDtypeStruct((nd,) + pack.shape, BF),
+            jax.ShapeDtypeStruct(runs, BF),
+            jax.ShapeDtypeStruct((ns, length, part), BF),
+            jax.ShapeDtypeStruct((ns, length, part), F32),
+            jax.ShapeDtypeStruct((nd * ns * rows, 3 * part), BF),
+            jax.ShapeDtypeStruct((part, 128), BF),
+            jax.ShapeDtypeStruct((part, 128), BF),
+            jax.ShapeDtypeStruct((16, part), F32),
             jax.ShapeDtypeStruct((ns,) + mask.shape, BF),
-            jax.ShapeDtypeStruct(lines, F32),
+            jax.ShapeDtypeStruct((8, modw.shape[1]), F32),
         ],
         in_specs=[HBM, HBM, HBM, HBM, VMEM, VMEM, VMEM, VMEM],
-        out_specs=[HBM, HBM, HBM, VMEM, VMEM],
+        out_specs=[HBM, HBM, HBM, HBM, VMEM, VMEM, VMEM, VMEM, VMEM],
         scratch_shapes=[
+            pltpu.VMEM((ns,) + hidden.shape, BF), pltpu.VMEM((nd * ns * rows, 3 * part), BF),
+            pltpu.VMEM((ns, length, width), BF), pltpu.VMEM((ns, length, part), BF), pltpu.VMEM((ns, length, part), F32),
+            pltpu.VMEM((nd,) + pack.shape, BF),
             pltpu.VMEM((nd,) + embedded.shape, BF), pltpu.VMEM((nd * 16, modw.shape[1]), F32),
             pltpu.VMEM((nd,) + lines, F32), pltpu.VMEM((nd,) + lines, F32), pltpu.VMEM((ns,) + lines, F32),
             DMA((ns - 1, nsub)), DMA((ns - 1, nsub)), DMA((ns - 1, nsub)), DMA((ns - 1, nsub)),
-            DMA((ns, 3)), DMA((nd * ns, 4)), DMA((nc, ns)), DMA((nc, ns)),
+            DMA((ns, 3)), DMA((nd * ns, 5)), DMA((2, nc, ns)), DMA((2, nc, ns)),
             DMA(()), DMA((nd,)), DMA((nc, ns)), DMA((nc, ns)),
             DMA((ns,)), DMA((ns,)), DMA((nd,)), DMA((nd,)),
-            DMA((nd,)), DMA((nd,)), DMA((ns,)), DMA((ns,)), DMA((5,)),
+            DMA((nd,)), DMA((nd,)), DMA((ns,)), DMA((ns,)), DMA((6,)), DMA((ns, 3)),
         ],
         compiler_params=pltpu.CompilerParams(
-            collective_id=cid, has_side_effects=True, vmem_limit_bytes=40 * 2**20),
+            collective_id=cid, has_side_effects=True, vmem_limit_bytes=56 * 2**20),
         name="start",
     )(hidden, win, wout, pack, mask, embedded, modw, modb)
 
@@ -1223,21 +1315,18 @@
     modb = jnp.zeros((-(-3 * width // 1024) * 1024,), F32)
     modb = lax.dynamic_update_slice(modb, modulation_bias.astype(F32), ((d * ns + q) * modulation_bias.shape[0],))
     row_pad = ((0, -rows_in % 16), (0, 0))
-    hid, wx, pack, mask, modulation = start(
+    fused = rows_in % 16 == 0
+    modded, inner_part, gate_branch, wx, select_q, mid, fil, mask, modulation = start(
         hidden[0], mask, jnp.pad(input_weight, row_pad), jnp.pad(output_weight.T, row_pad), pack,
         jnp.pad(embedded, ((0, 15), (0, 0))),
-        jnp.pad(modulation_weight, ((0, shard[0]), (0, 0))), modb.reshape(-1, 128), nd, ns, 4)
-    hid = hid.reshape(length, width)
-    wx = wx[:, :rows_in].reshape(width, 3 * part)
+        jnp.pad(modulation_weight, ((0, shard[0]), (0, 0))), modb.reshape(-1, 128), fused, nd, ns, 4)
+    wx = wx.reshape(nd * ns, -1, 3 * part)[:, :rows_in].reshape(width, 3 * part)
     win, wout = wx[:, : 2 * part], wx[:, 2 * part :]
     mask = mask[:, : local_len // 128].reshape(length, 1).astype(F32)
-    select_q = pack[:, :units].reshape(part, lanes)
-    mid = pack[:, units : 2 * units].reshape(part, lanes)
     step_q = mid[:, :rank].T
     log_f, log_r = mid[:, rank : rank + state], mid[:, rank + state :]
-    fil = pack[:, 2 * units :, :units].transpose(1, 0, 2).reshape(16, part).astype(F32)
     filt32, fbias, sbias = fil[:taps].T, fil[taps][None], fil[taps + 1][None]
-    modulation = modulation.reshape(1, -1)[:, : 3 * width]
+    modulation = modulation[:1]
     shifts = modulation[:, :width]
     scales = modulation[:, width : 2 * width]
     gate_scale = modulation[:, 2 * width :]
@@ -1248,10 +1337,14 @@
         inverse = lax.rsqrt(jnp.mean(centered * centered, axis=1, keepdims=True) + EPS)
         return centered * inverse, inverse
 
-    modded = (norm(hid)[0] * (1.0 + scales) + shifts).astype(BF)
-    projected = dot(modded, win)
-    inner_part = projected[:, :part].astype(BF).astype(F32) * mask
-    gate_branch = projected[:, part:]
+    if fused:
+        modded = modded.reshape(length, width)
+        inner_part, gate_branch = inner_part.reshape(length, part), gate_branch.reshape(length, part)
+    else:
+        modded = (norm(modded.reshape(length, width))[0] * (1.0 + scales) + shifts).astype(BF)
+        projected = dot(modded, win)
+        inner_part, gate_branch = projected[:, :part].astype(BF), projected[:, part:]
+    inner_part = inner_part.astype(F32) * mask
     padded = jnp.pad(inner_part, ((taps - 1, 0), (0, 0)))
     filtered = fbias
     for k in range(taps):
@@ -1290,7 +1383,10 @@
     grad_merged = grad_gated * silu_gate
     grad_gate_branch = grad_gated * merged * sigma_gate * (1.0 + gate_branch * (1.0 - sigma_gate))
     grad_gate_branch = grad_gate_branch.astype(BF)
-    early = jnp.concatenate([dot_tn(modded, grad_gate_branch), dot_tn(grad_branch, gated)], axis=1).astype(BF)
+    rows_first = Layout((0, 1))
+    early = jnp.concatenate([
+        with_layout_constraint(dot_tn(modded, grad_gate_branch).astype(BF), rows_first),
+        with_layout_constraint(dot_tn(grad_branch, gated).astype(BF), rows_first)], axis=1)
     early = lax.psum_scatter(early, "dp", scatter_dimension=0, tiled=True)
     dlog_f, dlog_r, adjb_f, adjb_r, bg_f, bg_r, cg_f, cg_r, rg_f, rg_r = bwd_scan(
         steps, drive.astype(BF), grad_merged, rates_f2, rates_r2, c_rows.T, blockdiag(b_rows), states_f, states_r)

time: 471 us -> 464 us (0.985)
  Pallas kernels: 316 us -> 330 us
  local copies, waits for them, and re-layouts: 39.4 us -> 27.4 us
  matrix products: 44.8 us -> 38.7 us
    unnamed x109 -> x88, local copies, waits for them, and re-layouts: 25.3 us -> 9.61 us
    pallas_call x1, Pallas kernels: 80.2 us -> 90.5 us  [start(): pl.pallas_call(functools.partial(start_kernel, nd, ns, nsub, fused), out_...]
    dot_general x4 -> x3, matrix products: 24.4 us -> 18 us  [dot(): return jnp.dot(a, b, preferred_element_type=F32)]
  transfers between devices with their start and end apart: 3 -> 3, of which waited for: 1 -> 1; matrix products, arithmetic and copies ran while one was open for 17% -> 16% of each run, Pallas kernels for 26% -> 27%
where the time goes in v7:
time: 464 us; the launch traced here: 456 us
  Pallas kernels  330 us (71%)
  other arithmetic  38.7 us (8%)
  matrix products  38.7 us (8%)
  local copies, waits for them, and re-layouts  27.4 us (6%)
  between operations  15.6 us (3%)
  waiting for transfers between devices  5.01 us (1%)
    pallas_call x1, Pallas kernels, end(): pl.pallas_call(functools.partial(end_kernel, nd, ns, nsub, rows, turned),...  102 us
    pallas_call x1, Pallas kernels, start(): pl.pallas_call(functools.partial(start_kernel, nd, ns, nsub, fused), out_...  90.5 us
    pallas_call x1, Pallas kernels, bwd_scan(): pl.pallas_call(bwd_kernel, grid=(blocks,), in_specs=[row_f, row_r, row_f,...  74.2 us
    pallas_call x1, Pallas kernels, fwd_scan(): pl.pallas_call(fwd_kernel, grid=(blocks,), in_specs=[row_f, row_r, row_f,...  34.9 us
    pallas_call x2, Pallas kernels, column_sum(): pl.pallas_call(functools.partial(column_sum_kernel, ns), out_shape=jax.Sh...  28.7 us
    dot_general x3, matrix products, dot(): return jnp.dot(a, b, preferred_element_type=F32)  18 us
    dot_general x3, matrix products, dot_nt(): lax.dot_general(a, b, (((1,), (1,)), ((), ())), preferred_element_type=F32)  12.4 us
    unnamed x88, local copies, waits for them, and re-layouts  9.61 us
  transfers between devices with their start and end apart: 3, of which 1 were waited for; matrix products, arithmetic and copies ran while one was open for 16% of the time, Pallas kernels for 27%

profile of v7, /device:TPU:0, one launch (start us, length us, event | category | flops | bytes accessed | tf_op | source)
XLA Modules:
  0.0 455.7 jit_solution(964337021678061525)
XLA Ops:
  17.3 90.5 %start.1 = (bf16[4,256,1536]{2,1,0:T(8,128)(2,1)}, bf16[4,256,768]{2,1,0:T(8,128)(2,1)}, f32[4,256,768]{2,1,0:T(8,128)}, bf16[1536,2304]{1,0:T(8,128)(2,1)}, bf1...) custom-call(bf16[4,64,1536]{2,1,0:T(8,128)(2,1)} %bitcast.115, ...), custom_call_target="tpu_custom_call" | custom-call | tf_op jit(solution)/shard_map/start/pallas_call | solution.py:891
  110.3 1.8 convert_multiply_fusion.2
  112.1 3.3 multiply_convert_fusion.3
  116.0 15.3 %column_sum.2 = bf16[4,256,128]{2,1,0:T(8,128)(2,1)S(1)} custom-call(bf16[4,256,128]{2,1,0:T(8,128)(2,1)S(1)} %bitcast.111), custom_call_target="tpu_custom_call" | custom-call | tf_op jit(solution)/shard_map/column_sum/pallas_call | solution.py:297
  133.8 7.3 %fusion.54 = (bf16[1024,768]{1,0:T(8,128)(2,1)}, f32[1024,768]{1,0:T(8,128)}, f32[1024,768]{1,0:T(8,128)}, f32[1024,768]{1,0:T(8,128)}) fusion(bf16[1024,768]{1,0:T(8,128)(2,1)S(1)} %get-tuple-element.126, f32[768]{0:T(1024)S(1)} %get-tuple-element.111, bf16[768,128]{1,0:T(8,128)(2,1)} %get-tuple-element.51, bf16[1024,128]{0,1:T(8,128)(2,1)S(1)} %copy.61), kind=kOutput, calls=%fused_computation.130 | convolution fusion | flops 158859264 | bytes 12980224 | tf_op jit(solution)/shard_map/dot_general | solution.py:1266
  143.0 34.9 %fwd_scan.1 = (f32[1024,768]{1,0:T(8,128)}, f32[1024,768]{1,0:T(8,128)}, bf16[16384,768]{1,0:T(8,128)(2,1)}, bf16[16384,768]{1,0:T(8,128)(2,1)}) custom-call(f32[1024,768]{1,0:T(8,128)} %get-tuple-element.123.step_f.step_r, f32[1024,768]{1,0:T(8,128)} %get-tuple-element.123.step_f.step_r, f32[1024,768]{1,0:T(8,128)} %get-tuple-element.122.u_f.u_r, ...), custom_call_target="tpu_custom_call" | custom-call | flops 40265318400 | bytes 62914560 | tf_op jit(solution)/shard_map/fwd_scan/pallas_call | solution.py:104
  177.9 5.8 %multiply_convert_fusion.2 = (bf16[1024,768]{1,0:T(8,128)(2,1)S(1)}, f32[1024,768]{1,0:T(8,128)}) fusion(f32[4,256,768]{2,1,0:T(8,128)S(1)} %copy-done.8, f32[1024,768]{1,0:T(8,128)} %get-tuple-element.52, f32[1024,768]{1,0:T(8,128)} %get-tuple-element.53), kind=kLoop, calls=%fused_computation.29 | loop fusion | flops 5505024 | bytes 14155776 | tf_op jit(solution)/shard_map/convert_element_type | solution.py:1371
  183.7 5.7 %convolution_convert_fusion = bf16[1024,1536]{1,0:T(8,128)(2,1)} fusion(bf16[1024,768]{1,0:T(8,128)(2,1)S(1)} %get-tuple-element.124, bf16[1536,2304]{1,0:T(8,128)(2,1)} %get-tuple-element.55.wx_h), kind=kOutput, calls=%fused_computation.5 | convolution fusion | flops 2417491968 | bytes 7077888 | tf_op jit(solution)/shard_map/dot_general | solution.py:1270
  189.4 5.0 %all-gather.2.cloned.1.call-done = bf16[1024,1536]{1,0:T(8,128)(2,1)} async-done(((bf16[256,1536]{1,0:T(8,128)(2,1)}), bf16[1024,1536]{1,0:T(8,128)(2,1)}) %all-gather.2.cloned.1.call-update) | async-done | bytes 3145744 | tf_op jit(solution)/shard_map/all_gather | solution.py:1357
  194.7 1.6 copy.55
  197.2 10.1 %fusion.21 = (f32[1024,768]{1,0:T(8,128)}, bf16[1024,768]{1,0:T(8,128)(2,1)S(1)}) fusion(f32[4,256,768]{2,1,0:T(8,128)} %get-tuple-element.54, f32[1024,768]{1,0:T(8,128)} %get-tuple-element.125, bf16[1536,2304]{1,0:T(8,128)(2,1)} %get-tuple-element.55.wx_h, bf16[1024,1536]{1,0:T(8,128)(2,1)} %all-gather.2.cloned.1.call-done, f32[1024]{0:T(1024)S(1)} %convert.18, ...), kind=kOutput, calls=%fused_computation.55 | convolution fusion | flops 2431647744 | bytes 16525312 | tf_op jit(solution)/shard_map/dot_general | solution.py:1266
  207.4 3.0 convolution_convert_fusion.2
  210.4 3.3 convolution_convert_fusion.1
  213.7 2.5 pad_maximum_fusion
  216.2 74.2 %bwd_scan.1 = (f32[1024,768]{1,0:T(8,128)}, f32[1024,768]{1,0:T(8,128)}, f32[1024,768]{1,0:T(8,128)}, f32[1024,768]{1,0:T(8,128)}, f32[64,256]{1,0:T(8,128)}, /*...) custom-call(f32[1024,768]{1,0:T(8,128)} %get-tuple-element.123.step_f.ste, ...), custom_call_target="tpu_custom_call" | custom-call | flops 85563801600 | bytes 78643200 | tf_op jit(solution)/shard_map/bwd_scan/pallas_call | solution.py:237
  290.5 6.2 %fusion.52 = (f32[768]{0:T(1024)S(1)}, bf16[1024,768]{1,0:T(8,128)(2,1)S(1)}) fusion(f32[1024,768]{1,0:T(8,128)S(1)} %copy-done.2, f32[768]{0:T(1024)S(1)} %copy-done.35, f32[1024,768]{1,0:T(8,128)} %get-tuple-element.61, f32[1024,768]{1,0:T(8,128)} %get-tuple-element.62, bf16[1024,768]{1,0:T(8,128)(2,1)S(1)} %get-tuple-element.126, ...), kind=kLoop, calls=%fused_computation.129 | loop fusion | flops 10222848 | bytes 18880512 | tf_op jit(solution)/shard_map/reduce_sum | solution.py:1400
  298.4 13.4 %column_sum.3 = bf16[4,256,128]{2,1,0:T(8,128)(2,1)S(1)} custom-call(bf16[4,256,128]{2,1,0:T(8,128)(2,1)S(1)} %pad_maximum_fusion.3.p_ref), custom_call_target="tpu_custom_call" | custom-call | tf_op jit(solution)/shard_map/column_sum/pallas_call | solution.py:297
  314.0 6.1 %add_multiply_fusion = f32[1024,768]{1,0:T(8,128)S(1)} fusion(f32[1024,768]{1,0:T(8,128)} %get-tuple-element.127, f32[1024,768]{1,0:T(8,128)} %get-tuple-element.123.step_f.step_r, bf16[1024,128]{1,0:T(8,128)(2,1)S(1)} %bitcast.108, bf16[768,128]{1,0:T(8,128)(2,1)S(1)} %copy-done.18, f32[1024,768]{1,0:T(8,128)} %get-tuple-element.61, ...), kind=kOutput, calls=%fused_computation.28 | convolution fusion | flops 209977344 | bytes 16187392 | tf_op jit(solution)/shard_map/dot_general | solution.py:1270
  320.2 3.9 fusion.50
  325.2 2.0 select_maximum_fusion.sm_ref
  327.2 1.9 pad_maximum_fusion.1.gp_h
  329.1 2.6 fusion.14
  332.4 101.8 %end.1 = (f32[48,6144]{1,0:T(8,128)}, f32[48,3072]{1,0:T(8,128)}, f32[208,128]{1,0:T(8,128)}, bf16[4,64,1536]{2,1,0:T(8,128)(2,1)}, f32[8,8,640]{2,1,0:T(8,128)}) custom-call(bf16[1024,1536]{1,0:T(8,128)(2,1)} %pad_maximum_fusion.1.gp_h, bf16[1024,1536]{1,0:T(8,128)(2,1)} %bitcast.118, bf16[1536,2304]{1,0:T(8,128)(2,1)} %get-tuple-element.55.wx_h, ...), custom_call_target="tpu_custom_call" | custom-call | tf_op jit(solution)/shard_map/end/pallas_call | solution.py:1228
  444.8 2.1 copy.68
  (156 shorter events, 35.9 us)
Async XLA Ops:
  7.2 187.2 %all-gather.2.cloned.1.call-start = ((), (), s32[]{:S(2)}) async-start(), calls=%async_computation.2 | async-start | bytes 3932160 | tf_op jit(solution)/shard_map/all_gather | solution.py:1357
  109.5 24.4 %copy-start.34 = (f32[768]{0:T(1024)}, f32[768]{0:T(1024)S(1)}, u32[]{:S(2)}) copy-start(f32[768]{0:T(1024)S(1)} %get-tuple-element.111) | copy-start | bytes 9220
  131.5 9.7 %copy-start.9 = (bf16[1024,128]{0,1:T(8,128)(2,1)}, bf16[1024,128]{0,1:T(8,128)(2,1)S(1)}, u32[]{:S(2)}) copy-start(bf16[1024,128]{0,1:T(8,128)(2,1)S(1)} %copy.61) | copy-start | bytes 786436
  131.5 197.6 %reduce-scatter.3.cloned.1.call-start = ((), (), s32[]{:S(2)}) async-start(), calls=%async_computation.3 | async-start | bytes 3932160 | tf_op jit(solution)/shard_map/reduce_scatter | solution.py:1374
  133.8 7.3 %copy-start.16 = (bf16[768,128]{0,1:T(8,128)(2,1)}, bf16[768,128]{0,1:T(8,128)(2,1)S(1)}, u32[]{:S(2)}) copy-start(bf16[768,128]{0,1:T(8,128)(2,1)S(1)} %copy.48) | copy-start | bytes 589828
  143.0 34.9 %copy-start.8 = (f32[4,256,768]{2,1,0:T(8,128)S(1)}, f32[4,256,768]{2,1,0:T(8,128)}, u32[]{:S(2)}) copy-start(f32[4,256,768]{2,1,0:T(8,128)} %get-tuple-element.54) | copy-start | bytes 9437188
  194.4 138.0 %reduce-scatter.5.cloned.1.call-start = ((), (), s32[]{:S(2)}) async-start(), calls=%async_computation.4 | async-start | bytes 5308416 | tf_op jit(solution)/shard_map/reduce_scatter | solution.py:1390
  197.2 10.1 %copy-start.7 = (bf16[4,256,1536]{2,1,0:T(8,128)(2,1)S(1)}, bf16[4,256,1536]{2,1,0:T(8,128)(2,1)}, u32[]{:S(2)}) copy-start(bf16[4,256,1536]{2,1,0:T(8,128)(2,1)} %get-tuple-element.69) | copy-start | bytes 9437188
  216.2 74.2 %copy-start.2 = (f32[1024,768]{1,0:T(8,128)S(1)}, f32[1024,768]{1,0:T(8,128)}, u32[]{:S(2)}) copy-start(f32[1024,768]{1,0:T(8,128)} %get-tuple-element.149) | copy-start | bytes 9437188
  216.2 74.2 %copy-start.35 = (f32[768]{0:T(1024)S(1)}, f32[768]{0:T(1024)}, u32[]{:S(2)}) copy-start(f32[768]{0:T(1024)} %copy-done.34) | copy-start | bytes 9220
  290.4 6.3 %copy-start.11 = (bf16[768,128]{1,0:T(8,128)(2,1)S(1)}, bf16[768,128]{1,0:T(8,128)(2,1)}, u32[]{:S(2)}) copy-start(bf16[768,128]{1,0:T(8,128)(2,1)} %get-tuple-element.51) | copy-start | bytes 589828
  290.5 7.1 %copy-start.22 = (f32[64,256]{1,0:T(8,128)S(1)}, f32[64,256]{1,0:T(8,128)}, u32[]{:S(2)}) copy-start(f32[64,256]{1,0:T(8,128)} %get-tuple-element.65) | copy-start | bytes 196612
  290.5 7.1 %copy-start.23 = (f32[64,256]{1,0:T(8,128)S(1)}, f32[64,256]{1,0:T(8,128)}, u32[]{:S(2)}) copy-start(f32[64,256]{1,0:T(8,128)} %get-tuple-element.66) | copy-start | bytes 196612
  290.5 7.4 %copy-start.20 = (f32[64,256]{1,0:T(8,128)S(1)}, f32[64,256]{1,0:T(8,128)}, u32[]{:S(2)}) copy-start(f32[64,256]{1,0:T(8,128)} %get-tuple-element.67) | copy-start | bytes 196612
  290.5 7.4 %copy-start.21 = (f32[64,256]{1,0:T(8,128)S(1)}, f32[64,256]{1,0:T(8,128)}, u32[]{:S(2)}) copy-start(f32[64,256]{1,0:T(8,128)} %get-tuple-element.68) | copy-start | bytes 196612
  296.7 15.0 %copy-start.24 = (f32[16,768]{1,0:T(8,128)S(1)}, f32[16,768]{1,0:T(8,128)}, u32[]{:S(2)}) copy-start(f32[16,768]{1,0:T(8,128)} %get-tuple-element.70) | copy-start | bytes 147460
  296.7 15.0 %copy-start.25 = (f32[16,768]{1,0:T(8,128)S(1)}, f32[16,768]{1,0:T(8,128)}, u32[]{:S(2)}) copy-start(f32[16,768]{1,0:T(8,128)} %get-tuple-element.71) | copy-start | bytes 147460
  296.8 15.8 %copy-start.10 = (bf16[1024,128]{0,1:T(8,128)(2,1)S(1)}, bf16[1024,128]{0,1:T(8,128)(2,1)}, u32[]{:S(2)}) copy-start(bf16[1024,128]{0,1:T(8,128)(2,1)} %copy-done.9) | copy-start | bytes 786436
  297.6 16.3 %copy-start.18 = (bf16[768,128]{1,0:T(8,128)(2,1)S(1)}, bf16[768,128]{1,0:T(8,128)(2,1)}, u32[]{:S(2)}) copy-start(bf16[768,128]{1,0:T(8,128)(2,1)} %get-tuple-element.49) | copy-start | bytes 589828
  313.9 6.2 %copy-start.29 = (f32[768]{0:T(1024)S(1)}, f32[768]{0:T(1024)}, u32[]{:S(2)}) copy-start(f32[768]{0:T(1024)} %copy-done.28) | copy-start | bytes 9220
  314.0 6.2 %copy-start.31 = (f32[768]{0:T(1024)S(1)}, f32[768]{0:T(1024)}, u32[]{:S(2)}) copy-start(f32[768]{0:T(1024)} %copy-done.30) | copy-start | bytes 9220
  314.0 6.2 %copy-start.33 = (f32[768]{0:T(1024)S(1)}, f32[768]{0:T(1024)}, u32[]{:S(2)}) copy-start(f32[768]{0:T(1024)} %copy-done.32) | copy-start | bytes 9220
  434.1 12.7 %copy-start.14 = (f32[48,6144]{1,0:T(8,128)S(1)}, f32[48,6144]{1,0:T(8,128)}, u32[]{:S(2)}) copy-start(f32[48,6144]{1,0:T(8,128)} %get-tuple-element.169) | copy-start | bytes 3538948
  434.2 13.7 %copy-start.15 = (f32[48,3072]{1,0:T(8,128)S(1)}, f32[48,3072]{1,0:T(8,128)}, u32[]{:S(2)}) copy-start(f32[48,3072]{1,0:T(8,128)} %get-tuple-element.75) | copy-start | bytes 1769476
  (18 other events, 72.7 us)
Sparse Core Ops, SparseCore 0:
  131.6 62.7 all-gather.1
  196.7 58.8 reduce-scatter.2
  259.1 54.0 reduce-scatter.4

commit v8 on v7

--- a/solution.py
+++ b/solution.py
@@ -174,15 +174,20 @@
             out.append(tuple(pair))
         return tuple(out)
 
+    mix_by = 256 if lanes % 256 == 0 else 128
+
     def mix(base, a_ref, l_ref, u, gy, bblk, s, dlog, adjb, bg, cg):
         here = pl.ds(base, SUB)
         line = pl.ds(base // SUB, 1)
-        a = a_ref[...]
-        dlog[here, :] = jnp.dot(onesb, l_ref[...], preferred_element_type=F32)
-        adjb[here, :] = jnp.dot(bblk[here, :], a, preferred_element_type=F32)
-        bgd = lax.dot_general(u[here, :], a, NT, preferred_element_type=F32)
-        block = s[pl.ds(pl.multiple_of(base * 16, 256), 256), :]
-        cgd = lax.dot_general(gy[here, :].astype(BF), block, NT, preferred_element_type=F32)
+        group = pl.ds(pl.multiple_of(base * 16, 256), 256)
+        bgd = cgd = zero
+        for c in range(0, lanes, mix_by):
+            cut = slice(c, c + mix_by)
+            dlog[here, cut] = jnp.dot(onesb, l_ref[:, cut], preferred_element_type=F32)
+            a = a_ref[:, cut]
+            adjb[here, cut] = jnp.dot(bblk[here, :], a, preferred_element_type=F32)
+            bgd = bgd + lax.dot_general(u[here, cut], a, NT, preferred_element_type=F32)
+            cgd = cgd + lax.dot_general(gy[here, cut].astype(BF), s[group, cut], NT, preferred_element_type=F32)
         bg[line, :] = jnp.sum(jnp.where(ones, bgd, zero), axis=0, keepdims=True)
         cg[line, :] = jnp.sum(jnp.where(ones, cgd, zero), axis=0, keepdims=True)
 
@@ -532,9 +537,9 @@
     return f, so, out.reshape(length // ns, width)
 
 
-def start_kernel(nd, ns, nsub, fused, hid, win, wout, pack, mask, emb, modw, modb,
-                 md_o, inner_o, gate_o, wx_o, select_o, mid_o, fil_o, mask_o, mod_o,
-                 hv, wv, mv, iv, gv, pack_v, eland, prod, rowp, land1, land2,
+def start_kernel(nd, ns, nsub, fused, hid, win, wout, mask, emb, modw, modb, select, step, dec_f, dec_r, taps, fbias, sbias,
+                 md_o, inner_o, gate_o, wx_o, select_o, step_o, rate_o, fil_o, mask_o, mod_o,
+                 hv, wv, mv, iv, gv, pack, modw_v, pack_v, eland, prod, rowp, land1, land2,
                  su, ru, sd, rd, swz, rwx, swp, swm, spz, rp, spp, spm, sk, rk, se, re, s1, r1, s2, r2, own, out):
     d, q = lax.axis_index("dp"), lax.axis_index("seq")
     nc = nd // 2
@@ -548,6 +553,20 @@
     part = wout.shape[1] // ns
     rw = wout.shape[0]
     units = part // nd
+    rank, states = step.shape[0], dec_f.shape[0]
+    above = units + -units % 16
+    taps_at = above + rank + 2 * states
+
+    pack[...] = jnp.zeros(pack.shape, BF)
+    pack[0:units, :] = select[...]
+    pack[above:above + rank, 0:units] = step[...]
+    pack[above + rank:above + rank + states, 0:units] = dec_f[...]
+    pack[above + rank + states:taps_at, 0:units] = dec_r[...]
+    pack[taps_at:taps_at + 16, 0:units] = jnp.concatenate(
+        [taps[...].astype(F32), fbias[...].astype(F32), sbias[...].astype(F32),
+         jnp.zeros((14 - taps.shape[0], units), F32)]).astype(BF)
+    modw_v[...] = jnp.zeros(modw_v.shape, BF)
+    modw_v[0:modw.shape[0], :] = modw[...]
     greet([(d, t) for t in others] + [(e, q) for e in peers])
 
     def column(ref, at):
@@ -590,8 +609,10 @@
     def embeds(k, e, src):
         return send(eland.at[src], eland.at[src], se.at[k], re.at[src], (e, q))
 
-    mask_o[q] = mask[...]
-    eland[d] = emb[...]
+    mask_o[q] = jnp.zeros(mask_o.shape[1:], BF)
+    mask_o[q, 0:mask.shape[0], :] = mask[...].astype(F32).astype(BF)
+    eland[d] = jnp.zeros(eland.shape[1:], BF)
+    eland[d, 0:1, :] = emb[...]
     for k, e in enumerate(peers):
         embeds(k, e, d).start()
     for k, t in enumerate(others):
@@ -656,14 +677,14 @@
 
     for k, e in enumerate(peers):
         embeds(k, e, e).wait_recv()
-    rows = modw.shape[0]
+    rows = modw_v.shape[0]
     here = lax.broadcasted_iota(jnp.int32, (FREQ, rows), 0)
     pick = here - lax.broadcasted_iota(jnp.int32, (FREQ, rows), 1)
     count = FREQ // (nd * ns)
     keep_col = lax.broadcasted_iota(jnp.int32, (FREQ, rows), 1) < count
     pick = jnp.where(jnp.logical_and(pick == me * count, keep_col), 1.0, 0.0).astype(BF)
     mine = jnp.dot(eland[...].reshape(nd * 16, FREQ), pick, preferred_element_type=F32).astype(BF)
-    prod[...] = jnp.dot(mine, modw[...], preferred_element_type=F32)
+    prod[...] = jnp.dot(mine, modw_v[...], preferred_element_type=F32)
 
     lines = prod.shape[1] // 128
     @pl.loop(0, nd)
@@ -824,8 +845,10 @@
     for j in range(nd):
         here = slice(j * units, (j + 1) * units)
         select_o[here, :] = pack_v[j, 0:units, :]
-        mid_o[here, :] = pack_v[j, units:2 * units, :]
-        fil_o[:, here] = pack_v[j, 2 * units:2 * units + 16, 0:units].astype(F32)
+        step_o[:, here] = pack_v[j, above:above + rank, 0:units]
+        rate_o[0:2 * states, here] = -jnp.exp(pack_v[j, above + rank:taps_at, 0:units].astype(F32))
+        fil_o[:, here] = pack_v[j, taps_at:taps_at + 16, 0:units].astype(F32)
+    rate_o[2 * states:4 * states, :] = rate_o[0:2 * states, :] * LOG2E
 
     project_at(q - ns + 1)
     project_at(q + ns - 1)
@@ -879,7 +902,7 @@
                 sink(k, s).wait_send()
 
 
-def start(hidden, mask, win, wout, pack, embedded, modw, modb, fused, nd, ns, cid):
+def start(hidden, mask, win, wout, embedded, modw, modb, small, fused, nd, ns, cid):
     nsub = 4
     length, width = hidden.shape
     rows, inner = wout.shape
@@ -887,6 +910,9 @@
     nc = nd // 2
     hidden = hidden.reshape(nsub, length // nsub, width)
     lines = modb.shape
+    rank, units, states = small[1].shape[0], part // nd, small[2].shape[0]
+    pack = (units + -units % 16 + rank + 2 * states + 16, 128)
+    held = modw.shape[0] + -modw.shape[0] % 16
     runs = (ns,) + (hidden.shape if not fused else (length, width))
     return pl.pallas_call(
         functools.partial(start_kernel, nd, ns, nsub, fused),
@@ -896,18 +922,19 @@
             jax.ShapeDtypeStruct((ns, length, part), F32),
             jax.ShapeDtypeStruct((nd * ns * rows, 3 * part), BF),
             jax.ShapeDtypeStruct((part, 128), BF),
-            jax.ShapeDtypeStruct((part, 128), BF),
+            jax.ShapeDtypeStruct((rank, part), BF),
+            jax.ShapeDtypeStruct((4 * states, part), F32),
             jax.ShapeDtypeStruct((16, part), F32),
-            jax.ShapeDtypeStruct((ns,) + mask.shape, BF),
+            jax.ShapeDtypeStruct((ns, 16, 128), BF),
             jax.ShapeDtypeStruct((8, modw.shape[1]), F32),
         ],
-        in_specs=[HBM, HBM, HBM, HBM, VMEM, VMEM, VMEM, VMEM],
-        out_specs=[HBM, HBM, HBM, HBM, VMEM, VMEM, VMEM, VMEM, VMEM],
+        in_specs=[HBM, HBM, HBM] + [VMEM] * 11,
+        out_specs=[HBM] * 4 + [VMEM] * 6,
         scratch_shapes=[
             pltpu.VMEM((ns,) + hidden.shape, BF), pltpu.VMEM((nd * ns * rows, 3 * part), BF),
             pltpu.VMEM((ns, length, width), BF), pltpu.VMEM((ns, length, part), BF), pltpu.VMEM((ns, length, part), F32),
-            pltpu.VMEM((nd,) + pack.shape, BF),
-            pltpu.VMEM((nd,) + embedded.shape, BF), pltpu.VMEM((nd * 16, modw.shape[1]), F32),
+            pltpu.VMEM(pack, BF), pltpu.VMEM((held, modw.shape[1]), BF), pltpu.VMEM((nd,) + pack, BF),
+            pltpu.VMEM((nd, 16, FREQ), BF), pltpu.VMEM((nd * 16, modw.shape[1]), F32),
             pltpu.VMEM((nd,) + lines, F32), pltpu.VMEM((nd,) + lines, F32), pltpu.VMEM((ns,) + lines, F32),
             DMA((ns - 1, nsub)), DMA((ns - 1, nsub)), DMA((ns - 1, nsub)), DMA((ns - 1, nsub)),
             DMA((ns, 3)), DMA((nd * ns, 5)), DMA((2, nc, ns)), DMA((2, nc, ns)),
@@ -918,13 +945,13 @@
         compiler_params=pltpu.CompilerParams(
             collective_id=cid, has_side_effects=True, vmem_limit_bytes=56 * 2**20),
         name="start",
-    )(hidden, win, wout, pack, mask, embedded, modw, modb)
+    )(hidden, win, wout, mask, embedded, modw, modb, *small)
 
 
 def end_kernel(nd, ns, nsub, rows, turned,
-               gp_h, md_h, wx_h, sm_ref, hid_ref, cot_ref, line_ref, early,
-               gin_o, gout_o, so_ref, gh_o, mod_o,
-               gp, md, wx, gm, made, pair, plane, spair, splane, ssum, fro, ready, up, down, own, acc, msg, mland,
+               gp_h, md_h, wx_h, gsel, gstep, gdf, gdr, gfil, hid_ref, cot_ref, line_ref, early,
+               gin_o, gout_o, sel_o, step_o, df_o, dr_o, taps_o, fb_o, sb_o, gh_o, mod_o,
+               gp, md, wx, sm_ref, so_ref, gm, made, pair, plane, spair, splane, ssum, fro, ready, up, down, own, acc, msg, mland,
                ld, sa, ra, sb, rb, sc, rc, se, re, ta, ra2, tb, rb2, tc, rc2, su, ru, sd, rd, s1, r1, s2, r2):
     d, q = lax.axis_index("dp"), lax.axis_index("seq")
     nc = nd // 2
@@ -952,6 +979,10 @@
     for copy in loads:
         copy.start()
 
+    units = part // nd
+    rank, states, taps = gstep.shape[0], gdf.shape[0], taps_o.shape[0]
+    above = units + -units % 16
+    taps_at = above + rank + 2 * states
     bar = pltpu.get_barrier_semaphore()
     friends = [(e, q) for e in peers] + [(d, t) for t in others]
     for to in friends:
@@ -1053,6 +1084,15 @@
                 for t in range(ns):
                     line = (h * ns + t) * rw
                     made[c, h, t, :, n] = full[line:line + rw]
+
+    sm_ref[...] = jnp.zeros(sm_ref.shape, F32)
+    for j in range(nd):
+        here = slice(j * units, (j + 1) * units)
+        sm_ref[j, 0:units, :] = gsel[here, :]
+        sm_ref[j, above:above + rank, 0:units] = gstep[:, here]
+        sm_ref[j, above + rank:above + rank + states, 0:units] = gdf[:, here]
+        sm_ref[j, above + rank + states:taps_at, 0:units] = gdr[:, here]
+        sm_ref[j, taps_at:taps_at + 8, 0:units] = gfil[:, here]
 
     loads[2].wait()
     order = chips + [chip]
@@ -1180,6 +1220,13 @@
         last.wait_recv()
         last.wait_send()
 
+    sel_o[...] = so_ref[0:units, :]
+    step_o[...] = so_ref[above:above + rank, 0:units]
+    df_o[...] = so_ref[above + rank:above + rank + states, 0:units]
+    dr_o[...] = so_ref[above + rank + states:taps_at, 0:units]
+    taps_o[...] = so_ref[taps_at:taps_at + taps, 0:units]
+    fb_o[...] = so_ref[taps_at + taps:taps_at + taps + 1, 0:units]
+    sb_o[...] = so_ref[taps_at + taps + 1:taps_at + taps + 2, 0:units]
     for c in order:
         first(c).wait_send()
         first_small(c).wait_send()
@@ -1202,7 +1249,7 @@
             sink(k, s, gm.at[k, s]).wait_send()
 
 
-def end(grad_projected, modded, wx, early, small, hidden, cot, line, rows, nd, ns, cid):
+def end(grad_projected, modded, wx, early, small, taps, hidden, cot, line, rows, nd, ns, cid):
     length, cols = grad_projected.shape
     part = cols // 2
     width = wx.shape[0]
@@ -1220,23 +1267,31 @@
         modded = turn(modded)
     early = jnp.pad(early.reshape(ns, rows, cols), ((0, 0), (0, rw - rows), (0, 0)))
     short = -(-(3 * width + FREQ) // 1024) * 128
-    v = small.shape[1:]
+    units, rank, states = part // nd, small[1].shape[0], small[2].shape[0]
+    v = (units + -units % 16 + rank + 2 * states + 16, 128)
     hidden, cot = hidden.reshape(nsub, sub, width), cot.reshape(nsub, sub, width)
     blocks = pltpu.VMEM((nc, ns, rw, part), BF)
     smalls = pltpu.VMEM((nc,) + v, F32)
     runs = pltpu.VMEM((ns, nsub, sub, width), BF)
-    gin, gout, so, gh, mod = pl.pallas_call(
+    gin, gout, *own, gh, mod = pl.pallas_call(
         functools.partial(end_kernel, nd, ns, nsub, rows, turned),
         out_shape=[
             jax.ShapeDtypeStruct((rows, 2 * inner), F32),
             jax.ShapeDtypeStruct((rows, inner), F32),
-            jax.ShapeDtypeStruct(v, F32),
+            jax.ShapeDtypeStruct((units, 128), F32),
+            jax.ShapeDtypeStruct((rank, units), F32),
+            jax.ShapeDtypeStruct((states, units), F32),
+            jax.ShapeDtypeStruct((states, units), F32),
+            jax.ShapeDtypeStruct((taps, units), F32),
+            jax.ShapeDtypeStruct((1, units), F32),
+            jax.ShapeDtypeStruct((1, units), F32),
             jax.ShapeDtypeStruct((nsub, sub, width), BF),
             jax.ShapeDtypeStruct((nd, 8, short), F32),
         ],
-        in_specs=[HBM] * 3 + [VMEM] * 5, out_specs=[VMEM] * 5,
+        in_specs=[HBM] * 3 + [VMEM] * 9, out_specs=[VMEM] * 11,
         scratch_shapes=[
-            pltpu.VMEM(grad_projected.shape, BF), pltpu.VMEM(modded.shape, BF), pltpu.VMEM((width, cols), BF), runs,
+            pltpu.VMEM(grad_projected.shape, BF), pltpu.VMEM(modded.shape, BF), pltpu.VMEM((width, cols), BF),
+            pltpu.VMEM((nd,) + v, F32), pltpu.VMEM(v, F32), runs,
             pltpu.VMEM((nc, 2, ns, rw, part), BF), blocks, blocks,
             smalls, smalls, pltpu.VMEM(v, F32), pltpu.VMEM((ns, rw, part), BF), pltpu.VMEM((ns, rw, cols), BF), runs, runs,
             pltpu.VMEM((sub, width), F32), pltpu.VMEM((8, width), F32), pltpu.VMEM((8, short), F32),
@@ -1250,8 +1305,8 @@
         compiler_params=pltpu.CompilerParams(
             collective_id=cid, has_side_effects=True, vmem_limit_bytes=60 * 2**20),
         name="end",
-    )(grad_projected, modded, wx, small, hidden, cot, line, early)
-    return gin, gout, so, gh.reshape(local, width), mod
+    )(grad_projected, modded, wx, *small, hidden, cot, line, early)
+    return gin, gout, own, gh.reshape(local, width), mod
 
 
 def frequency_embed(timestep):
@@ -1306,26 +1361,19 @@
 
     units = part // nd
     embedded = jax.nn.silu(frequency_embed(timestep)).astype(BF)
-    fil = jnp.concatenate([filter_weight, filter_bias[None], step_bias[None]])
-    fil = jnp.pad(fil, ((0, 16 - fil.shape[0]), (0, lanes - units)))
-    mid = jnp.concatenate([step_weight.T, decay_forward, decay_reverse], axis=1)
-    pack = jnp.concatenate([select_weight, mid, fil])
-    mask = jnp.pad(pad_mask[0].astype(BF).reshape(-1, 128), ((0, 16 - local_len // 128), (0, 0)))
-    shard = (-modulation_weight.shape[0] % 16, 0)
     modb = jnp.zeros((-(-3 * width // 1024) * 1024,), F32)
     modb = lax.dynamic_update_slice(modb, modulation_bias.astype(F32), ((d * ns + q) * modulation_bias.shape[0],))
     row_pad = ((0, -rows_in % 16), (0, 0))
     fused = rows_in % 16 == 0
-    modded, inner_part, gate_branch, wx, select_q, mid, fil, mask, modulation = start(
-        hidden[0], mask, jnp.pad(input_weight, row_pad), jnp.pad(output_weight.T, row_pad), pack,
-        jnp.pad(embedded, ((0, 15), (0, 0))),
-        jnp.pad(modulation_weight, ((0, shard[0]), (0, 0))), modb.reshape(-1, 128), fused, nd, ns, 4)
+    modded, inner_part, gate_branch, wx, select_q, step_q, rates, fil, mask, modulation = start(
+        hidden[0], pad_mask.reshape(-1, 128), jnp.pad(input_weight, row_pad), jnp.pad(output_weight.T, row_pad),
+        embedded, modulation_weight, modb.reshape(-1, 128),
+        (select_weight, step_weight, decay_forward.T, decay_reverse.T, filter_weight, filter_bias[None], step_bias[None]),
+        fused, nd, ns, 4)
     wx = wx.reshape(nd * ns, -1, 3 * part)[:, :rows_in].reshape(width, 3 * part)
     win, wout = wx[:, : 2 * part], wx[:, 2 * part :]
     mask = mask[:, : local_len // 128].reshape(length, 1).astype(F32)
-    step_q = mid[:, :rank].T
-    log_f, log_r = mid[:, rank : rank + state], mid[:, rank + state :]
-    filt32, fbias, sbias = fil[:taps].T, fil[taps][None], fil[taps + 1][None]
+    rates_f, rates_r, rates_f2, rates_r2 = [rates[k * state : (k + 1) * state] for k in range(4)]
     modulation = modulation[:1]
     shifts = modulation[:, :width]
     scales = modulation[:, width : 2 * width]
@@ -1346,9 +1394,9 @@
         inner_part, gate_branch = projected[:, :part].astype(BF), projected[:, part:]
     inner_part = inner_part.astype(F32) * mask
     padded = jnp.pad(inner_part, ((taps - 1, 0), (0, 0)))
-    filtered = fbias
+    filtered = fil[taps][None]
     for k in range(taps):
-        filtered = filtered + filt32[:, k][None, :] * padded[k : k + length]
+        filtered = filtered + fil[k][None] * padded[k : k + length]
     sigma_filter = jax.nn.sigmoid(filtered)
     active = (filtered * sigma_filter).astype(BF)
     active32 = active.astype(F32)
@@ -1358,12 +1406,9 @@
     low_rank = selected[:, :rank].astype(BF)
     b_rows = selected[:, rank : rank + state].astype(F32)
     c_rows = selected[:, rank + state :].astype(F32)
-    pre_steps = dot(low_rank, step_q) + sbias
+    pre_steps = dot(low_rank, step_q) + fil[taps + 1][None]
     steps = jax.nn.softplus(pre_steps)
-    rates_f = -jnp.exp(log_f.astype(F32)).T
-    rates_r = -jnp.exp(log_r.astype(F32)).T
     drive = steps * active32
-    rates_f2, rates_r2 = rates_f * LOG2E, rates_r * LOG2E
     mixed_f, mixed_r, states_f, states_r = fwd_scan(steps, drive, rates_f2, rates_r2, b_rows.T, blockdiag(c_rows))
     merged = mixed_f + mixed_r
     sigma_gate = jax.nn.sigmoid(gate_branch)
@@ -1378,7 +1423,7 @@
     block_out = (hidden[0].astype(F32) + gate_scale * mask_here * branch).astype(BF)
     grad_gate = jnp.sum(mask_here * cot_here * branch, axis=0)
 
-    grad_branch = (cot.astype(F32) * gate_scale * mask).astype(BF)
+    grad_branch = lax.optimization_barrier((cot.astype(F32) * gate_scale * mask).astype(BF))
     grad_gated = dot(grad_branch, wout)
     grad_merged = grad_gated * silu_gate
     grad_gate_branch = grad_gated * merged * sigma_gate * (1.0 + gate_branch * (1.0 - sigma_gate))
@@ -1399,7 +1444,7 @@
     grad_pre = grad_steps * jax.nn.sigmoid(pre_steps)
     grad_step_bias = jnp.sum(grad_pre, axis=0)
     grad_pre_low = grad_pre.astype(BF)
-    grad_step_t = dot_tn(grad_pre_low, low_rank)
+    grad_step = dot_tn(low_rank, grad_pre_low)
     grad_low_rank = dot_nt(grad_pre_low, step_q)
     grad_selected = column_sum(jnp.concatenate([grad_low_rank, grad_b, grad_c], axis=1).astype(BF), ns, BF, 1)
     grad_select = dot_tn(active, grad_selected)
@@ -1410,24 +1455,17 @@
     filter_rows = []
     for k in range(taps):
         lead = taps - 1 - k
-        grad_inner = grad_inner + filt32[:, k][None, :] * extended[lead : lead + length]
+        grad_inner = grad_inner + fil[k][None] * extended[lead : lead + length]
         filter_rows.append(jnp.sum(grad_filtered * padded[k : k + length], axis=0))
     grad_filter_bias = jnp.sum(grad_filtered, axis=0)
     grad_projected = jnp.concatenate([(grad_inner * mask).astype(BF), grad_gate_branch], axis=1)
-    fil = jnp.stack(filter_rows + [grad_filter_bias, grad_step_bias])
-    fil = fil.reshape(-1, nd, units).transpose(1, 0, 2)
-    fil = jnp.pad(fil, ((0, 0), (0, 16 - fil.shape[1]), (0, lanes - units)))
-    mid = jnp.concatenate([grad_step_t, grad_decay_f.T, grad_decay_r.T], axis=1)
-    small = jnp.concatenate([grad_select.reshape(nd, units, lanes), mid.reshape(nd, units, lanes), fil], axis=1)
+    grad_fil = jnp.stack(filter_rows + [grad_filter_bias, grad_step_bias])
+    grad_fil = jnp.pad(grad_fil, ((0, 8 - grad_fil.shape[0]), (0, 0)))
     line = jnp.concatenate([scales, grad_gate[None], jnp.pad(embedded.astype(F32) / ns, ((0, 0), (0, width - FREQ))),
                             jnp.zeros((5, width), F32)])
-    g_in, g_out, small, grad_hidden, sums = end(
-        grad_projected, modded, wx, early, small, hidden[0], cotangent[0], line, rows_in, nd, ns, 2)
-    gs_select = small[:units]
-    mid = small[units : 2 * units]
-    gs_step, gs_f, gs_r = mid[:, :rank], mid[:, rank : rank + state], mid[:, rank + state :]
-    fil = small[2 * units :, :units]
-
+    g_in, g_out, own, grad_hidden, sums = end(
+        grad_projected, modded, wx, early, (grad_select, grad_step, grad_decay_f, grad_decay_r, grad_fil), taps, hidden[0], cotangent[0], line, rows_in, nd, ns, 2)
+    gs_select, gs_step, gs_f, gs_r, gs_taps, gs_fbias, gs_sbias = own
     sums = sums.reshape(nd, -1)
     embeds = sums[:, 3 * width : 3 * width + FREQ]
     grad_mod = sums[:, : 3 * width]
@@ -1441,13 +1479,13 @@
         grad_hidden[None],
         g_in,
         gs_select,
-        gs_step.T,
+        gs_step,
         g_out.T,
-        gs_f,
-        gs_r,
-        fil[:taps],
-        fil[taps],
-        fil[taps + 1],
+        gs_f.T,
+        gs_r.T,
+        gs_taps,
+        gs_fbias[0],
+        gs_sbias[0],
         g_modw,
         g_modb,
     )

time: 464 us -> 453 us (0.976)
  local copies, waits for them, and re-layouts: 27.4 us -> 21 us
  Pallas kernels: 330 us -> 324 us
    unnamed x88 -> x107, local copies, waits for them, and re-layouts: 9.61 us -> 12 us
  transfers between devices with their start and end apart: 3 -> 3, of which waited for: 1 -> 1; matrix products, arithmetic and copies ran while one was open for 16% -> 17% of each run, Pallas kernels for 27% -> 27%
where the time goes in v8:
time: 453 us; the launch traced here: 445 us
  Pallas kernels  324 us (72%)
  other arithmetic  41.6 us (9%)
  matrix products  37.9 us (8%)
  local copies, waits for them, and re-layouts  21 us (5%)
  between operations  15.6 us (3%)
    pallas_call x1, Pallas kernels, end(): pl.pallas_call(functools.partial(end_kernel, nd, ns, nsub, rows, turned),...  97.7 us
    pallas_call x1, Pallas kernels, start(): pl.pallas_call(functools.partial(start_kernel, nd, ns, nsub, fused), out_...  91.1 us
    pallas_call x1, Pallas kernels, bwd_scan(): pl.pallas_call(bwd_kernel, grid=(blocks,), in_specs=[row_f, row_r, row_f,...  70.9 us
    pallas_call x1, Pallas kernels, fwd_scan(): pl.pallas_call(fwd_kernel, grid=(blocks,), in_specs=[row_f, row_r, row_f,...  34.9 us
    pallas_call x2, Pallas kernels, column_sum(): pl.pallas_call(functools.partial(column_sum_kernel, ns), out_shape=jax.Sh...  29.8 us
    dot_general x3, matrix products, dot(): return jnp.dot(a, b, preferred_element_type=F32)  14.4 us
    dot_general x3, matrix products, dot_nt(): lax.dot_general(a, b, (((1,), (1,)), ((), ())), preferred_element_type=F32)  13.1 us
    unnamed x107, local copies, waits for them, and re-layouts  12 us
  transfers between devices with their start and end apart: 3, of which 1 were waited for; matrix products, arithmetic and copies ran while one was open for 17% of the time, Pallas kernels for 27%

profile of v8, /device:TPU:0, one launch (start us, length us, event | category | flops | bytes accessed | tf_op | source)
XLA Modules:
  0.0 444.6 jit_solution(13239558624720364634)
XLA Ops:
  9.9 91.1 %start.1 = (bf16[4,256,1536]{2,1,0:T(8,128)(2,1)}, bf16[4,256,768]{2,1,0:T(8,128)(2,1)}, f32[4,256,768]{2,1,0:T(8,128)}, bf16[1536,2304]{1,0:T(8,128)(2,1)}, bf1...) custom-call(bf16[4,64,1536]{2,1,0:T(8,128)(2,1)} %bitcast.93, ...), custom_call_target="tpu_custom_call" | custom-call | tf_op jit(solution)/shard_map/start/pallas_call | solution.py:917
  105.2 3.3 multiply_convert_fusion.3
  109.2 15.4 %column_sum.2 = bf16[4,256,128]{2,1,0:T(8,128)(2,1)S(1)} custom-call(bf16[4,256,128]{2,1,0:T(8,128)(2,1)S(1)} %bitcast.92), custom_call_target="tpu_custom_call" | custom-call | tf_op jit(solution)/shard_map/column_sum/pallas_call | solution.py:302
  127.9 7.0 %fusion.41 = (bf16[1024,768]{1,0:T(8,128)(2,1)}, f32[1024,768]{1,0:T(8,128)}, f32[1024,768]{1,0:T(8,128)}, f32[1024,768]{1,0:T(8,128)}) fusion(bf16[1024,768]{1,0:T(8,128)(2,1)S(1)} %get-tuple-element.114, f32[768]{0:T(1024)} %get-tuple-element.99, bf16[96,768]{1,0:T(8,128)(2,1)S(1)} %copy-done.19, bf16[1024,128]{0,1:T(8,128)(2,1)S(1)} %copy.41), kind=kOutput, calls=%fused_computation.102 | convolution fusion | flops 158859264 | bytes 12930048 | tf_op jit(solution)/shard_map/dot_general | solution.py:1321
  136.1 34.9 %fwd_scan.1 = (f32[1024,768]{1,0:T(8,128)}, f32[1024,768]{1,0:T(8,128)}, bf16[16384,768]{1,0:T(8,128)(2,1)}, bf16[16384,768]{1,0:T(8,128)(2,1)}) custom-call(f32[1024,768]{1,0:T(8,128)} %get-tuple-element.111.step_f.step_r, f32[1024,768]{1,0:T(8,128)} %get-tuple-element.111.step_f.step_r, f32[1024,768]{1,0:T(8,128)} %get-tuple-element.110.u_f.u_r, ...), custom_call_target="tpu_custom_call" | custom-call | flops 40265318400 | bytes 62914560 | tf_op jit(solution)/shard_map/fwd_scan/pallas_call | solution.py:104
  171.0 5.8 %multiply_convert_fusion.2 = (bf16[1024,768]{1,0:T(8,128)(2,1)S(1)}, f32[1024,768]{1,0:T(8,128)}) fusion(f32[4,256,768]{2,1,0:T(8,128)S(1)} %copy-done.10, f32[1024,768]{1,0:T(8,128)} %get-tuple-element.60, f32[1024,768]{1,0:T(8,128)} %get-tuple-element.61), kind=kLoop, calls=%fused_computation.29 | loop fusion | flops 5505024 | bytes 14155776 | tf_op jit(solution)/shard_map/convert_element_type | solution.py:1416
  177.9 5.7 %convolution_convert_fusion = bf16[1024,1536]{1,0:T(8,128)(2,1)} fusion(bf16[1024,768]{1,0:T(8,128)(2,1)S(1)} %get-tuple-element.112, bf16[1536,2304]{1,0:T(8,128)(2,1)} %get-tuple-element.63.wx_h), kind=kOutput, calls=%fused_computation.5 | convolution fusion | flops 2417491968 | bytes 7077888 | tf_op jit(solution)/shard_map/dot_general | solution.py:1325
  183.6 3.7 all-gather.2.cloned.1.call-done
  188.6 2.8 multiply_convert_fusion
  191.4 3.0 convolution_convert_fusion.1
  194.4 6.9 %fusion.21 = (f32[1024,768]{1,0:T(8,128)}, bf16[1024,768]{1,0:T(8,128)(2,1)S(1)}) fusion(f32[4,256,768]{2,1,0:T(8,128)S(1)} %copy-done.10, f32[1024,768]{1,0:T(8,128)S(1)} %copy-done.11, bf16[1024,1536]{1,0:T(8,128)(2,1)S(1)} %multiply_convert_fusion, bf16[1536,2304]{1,0:T(8,128)(2,1)} %get-tuple-element.63.wx_h), kind=kOutput, calls=%fused_computation.53 | convolution fusion | flops 2425356288 | bytes 16515072 | tf_op jit(solution)/shard_map/dot_general | solution.py:1321
  202.4 2.9 convolution_convert_fusion.2
  205.4 2.5 pad_maximum_fusion
  207.9 70.9 %bwd_scan.1 = (f32[1024,768]{1,0:T(8,128)}, f32[1024,768]{1,0:T(8,128)}, f32[1024,768]{1,0:T(8,128)}, f32[1024,768]{1,0:T(8,128)}, f32[64,256]{1,0:T(8,128)}, /*...) custom-call(f32[1024,768]{1,0:T(8,128)} %get-tuple-element.111.step_f.ste, ...), custom_call_target="tpu_custom_call" | custom-call | flops 85563801600 | bytes 78643200 | tf_op jit(solution)/shard_map/bwd_scan/pallas_call | solution.py:242
  278.9 6.2 %fusion.39 = (f32[768]{0:T(1024)S(1)}, bf16[1024,768]{1,0:T(8,128)(2,1)S(1)}) fusion(f32[1024,768]{1,0:T(8,128)S(1)} %copy-done.4, f32[768]{0:T(1024)S(1)} %copy-done.38, f32[1024,768]{1,0:T(8,128)} %get-tuple-element.69, f32[1024,768]{1,0:T(8,128)} %get-tuple-element.70, bf16[1024,768]{1,0:T(8,128)(2,1)S(1)} %copy-done.1, ...), kind=kLoop, calls=%fused_computation.101 | loop fusion | flops 10222848 | bytes 18880512 | tf_op jit(solution)/shard_map/reduce_sum | solution.py:1445
  292.3 14.4 %column_sum.3 = bf16[4,256,128]{2,1,0:T(8,128)(2,1)S(1)} custom-call(bf16[4,256,128]{2,1,0:T(8,128)(2,1)S(1)} %pad_maximum_fusion.2.p_ref), custom_call_target="tpu_custom_call" | custom-call | tf_op jit(solution)/shard_map/column_sum/pallas_call | solution.py:302
  306.8 6.2 %add_multiply_fusion = f32[1024,768]{1,0:T(8,128)S(1)} fusion(f32[1024,768]{1,0:T(8,128)} %get-tuple-element.115, f32[1024,768]{1,0:T(8,128)} %get-tuple-element.111.step_f.step_r, bf16[1024,128]{1,0:T(8,128)(2,1)S(1)} %bitcast.89, bf16[768,128]{1,0:T(8,128)(2,1)} %get-tuple-element.56, f32[1024,768]{1,0:T(8,128)} %get-tuple-element.69, ...), kind=kOutput, calls=%fused_computation.28 | convolution fusion | flops 209977344 | bytes 16187392 | tf_op jit(solution)/shard_map/dot_general | solution.py:1325
  313.1 4.7 %fusion.37 = (f32[768]{0:T(1024)S(1)}, f32[768]{0:T(1024)S(1)}, f32[768]{0:T(1024)S(1)}, f32[768]{0:T(1024)S(1)}, f32[768]{0:T(1024)S(1)}, /*index=5*/bf16[1024,768]{1,0:T(8,128)(2,1)}) fusion(f32[1024,768]{1,0:T(8,128)S(1)} %add_multiply_fusion, f32[1024]{0:T(1024)S(1)} %copy-done.26, bf16[4,256,768]{2,1,0:T(8,128)(2,1)S(1)} %copy-done.7, ...), kind=kLoop, calls=%fused_computation.100 | loop fusion | flops 15724800 | bytes 9468928 | tf_op jit(solution)/shard_map/reduce_sum | solution.py:1460
  318.5 1.8 slice_multiply_fusion
  320.3 2.0 fusion.18.gstep
  323.7 1.9 pad_maximum_fusion.1.gp_h
  325.6 2.6 fusion.14
  328.9 97.7 %end.1 = (f32[48,6144]{1,0:T(8,128)}, f32[48,3072]{1,0:T(8,128)}, f32[96,128]{1,0:T(8,128)}, f32[96,96]{1,0:T(8,128)}, f32[16,96]{1,0:T(8,128)}, /*index=5*/f32[...) custom-call(bf16[1024,1536]{1,0:T(8,128)(2,1)} %pad_maximum_fusion.1, ...), custom_call_target="tpu_custom_call" | custom-call | tf_op jit(solution)/shard_map/end/pallas_call | solution.py:1276
  429.6 2.1 copy.55
  (159 shorter events, 33.6 us)
Async XLA Ops:
  7.2 180.2 %all-gather.2.cloned.1.call-start = ((), (), s32[]{:S(2)}) async-start(), calls=%async_computation.2 | async-start | bytes 3932160 | tf_op jit(solution)/shard_map/all_gather | solution.py:1405
  108.6 19.3 %copy-start = (bf16[1024,768]{1,0:T(8,128)(2,1)}, bf16[1024,768]{1,0:T(8,128)(2,1)S(1)}, u32[]{:S(2)}) copy-start(bf16[1024,768]{1,0:T(8,128)(2,1)S(1)} %get-tuple-element.114) | copy-start | bytes 4718596
  108.6 17.4 %copy-start.21 = (f32[64,768]{1,0:T(8,128)S(1)}, f32[64,768]{1,0:T(8,128)}, u32[]{:S(2)}) copy-start(f32[64,768]{1,0:T(8,128)} %get-tuple-element.59) | copy-start | bytes 589828
  109.2 18.7 %copy-start.19 = (bf16[96,768]{1,0:T(8,128)(2,1)S(1)}, bf16[96,768]{1,0:T(8,128)(2,1)}, u32[]{:S(2)}) copy-start(bf16[96,768]{1,0:T(8,128)(2,1)} %get-tuple-element.58) | copy-start | bytes 442372
  124.7 10.1 %copy-start.12 = (bf16[1024,128]{0,1:T(8,128)(2,1)}, bf16[1024,128]{0,1:T(8,128)(2,1)S(1)}, u32[]{:S(2)}) copy-start(bf16[1024,128]{0,1:T(8,128)(2,1)S(1)} %copy.41) | copy-start | bytes 786436
  124.8 200.9 %reduce-scatter.3.cloned.1.call-start = ((), (), s32[]{:S(2)}) async-start(), calls=%async_computation.3 | async-start | bytes 3932160 | tf_op jit(solution)/shard_map/reduce_scatter | solution.py:1419
  127.8 7.0 %copy-start.39 = (s32[1024]{0:T(1024)S(1)}, s32[1024]{0:T(1024)}, u32[]{:S(2)}) copy-start(s32[1024]{0:T(1024)} %add_select_fusion) | copy-start | bytes 12292
  127.9 7.0 %copy-start.45 = (s32[256]{0:T(256)S(1)}, s32[256]{0:T(256)}, u32[]{:S(2)}) copy-start(s32[256]{0:T(256)} %and_select_fusion) | copy-start | bytes 3076
  136.1 34.9 %copy-start.10 = (f32[4,256,768]{2,1,0:T(8,128)S(1)}, f32[4,256,768]{2,1,0:T(8,128)}, u32[]{:S(2)}) copy-start(f32[4,256,768]{2,1,0:T(8,128)} %get-tuple-element.62) | copy-start | bytes 9437188
  187.4 141.6 %reduce-scatter.5.cloned.1.call-start = ((), (), s32[]{:S(2)}) async-start(), calls=%async_computation.4 | async-start | bytes 5308416 | tf_op jit(solution)/shard_map/reduce_scatter | solution.py:1435
  194.4 8.1 %copy-start.9 = (bf16[4,256,1536]{2,1,0:T(8,128)(2,1)S(1)}, bf16[4,256,1536]{2,1,0:T(8,128)(2,1)}, u32[]{:S(2)}) copy-start(bf16[4,256,1536]{2,1,0:T(8,128)(2,1)} %get-tuple-element.77) | copy-start | bytes 9437188
  207.9 70.9 %copy-start.1 = (bf16[1024,768]{1,0:T(8,128)(2,1)S(1)}, bf16[1024,768]{1,0:T(8,128)(2,1)}, u32[]{:S(2)}) copy-start(bf16[1024,768]{1,0:T(8,128)(2,1)} %copy-done) | copy-start | bytes 4718596
  207.9 70.9 %copy-start.4 = (f32[1024,768]{1,0:T(8,128)S(1)}, f32[1024,768]{1,0:T(8,128)}, u32[]{:S(2)}) copy-start(f32[1024,768]{1,0:T(8,128)} %get-tuple-element.133) | copy-start | bytes 9437188
  207.9 70.9 %copy-start.38 = (f32[768]{0:T(1024)S(1)}, f32[768]{0:T(1024)}, u32[]{:S(2)}) copy-start(f32[768]{0:T(1024)} %get-tuple-element.99) | copy-start | bytes 9220
  278.9 10.4 %copy-start.24 = (f32[64,256]{1,0:T(8,128)S(1)}, f32[64,256]{1,0:T(8,128)}, u32[]{:S(2)}) copy-start(f32[64,256]{1,0:T(8,128)} %get-tuple-element.73) | copy-start | bytes 196612
  306.8 6.2 %copy-start.3 = (f32[1024,768]{1,0:T(8,128)S(1)}, f32[1024,768]{1,0:T(8,128)}, u32[]{:S(2)}) copy-start(f32[1024,768]{1,0:T(8,128)} %copy-done.2) | copy-start | bytes 9437188
  306.8 6.2 %copy-start.7 = (bf16[4,256,768]{2,1,0:T(8,128)(2,1)S(1)}, bf16[4,256,768]{2,1,0:T(8,128)(2,1)}, u32[]{:S(2)}) copy-start(bf16[4,256,768]{2,1,0:T(8,128)(2,1)} %get-tuple-element.54) | copy-start | bytes 4718596
  426.7 6.6 %copy-start.28 = (f32[96,96]{1,0:T(8,128)S(1)}, f32[96,96]{1,0:T(8,128)}, u32[]{:S(2)}) copy-start(f32[96,96]{1,0:T(8,128)} %get-tuple-element.155) | copy-start | bytes 110596
  426.7 7.2 %copy-start.18 = (f32[48,3072]{1,0:T(8,128)S(1)}, f32[48,3072]{1,0:T(8,128)}, u32[]{:S(2)}) copy-start(f32[48,3072]{1,0:T(8,128)} %get-tuple-element.84) | copy-start | bytes 1769476
  426.7 8.0 %copy-start.41 = (f32[16,96]{1,0:T(8,128)S(1)}, f32[16,96]{1,0:T(8,128)}, u32[]{:S(2)}) copy-start(f32[16,96]{1,0:T(8,128)} %get-tuple-element.85) | copy-start | bytes 18436
  426.7 8.6 %copy-start.40 = (f32[16,96]{1,0:T(8,128)S(1)}, f32[16,96]{1,0:T(8,128)}, u32[]{:S(2)}) copy-start(f32[16,96]{1,0:T(8,128)} %get-tuple-element.86) | copy-start | bytes 18436
  426.7 9.2 %copy-start.44 = (f32[4,96]{1,0:T(4,128)S(1)}, f32[4,96]{1,0:T(4,128)}, u32[]{:S(2)}) copy-start(f32[4,96]{1,0:T(4,128)} %get-tuple-element.159) | copy-start | bytes 4612
  426.7 9.8 %copy-start.47 = (f32[1,96]{1,0:T(1,128)S(1)}, f32[1,96]{1,0:T(1,128)}, u32[]{:S(2)}) copy-start(f32[1,96]{1,0:T(1,128)} %get-tuple-element.88) | copy-start | bytes 1156
  426.8 10.3 %copy-start.46 = (f32[1,96]{1,0:T(1,128)S(1)}, f32[1,96]{1,0:T(1,128)}, u32[]{:S(2)}) copy-start(f32[1,96]{1,0:T(1,128)} %get-tuple-element.89) | copy-start | bytes 1156
  (27 other events, 114.0 us)
Sparse Core Ops, SparseCore 0:
  124.9 62.4 all-gather.1
  189.6 58.8 reduce-scatter.2
  252.0 53.8 reduce-scatter.4

commit v9 on v8

--- a/solution.py
+++ b/solution.py
@@ -538,8 +538,8 @@
 
 
 def start_kernel(nd, ns, nsub, fused, hid, win, wout, mask, emb, modw, modb, select, step, dec_f, dec_r, taps, fbias, sbias,
-                 md_o, inner_o, gate_o, wx_o, select_o, step_o, rate_o, fil_o, mask_o, mod_o,
-                 hv, wv, mv, iv, gv, pack, modw_v, pack_v, eland, prod, rowp, land1, land2,
+                 md_o, nm_o, inner_o, gate_o, wx_o, select_o, step_o, rate_o, fil_o, mask_o, mod_o,
+                 hv, wv, mv, nv, iv, gv, pack, modw_v, pack_v, eland, prod, rowp, land1, land2,
                  su, ru, sd, rd, swz, rwx, swp, swm, spz, rp, spp, spm, sk, rk, se, re, s1, r1, s2, r2, own, out):
     d, q = lax.axis_index("dp"), lax.axis_index("seq")
     nc = nd // 2
@@ -752,7 +752,7 @@
 
     def own_copies(t):
         return [pltpu.make_async_copy(src.at[t], dst.at[t], out.at[t, i]) for i, (src, dst) in enumerate(
-            ((mv, md_o), (iv, inner_o), (gv, gate_o)) if fused else ((hv, md_o),))]
+            ((mv, md_o), (iv, inner_o), (gv, gate_o), (nv, nm_o)) if fused else ((hv, md_o),))]
 
     local = hv.shape[1] * hv.shape[2]
     width = hv.shape[3]
@@ -767,6 +767,7 @@
                     x = x - jnp.mean(x, axis=1, keepdims=True)
                     x = x * lax.rsqrt(jnp.mean(x * x, axis=1, keepdims=True) + EPS)
                     to = pl.multiple_of(s * (local // nsub) + r * 16, 16)
+                    nv[t, pl.ds(to, 16), :] = x.astype(BF)
                     mv[t, pl.ds(to, 16), :] = (x * scale + shift).astype(BF)
             tile = part if part % 256 else part // 2
 
@@ -918,6 +919,7 @@
         functools.partial(start_kernel, nd, ns, nsub, fused),
         out_shape=[
             jax.ShapeDtypeStruct(runs, BF),
+            jax.ShapeDtypeStruct((ns, length, width), BF),
             jax.ShapeDtypeStruct((ns, length, part), BF),
             jax.ShapeDtypeStruct((ns, length, part), F32),
             jax.ShapeDtypeStruct((nd * ns * rows, 3 * part), BF),
@@ -929,10 +931,10 @@
             jax.ShapeDtypeStruct((8, modw.shape[1]), F32),
         ],
         in_specs=[HBM, HBM, HBM] + [VMEM] * 11,
-        out_specs=[HBM] * 4 + [VMEM] * 6,
+        out_specs=[HBM] * 5 + [VMEM] * 6,
         scratch_shapes=[
             pltpu.VMEM((ns,) + hidden.shape, BF), pltpu.VMEM((nd * ns * rows, 3 * part), BF),
-            pltpu.VMEM((ns, length, width), BF), pltpu.VMEM((ns, length, part), BF), pltpu.VMEM((ns, length, part), F32),
+            pltpu.VMEM((ns, length, width), BF), pltpu.VMEM((ns, length, width), BF), pltpu.VMEM((ns, length, part), BF), pltpu.VMEM((ns, length, part), F32),
             pltpu.VMEM(pack, BF), pltpu.VMEM((held, modw.shape[1]), BF), pltpu.VMEM((nd,) + pack, BF),
             pltpu.VMEM((nd, 16, FREQ), BF), pltpu.VMEM((nd * 16, modw.shape[1]), F32),
             pltpu.VMEM((nd,) + lines, F32), pltpu.VMEM((nd,) + lines, F32), pltpu.VMEM((ns,) + lines, F32),
@@ -940,7 +942,7 @@
             DMA((ns, 3)), DMA((nd * ns, 5)), DMA((2, nc, ns)), DMA((2, nc, ns)),
             DMA(()), DMA((nd,)), DMA((nc, ns)), DMA((nc, ns)),
             DMA((ns,)), DMA((ns,)), DMA((nd,)), DMA((nd,)),
-            DMA((nd,)), DMA((nd,)), DMA((ns,)), DMA((ns,)), DMA((6,)), DMA((ns, 3)),
+            DMA((nd,)), DMA((nd,)), DMA((ns,)), DMA((ns,)), DMA((6,)), DMA((ns, 4)),
         ],
         compiler_params=pltpu.CompilerParams(
             collective_id=cid, has_side_effects=True, vmem_limit_bytes=56 * 2**20),
@@ -949,9 +951,9 @@
 
 
 def end_kernel(nd, ns, nsub, rows, turned,
-               gp_h, md_h, wx_h, gsel, gstep, gdf, gdr, gfil, hid_ref, cot_ref, line_ref, early,
+               gi_h, gg_h, md_h, nm_h, wx_h, gsel, gstep, gdf, gdr, gfil, hid_ref, cot_ref, line_ref, early,
                gin_o, gout_o, sel_o, step_o, df_o, dr_o, taps_o, fb_o, sb_o, gh_o, mod_o,
-               gp, md, wx, sm_ref, so_ref, gm, made, pair, plane, spair, splane, ssum, fro, ready, up, down, own, acc, msg, mland,
+               gp, md, nm, wx, sm_ref, so_ref, gm, made, pair, plane, spair, splane, ssum, fro, ready, up, down, own, acc, msg, mland,
                ld, sa, ra, sb, rb, sc, rc, se, re, ta, ra2, tb, rb2, tc, rc2, su, ru, sd, rd, s1, r1, s2, r2):
     d, q = lax.axis_index("dp"), lax.axis_index("seq")
     nc = nd // 2
@@ -975,7 +977,7 @@
     half = ns * rw
 
     loads = [pltpu.make_async_copy(src, dst, ld.at[i]) for i, (src, dst) in enumerate(
-        ((gp_h, gp), (wx_h.at[:, 0:cols], wx), (md_h, md)))]
+        ((gi_h, gp.at[:, 0:part]), (gg_h, gp.at[:, part:cols]), (wx_h.at[:, 0:cols], wx), (nm_h, nm), (md_h, md)))]
     for copy in loads:
         copy.start()
 
@@ -995,7 +997,10 @@
         @pl.loop(0, width // 512)
         def _(j):
             here = pl.ds(pl.multiple_of(j * 512, 512), 512)
-            full = lax.dot_general(gp[t * local:(t + 1) * local, :], wx[here, :], NT, preferred_element_type=F32)
+            lines = slice(t * local, (t + 1) * local)
+            full = lax.dot_general(gp[lines, :], wx[here, :], NT, preferred_element_type=F32)
+            acc[0:1, here] += jnp.sum(full, axis=0, keepdims=True)
+            acc[1:2, here] += jnp.sum(full * nm[lines, here].astype(F32), axis=0, keepdims=True)
             full = full.astype(BF)
             for s in range(nsub):
                 gm[t, s, :, here] = full[s * sub:(s + 1) * sub]
@@ -1054,8 +1059,10 @@
 
     for t in others:
         whole(t, q).start()
-    loads[0].wait()
-    loads[1].wait()
+    for copy in loads[:4]:
+        copy.wait()
+    acc[...] = jnp.zeros(acc.shape, F32)
+    acc[2:4, :] = line_ref[1:3, :]
     far(0)
     steps = [(k, s) for k in range(ns - 1) for s in range(nsub)]
 
@@ -1094,7 +1101,7 @@
         sm_ref[j, above + rank + states:taps_at, 0:units] = gdr[:, here]
         sm_ref[j, taps_at:taps_at + 8, 0:units] = gfil[:, here]
 
-    loads[2].wait()
+    loads[4].wait()
     order = chips + [chip]
 
     def give(c):
@@ -1105,6 +1112,15 @@
     give(order[0])
     for k in range(1, ns // 2):
         far(k)
+    msg[...] = jnp.zeros(msg.shape, F32)
+    long = msg.shape[1] // 128
+    for i in range(3 * width // 128 + FREQ // 128):
+        r, c = divmod(i * 128, width)
+        to = (i % long) * 128
+        msg[i // long:i // long + 1, to:to + 128] = acc[r:r + 1, c:c + 128]
+    for k, t in enumerate(others):
+        send(msg, mland.at[q], s1.at[k], r1.at[q], (d, t)).start()
+
     for i, c in enumerate(order):
         if i + 1 < nc:
             give(order[i + 1])
@@ -1153,8 +1169,13 @@
     for k, s in steps[max(nc, late):]:
         step(k, s)
 
-    acc[...] = jnp.zeros(acc.shape, F32)
-    acc[2:4, :] = line_ref[1:3, :]
+    total = msg[...]
+    for k, t in enumerate(others):
+        send(msg, mland.at[t], s1.at[k], r1.at[t], (d, t)).wait_recv()
+        total = total + mland[t]
+    mod_o[d] = total
+    for k, e in enumerate(peers):
+        send(mod_o.at[d], mod_o.at[d], s2.at[k], r2.at[d], (e, q)).start()
     scale = 1.0 + line_ref[0:1, :]
     for s in range(nsub):
         own[...] = gm[q, s].astype(F32)
@@ -1177,21 +1198,10 @@
             x = x - jnp.mean(x, axis=1, keepdims=True)
             inverse = lax.rsqrt(jnp.mean(x * x, axis=1, keepdims=True) + EPS)
             normed = x * inverse
-            acc[0:1, :] += jnp.sum(grad, axis=0, keepdims=True)
-            acc[1:2, :] += jnp.sum(grad * normed, axis=0, keepdims=True)
             grad = grad * scale
             grad = grad - jnp.mean(grad, axis=1, keepdims=True) - normed * jnp.mean(
                 grad * normed, axis=1, keepdims=True)
             gh_o[s, here, :] = (cot_ref[s, here, :].astype(F32) + inverse * grad).astype(BF)
-
-    msg[...] = jnp.zeros(msg.shape, F32)
-    long = msg.shape[1] // 128
-    for i in range(3 * width // 128 + FREQ // 128):
-        r, c = divmod(i * 128, width)
-        to = (i % long) * 128
-        msg[i // long:i // long + 1, to:to + 128] = acc[r:r + 1, c:c + 128]
-    for k, t in enumerate(others):
-        send(msg, mland.at[q], s1.at[k], r1.at[q], (d, t)).start()
 
     inner = part * ns
 
@@ -1202,13 +1212,6 @@
         gout_o[:, pl.ds(pl.multiple_of(at, 128), part)] = rest[0:rows, part:2 * part].astype(F32)
 
     place(q, early[q])
-    total = msg[...]
-    for k, t in enumerate(others):
-        send(msg, mland.at[t], s1.at[k], r1.at[t], (d, t)).wait_recv()
-        total = total + mland[t]
-    mod_o[d] = total
-    for k, e in enumerate(peers):
-        send(mod_o.at[d], mod_o.at[d], s2.at[k], r2.at[d], (e, q)).start()
     for t in others:
         third(t, t).wait_recv()
         whole(t, t).wait_recv()
@@ -1249,9 +1252,9 @@
             sink(k, s, gm.at[k, s]).wait_send()
 
 
-def end(grad_projected, modded, wx, early, small, taps, hidden, cot, line, rows, nd, ns, cid):
-    length, cols = grad_projected.shape
-    part = cols // 2
+def end(grad_inner, grad_gate, modded, normed, wx, early, small, taps, hidden, cot, line, rows, nd, ns, cid):
+    length, part = grad_inner.shape
+    cols = 2 * part
     width = wx.shape[0]
     inner = part * ns
     nc, nsub = nd // 2, 4
@@ -1288,15 +1291,16 @@
             jax.ShapeDtypeStruct((nsub, sub, width), BF),
             jax.ShapeDtypeStruct((nd, 8, short), F32),
         ],
-        in_specs=[HBM] * 3 + [VMEM] * 9, out_specs=[VMEM] * 11,
+        in_specs=[HBM] * 5 + [VMEM] * 9, out_specs=[VMEM] * 11,
         scratch_shapes=[
-            pltpu.VMEM(grad_projected.shape, BF), pltpu.VMEM(modded.shape, BF), pltpu.VMEM((width, cols), BF),
+            pltpu.VMEM((length, cols), BF), pltpu.VMEM(modded.shape, BF), pltpu.VMEM(normed.shape, BF),
+            pltpu.VMEM((width, cols), BF),
             pltpu.VMEM((nd,) + v, F32), pltpu.VMEM(v, F32), runs,
             pltpu.VMEM((nc, 2, ns, rw, part), BF), blocks, blocks,
             smalls, smalls, pltpu.VMEM(v, F32), pltpu.VMEM((ns, rw, part), BF), pltpu.VMEM((ns, rw, cols), BF), runs, runs,
             pltpu.VMEM((sub, width), F32), pltpu.VMEM((8, width), F32), pltpu.VMEM((8, short), F32),
             pltpu.VMEM((ns, 8, short), F32),
-            DMA((3,)),
+            DMA((5,)),
             DMA((nc,)), DMA((nc,)), DMA((nc,)), DMA((nc,)), DMA((ns,)), DMA((ns,)), DMA((ns,)), DMA((ns,)),
             DMA((nc,)), DMA((nc,)), DMA((nc,)), DMA((nc,)), DMA(()), DMA(()),
             DMA((ns, nsub)), DMA((ns, nsub)), DMA((ns, nsub)), DMA((ns, nsub)),
@@ -1305,7 +1309,7 @@
         compiler_params=pltpu.CompilerParams(
             collective_id=cid, has_side_effects=True, vmem_limit_bytes=60 * 2**20),
         name="end",
-    )(grad_projected, modded, wx, *small, hidden, cot, line, early)
+    )(grad_inner, grad_gate, modded, normed, wx, *small, hidden, cot, line, early)
     return gin, gout, own, gh.reshape(local, width), mod
 
 
@@ -1365,7 +1369,7 @@
     modb = lax.dynamic_update_slice(modb, modulation_bias.astype(F32), ((d * ns + q) * modulation_bias.shape[0],))
     row_pad = ((0, -rows_in % 16), (0, 0))
     fused = rows_in % 16 == 0
-    modded, inner_part, gate_branch, wx, select_q, step_q, rates, fil, mask, modulation = start(
+    modded, normed, inner_part, gate_branch, wx, select_q, step_q, rates, fil, mask, modulation = start(
         hidden[0], pad_mask.reshape(-1, 128), jnp.pad(input_weight, row_pad), jnp.pad(output_weight.T, row_pad),
         embedded, modulation_weight, modb.reshape(-1, 128),
         (select_weight, step_weight, decay_forward.T, decay_reverse.T, filter_weight, filter_bias[None], step_bias[None]),
@@ -1386,10 +1390,11 @@
         return centered * inverse, inverse
 
     if fused:
-        modded = modded.reshape(length, width)
+        modded, normed = modded.reshape(length, width), normed.reshape(length, width)
         inner_part, gate_branch = inner_part.reshape(length, part), gate_branch.reshape(length, part)
     else:
-        modded = (norm(modded.reshape(length, width))[0] * (1.0 + scales) + shifts).astype(BF)
+        normed = norm(modded.reshape(length, width))[0]
+        modded, normed = (normed * (1.0 + scales) + shifts).astype(BF), normed.astype(BF)
         projected = dot(modded, win)
         inner_part, gate_branch = projected[:, :part].astype(BF), projected[:, part:]
     inner_part = inner_part.astype(F32) * mask
@@ -1458,13 +1463,13 @@
         grad_inner = grad_inner + fil[k][None] * extended[lead : lead + length]
         filter_rows.append(jnp.sum(grad_filtered * padded[k : k + length], axis=0))
     grad_filter_bias = jnp.sum(grad_filtered, axis=0)
-    grad_projected = jnp.concatenate([(grad_inner * mask).astype(BF), grad_gate_branch], axis=1)
+    grad_inner = (grad_inner * mask).astype(BF)
     grad_fil = jnp.stack(filter_rows + [grad_filter_bias, grad_step_bias])
     grad_fil = jnp.pad(grad_fil, ((0, 8 - grad_fil.shape[0]), (0, 0)))
     line = jnp.concatenate([scales, grad_gate[None], jnp.pad(embedded.astype(F32) / ns, ((0, 0), (0, width - FREQ))),
                             jnp.zeros((5, width), F32)])
     g_in, g_out, own, grad_hidden, sums = end(
-        grad_projected, modded, wx, early, (grad_select, grad_step, grad_decay_f, grad_decay_r, grad_fil), taps, hidden[0], cotangent[0], line, rows_in, nd, ns, 2)
+        grad_inner, grad_gate_branch, modded, normed, wx, early, (grad_select, grad_step, grad_decay_f, grad_decay_r, grad_fil), taps, hidden[0], cotangent[0], line, rows_in, nd, ns, 2)
     gs_select, gs_step, gs_f, gs_r, gs_taps, gs_fbias, gs_sbias = own
     sums = sums.reshape(nd, -1)
     embeds = sums[:, 3 * width : 3 * width + FREQ]

time: 453 us -> 446 us (0.985)
  Pallas kernels: 324 us -> 319 us
    pallas_call x1, Pallas kernels: 97.7 us -> 92.2 us  [end(): pl.pallas_call(functools.partial(end_kernel, nd, ns, nsub, rows, turned),...]
    unnamed x107 -> x99, local copies, waits for them, and re-layouts: 12 us -> 12 us
where the time goes in v9:
time: 446 us; the launch traced here: 438 us
  Pallas kernels  319 us (72%)
  other arithmetic  39.8 us (9%)
  matrix products  37.9 us (8%)
  local copies, waits for them, and re-layouts  20.9 us (5%)
  between operations  15.6 us (3%)
    pallas_call x1, Pallas kernels, end(): pl.pallas_call(functools.partial(end_kernel, nd, ns, nsub, rows, turned),...  92.2 us
    pallas_call x1, Pallas kernels, start(): pl.pallas_call(functools.partial(start_kernel, nd, ns, nsub, fused), out_...  91.5 us
    pallas_call x1, Pallas kernels, bwd_scan(): pl.pallas_call(bwd_kernel, grid=(blocks,), in_specs=[row_f, row_r, row_f,...  70.8 us
    pallas_call x1, Pallas kernels, fwd_scan(): pl.pallas_call(fwd_kernel, grid=(blocks,), in_specs=[row_f, row_r, row_f,...  34.9 us
    pallas_call x2, Pallas kernels, column_sum(): pl.pallas_call(functools.partial(column_sum_kernel, ns), out_shape=jax.Sh...  29.7 us
    dot_general x3, matrix products, dot(): return jnp.dot(a, b, preferred_element_type=F32)  14.4 us
    dot_general x3, matrix products, dot_nt(): lax.dot_general(a, b, (((1,), (1,)), ((), ())), preferred_element_type=F32)  13.1 us
    unnamed x99, local copies, waits for them, and re-layouts  12 us
  transfers between devices with their start and end apart: 3, of which 1 were waited for; matrix products, arithmetic and copies ran while one was open for 17% of the time, Pallas kernels for 27%

profile of v9, /device:TPU:0, one launch (start us, length us, event | category | flops | bytes accessed | tf_op | source)
XLA Modules:
  0.0 437.6 jit_solution(13734866498517281924)
XLA Ops:
  9.9 91.5 %start.1 = (bf16[4,256,1536]{2,1,0:T(8,128)(2,1)}, bf16[4,256,1536]{2,1,0:T(8,128)(2,1)}, bf16[4,256,768]{2,1,0:T(8,128)(2,1)}, f32[4,256,768]{2,1,0:T(8,128)}, ...) custom-call(bf16[4,64,1536]{2,1,0:T(8,128)(2,1)} %bitcast.94, ...), custom_call_target="tpu_custom_call" | custom-call | tf_op jit(solution)/shard_map/start/pallas_call | solution.py:918
  102.1 1.7 slice_reduce_fusion.2
  103.7 1.8 convert_multiply_fusion.2
  105.6 3.3 multiply_convert_fusion.3
  109.5 15.3 %column_sum.2 = bf16[4,256,128]{2,1,0:T(8,128)(2,1)S(1)} custom-call(bf16[4,256,128]{2,1,0:T(8,128)(2,1)S(1)} %bitcast.93), custom_call_target="tpu_custom_call" | custom-call | tf_op jit(solution)/shard_map/column_sum/pallas_call | solution.py:302
  128.2 6.9 %fusion.41 = (bf16[1024,768]{1,0:T(8,128)(2,1)}, f32[1024,768]{1,0:T(8,128)}, f32[1024,768]{1,0:T(8,128)}, f32[1024,768]{1,0:T(8,128)}) fusion(bf16[1024,768]{1,0:T(8,128)(2,1)S(1)} %get-tuple-element.116, f32[768]{0:T(1024)} %get-tuple-element.101, bf16[96,768]{1,0:T(8,128)(2,1)S(1)} %copy-done.15, bf16[1024,128]{0,1:T(8,128)(2,1)S(1)} %copy.36), kind=kOutput, calls=%fused_computation.101 | convolution fusion | flops 158859264 | bytes 12930048 | tf_op jit(solution)/shard_map/dot_general | solution.py:1325
  136.4 34.9 %fwd_scan.1 = (f32[1024,768]{1,0:T(8,128)}, f32[1024,768]{1,0:T(8,128)}, bf16[16384,768]{1,0:T(8,128)(2,1)}, bf16[16384,768]{1,0:T(8,128)(2,1)}) custom-call(f32[1024,768]{1,0:T(8,128)} %get-tuple-element.113.step_f.step_r, f32[1024,768]{1,0:T(8,128)} %get-tuple-element.113.step_f.step_r, f32[1024,768]{1,0:T(8,128)} %get-tuple-element.112.u_f.u_r, ...), custom_call_target="tpu_custom_call" | custom-call | flops 40265318400 | bytes 62914560 | tf_op jit(solution)/shard_map/fwd_scan/pallas_call | solution.py:104
  171.2 5.8 %multiply_convert_fusion.2 = (bf16[1024,768]{1,0:T(8,128)(2,1)S(1)}, f32[1024,768]{1,0:T(8,128)}) fusion(f32[4,256,768]{2,1,0:T(8,128)S(1)} %copy-done.6, f32[1024,768]{1,0:T(8,128)} %get-tuple-element.61, f32[1024,768]{1,0:T(8,128)} %get-tuple-element.62), kind=kLoop, calls=%fused_computation.28 | loop fusion | flops 5505024 | bytes 14155776 | tf_op jit(solution)/shard_map/convert_element_type | solution.py:1421
  178.2 5.7 %convolution_convert_fusion = bf16[1024,1536]{1,0:T(8,128)(2,1)} fusion(bf16[1024,768]{1,0:T(8,128)(2,1)S(1)} %get-tuple-element.114, bf16[1536,2304]{1,0:T(8,128)(2,1)} %get-tuple-element.64.wx_h), kind=kOutput, calls=%fused_computation.5 | convolution fusion | flops 2417491968 | bytes 7077888 | tf_op jit(solution)/shard_map/dot_general | solution.py:1329
  183.8 3.9 all-gather.2.cloned.1.call-done
  189.0 2.8 multiply_convert_fusion
  191.8 3.0 convolution_convert_fusion.1
  194.8 6.9 %fusion.7 = (bf16[1024,768]{1,0:T(8,128)(2,1)S(1)}, f32[1024,768]{1,0:T(8,128)}) fusion(f32[4,256,768]{2,1,0:T(8,128)S(1)} %copy-done.6, f32[1024,768]{1,0:T(8,128)S(1)} %copy-done.7, bf16[1024,1536]{1,0:T(8,128)(2,1)S(1)} %multiply_convert_fusion, bf16[1536,2304]{1,0:T(8,128)(2,1)} %get-tuple-element.64.wx_h), kind=kOutput, calls=%fused_computation.19 | convolution fusion | flops 2425356288 | bytes 16515072 | tf_op jit(solution)/shard_map/dot_general | solution.py:1325
  202.8 2.9 convolution_convert_fusion.2
  205.8 2.5 pad_maximum_fusion
  208.3 70.8 %bwd_scan.1 = (f32[1024,768]{1,0:T(8,128)}, f32[1024,768]{1,0:T(8,128)}, f32[1024,768]{1,0:T(8,128)}, f32[1024,768]{1,0:T(8,128)}, f32[64,256]{1,0:T(8,128)}, /*...) custom-call(f32[1024,768]{1,0:T(8,128)} %get-tuple-element.113.step_f.ste, ...), custom_call_target="tpu_custom_call" | custom-call | flops 85563801600 | bytes 78643200 | tf_op jit(solution)/shard_map/bwd_scan/pallas_call | solution.py:242
  279.2 6.2 %fusion.39 = (f32[768]{0:T(1024)S(1)}, bf16[1024,768]{1,0:T(8,128)(2,1)S(1)}) fusion(f32[1024,768]{1,0:T(8,128)S(1)} %copy-done.4, f32[768]{0:T(1024)S(1)} %copy-done.34, f32[1024,768]{1,0:T(8,128)} %get-tuple-element.70, f32[1024,768]{1,0:T(8,128)} %get-tuple-element.71, bf16[1024,768]{1,0:T(8,128)(2,1)S(1)} %copy-done.1, ...), kind=kLoop, calls=%fused_computation.100 | loop fusion | flops 10222848 | bytes 18880512 | tf_op jit(solution)/shard_map/reduce_sum | solution.py:1450
  292.7 14.4 %column_sum.3 = bf16[4,256,128]{2,1,0:T(8,128)(2,1)S(1)} custom-call(bf16[4,256,128]{2,1,0:T(8,128)(2,1)S(1)} %pad_maximum_fusion.1.p_ref), custom_call_target="tpu_custom_call" | custom-call | tf_op jit(solution)/shard_map/column_sum/pallas_call | solution.py:302
  307.1 6.2 %add_multiply_fusion = f32[1024,768]{1,0:T(8,128)S(1)} fusion(f32[1024,768]{1,0:T(8,128)} %get-tuple-element.117, f32[1024,768]{1,0:T(8,128)} %get-tuple-element.113.step_f.step_r, bf16[1024,128]{1,0:T(8,128)(2,1)S(1)} %bitcast.90, bf16[768,128]{1,0:T(8,128)(2,1)} %get-tuple-element.57, f32[1024,768]{1,0:T(8,128)} %get-tuple-element.70, ...), kind=kOutput, calls=%fused_computation.27 | convolution fusion | flops 209977344 | bytes 16187392 | tf_op jit(solution)/shard_map/dot_general | solution.py:1329
  313.4 4.7 %fusion.37 = (f32[768]{0:T(1024)S(1)}, f32[768]{0:T(1024)S(1)}, f32[768]{0:T(1024)S(1)}, f32[768]{0:T(1024)S(1)}, f32[768]{0:T(1024)S(1)}, /*index=5*/bf16[1024,768]{1,0:T(8,128)(2,1)}) fusion(f32[1024,768]{1,0:T(8,128)S(1)} %add_multiply_fusion, f32[1024]{0:T(1024)S(1)} %copy-done.22, bf16[4,256,768]{2,1,0:T(8,128)(2,1)S(1)} %copy-done.5, ...), kind=kLoop, calls=%fused_computation.99 | loop fusion | flops 15724800 | bytes 9468928 | tf_op jit(solution)/shard_map/reduce_sum | solution.py:1465
  320.2 2.0 fusion.18.gstep
  323.6 3.1 fusion.14
  327.4 92.2 %end.1 = (f32[48,6144]{1,0:T(8,128)}, f32[48,3072]{1,0:T(8,128)}, f32[96,128]{1,0:T(8,128)}, f32[96,96]{1,0:T(8,128)}, f32[16,96]{1,0:T(8,128)}, /*index=5*/f32[...) custom-call(bf16[1024,768]{1,0:T(8,128)(2,1)} %get-tuple-element.120, ...), custom_call_target="tpu_custom_call" | custom-call | tf_op jit(solution)/shard_map/end/pallas_call | solution.py:1279
  422.6 2.1 copy.50
  (150 shorter events, 31.5 us)
Async XLA Ops:
  7.2 180.6 %all-gather.2.cloned.1.call-start = ((), (), s32[]{:S(2)}) async-start(), calls=%async_computation.2 | async-start | bytes 3932160 | tf_op jit(solution)/shard_map/all_gather | solution.py:1410
  108.9 19.2 %copy-start = (bf16[1024,768]{1,0:T(8,128)(2,1)}, bf16[1024,768]{1,0:T(8,128)(2,1)S(1)}, u32[]{:S(2)}) copy-start(bf16[1024,768]{1,0:T(8,128)(2,1)S(1)} %get-tuple-element.116) | copy-start | bytes 4718596
  108.9 17.4 %copy-start.17 = (f32[64,768]{1,0:T(8,128)S(1)}, f32[64,768]{1,0:T(8,128)}, u32[]{:S(2)}) copy-start(f32[64,768]{1,0:T(8,128)} %get-tuple-element.60) | copy-start | bytes 589828
  109.5 18.6 %copy-start.15 = (bf16[96,768]{1,0:T(8,128)(2,1)S(1)}, bf16[96,768]{1,0:T(8,128)(2,1)}, u32[]{:S(2)}) copy-start(bf16[96,768]{1,0:T(8,128)(2,1)} %get-tuple-element.59) | copy-start | bytes 442372
  125.0 10.1 %copy-start.9 = (bf16[1024,128]{0,1:T(8,128)(2,1)}, bf16[1024,128]{0,1:T(8,128)(2,1)S(1)}, u32[]{:S(2)}) copy-start(bf16[1024,128]{0,1:T(8,128)(2,1)S(1)} %copy.36) | copy-start | bytes 786436
  125.0 198.6 %reduce-scatter.3.cloned.1.call-start = ((), (), s32[]{:S(2)}) async-start(), calls=%async_computation.3 | async-start | bytes 3932160 | tf_op jit(solution)/shard_map/reduce_scatter | solution.py:1424
  128.1 7.0 %copy-start.35 = (s32[1024]{0:T(1024)S(1)}, s32[1024]{0:T(1024)}, u32[]{:S(2)}) copy-start(s32[1024]{0:T(1024)} %add_select_fusion) | copy-start | bytes 12292
  128.1 7.0 %copy-start.41 = (s32[256]{0:T(256)S(1)}, s32[256]{0:T(256)}, u32[]{:S(2)}) copy-start(s32[256]{0:T(256)} %and_select_fusion) | copy-start | bytes 3076
  136.4 34.9 %copy-start.6 = (f32[4,256,768]{2,1,0:T(8,128)S(1)}, f32[4,256,768]{2,1,0:T(8,128)}, u32[]{:S(2)}) copy-start(f32[4,256,768]{2,1,0:T(8,128)} %get-tuple-element.63) | copy-start | bytes 9437188
  187.8 139.6 %reduce-scatter.5.cloned.1.call-start = ((), (), s32[]{:S(2)}) async-start(), calls=%async_computation.4 | async-start | bytes 5308416 | tf_op jit(solution)/shard_map/reduce_scatter | solution.py:1440
  194.8 8.1 %copy-start.8 = (bf16[4,256,1536]{2,1,0:T(8,128)(2,1)S(1)}, bf16[4,256,1536]{2,1,0:T(8,128)(2,1)}, u32[]{:S(2)}) copy-start(bf16[4,256,1536]{2,1,0:T(8,128)(2,1)} %get-tuple-element.78) | copy-start | bytes 9437188
  208.3 70.8 %copy-start.1 = (bf16[1024,768]{1,0:T(8,128)(2,1)S(1)}, bf16[1024,768]{1,0:T(8,128)(2,1)}, u32[]{:S(2)}) copy-start(bf16[1024,768]{1,0:T(8,128)(2,1)} %copy-done) | copy-start | bytes 4718596
  208.3 70.8 %copy-start.4 = (f32[1024,768]{1,0:T(8,128)S(1)}, f32[1024,768]{1,0:T(8,128)}, u32[]{:S(2)}) copy-start(f32[1024,768]{1,0:T(8,128)} %get-tuple-element.135) | copy-start | bytes 9437188
  208.3 70.8 %copy-start.34 = (f32[768]{0:T(1024)S(1)}, f32[768]{0:T(1024)}, u32[]{:S(2)}) copy-start(f32[768]{0:T(1024)} %get-tuple-element.101) | copy-start | bytes 9220
  279.2 10.4 %copy-start.20 = (f32[64,256]{1,0:T(8,128)S(1)}, f32[64,256]{1,0:T(8,128)}, u32[]{:S(2)}) copy-start(f32[64,256]{1,0:T(8,128)} %get-tuple-element.74) | copy-start | bytes 196612
  307.1 6.2 %copy-start.3 = (f32[1024,768]{1,0:T(8,128)S(1)}, f32[1024,768]{1,0:T(8,128)}, u32[]{:S(2)}) copy-start(f32[1024,768]{1,0:T(8,128)} %copy-done.2) | copy-start | bytes 9437188
  307.1 6.2 %copy-start.5 = (bf16[4,256,768]{2,1,0:T(8,128)(2,1)S(1)}, bf16[4,256,768]{2,1,0:T(8,128)(2,1)}, u32[]{:S(2)}) copy-start(bf16[4,256,768]{2,1,0:T(8,128)(2,1)} %get-tuple-element.55) | copy-start | bytes 4718596
  419.7 6.6 %copy-start.24 = (f32[96,96]{1,0:T(8,128)S(1)}, f32[96,96]{1,0:T(8,128)}, u32[]{:S(2)}) copy-start(f32[96,96]{1,0:T(8,128)} %get-tuple-element.157) | copy-start | bytes 110596
  419.7 7.2 %copy-start.14 = (f32[48,3072]{1,0:T(8,128)S(1)}, f32[48,3072]{1,0:T(8,128)}, u32[]{:S(2)}) copy-start(f32[48,3072]{1,0:T(8,128)} %get-tuple-element.86) | copy-start | bytes 1769476
  419.7 8.0 %copy-start.37 = (f32[16,96]{1,0:T(8,128)S(1)}, f32[16,96]{1,0:T(8,128)}, u32[]{:S(2)}) copy-start(f32[16,96]{1,0:T(8,128)} %get-tuple-element.87) | copy-start | bytes 18436
  419.7 8.6 %copy-start.36 = (f32[16,96]{1,0:T(8,128)S(1)}, f32[16,96]{1,0:T(8,128)}, u32[]{:S(2)}) copy-start(f32[16,96]{1,0:T(8,128)} %get-tuple-element.88) | copy-start | bytes 18436
  419.7 9.2 %copy-start.40 = (f32[4,96]{1,0:T(4,128)S(1)}, f32[4,96]{1,0:T(4,128)}, u32[]{:S(2)}) copy-start(f32[4,96]{1,0:T(4,128)} %get-tuple-element.161) | copy-start | bytes 4612
  419.7 9.8 %copy-start.43 = (f32[1,96]{1,0:T(1,128)S(1)}, f32[1,96]{1,0:T(1,128)}, u32[]{:S(2)}) copy-start(f32[1,96]{1,0:T(1,128)} %get-tuple-element.90) | copy-start | bytes 1156
  419.7 10.3 %copy-start.42 = (f32[1,96]{1,0:T(1,128)S(1)}, f32[1,96]{1,0:T(1,128)}, u32[]{:S(2)}) copy-start(f32[1,96]{1,0:T(1,128)} %get-tuple-element.91) | copy-start | bytes 1156
  (23 other events, 100.6 us)
Sparse Core Ops, SparseCore 0:
  125.2 62.5 all-gather.1
  190.0 58.8 reduce-scatter.2
  252.4 53.9 reduce-scatter.4

commit v10 on v9

--- a/solution.py
+++ b/solution.py
@@ -186,7 +186,7 @@
             dlog[here, cut] = jnp.dot(onesb, l_ref[:, cut], preferred_element_type=F32)
             a = a_ref[:, cut]
             adjb[here, cut] = jnp.dot(bblk[here, :], a, preferred_element_type=F32)
-            bgd = bgd + lax.dot_general(u[here, cut], a, NT, preferred_element_type=F32)
+            bgd = bgd + lax.dot_general(u[here, cut].astype(BF), a, NT, preferred_element_type=F32)
             cgd = cgd + lax.dot_general(gy[here, cut].astype(BF), s[group, cut], NT, preferred_element_type=F32)
         bg[line, :] = jnp.sum(jnp.where(ones, bgd, zero), axis=0, keepdims=True)
         cg[line, :] = jnp.sum(jnp.where(ones, cgd, zero), axis=0, keepdims=True)
@@ -311,230 +311,39 @@
     return out.reshape(rows, lanes)
 
 
-def mod_gather_kernel(nd, ns, g_ref, o_ref, land, s1, r1, s2, r2):
-    d, q = lax.axis_index("dp"), lax.axis_index("seq")
-    others = [lax.rem(q + k, ns) for k in range(1, ns)]
-    peers = [lax.rem(d + k, nd) for k in range(1, nd)]
-    greet([(d, t) for t in others] + [(e, q) for e in peers])
-    for k, t in enumerate(others):
-        send(g_ref, land.at[q], s1.at[k], r1.at[q], (d, t)).start()
-    total = g_ref[...]
-    for k, t in enumerate(others):
-        send(g_ref, land.at[t], s1.at[k], r1.at[t], (d, t)).wait_recv()
-        total = total + land[t]
-    o_ref[d] = total
-    for k, e in enumerate(peers):
-        send(o_ref.at[d], o_ref.at[d], s2.at[k], r2.at[d], (e, q)).start()
-    for k, e in enumerate(peers):
-        send(o_ref.at[e], o_ref.at[e], s2.at[k], r2.at[e], (e, q)).wait_recv()
-    for k, t in enumerate(others):
-        send(g_ref, land.at[q], s1.at[k], r1.at[q], (d, t)).wait_send()
-    for k, e in enumerate(peers):
-        send(o_ref.at[d], o_ref.at[d], s2.at[k], r2.at[d], (e, q)).wait_send()
-
-
-def mod_gather(g, nd, ns, cid):
-    rows, lanes = g.shape
-    return pl.pallas_call(
-        functools.partial(mod_gather_kernel, nd, ns),
-        out_shape=jax.ShapeDtypeStruct((nd, rows, lanes), F32),
-        in_specs=[VMEM], out_specs=VMEM,
-        scratch_shapes=[pltpu.VMEM((ns, rows, lanes), F32), DMA((ns,)), DMA((ns,)), DMA((nd,)), DMA((nd,))],
+def column_grads_kernel(ns, pre_ref, step_ref, bf_ref, br_ref, cf_ref, cr_ref, o_ref, state_ref, rows_ref, p_ref, *rest):
+    rank = step_ref.shape[0]
+    local = p_ref.shape[1]
+    groups = local // 16
+    rows_ref[...] = jnp.zeros(rows_ref.shape, BF)
+    rows_ref[0:rank, :] = step_ref[...]
+    for t in range(ns):
+        lines = slice(t * groups, (t + 1) * groups)
+        b, c = bf_ref[lines, :] + br_ref[lines, :], cf_ref[lines, :] + cr_ref[lines, :]
+        for l in range(16):
+            here = slice(l * 16, (l + 1) * 16)
+            state_ref[pl.ds(l, groups, stride=16), :] = jnp.concatenate(
+                [jnp.zeros((groups, rank), F32), b[:, here], c[:, here]], axis=1)
+        low = lax.dot_general(pre_ref[t * local:(t + 1) * local, :], rows_ref[...], NT, preferred_element_type=F32)
+        p_ref[t] = (low + state_ref[...]).astype(BF)
+    column_sum_kernel(ns, p_ref, o_ref, *rest)
+
+
+def column_grads(pre, step, b_f, b_r, c_f, c_r, ns, cid):
+    rows, lanes = pre.shape[0], step.shape[0] + 32
+    block = (ns, rows // ns, lanes)
+    out = pl.pallas_call(
+        functools.partial(column_grads_kernel, ns),
+        out_shape=jax.ShapeDtypeStruct(block, BF),
+        in_specs=[VMEM] * 6, out_specs=VMEM,
+        scratch_shapes=[
+            pltpu.VMEM((rows // ns, lanes), F32), pltpu.VMEM((lanes, pre.shape[1]), BF), pltpu.VMEM(block, BF),
+            pltpu.VMEM(block, BF), DMA((ns,)), DMA((ns,)), DMA((ns,)), DMA((ns,))],
         compiler_params=pltpu.CompilerParams(
             collective_id=cid, has_side_effects=True, vmem_limit_bytes=32 * 2**20),
-        name="mod_gather",
-    )(g)
-
-
-def home_kernel(nd, ns, nsub, g_ref, sm_ref, gm_ref, f_ref, so_ref, out_ref,
-                pair, plane, spair, splane, ssum, up, down,
-                sa, ra, sb, rb, sc, rc, ta, ra2, tb, rb2, tc, rc2, su, ru, sd, rd):
-    d, q = lax.axis_index("dp"), lax.axis_index("seq")
-    nc = nd // 2
-    chip, core = d // 2, lax.rem(d, 2)
-    mate = chip * 2 + 1 - core
-    chips = [lax.rem(chip + k, nc) for k in range(1, nc)]
-    others = [lax.rem(q + k, ns) for k in range(1, ns)]
-    spread = nd // ns
-    final_to = (spread * q + d // ns, lax.rem(d, ns))
-    mine = d * ns + q
-    final_from = (lax.rem(mine, nd), mine // nd)
-    stays = jnp.logical_and(final_to[0] == d, final_to[1] == q)
-    bar = pltpu.get_barrier_semaphore()
-    friends = [(mate, q)] + [(c * 2 + core, q) for c in chips] + [(d, t) for t in others]
-    for to in friends:
-        pl.semaphore_signal(bar, inc=1, device_id=to, device_id_type=MESH)
-    @pl.when(jnp.logical_not(stays))
-    def _():
-        pl.semaphore_signal(bar, inc=1, device_id=final_from, device_id_type=MESH)
-        pl.semaphore_wait(bar, len(friends) + 1)
-    @pl.when(stays)
-    def _():
-        pl.semaphore_wait(bar, len(friends))
-
-    def first(c):
-        return send(g_ref.at[c * 2 + 1 - core], pair.at[c], sa.at[c], ra.at[c], (mate, q))
-
-    def first_small(c):
-        return send(sm_ref.at[c * 2 + 1 - core], spair.at[c], ta.at[c], ra2.at[c], (mate, q))
-
-    order = chips + [chip]
-    for c in order:
-        first(c).start()
-        first_small(c).start()
-
-    def rise(t, s, src):
-        return send(src, up.at[t, s], su.at[t, s], ru.at[t, s], (d, q + 1))
-
-    def sink(t, s, src):
-        return send(src, down.at[t, s], sd.at[t, s], rd.at[t, s], (d, q - 1))
-
-    def added(land, t, s):
-        land[t, s] = (land[t, s].astype(F32) + gm_ref[t, s].astype(F32)).astype(BF)
-
-    def step_up(t, s):
-        @pl.when(q < t)
-        def _():
-            @pl.when(q == 0)
-            def _():
-                rise(t, s, gm_ref.at[t, s]).start()
-            @pl.when(q > 0)
-            def _():
-                rise(t, s, up.at[t, s]).wait_recv()
-                added(up, t, s)
-                rise(t, s, up.at[t, s]).start()
-
-    def step_down(t, s):
-        @pl.when(q > t)
-        def _():
-            @pl.when(q == ns - 1)
-            def _():
-                sink(t, s, gm_ref.at[t, s]).start()
-            @pl.when(q < ns - 1)
-            def _():
-                sink(t, s, down.at[t, s]).wait_recv()
-                added(down, t, s)
-                sink(t, s, down.at[t, s]).start()
-
-    steps = [(k, s) for k in range(ns - 1) for s in range(nsub)]
-    middle = len(steps) * 2 // 3
-
-    def walk(some):
-        for k, s in some:
-            step_up(ns - 1 - k, s)
-            step_down(k, s)
-
-    def second(c, src):
-        return send(pair.at[c], plane.at[src], sb.at[c], rb.at[src], (c * 2 + core, q))
-
-    def second_small(c, src):
-        return send(spair.at[c], splane.at[src], tb.at[c], rb2.at[src], (c * 2 + core, q))
-
-    walk(steps[:1])
-    for c in order:
-        first(c).wait_recv()
-        @pl.loop(0, ns)
-        def _(t):
-            pair[c, t] = (pair[c, t].astype(F32) + g_ref[c * 2 + core, t].astype(F32)).astype(BF)
-        first_small(c).wait_recv()
-        spair[c] = spair[c] + sm_ref[c * 2 + core]
-        if c is not chip:
-            second(c, chip).start()
-            second_small(c, chip).start()
-    walk(steps[1:middle])
-
-    for c in chips:
-        second(c, c).wait_recv()
-        second_small(c, c).wait_recv()
-    @pl.loop(0, ns)
-    def _(t):
-        total = pair[chip, t].astype(F32)
-        for c in chips:
-            total = total + plane[c, t].astype(F32)
-        pair[chip, t] = total.astype(BF)
-    small = spair[chip]
-    for c in chips:
-        small = small + splane[c]
-    ssum[...] = small
-
-    def third(t, src):
-        return send(pair.at[chip, t], f_ref.at[src], sc.at[t], rc.at[src], (d, t))
-
-    last = send(ssum, so_ref, tc, rc2, final_to)
-    @pl.when(stays)
-    def _():
-        so_ref[...] = ssum[...]
-    @pl.when(jnp.logical_not(stays))
-    def _():
-        last.start()
-    for t in others:
-        third(t, q).start()
-    f_ref[q] = pair[chip, q]
-    walk(steps[middle:])
-
-    for s in range(nsub):
-        total = gm_ref[q, s].astype(F32)
-        out_ref[s] = total
-        @pl.when(q > 0)
-        def _():
-            rise(q, s, gm_ref.at[q, s]).wait_recv()
-            out_ref[s] += up[q, s].astype(F32)
-        @pl.when(q < ns - 1)
-        def _():
-            sink(q, s, gm_ref.at[q, s]).wait_recv()
-            out_ref[s] += down[q, s].astype(F32)
-    for t in others:
-        third(t, t).wait_recv()
-    @pl.when(jnp.logical_not(stays))
-    def _():
-        last.wait_recv()
-        last.wait_send()
-    for c in order:
-        first(c).wait_send()
-        first_small(c).wait_send()
-    for c in chips:
-        second(c, chip).wait_send()
-        second_small(c, chip).wait_send()
-    for t in others:
-        third(t, q).wait_send()
-    for k, s in steps:
-        t = ns - 1 - k
-        @pl.when(q < t)
-        def _():
-            rise(t, s, gm_ref.at[t, s]).wait_send()
-        @pl.when(q > k)
-        def _():
-            sink(k, s, gm_ref.at[k, s]).wait_send()
-
-
-def home(g, small, gm, nd, ns, cid):
-    rows, cols = g.shape[2:]
-    nc, nsub = nd // 2, 4
-    length, width = gm.shape
-    part = length // ns // nsub
-    v = small.shape[1:]
-    gm = gm.reshape(ns, nsub, part, width)
-    f, so, out = pl.pallas_call(
-        functools.partial(home_kernel, nd, ns, nsub),
-        out_shape=[
-            jax.ShapeDtypeStruct((ns, rows, cols), BF),
-            jax.ShapeDtypeStruct(v, F32),
-            jax.ShapeDtypeStruct((nsub, part, width), F32),
-        ],
-        in_specs=[VMEM] * 3, out_specs=[VMEM] * 3,
-        scratch_shapes=[
-            pltpu.VMEM((nc, ns, rows, cols), BF), pltpu.VMEM((nc, ns, rows, cols), BF),
-            pltpu.VMEM((nc,) + v, F32), pltpu.VMEM((nc,) + v, F32), pltpu.VMEM(v, F32),
-            pltpu.VMEM((ns, nsub, part, width), BF), pltpu.VMEM((ns, nsub, part, width), BF),
-            DMA((nc,)), DMA((nc,)), DMA((nc,)), DMA((nc,)), DMA((ns,)), DMA((ns,)),
-            DMA((nc,)), DMA((nc,)), DMA((nc,)), DMA((nc,)), DMA(()), DMA(()),
-            DMA((ns, nsub)), DMA((ns, nsub)), DMA((ns, nsub)), DMA((ns, nsub)),
-        ],
-        compiler_params=pltpu.CompilerParams(
-            collective_id=cid, has_side_effects=True, vmem_limit_bytes=56 * 2**20),
-        name="home",
-    )(g, small, gm)
-    return f, so, out.reshape(length // ns, width)
+        name="column_grads",
+    )(pre, step, b_f, b_r, c_f, c_r)
+    return out.reshape(rows, lanes)
 
 
 def start_kernel(nd, ns, nsub, fused, hid, win, wout, mask, emb, modw, modb, select, step, dec_f, dec_r, taps, fbias, sbias,
@@ -950,11 +759,12 @@
     )(hidden, win, wout, mask, embedded, modw, modb, *small)
 
 
-def end_kernel(nd, ns, nsub, rows, turned,
-               gi_h, gg_h, md_h, nm_h, wx_h, gsel, gstep, gdf, gdr, gfil, hid_ref, cot_ref, line_ref, early,
-               gin_o, gout_o, sel_o, step_o, df_o, dr_o, taps_o, fb_o, sb_o, gh_o, mod_o,
+def end_kernel(nd, ns, nsub, rows, turned, nfil,
+               gi_h, gg_h, md_h, nm_h, wx_h, gsel, gstep, gdf, gdr, rates, hid_ref, cot_ref, mod_ref, gate_ref, emb_ref, early, *rest):
+    gfil = rest[:nfil]
+    (gin_o, gout_o, sel_o, step_o, df_o, dr_o, taps_o, fb_o, sb_o, gh_o, mod_o,
                gp, md, nm, wx, sm_ref, so_ref, gm, made, pair, plane, spair, splane, ssum, fro, ready, up, down, own, acc, msg, mland,
-               ld, sa, ra, sb, rb, sc, rc, se, re, ta, ra2, tb, rb2, tc, rc2, su, ru, sd, rd, s1, r1, s2, r2):
+               ld, sa, ra, sb, rb, sc, rc, se, re, ta, ra2, tb, rb2, tc, rc2, su, ru, sd, rd, s1, r1, s2, r2) = rest[nfil:]
     d, q = lax.axis_index("dp"), lax.axis_index("seq")
     nc = nd // 2
     chip, core = d // 2, lax.rem(d, 2)
@@ -1062,7 +872,8 @@
     for copy in loads[:4]:
         copy.wait()
     acc[...] = jnp.zeros(acc.shape, F32)
-    acc[2:4, :] = line_ref[1:3, :]
+    acc[2:3, :] = jnp.sum(gate_ref[...], axis=0, keepdims=True)
+    acc[3:4, 0:FREQ] = emb_ref[...].astype(F32) * (1.0 / ns)
     far(0)
     steps = [(k, s) for k in range(ns - 1) for s in range(nsub)]
 
@@ -1097,9 +908,10 @@
         here = slice(j * units, (j + 1) * units)
         sm_ref[j, 0:units, :] = gsel[here, :]
         sm_ref[j, above:above + rank, 0:units] = gstep[:, here]
-        sm_ref[j, above + rank:above + rank + states, 0:units] = gdf[:, here]
-        sm_ref[j, above + rank + states:taps_at, 0:units] = gdr[:, here]
-        sm_ref[j, taps_at:taps_at + 8, 0:units] = gfil[:, here]
+        sm_ref[j, above + rank:above + rank + states, 0:units] = gdf[:, here] * rates[0:states, here]
+        sm_ref[j, above + rank + states:taps_at, 0:units] = gdr[:, here] * rates[states:2 * states, here]
+        for i, line in enumerate(gfil):
+            sm_ref[j, taps_at + i:taps_at + i + 1, 0:units] = jnp.sum(line[:, here], axis=0, keepdims=True)
 
     loads[4].wait()
     order = chips + [chip]
@@ -1176,7 +988,7 @@
     mod_o[d] = total
     for k, e in enumerate(peers):
         send(mod_o.at[d], mod_o.at[d], s2.at[k], r2.at[d], (e, q)).start()
-    scale = 1.0 + line_ref[0:1, :]
+    scale = 1.0 + mod_ref[0:1, width:2 * width]
     for s in range(nsub):
         own[...] = gm[q, s].astype(F32)
 
@@ -1252,7 +1064,7 @@
             sink(k, s, gm.at[k, s]).wait_send()
 
 
-def end(grad_inner, grad_gate, modded, normed, wx, early, small, taps, hidden, cot, line, rows, nd, ns, cid):
+def end(grad_inner, grad_gate, modded, normed, wx, early, small, fil, hidden, cot, modulation, grad_gate_scale, embedded, rows, nd, ns, cid):
     length, part = grad_inner.shape
     cols = 2 * part
     width = wx.shape[0]
@@ -1277,7 +1089,7 @@
     smalls = pltpu.VMEM((nc,) + v, F32)
     runs = pltpu.VMEM((ns, nsub, sub, width), BF)
     gin, gout, *own, gh, mod = pl.pallas_call(
-        functools.partial(end_kernel, nd, ns, nsub, rows, turned),
+        functools.partial(end_kernel, nd, ns, nsub, rows, turned, len(fil)),
         out_shape=[
             jax.ShapeDtypeStruct((rows, 2 * inner), F32),
             jax.ShapeDtypeStruct((rows, inner), F32),
@@ -1285,13 +1097,13 @@
             jax.ShapeDtypeStruct((rank, units), F32),
             jax.ShapeDtypeStruct((states, units), F32),
             jax.ShapeDtypeStruct((states, units), F32),
-            jax.ShapeDtypeStruct((taps, units), F32),
+            jax.ShapeDtypeStruct((len(fil) - 2, units), F32),
             jax.ShapeDtypeStruct((1, units), F32),
             jax.ShapeDtypeStruct((1, units), F32),
             jax.ShapeDtypeStruct((nsub, sub, width), BF),
             jax.ShapeDtypeStruct((nd, 8, short), F32),
         ],
-        in_specs=[HBM] * 5 + [VMEM] * 9, out_specs=[VMEM] * 11,
+        in_specs=[HBM] * 5 + [VMEM] * (11 + len(fil)), out_specs=[VMEM] * 11,
         scratch_shapes=[
             pltpu.VMEM((length, cols), BF), pltpu.VMEM(modded.shape, BF), pltpu.VMEM(normed.shape, BF),
             pltpu.VMEM((width, cols), BF),
@@ -1309,7 +1121,7 @@
         compiler_params=pltpu.CompilerParams(
             collective_id=cid, has_side_effects=True, vmem_limit_bytes=60 * 2**20),
         name="end",
-    )(grad_inner, grad_gate, modded, normed, wx, *small, hidden, cot, line, early)
+    )(grad_inner, grad_gate, modded, normed, wx, *small, hidden, cot, modulation, grad_gate_scale, embedded, early, *fil)
     return gin, gout, own, gh.reshape(local, width), mod
 
 
@@ -1331,6 +1143,10 @@
 
 def dot_tn(a, b):
     return lax.dot_general(a, b, (((0,), (0,)), ((), ())), preferred_element_type=F32)
+
+
+def by_eight(a):
+    return jnp.sum(a.reshape(-1, 8, a.shape[1]), axis=0)
 
 
 def body(
@@ -1378,7 +1194,7 @@
     win, wout = wx[:, : 2 * part], wx[:, 2 * part :]
     mask = mask[:, : local_len // 128].reshape(length, 1).astype(F32)
     rates_f, rates_r, rates_f2, rates_r2 = [rates[k * state : (k + 1) * state] for k in range(4)]
-    modulation = modulation[:1]
+    modulation_rows, modulation = modulation, modulation[:1]
     shifts = modulation[:, :width]
     scales = modulation[:, width : 2 * width]
     gate_scale = modulation[:, 2 * width :]
@@ -1426,7 +1242,7 @@
     mask_here = pad_mask[0].astype(F32)[:, None]
     cot_here = cotangent[0].astype(F32)
     block_out = (hidden[0].astype(F32) + gate_scale * mask_here * branch).astype(BF)
-    grad_gate = jnp.sum(mask_here * cot_here * branch, axis=0)
+    grad_gate = by_eight(mask_here * cot_here * branch)
 
     grad_branch = lax.optimization_barrier((cot.astype(F32) * gate_scale * mask).astype(BF))
     grad_gated = dot(grad_branch, wout)
@@ -1439,19 +1255,14 @@
         with_layout_constraint(dot_tn(grad_branch, gated).astype(BF), rows_first)], axis=1)
     early = lax.psum_scatter(early, "dp", scatter_dimension=0, tiled=True)
     dlog_f, dlog_r, adjb_f, adjb_r, bg_f, bg_r, cg_f, cg_r, rg_f, rg_r = bwd_scan(
-        steps, drive.astype(BF), grad_merged, rates_f2, rates_r2, c_rows.T, blockdiag(b_rows), states_f, states_r)
+        steps, drive, grad_merged, rates_f2, rates_r2, c_rows.T, blockdiag(b_rows), states_f, states_r)
     adjb = adjb_f + adjb_r
     grad_steps = (dlog_f + dlog_r) * (1.0 / LOG2E) + active32 * adjb
-    grad_b = (bg_f + bg_r).reshape(length, state)
-    grad_c = (cg_f + cg_r).reshape(length, state)
-    grad_decay_f = rg_f * rates_f
-    grad_decay_r = rg_r * rates_r
-    grad_pre = grad_steps * jax.nn.sigmoid(pre_steps)
-    grad_step_bias = jnp.sum(grad_pre, axis=0)
+    grad_pre = grad_steps * -jnp.expm1(-steps)
+    grad_step_bias = jnp.sum(grad_pre, axis=0, keepdims=True)
     grad_pre_low = grad_pre.astype(BF)
     grad_step = dot_tn(low_rank, grad_pre_low)
-    grad_low_rank = dot_nt(grad_pre_low, step_q)
-    grad_selected = column_sum(jnp.concatenate([grad_low_rank, grad_b, grad_c], axis=1).astype(BF), ns, BF, 1)
+    grad_selected = column_grads(grad_pre_low, step_q, bg_f, bg_r, cg_f, cg_r, ns, 1)
     grad_select = dot_tn(active, grad_selected)
     grad_active = steps * adjb + dot_nt(grad_selected, select_q)
     grad_filtered = grad_active * sigma_filter * (1.0 + filtered * (1.0 - sigma_filter))
@@ -1461,15 +1272,13 @@
     for k in range(taps):
         lead = taps - 1 - k
         grad_inner = grad_inner + fil[k][None] * extended[lead : lead + length]
-        filter_rows.append(jnp.sum(grad_filtered * padded[k : k + length], axis=0))
-    grad_filter_bias = jnp.sum(grad_filtered, axis=0)
+        filter_rows.append(by_eight(grad_filtered * padded[k : k + length]))
+    grad_filter_bias = by_eight(grad_filtered)
     grad_inner = (grad_inner * mask).astype(BF)
-    grad_fil = jnp.stack(filter_rows + [grad_filter_bias, grad_step_bias])
-    grad_fil = jnp.pad(grad_fil, ((0, 8 - grad_fil.shape[0]), (0, 0)))
-    line = jnp.concatenate([scales, grad_gate[None], jnp.pad(embedded.astype(F32) / ns, ((0, 0), (0, width - FREQ))),
-                            jnp.zeros((5, width), F32)])
     g_in, g_out, own, grad_hidden, sums = end(
-        grad_inner, grad_gate_branch, modded, normed, wx, early, (grad_select, grad_step, grad_decay_f, grad_decay_r, grad_fil), taps, hidden[0], cotangent[0], line, rows_in, nd, ns, 2)
+        grad_inner, grad_gate_branch, modded, normed, wx, early, (grad_select, grad_step, rg_f, rg_r, rates),
+        filter_rows + [grad_filter_bias, grad_step_bias], hidden[0], cotangent[0], modulation_rows, grad_gate, embedded,
+        rows_in, nd, ns, 2)
     gs_select, gs_step, gs_f, gs_r, gs_taps, gs_fbias, gs_sbias = own
     sums = sums.reshape(nd, -1)
     embeds = sums[:, 3 * width : 3 * width + FREQ]

time: 446 us -> 434 us (0.973)
  matrix products: 37.9 us -> 32.2 us
  other arithmetic: 39.8 us -> 34.7 us
    pallas_call x1 -> x2, Pallas kernels: 92.2 us -> 107 us  [the longest x1 92.4 us: end(): pl.pallas_call(functools.partial(end_kernel, nd, ns, nsub, rows, turned,...]
    pallas_call x2 -> x1, Pallas kernels: 29.7 us -> 15.4 us  [column_sum(): pl.pallas_call(functools.partial(column_sum_kernel, ns), out_shape=jax.Sh...]
    reduce_sum x3 -> x2, other arithmetic: 13.9 us -> 8.89 us  [the longest x1 6.81 us: body(): grad_step_bias = jnp.sum(grad_pre, axis=0, keepdims=True)]
    dot_general x3 -> x2, matrix products: 13.1 us -> 9.77 us  [dot_nt(): lax.dot_general(a, b, (((1,), (1,)), ((), ())), preferred_element_type=F32)]
    unnamed x99 -> x111, local copies, waits for them, and re-layouts: 12 us -> 12.1 us
  transfers between devices with their start and end apart: 3 -> 3, of which waited for: 1 -> 1; matrix products, arithmetic and copies ran while one was open for 17% -> 14% of each run, Pallas kernels for 27% -> 28%
where the time goes in v10:
time: 434 us; the launch traced here: 426 us
  Pallas kernels  320 us (74%)
  other arithmetic  34.7 us (8%)
  matrix products  32.2 us (7%)
  local copies, waits for them, and re-layouts  17.8 us (4%)
  between operations  15.3 us (4%)
  waiting for transfers between devices  5.3 us (1%)
    pallas_call x1, Pallas kernels, end(): pl.pallas_call(functools.partial(end_kernel, nd, ns, nsub, rows, turned,...  92.4 us
    pallas_call x1, Pallas kernels, start(): pl.pallas_call(functools.partial(start_kernel, nd, ns, nsub, fused), out_...  91.5 us
    pallas_call x1, Pallas kernels, bwd_scan(): pl.pallas_call(bwd_kernel, grid=(blocks,), in_specs=[row_f, row_r, row_f,...  71.4 us
    pallas_call x1, Pallas kernels, fwd_scan(): pl.pallas_call(fwd_kernel, grid=(blocks,), in_specs=[row_f, row_r, row_f,...  34.9 us
    pallas_call x1, Pallas kernels, column_sum(): pl.pallas_call(functools.partial(column_sum_kernel, ns), out_shape=jax.Sh...  15.4 us
    pallas_call x1, Pallas kernels, column_grads(): pl.pallas_call(functools.partial(column_grads_kernel, ns), out_shape=jax....  14.9 us
    dot_general x3, matrix products, dot(): return jnp.dot(a, b, preferred_element_type=F32)  13 us
    unnamed x111, local copies, waits for them, and re-layouts  12.1 us
  transfers between devices with their start and end apart: 3, of which 1 were waited for; matrix products, arithmetic and copies ran while one was open for 14% of the time, Pallas kernels for 28%

profile of v10, /device:TPU:0, one launch (start us, length us, event | category | flops | bytes accessed | tf_op | source)
XLA Modules:
  0.0 426.3 jit_solution(8223943983013634206)
XLA Ops:
  9.9 91.5 %start.1 = (bf16[4,256,1536]{2,1,0:T(8,128)(2,1)}, bf16[4,256,1536]{2,1,0:T(8,128)(2,1)}, bf16[4,256,768]{2,1,0:T(8,128)(2,1)}, f32[4,256,768]{2,1,0:T(8,128)}, ...) custom-call(bf16[4,64,1536]{2,1,0:T(8,128)(2,1)} %bitcast.105, ...), custom_call_target="tpu_custom_call" | custom-call | tf_op jit(solution)/shard_map/start/pallas_call | solution.py:727
  101.4 1.7 slice_reduce_fusion.7
  103.8 1.8 convert_multiply_fusion.2
  105.6 3.2 multiply_convert_fusion.3
  109.5 15.4 %column_sum.1 = bf16[4,256,128]{2,1,0:T(8,128)(2,1)S(1)} custom-call(bf16[4,256,128]{2,1,0:T(8,128)(2,1)S(1)} %bitcast.104), custom_call_target="tpu_custom_call" | custom-call | tf_op jit(solution)/shard_map/column_sum/pallas_call | solution.py:302
  128.2 5.5 %convert_multiply_fusion.1 = (f32[1024,768]{1,0:T(8,128)}, f32[1024,768]{1,0:T(8,128)}) fusion(bf16[1024,768]{1,0:T(8,128)(2,1)S(1)} %get-tuple-element.111, f32[768]{0:T(1024)} %get-tuple-element.102, bf16[96,768]{1,0:T(8,128)(2,1)S(1)} %copy-done, bf16[1024,128]{0,1:T(8,128)(2,1)S(1)} %copy.34), kind=kOutput, calls=%fused_computation.4 | convolution fusion | flops 158072832 | bytes 8211456 | tf_op jit(solution)/shard_map/dot_general | solution.py:1137
  135.0 34.9 %fwd_scan.1 = (f32[1024,768]{1,0:T(8,128)}, f32[1024,768]{1,0:T(8,128)}, bf16[16384,768]{1,0:T(8,128)(2,1)}, bf16[16384,768]{1,0:T(8,128)(2,1)}) custom-call(f32[1024,768]{1,0:T(8,128)} %get-tuple-element.124.step_f.step_r, f32[1024,768]{1,0:T(8,128)} %get-tuple-element.124.step_f.step_r, f32[1024,768]{1,0:T(8,128)} %get-tuple-element.123.u_f.u_r, ...), custom_call_target="tpu_custom_call" | custom-call | flops 40265318400 | bytes 62914560 | tf_op jit(solution)/shard_map/fwd_scan/pallas_call | solution.py:104
  169.9 5.8 %multiply_convert_fusion.2 = (bf16[1024,768]{1,0:T(8,128)(2,1)S(1)}, f32[1024,768]{1,0:T(8,128)}) fusion(f32[4,256,768]{2,1,0:T(8,128)S(1)} %copy-done.13, f32[1024,768]{1,0:T(8,128)} %get-tuple-element.61, f32[1024,768]{1,0:T(8,128)} %get-tuple-element.62), kind=kLoop, calls=%fused_computation.29 | loop fusion | flops 5505024 | bytes 14155776 | tf_op jit(solution)/shard_map/convert_element_type | solution.py:1237
  176.8 5.7 %convolution_convert_fusion = bf16[1024,1536]{1,0:T(8,128)(2,1)} fusion(bf16[1024,768]{1,0:T(8,128)(2,1)S(1)} %get-tuple-element.109, bf16[1536,2304]{1,0:T(8,128)(2,1)} %get-tuple-element.64.wx_h), kind=kOutput, calls=%fused_computation.5 | convolution fusion | flops 2417491968 | bytes 7077888 | tf_op jit(solution)/shard_map/dot_general | solution.py:1141
  182.5 5.2 %all-gather.2.cloned.1.call-done = bf16[1024,1536]{1,0:T(8,128)(2,1)} async-done(((bf16[256,1536]{1,0:T(8,128)(2,1)}), bf16[1024,1536]{1,0:T(8,128)(2,1)}) %all-gather.2.cloned.1.call-update) | async-done | bytes 3145744 | tf_op jit(solution)/shard_map/all_gather | solution.py:1226
  189.1 2.8 multiply_convert_fusion
  191.9 3.0 convolution_convert_fusion.1
  194.9 6.9 %fusion.7 = (bf16[1024,768]{1,0:T(8,128)(2,1)S(1)}, f32[1024,768]{1,0:T(8,128)}) fusion(f32[4,256,768]{2,1,0:T(8,128)S(1)} %copy-done.13, f32[1024,768]{1,0:T(8,128)S(1)} %copy-done.14, bf16[1024,1536]{1,0:T(8,128)(2,1)S(1)} %multiply_convert_fusion, bf16[1536,2304]{1,0:T(8,128)(2,1)} %get-tuple-element.64.wx_h), kind=kOutput, calls=%fused_computation.24 | convolution fusion | flops 2425356288 | bytes 16515072 | tf_op jit(solution)/shard_map/dot_general | solution.py:1137
  202.9 2.9 convolution_convert_fusion.2
  205.8 2.5 pad_maximum_fusion
  208.4 71.4 %bwd_scan.1 = (f32[1024,768]{1,0:T(8,128)}, f32[1024,768]{1,0:T(8,128)}, f32[1024,768]{1,0:T(8,128)}, f32[1024,768]{1,0:T(8,128)}, f32[64,256]{1,0:T(8,128)}, /*...) custom-call(f32[1024,768]{1,0:T(8,128)} %get-tuple-element.124.step_f.ste, ...), custom_call_target="tpu_custom_call" | custom-call | flops 85563801600 | bytes 78643200 | tf_op jit(solution)/shard_map/bwd_scan/pallas_call | solution.py:242
  279.9 6.8 %fusion.33 = (f32[768]{0:T(1024)S(1)}, bf16[1024,768]{1,0:T(8,128)(2,1)S(1)}) fusion(f32[1024,768]{1,0:T(8,128)S(1)} %copy-done.12, f32[1024,768]{1,0:T(8,128)} %get-tuple-element.70, f32[1024,768]{1,0:T(8,128)} %get-tuple-element.71, bf16[1024,768]{1,0:T(8,128)(2,1)S(1)} %copy-done.6, f32[1024,768]{1,0:T(8,128)} %get-tuple-element.72, ...), kind=kLoop, calls=%fused_computation.86 | loop fusion | flops 8649984 | bytes 18877440 | tf_op jit(solution)/shard_map/reduce_sum | solution.py:1262
  287.3 14.9 %column_grads.1 = bf16[4,256,128]{2,1,0:T(8,128)(2,1)S(1)} custom-call(bf16[1024,768]{1,0:T(8,128)(2,1)S(1)} %get-tuple-element.108.pre_ref, bf16[96,768]{1,0:T(8,128)(2,1)S(1)} %copy-done, f32[64,256]{1,0:T(8,128)S(1)} %copy-done.1, f32[64,256]{1,0:T(8,128)S(1)} %copy-done.2, f32[64,256]{1,0:T(8,128)S(1)} %copy-done.3, f32[64,256]{1,0:T(8,128)S(1)} %copy-done.4), custom_call_target="tpu_custom_call" | custom-call | tf_op jit(solution)/shard_map/column_grads/pallas_call | solution.py:335
  304.8 4.1 bitcast_reduce_fusion
  308.9 2.9 multiply_convert_fusion.1.gi_h
  311.8 2.1 fusion.15.gate_ref
  313.9 2.4 fusion.18
  316.3 92.4 %end.1 = (f32[48,6144]{1,0:T(8,128)}, f32[48,3072]{1,0:T(8,128)}, f32[96,128]{1,0:T(8,128)}, f32[96,96]{1,0:T(8,128)}, f32[16,96]{1,0:T(8,128)}, /*index=5*/f32[...) custom-call(bf16[1024,768]{1,0:T(8,128)(2,1)} %multiply_convert_fusi, ...), custom_call_target="tpu_custom_call" | custom-call | tf_op jit(solution)/shard_map/end/pallas_call | solution.py:1091
  411.6 2.1 copy.48
  (144 shorter events, 23.2 us)
Async XLA Ops:
  7.2 180.6 %all-gather.2.cloned.1.call-start = ((), (), s32[]{:S(2)}) async-start(), calls=%async_computation.2 | async-start | bytes 3932160 | tf_op jit(solution)/shard_map/all_gather | solution.py:1226
  108.9 19.3 %copy-start.5 = (bf16[1024,768]{1,0:T(8,128)(2,1)}, bf16[1024,768]{1,0:T(8,128)(2,1)S(1)}, u32[]{:S(2)}) copy-start(bf16[1024,768]{1,0:T(8,128)(2,1)S(1)} %get-tuple-element.111) | copy-start | bytes 4718596
  108.9 17.4 %copy-start.26 = (f32[64,768]{1,0:T(8,128)S(1)}, f32[64,768]{1,0:T(8,128)}, u32[]{:S(2)}) copy-start(f32[64,768]{1,0:T(8,128)} %get-tuple-element.60.rates) | copy-start | bytes 589828
  109.5 18.7 %copy-start = (bf16[96,768]{1,0:T(8,128)(2,1)S(1)}, bf16[96,768]{1,0:T(8,128)(2,1)}, u32[]{:S(2)}) copy-start(bf16[96,768]{1,0:T(8,128)(2,1)} %get-tuple-element.59.step_ref) | copy-start | bytes 442372
  125.1 8.7 %copy-start.23 = (bf16[1024,128]{0,1:T(8,128)(2,1)}, bf16[1024,128]{0,1:T(8,128)(2,1)S(1)}, u32[]{:S(2)}) copy-start(bf16[1024,128]{0,1:T(8,128)(2,1)S(1)} %copy.34) | copy-start | bytes 786436
  125.1 186.7 %reduce-scatter.3.cloned.1.call-start = ((), (), s32[]{:S(2)}) async-start(), calls=%async_computation.3 | async-start | bytes 3932160 | tf_op jit(solution)/shard_map/reduce_scatter | solution.py:1240
  135.0 34.9 %copy-start.13 = (f32[4,256,768]{2,1,0:T(8,128)S(1)}, f32[4,256,768]{2,1,0:T(8,128)}, u32[]{:S(2)}) copy-start(f32[4,256,768]{2,1,0:T(8,128)} %get-tuple-element.63) | copy-start | bytes 9437188
  187.8 128.5 %reduce-scatter.5.cloned.1.call-start = ((), (), s32[]{:S(2)}) async-start(), calls=%async_computation.4 | async-start | bytes 5308416 | tf_op jit(solution)/shard_map/reduce_scatter | solution.py:1256
  194.9 8.0 %copy-start.17 = (bf16[4,256,1536]{2,1,0:T(8,128)(2,1)S(1)}, bf16[4,256,1536]{2,1,0:T(8,128)(2,1)}, u32[]{:S(2)}) copy-start(bf16[4,256,1536]{2,1,0:T(8,128)(2,1)} %get-tuple-element.78) | copy-start | bytes 9437188
  208.3 71.4 %copy-start.6 = (bf16[1024,768]{1,0:T(8,128)(2,1)S(1)}, bf16[1024,768]{1,0:T(8,128)(2,1)}, u32[]{:S(2)}) copy-start(bf16[1024,768]{1,0:T(8,128)(2,1)} %copy-done.5) | copy-start | bytes 4718596
  208.4 71.4 %copy-start.12 = (f32[1024,768]{1,0:T(8,128)S(1)}, f32[1024,768]{1,0:T(8,128)}, u32[]{:S(2)}) copy-start(f32[1024,768]{1,0:T(8,128)} %get-tuple-element.124.step_f.step_r) | copy-start | bytes 9437188
  279.8 7.5 %copy-start.1 = (f32[64,256]{1,0:T(8,128)S(1)}, f32[64,256]{1,0:T(8,128)}, u32[]{:S(2)}) copy-start(f32[64,256]{1,0:T(8,128)} %get-tuple-element.74.bf_ref) | copy-start | bytes 196612
  279.9 22.4 %copy-start.24 = (bf16[1024,128]{0,1:T(8,128)(2,1)S(1)}, bf16[1024,128]{0,1:T(8,128)(2,1)}, u32[]{:S(2)}) copy-start(bf16[1024,128]{0,1:T(8,128)(2,1)} %copy-done.23) | copy-start | bytes 786436
  279.9 24.9 %copy-start.15 = (f32[1024,768]{1,0:T(8,128)S(1)}, f32[1024,768]{1,0:T(8,128)}, u32[]{:S(2)}) copy-start(f32[1024,768]{1,0:T(8,128)} %get-tuple-element.70) | copy-start | bytes 9437188
  279.9 24.8 %copy-start.16 = (f32[1024,768]{1,0:T(8,128)S(1)}, f32[1024,768]{1,0:T(8,128)}, u32[]{:S(2)}) copy-start(f32[1024,768]{1,0:T(8,128)} %get-tuple-element.71) | copy-start | bytes 9437188
  279.9 24.8 %copy-start.21 = (bf16[4,256,768]{2,1,0:T(8,128)(2,1)S(1)}, bf16[4,256,768]{2,1,0:T(8,128)(2,1)}, u32[]{:S(2)}) copy-start(bf16[4,256,768]{2,1,0:T(8,128)(2,1)} %get-tuple-element.55) | copy-start | bytes 4718596
  287.3 17.4 %copy-start.8 = (f32[1024,768]{1,0:T(8,128)S(1)}, f32[1024,768]{1,0:T(8,128)}, u32[]{:S(2)}) copy-start(f32[1024,768]{1,0:T(8,128)} %copy-done.7) | copy-start | bytes 9437188
  287.3 17.4 %copy-start.11 = (f32[1024,768]{1,0:T(8,128)S(1)}, f32[1024,768]{1,0:T(8,128)}, u32[]{:S(2)}) copy-start(f32[1024,768]{1,0:T(8,128)} %get-tuple-element.112) | copy-start | bytes 9437188
  287.3 17.4 %copy-start.28 = (bf16[768,128]{1,0:T(8,128)(2,1)S(1)}, bf16[768,128]{1,0:T(8,128)(2,1)}, u32[]{:S(2)}) copy-start(bf16[768,128]{1,0:T(8,128)(2,1)} %get-tuple-element.57) | copy-start | bytes 589828
  408.7 8.0 %copy-start.44 = (f32[16,96]{1,0:T(8,128)S(1)}, f32[16,96]{1,0:T(8,128)}, u32[]{:S(2)}) copy-start(f32[16,96]{1,0:T(8,128)} %get-tuple-element.87) | copy-start | bytes 18436
  408.7 8.6 %copy-start.43 = (f32[16,96]{1,0:T(8,128)S(1)}, f32[16,96]{1,0:T(8,128)}, u32[]{:S(2)}) copy-start(f32[16,96]{1,0:T(8,128)} %get-tuple-element.88) | copy-start | bytes 18436
  408.7 9.2 %copy-start.46 = (f32[4,96]{1,0:T(4,128)S(1)}, f32[4,96]{1,0:T(4,128)}, u32[]{:S(2)}) copy-start(f32[4,96]{1,0:T(4,128)} %get-tuple-element.151) | copy-start | bytes 4612
  408.7 9.8 %copy-start.49 = (f32[1,96]{1,0:T(1,128)S(1)}, f32[1,96]{1,0:T(1,128)}, u32[]{:S(2)}) copy-start(f32[1,96]{1,0:T(1,128)} %get-tuple-element.90) | copy-start | bytes 1156
  408.7 10.3 %copy-start.48 = (f32[1,96]{1,0:T(1,128)S(1)}, f32[1,96]{1,0:T(1,128)}, u32[]{:S(2)}) copy-start(f32[1,96]{1,0:T(1,128)} %get-tuple-element.91) | copy-start | bytes 1156
  (29 other events, 138.5 us)
Sparse Core Ops, SparseCore 0:
  125.3 62.4 all-gather.1
  190.1 58.8 reduce-scatter.2
  252.5 53.9 reduce-scatter.4

commit v11 on v10

--- a/solution.py
+++ b/solution.py
@@ -434,12 +434,12 @@
     def rise(k, s):
         t = jnp.maximum(q - k, 0)
         src = hid.at[s] if k == 0 else hv.at[t, s]
-        return send(src, hv.at[t, s], su.at[k, s], ru.at[k, s], (d, q + 1))
+        return send(src, hv.at[t, s], su.at[k, s], ru.at[k, s], (d, jnp.minimum(q + 1, ns - 1)))
 
     def sink(k, s):
         t = jnp.minimum(q + k, ns - 1)
         src = hid.at[s] if k == 0 else hv.at[t, s]
-        return send(src, hv.at[t, s], sd.at[k, s], rd.at[k, s], (d, q - 1))
+        return send(src, hv.at[t, s], sd.at[k, s], rd.at[k, s], (d, jnp.maximum(q - 1, 0)))
 
     def hop(k, s):
         @pl.when(q >= k)
@@ -816,10 +816,10 @@
                 gm[t, s, :, here] = full[s * sub:(s + 1) * sub]
 
     def rise(t, s, src):
-        return send(src, up.at[t, s], su.at[t, s], ru.at[t, s], (d, q + 1))
+        return send(src, up.at[t, s], su.at[t, s], ru.at[t, s], (d, jnp.minimum(q + 1, ns - 1)))
 
     def sink(t, s, src):
-        return send(src, down.at[t, s], sd.at[t, s], rd.at[t, s], (d, q - 1))
+        return send(src, down.at[t, s], sd.at[t, s], rd.at[t, s], (d, jnp.maximum(q - 1, 0)))
 
     def added(land, t, s):
         land[t, s] = (land[t, s].astype(F32) + gm[t, s].astype(F32)).astype(BF)

time: 434 us -> 435 us (level)
  no operation moved by 1% of the time
where the time goes in v11:
time: 435 us; the launch traced here: 426 us
  Pallas kernels  320 us (74%)
  other arithmetic  34.7 us (8%)
  matrix products  32.2 us (7%)
  local copies, waits for them, and re-layouts  17.8 us (4%)
  between operations  15.3 us (4%)
  waiting for transfers between devices  5.32 us (1%)
    pallas_call x1, Pallas kernels, end(): pl.pallas_call(functools.partial(end_kernel, nd, ns, nsub, rows, turned,...  92.4 us
    pallas_call x1, Pallas kernels, start(): pl.pallas_call(functools.partial(start_kernel, nd, ns, nsub, fused), out_...  91.5 us
    pallas_call x1, Pallas kernels, bwd_scan(): pl.pallas_call(bwd_kernel, grid=(blocks,), in_specs=[row_f, row_r, row_f,...  71.4 us
    pallas_call x1, Pallas kernels, fwd_scan(): pl.pallas_call(fwd_kernel, grid=(blocks,), in_specs=[row_f, row_r, row_f,...  34.9 us
    pallas_call x1, Pallas kernels, column_sum(): pl.pallas_call(functools.partial(column_sum_kernel, ns), out_shape=jax.Sh...  15.4 us
    pallas_call x1, Pallas kernels, column_grads(): pl.pallas_call(functools.partial(column_grads_kernel, ns), out_shape=jax....  14.9 us
    dot_general x3, matrix products, dot(): return jnp.dot(a, b, preferred_element_type=F32)  12.9 us
    unnamed x111, local copies, waits for them, and re-layouts  12.1 us
  transfers between devices with their start and end apart: 3, of which 1 were waited for; matrix products, arithmetic and copies ran while one was open for 14% of the time, Pallas kernels for 28%

profile of v11, /device:TPU:0, one launch (start us, length us, event | category | flops | bytes accessed | tf_op | source)
XLA Modules:
  0.0 426.3 jit_solution(18179967416359256578)
XLA Ops:
  9.9 91.5 %start.1 = (bf16[4,256,1536]{2,1,0:T(8,128)(2,1)}, bf16[4,256,1536]{2,1,0:T(8,128)(2,1)}, bf16[4,256,768]{2,1,0:T(8,128)(2,1)}, f32[4,256,768]{2,1,0:T(8,128)}, ...) custom-call(bf16[4,64,1536]{2,1,0:T(8,128)(2,1)} %bitcast.105, ...), custom_call_target="tpu_custom_call" | custom-call | tf_op jit(solution)/shard_map/start/pallas_call | solution.py:727
  101.4 1.7 slice_reduce_fusion.7
  103.8 1.8 convert_multiply_fusion.2
  105.6 3.2 multiply_convert_fusion.3
  109.5 15.4 %column_sum.1 = bf16[4,256,128]{2,1,0:T(8,128)(2,1)S(1)} custom-call(bf16[4,256,128]{2,1,0:T(8,128)(2,1)S(1)} %bitcast.104), custom_call_target="tpu_custom_call" | custom-call | tf_op jit(solution)/shard_map/column_sum/pallas_call | solution.py:302
  128.2 5.5 %convert_multiply_fusion.1 = (f32[1024,768]{1,0:T(8,128)}, f32[1024,768]{1,0:T(8,128)}) fusion(bf16[1024,768]{1,0:T(8,128)(2,1)S(1)} %get-tuple-element.111, f32[768]{0:T(1024)} %get-tuple-element.102, bf16[96,768]{1,0:T(8,128)(2,1)S(1)} %copy-done, bf16[1024,128]{0,1:T(8,128)(2,1)S(1)} %copy.34), kind=kOutput, calls=%fused_computation.4 | convolution fusion | flops 158072832 | bytes 8211456 | tf_op jit(solution)/shard_map/dot_general | solution.py:1137
  135.0 34.9 %fwd_scan.1 = (f32[1024,768]{1,0:T(8,128)}, f32[1024,768]{1,0:T(8,128)}, bf16[16384,768]{1,0:T(8,128)(2,1)}, bf16[16384,768]{1,0:T(8,128)(2,1)}) custom-call(f32[1024,768]{1,0:T(8,128)} %get-tuple-element.124.step_f.step_r, f32[1024,768]{1,0:T(8,128)} %get-tuple-element.124.step_f.step_r, f32[1024,768]{1,0:T(8,128)} %get-tuple-element.123.u_f.u_r, ...), custom_call_target="tpu_custom_call" | custom-call | flops 40265318400 | bytes 62914560 | tf_op jit(solution)/shard_map/fwd_scan/pallas_call | solution.py:104
  169.9 5.8 %multiply_convert_fusion.2 = (bf16[1024,768]{1,0:T(8,128)(2,1)S(1)}, f32[1024,768]{1,0:T(8,128)}) fusion(f32[4,256,768]{2,1,0:T(8,128)S(1)} %copy-done.13, f32[1024,768]{1,0:T(8,128)} %get-tuple-element.61, f32[1024,768]{1,0:T(8,128)} %get-tuple-element.62), kind=kLoop, calls=%fused_computation.29 | loop fusion | flops 5505024 | bytes 14155776 | tf_op jit(solution)/shard_map/convert_element_type | solution.py:1237
  176.8 5.7 %convolution_convert_fusion = bf16[1024,1536]{1,0:T(8,128)(2,1)} fusion(bf16[1024,768]{1,0:T(8,128)(2,1)S(1)} %get-tuple-element.109, bf16[1536,2304]{1,0:T(8,128)(2,1)} %get-tuple-element.64.wx_h), kind=kOutput, calls=%fused_computation.5 | convolution fusion | flops 2417491968 | bytes 7077888 | tf_op jit(solution)/shard_map/dot_general | solution.py:1141
  182.5 5.3 %all-gather.2.cloned.1.call-done = bf16[1024,1536]{1,0:T(8,128)(2,1)} async-done(((bf16[256,1536]{1,0:T(8,128)(2,1)}), bf16[1024,1536]{1,0:T(8,128)(2,1)}) %all-gather.2.cloned.1.call-update) | async-done | bytes 3145744 | tf_op jit(solution)/shard_map/all_gather | solution.py:1226
  189.1 2.8 multiply_convert_fusion
  191.9 3.0 convolution_convert_fusion.1
  194.9 6.8 %fusion.7 = (bf16[1024,768]{1,0:T(8,128)(2,1)S(1)}, f32[1024,768]{1,0:T(8,128)}) fusion(f32[4,256,768]{2,1,0:T(8,128)S(1)} %copy-done.13, f32[1024,768]{1,0:T(8,128)S(1)} %copy-done.14, bf16[1024,1536]{1,0:T(8,128)(2,1)S(1)} %multiply_convert_fusion, bf16[1536,2304]{1,0:T(8,128)(2,1)} %get-tuple-element.64.wx_h), kind=kOutput, calls=%fused_computation.24 | convolution fusion | flops 2425356288 | bytes 16515072 | tf_op jit(solution)/shard_map/dot_general | solution.py:1137
  202.9 3.0 convolution_convert_fusion.2
  205.9 2.5 pad_maximum_fusion
  208.4 71.4 %bwd_scan.1 = (f32[1024,768]{1,0:T(8,128)}, f32[1024,768]{1,0:T(8,128)}, f32[1024,768]{1,0:T(8,128)}, f32[1024,768]{1,0:T(8,128)}, f32[64,256]{1,0:T(8,128)}, /*...) custom-call(f32[1024,768]{1,0:T(8,128)} %get-tuple-element.124.step_f.ste, ...), custom_call_target="tpu_custom_call" | custom-call | flops 85563801600 | bytes 78643200 | tf_op jit(solution)/shard_map/bwd_scan/pallas_call | solution.py:242
  279.9 6.8 %fusion.33 = (f32[768]{0:T(1024)S(1)}, bf16[1024,768]{1,0:T(8,128)(2,1)S(1)}) fusion(f32[1024,768]{1,0:T(8,128)S(1)} %copy-done.12, f32[1024,768]{1,0:T(8,128)} %get-tuple-element.70, f32[1024,768]{1,0:T(8,128)} %get-tuple-element.71, bf16[1024,768]{1,0:T(8,128)(2,1)S(1)} %copy-done.6, f32[1024,768]{1,0:T(8,128)} %get-tuple-element.72, ...), kind=kLoop, calls=%fused_computation.86 | loop fusion | flops 8649984 | bytes 18877440 | tf_op jit(solution)/shard_map/reduce_sum | solution.py:1262
  287.3 14.9 %column_grads.1 = bf16[4,256,128]{2,1,0:T(8,128)(2,1)S(1)} custom-call(bf16[1024,768]{1,0:T(8,128)(2,1)S(1)} %get-tuple-element.108.pre_ref, bf16[96,768]{1,0:T(8,128)(2,1)S(1)} %copy-done, f32[64,256]{1,0:T(8,128)S(1)} %copy-done.1, f32[64,256]{1,0:T(8,128)S(1)} %copy-done.2, f32[64,256]{1,0:T(8,128)S(1)} %copy-done.3, f32[64,256]{1,0:T(8,128)S(1)} %copy-done.4), custom_call_target="tpu_custom_call" | custom-call | tf_op jit(solution)/shard_map/column_grads/pallas_call | solution.py:335
  304.8 4.1 bitcast_reduce_fusion
  308.9 2.9 multiply_convert_fusion.1.gi_h
  311.8 2.1 fusion.15.gate_ref
  313.9 2.4 fusion.18
  316.3 92.4 %end.1 = (f32[48,6144]{1,0:T(8,128)}, f32[48,3072]{1,0:T(8,128)}, f32[96,128]{1,0:T(8,128)}, f32[96,96]{1,0:T(8,128)}, f32[16,96]{1,0:T(8,128)}, /*index=5*/f32[...) custom-call(bf16[1024,768]{1,0:T(8,128)(2,1)} %multiply_convert_fusi, ...), custom_call_target="tpu_custom_call" | custom-call | tf_op jit(solution)/shard_map/end/pallas_call | solution.py:1091
  411.6 2.1 copy.48
  (144 shorter events, 23.2 us)
Async XLA Ops:
  7.2 180.6 %all-gather.2.cloned.1.call-start = ((), (), s32[]{:S(2)}) async-start(), calls=%async_computation.2 | async-start | bytes 3932160 | tf_op jit(solution)/shard_map/all_gather | solution.py:1226
  108.9 19.3 %copy-start.5 = (bf16[1024,768]{1,0:T(8,128)(2,1)}, bf16[1024,768]{1,0:T(8,128)(2,1)S(1)}, u32[]{:S(2)}) copy-start(bf16[1024,768]{1,0:T(8,128)(2,1)S(1)} %get-tuple-element.111) | copy-start | bytes 4718596
  108.9 17.4 %copy-start.26 = (f32[64,768]{1,0:T(8,128)S(1)}, f32[64,768]{1,0:T(8,128)}, u32[]{:S(2)}) copy-start(f32[64,768]{1,0:T(8,128)} %get-tuple-element.60.rates) | copy-start | bytes 589828
  109.5 18.7 %copy-start = (bf16[96,768]{1,0:T(8,128)(2,1)S(1)}, bf16[96,768]{1,0:T(8,128)(2,1)}, u32[]{:S(2)}) copy-start(bf16[96,768]{1,0:T(8,128)(2,1)} %get-tuple-element.59.step_ref) | copy-start | bytes 442372
  125.1 8.7 %copy-start.23 = (bf16[1024,128]{0,1:T(8,128)(2,1)}, bf16[1024,128]{0,1:T(8,128)(2,1)S(1)}, u32[]{:S(2)}) copy-start(bf16[1024,128]{0,1:T(8,128)(2,1)S(1)} %copy.34) | copy-start | bytes 786436
  125.1 186.7 %reduce-scatter.3.cloned.1.call-start = ((), (), s32[]{:S(2)}) async-start(), calls=%async_computation.3 | async-start | bytes 3932160 | tf_op jit(solution)/shard_map/reduce_scatter | solution.py:1240
  135.0 34.9 %copy-start.13 = (f32[4,256,768]{2,1,0:T(8,128)S(1)}, f32[4,256,768]{2,1,0:T(8,128)}, u32[]{:S(2)}) copy-start(f32[4,256,768]{2,1,0:T(8,128)} %get-tuple-element.63) | copy-start | bytes 9437188
  187.8 128.5 %reduce-scatter.5.cloned.1.call-start = ((), (), s32[]{:S(2)}) async-start(), calls=%async_computation.4 | async-start | bytes 5308416 | tf_op jit(solution)/shard_map/reduce_scatter | solution.py:1256
  194.9 8.0 %copy-start.17 = (bf16[4,256,1536]{2,1,0:T(8,128)(2,1)S(1)}, bf16[4,256,1536]{2,1,0:T(8,128)(2,1)}, u32[]{:S(2)}) copy-start(bf16[4,256,1536]{2,1,0:T(8,128)(2,1)} %get-tuple-element.78) | copy-start | bytes 9437188
  208.3 71.4 %copy-start.6 = (bf16[1024,768]{1,0:T(8,128)(2,1)S(1)}, bf16[1024,768]{1,0:T(8,128)(2,1)}, u32[]{:S(2)}) copy-start(bf16[1024,768]{1,0:T(8,128)(2,1)} %copy-done.5) | copy-start | bytes 4718596
  208.4 71.4 %copy-start.12 = (f32[1024,768]{1,0:T(8,128)S(1)}, f32[1024,768]{1,0:T(8,128)}, u32[]{:S(2)}) copy-start(f32[1024,768]{1,0:T(8,128)} %get-tuple-element.124.step_f.step_r) | copy-start | bytes 9437188
  279.8 7.5 %copy-start.1 = (f32[64,256]{1,0:T(8,128)S(1)}, f32[64,256]{1,0:T(8,128)}, u32[]{:S(2)}) copy-start(f32[64,256]{1,0:T(8,128)} %get-tuple-element.74.bf_ref) | copy-start | bytes 196612
  279.9 22.4 %copy-start.24 = (bf16[1024,128]{0,1:T(8,128)(2,1)S(1)}, bf16[1024,128]{0,1:T(8,128)(2,1)}, u32[]{:S(2)}) copy-start(bf16[1024,128]{0,1:T(8,128)(2,1)} %copy-done.23) | copy-start | bytes 786436
  279.9 24.9 %copy-start.15 = (f32[1024,768]{1,0:T(8,128)S(1)}, f32[1024,768]{1,0:T(8,128)}, u32[]{:S(2)}) copy-start(f32[1024,768]{1,0:T(8,128)} %get-tuple-element.70) | copy-start | bytes 9437188
  279.9 24.8 %copy-start.16 = (f32[1024,768]{1,0:T(8,128)S(1)}, f32[1024,768]{1,0:T(8,128)}, u32[]{:S(2)}) copy-start(f32[1024,768]{1,0:T(8,128)} %get-tuple-element.71) | copy-start | bytes 9437188
  279.9 24.8 %copy-start.21 = (bf16[4,256,768]{2,1,0:T(8,128)(2,1)S(1)}, bf16[4,256,768]{2,1,0:T(8,128)(2,1)}, u32[]{:S(2)}) copy-start(bf16[4,256,768]{2,1,0:T(8,128)(2,1)} %get-tuple-element.55) | copy-start | bytes 4718596
  287.3 17.4 %copy-start.8 = (f32[1024,768]{1,0:T(8,128)S(1)}, f32[1024,768]{1,0:T(8,128)}, u32[]{:S(2)}) copy-start(f32[1024,768]{1,0:T(8,128)} %copy-done.7) | copy-start | bytes 9437188
  287.3 17.4 %copy-start.11 = (f32[1024,768]{1,0:T(8,128)S(1)}, f32[1024,768]{1,0:T(8,128)}, u32[]{:S(2)}) copy-start(f32[1024,768]{1,0:T(8,128)} %get-tuple-element.112) | copy-start | bytes 9437188
  287.3 17.4 %copy-start.28 = (bf16[768,128]{1,0:T(8,128)(2,1)S(1)}, bf16[768,128]{1,0:T(8,128)(2,1)}, u32[]{:S(2)}) copy-start(bf16[768,128]{1,0:T(8,128)(2,1)} %get-tuple-element.57) | copy-start | bytes 589828
  408.7 8.0 %copy-start.44 = (f32[16,96]{1,0:T(8,128)S(1)}, f32[16,96]{1,0:T(8,128)}, u32[]{:S(2)}) copy-start(f32[16,96]{1,0:T(8,128)} %get-tuple-element.87) | copy-start | bytes 18436
  408.7 8.6 %copy-start.43 = (f32[16,96]{1,0:T(8,128)S(1)}, f32[16,96]{1,0:T(8,128)}, u32[]{:S(2)}) copy-start(f32[16,96]{1,0:T(8,128)} %get-tuple-element.88) | copy-start | bytes 18436
  408.7 9.2 %copy-start.46 = (f32[4,96]{1,0:T(4,128)S(1)}, f32[4,96]{1,0:T(4,128)}, u32[]{:S(2)}) copy-start(f32[4,96]{1,0:T(4,128)} %get-tuple-element.151) | copy-start | bytes 4612
  408.7 9.8 %copy-start.49 = (f32[1,96]{1,0:T(1,128)S(1)}, f32[1,96]{1,0:T(1,128)}, u32[]{:S(2)}) copy-start(f32[1,96]{1,0:T(1,128)} %get-tuple-element.90) | copy-start | bytes 1156
  408.7 10.3 %copy-start.48 = (f32[1,96]{1,0:T(1,128)S(1)}, f32[1,96]{1,0:T(1,128)}, u32[]{:S(2)}) copy-start(f32[1,96]{1,0:T(1,128)} %get-tuple-element.91) | copy-start | bytes 1156
  (29 other events, 138.6 us)
Sparse Core Ops, SparseCore 0:
  125.2 62.4 all-gather.1
  190.1 58.8 reduce-scatter.2
  252.5 53.9 reduce-scatter.4

commit v12 on v11

--- a/solution.py
+++ b/solution.py
@@ -945,10 +945,10 @@
         if i < nc - 1:
             second(c, chip).start()
             second_small(c, chip).start()
-        for k, s in steps[i:i + 1]:
+        for k, s in steps[2 * i:2 * i + 2]:
             step(k, s)
     late = len(steps) * 3 // 4
-    for k, s in steps[nc:late]:
+    for k, s in steps[2 * nc:late]:
         step(k, s)
 
     for c in chips:
@@ -978,7 +978,7 @@
     for t in others:
         third(t, q).start()
     fro[q] = pair[chip, q]
-    for k, s in steps[max(nc, late):]:
+    for k, s in steps[max(2 * nc, late):]:
         step(k, s)
 
     total = msg[...]
@@ -1069,7 +1069,7 @@
     cols = 2 * part
     width = wx.shape[0]
     inner = part * ns
-    nc, nsub = nd // 2, 4
+    nc, nsub = nd // 2, 8
     local = length // ns
     sub = local // nsub
     rw = rows + -rows % 16

time: 435 us -> 447 us (1.028)
  Pallas kernels: 320 us -> 333 us
    pallas_call x1, Pallas kernels: 92.4 us -> 104 us  [end(): pl.pallas_call(functools.partial(end_kernel, nd, ns, nsub, rows, turned,...]
where the time goes in v12:
time: 447 us; the launch traced here: 438 us
  Pallas kernels  333 us (74%)
  other arithmetic  34.7 us (8%)
  matrix products  32.2 us (7%)
  local copies, waits for them, and re-layouts  17.8 us (4%)
  between operations  15.5 us (3%)
  waiting for transfers between devices  5.36 us (1%)
    pallas_call x1, Pallas kernels, end(): pl.pallas_call(functools.partial(end_kernel, nd, ns, nsub, rows, turned,...  104 us
    pallas_call x1, Pallas kernels, start(): pl.pallas_call(functools.partial(start_kernel, nd, ns, nsub, fused), out_...  91.5 us
    pallas_call x1, Pallas kernels, bwd_scan(): pl.pallas_call(bwd_kernel, grid=(blocks,), in_specs=[row_f, row_r, row_f,...  71.5 us
    pallas_call x1, Pallas kernels, fwd_scan(): pl.pallas_call(fwd_kernel, grid=(blocks,), in_specs=[row_f, row_r, row_f,...  34.9 us
    pallas_call x1, Pallas kernels, column_sum(): pl.pallas_call(functools.partial(column_sum_kernel, ns), out_shape=jax.Sh...  15.3 us
    pallas_call x1, Pallas kernels, column_grads(): pl.pallas_call(functools.partial(column_grads_kernel, ns), out_shape=jax....  15 us
    dot_general x3, matrix products, dot(): return jnp.dot(a, b, preferred_element_type=F32)  13 us
    unnamed x111, local copies, waits for them, and re-layouts  12.1 us
  transfers between devices with their start and end apart: 3, of which 1 were waited for; matrix products, arithmetic and copies ran while one was open for 14% of the time, Pallas kernels for 28%

profile of v12, /device:TPU:0, one launch (start us, length us, event | category | flops | bytes accessed | tf_op | source)
XLA Modules:
  0.0 438.5 jit_solution(370358445365714571)
XLA Ops:
  9.9 91.5 %start.1 = (bf16[4,256,1536]{2,1,0:T(8,128)(2,1)}, bf16[4,256,1536]{2,1,0:T(8,128)(2,1)}, bf16[4,256,768]{2,1,0:T(8,128)(2,1)}, f32[4,256,768]{2,1,0:T(8,128)}, ...) custom-call(bf16[4,64,1536]{2,1,0:T(8,128)(2,1)} %bitcast.106, ...), custom_call_target="tpu_custom_call" | custom-call | tf_op jit(solution)/shard_map/start/pallas_call | solution.py:727
  101.4 1.7 slice_reduce_fusion.7
  103.8 1.8 convert_multiply_fusion.2
  105.6 3.2 multiply_convert_fusion.3
  109.5 15.3 %column_sum.1 = bf16[4,256,128]{2,1,0:T(8,128)(2,1)S(1)} custom-call(bf16[4,256,128]{2,1,0:T(8,128)(2,1)S(1)} %bitcast.105), custom_call_target="tpu_custom_call" | custom-call | tf_op jit(solution)/shard_map/column_sum/pallas_call | solution.py:302
  128.2 5.5 %convert_multiply_fusion.1 = (f32[1024,768]{1,0:T(8,128)}, f32[1024,768]{1,0:T(8,128)}) fusion(bf16[1024,768]{1,0:T(8,128)(2,1)S(1)} %get-tuple-element.111, f32[768]{0:T(1024)} %get-tuple-element.102, bf16[96,768]{1,0:T(8,128)(2,1)S(1)} %copy-done, bf16[1024,128]{0,1:T(8,128)(2,1)S(1)} %copy.34), kind=kOutput, calls=%fused_computation.4 | convolution fusion | flops 158072832 | bytes 8211456 | tf_op jit(solution)/shard_map/dot_general | solution.py:1137
  135.0 34.9 %fwd_scan.1 = (f32[1024,768]{1,0:T(8,128)}, f32[1024,768]{1,0:T(8,128)}, bf16[16384,768]{1,0:T(8,128)(2,1)}, bf16[16384,768]{1,0:T(8,128)(2,1)}) custom-call(f32[1024,768]{1,0:T(8,128)} %get-tuple-element.124.step_f.step_r, f32[1024,768]{1,0:T(8,128)} %get-tuple-element.124.step_f.step_r, f32[1024,768]{1,0:T(8,128)} %get-tuple-element.123.u_f.u_r, ...), custom_call_target="tpu_custom_call" | custom-call | flops 40265318400 | bytes 62914560 | tf_op jit(solution)/shard_map/fwd_scan/pallas_call | solution.py:104
  169.9 5.8 %multiply_convert_fusion.2 = (bf16[1024,768]{1,0:T(8,128)(2,1)S(1)}, f32[1024,768]{1,0:T(8,128)}) fusion(f32[4,256,768]{2,1,0:T(8,128)S(1)} %copy-done.13, f32[1024,768]{1,0:T(8,128)} %get-tuple-element.61, f32[1024,768]{1,0:T(8,128)} %get-tuple-element.62), kind=kLoop, calls=%fused_computation.29 | loop fusion | flops 5505024 | bytes 14155776 | tf_op jit(solution)/shard_map/convert_element_type | solution.py:1237
  176.8 5.7 %convolution_convert_fusion = bf16[1024,1536]{1,0:T(8,128)(2,1)} fusion(bf16[1024,768]{1,0:T(8,128)(2,1)S(1)} %get-tuple-element.109, bf16[1536,2304]{1,0:T(8,128)(2,1)} %get-tuple-element.64.wx_h), kind=kOutput, calls=%fused_computation.5 | convolution fusion | flops 2417491968 | bytes 7077888 | tf_op jit(solution)/shard_map/dot_general | solution.py:1141
  182.5 5.3 %all-gather.2.cloned.1.call-done = bf16[1024,1536]{1,0:T(8,128)(2,1)} async-done(((bf16[256,1536]{1,0:T(8,128)(2,1)}), bf16[1024,1536]{1,0:T(8,128)(2,1)}) %all-gather.2.cloned.1.call-update) | async-done | bytes 3145744 | tf_op jit(solution)/shard_map/all_gather | solution.py:1226
  188.9 2.8 multiply_convert_fusion
  191.7 3.0 convolution_convert_fusion.1
  194.6 6.9 %fusion.7 = (bf16[1024,768]{1,0:T(8,128)(2,1)S(1)}, f32[1024,768]{1,0:T(8,128)}) fusion(f32[4,256,768]{2,1,0:T(8,128)S(1)} %copy-done.13, f32[1024,768]{1,0:T(8,128)S(1)} %copy-done.14, bf16[1024,1536]{1,0:T(8,128)(2,1)S(1)} %multiply_convert_fusion, bf16[1536,2304]{1,0:T(8,128)(2,1)} %get-tuple-element.64.wx_h), kind=kOutput, calls=%fused_computation.24 | convolution fusion | flops 2425356288 | bytes 16515072 | tf_op jit(solution)/shard_map/dot_general | solution.py:1137
  202.7 2.9 convolution_convert_fusion.2
  205.7 2.5 pad_maximum_fusion
  208.2 71.5 %bwd_scan.1 = (f32[1024,768]{1,0:T(8,128)}, f32[1024,768]{1,0:T(8,128)}, f32[1024,768]{1,0:T(8,128)}, f32[1024,768]{1,0:T(8,128)}, f32[64,256]{1,0:T(8,128)}, /*...) custom-call(f32[1024,768]{1,0:T(8,128)} %get-tuple-element.124.step_f.ste, ...), custom_call_target="tpu_custom_call" | custom-call | flops 85563801600 | bytes 78643200 | tf_op jit(solution)/shard_map/bwd_scan/pallas_call | solution.py:242
  279.8 6.8 %fusion.33 = (f32[768]{0:T(1024)S(1)}, bf16[1024,768]{1,0:T(8,128)(2,1)S(1)}) fusion(f32[1024,768]{1,0:T(8,128)S(1)} %copy-done.12, f32[1024,768]{1,0:T(8,128)} %get-tuple-element.70, f32[1024,768]{1,0:T(8,128)} %get-tuple-element.71, bf16[1024,768]{1,0:T(8,128)(2,1)S(1)} %copy-done.6, f32[1024,768]{1,0:T(8,128)} %get-tuple-element.72, ...), kind=kLoop, calls=%fused_computation.86 | loop fusion | flops 8649984 | bytes 18877440 | tf_op jit(solution)/shard_map/reduce_sum | solution.py:1262
  287.2 15.0 %column_grads.1 = bf16[4,256,128]{2,1,0:T(8,128)(2,1)S(1)} custom-call(bf16[1024,768]{1,0:T(8,128)(2,1)S(1)} %get-tuple-element.108.pre_ref, bf16[96,768]{1,0:T(8,128)(2,1)S(1)} %copy-done, f32[64,256]{1,0:T(8,128)S(1)} %copy-done.1, f32[64,256]{1,0:T(8,128)S(1)} %copy-done.2, f32[64,256]{1,0:T(8,128)S(1)} %copy-done.3, f32[64,256]{1,0:T(8,128)S(1)} %copy-done.4), custom_call_target="tpu_custom_call" | custom-call | tf_op jit(solution)/shard_map/column_grads/pallas_call | solution.py:335
  304.7 4.1 bitcast_reduce_fusion
  308.9 2.9 multiply_convert_fusion.1.gi_h
  311.8 2.1 fusion.15.gate_ref
  313.8 2.4 fusion.18
  316.2 104.4 %end.1 = (f32[48,6144]{1,0:T(8,128)}, f32[48,3072]{1,0:T(8,128)}, f32[96,128]{1,0:T(8,128)}, f32[96,96]{1,0:T(8,128)}, f32[16,96]{1,0:T(8,128)}, /*index=5*/f32[...) custom-call(bf16[1024,768]{1,0:T(8,128)(2,1)} %multiply_convert_fusi, ...), custom_call_target="tpu_custom_call" | custom-call | tf_op jit(solution)/shard_map/end/pallas_call | solution.py:1091
  423.5 2.1 copy.48
  (144 shorter events, 23.0 us)
Async XLA Ops:
  7.2 180.6 %all-gather.2.cloned.1.call-start = ((), (), s32[]{:S(2)}) async-start(), calls=%async_computation.2 | async-start | bytes 3932160 | tf_op jit(solution)/shard_map/all_gather | solution.py:1226
  108.9 19.2 %copy-start.5 = (bf16[1024,768]{1,0:T(8,128)(2,1)}, bf16[1024,768]{1,0:T(8,128)(2,1)S(1)}, u32[]{:S(2)}) copy-start(bf16[1024,768]{1,0:T(8,128)(2,1)S(1)} %get-tuple-element.111) | copy-start | bytes 4718596
  108.9 17.4 %copy-start.26 = (f32[64,768]{1,0:T(8,128)S(1)}, f32[64,768]{1,0:T(8,128)}, u32[]{:S(2)}) copy-start(f32[64,768]{1,0:T(8,128)} %get-tuple-element.60.rates) | copy-start | bytes 589828
  109.5 18.6 %copy-start = (bf16[96,768]{1,0:T(8,128)(2,1)S(1)}, bf16[96,768]{1,0:T(8,128)(2,1)}, u32[]{:S(2)}) copy-start(bf16[96,768]{1,0:T(8,128)(2,1)} %get-tuple-element.59.step_ref) | copy-start | bytes 442372
  125.0 8.7 %copy-start.23 = (bf16[1024,128]{0,1:T(8,128)(2,1)}, bf16[1024,128]{0,1:T(8,128)(2,1)S(1)}, u32[]{:S(2)}) copy-start(bf16[1024,128]{0,1:T(8,128)(2,1)S(1)} %copy.34) | copy-start | bytes 786436
  125.1 186.7 %reduce-scatter.3.cloned.1.call-start = ((), (), s32[]{:S(2)}) async-start(), calls=%async_computation.3 | async-start | bytes 3932160 | tf_op jit(solution)/shard_map/reduce_scatter | solution.py:1240
  135.0 34.9 %copy-start.13 = (f32[4,256,768]{2,1,0:T(8,128)S(1)}, f32[4,256,768]{2,1,0:T(8,128)}, u32[]{:S(2)}) copy-start(f32[4,256,768]{2,1,0:T(8,128)} %get-tuple-element.63) | copy-start | bytes 9437188
  187.8 128.4 %reduce-scatter.5.cloned.1.call-start = ((), (), s32[]{:S(2)}) async-start(), calls=%async_computation.4 | async-start | bytes 5308416 | tf_op jit(solution)/shard_map/reduce_scatter | solution.py:1256
  194.6 8.1 %copy-start.17 = (bf16[4,256,1536]{2,1,0:T(8,128)(2,1)S(1)}, bf16[4,256,1536]{2,1,0:T(8,128)(2,1)}, u32[]{:S(2)}) copy-start(bf16[4,256,1536]{2,1,0:T(8,128)(2,1)} %get-tuple-element.78) | copy-start | bytes 9437188
  208.2 71.5 %copy-start.6 = (bf16[1024,768]{1,0:T(8,128)(2,1)S(1)}, bf16[1024,768]{1,0:T(8,128)(2,1)}, u32[]{:S(2)}) copy-start(bf16[1024,768]{1,0:T(8,128)(2,1)} %copy-done.5) | copy-start | bytes 4718596
  208.2 71.5 %copy-start.12 = (f32[1024,768]{1,0:T(8,128)S(1)}, f32[1024,768]{1,0:T(8,128)}, u32[]{:S(2)}) copy-start(f32[1024,768]{1,0:T(8,128)} %get-tuple-element.124.step_f.step_r) | copy-start | bytes 9437188
  279.7 7.5 %copy-start.1 = (f32[64,256]{1,0:T(8,128)S(1)}, f32[64,256]{1,0:T(8,128)}, u32[]{:S(2)}) copy-start(f32[64,256]{1,0:T(8,128)} %get-tuple-element.74.bf_ref) | copy-start | bytes 196612
  279.7 22.5 %copy-start.24 = (bf16[1024,128]{0,1:T(8,128)(2,1)S(1)}, bf16[1024,128]{0,1:T(8,128)(2,1)}, u32[]{:S(2)}) copy-start(bf16[1024,128]{0,1:T(8,128)(2,1)} %copy-done.23) | copy-start | bytes 786436
  279.7 24.9 %copy-start.15 = (f32[1024,768]{1,0:T(8,128)S(1)}, f32[1024,768]{1,0:T(8,128)}, u32[]{:S(2)}) copy-start(f32[1024,768]{1,0:T(8,128)} %get-tuple-element.70) | copy-start | bytes 9437188
  279.7 24.9 %copy-start.16 = (f32[1024,768]{1,0:T(8,128)S(1)}, f32[1024,768]{1,0:T(8,128)}, u32[]{:S(2)}) copy-start(f32[1024,768]{1,0:T(8,128)} %get-tuple-element.71) | copy-start | bytes 9437188
  279.7 24.9 %copy-start.21 = (bf16[4,256,768]{2,1,0:T(8,128)(2,1)S(1)}, bf16[4,256,768]{2,1,0:T(8,128)(2,1)}, u32[]{:S(2)}) copy-start(bf16[4,256,768]{2,1,0:T(8,128)(2,1)} %get-tuple-element.55) | copy-start | bytes 4718596
  287.2 17.5 %copy-start.8 = (f32[1024,768]{1,0:T(8,128)S(1)}, f32[1024,768]{1,0:T(8,128)}, u32[]{:S(2)}) copy-start(f32[1024,768]{1,0:T(8,128)} %copy-done.7) | copy-start | bytes 9437188
  287.2 17.5 %copy-start.11 = (f32[1024,768]{1,0:T(8,128)S(1)}, f32[1024,768]{1,0:T(8,128)}, u32[]{:S(2)}) copy-start(f32[1024,768]{1,0:T(8,128)} %get-tuple-element.112) | copy-start | bytes 9437188
  287.2 17.5 %copy-start.28 = (bf16[768,128]{1,0:T(8,128)(2,1)S(1)}, bf16[768,128]{1,0:T(8,128)(2,1)}, u32[]{:S(2)}) copy-start(bf16[768,128]{1,0:T(8,128)(2,1)} %get-tuple-element.57) | copy-start | bytes 589828
  420.7 8.0 %copy-start.44 = (f32[16,96]{1,0:T(8,128)S(1)}, f32[16,96]{1,0:T(8,128)}, u32[]{:S(2)}) copy-start(f32[16,96]{1,0:T(8,128)} %get-tuple-element.87) | copy-start | bytes 18436
  420.7 8.6 %copy-start.43 = (f32[16,96]{1,0:T(8,128)S(1)}, f32[16,96]{1,0:T(8,128)}, u32[]{:S(2)}) copy-start(f32[16,96]{1,0:T(8,128)} %get-tuple-element.88) | copy-start | bytes 18436
  420.7 9.2 %copy-start.46 = (f32[4,96]{1,0:T(4,128)S(1)}, f32[4,96]{1,0:T(4,128)}, u32[]{:S(2)}) copy-start(f32[4,96]{1,0:T(4,128)} %get-tuple-element.151) | copy-start | bytes 4612
  420.7 9.8 %copy-start.49 = (f32[1,96]{1,0:T(1,128)S(1)}, f32[1,96]{1,0:T(1,128)}, u32[]{:S(2)}) copy-start(f32[1,96]{1,0:T(1,128)} %get-tuple-element.90) | copy-start | bytes 1156
  420.7 10.3 %copy-start.48 = (f32[1,96]{1,0:T(1,128)S(1)}, f32[1,96]{1,0:T(1,128)}, u32[]{:S(2)}) copy-start(f32[1,96]{1,0:T(1,128)} %get-tuple-element.91) | copy-start | bytes 1156
  (29 other events, 134.9 us)
Sparse Core Ops, SparseCore 0:
  125.2 62.5 all-gather.1
  190.1 58.8 reduce-scatter.2
  252.4 53.8 reduce-scatter.4
